TPU v7x, 32 devices: a whole 2x2x4 slice. The times are simulated.
32 devices in a mesh: dp: 4 (over y, x), fsdp: 8 (over z, core).
Axes of the slice: x: 2, y: 2, z: 4, core: 2. Of those that a mesh axis runs over, the one named last changes fastest.
Arguments:
- tokens: bfloat16 [2, 96, 128, 768], P(None, ('dp', 'fsdp')), may hold values from -6 to 6
- timesteps: int32 [2, 96], P(None, ('dp', 'fsdp')), may hold values from 0 to 999
- segments: int32 [2, 96, 128], P(None, ('dp', 'fsdp')), may hold values from 0 to 7, never falling along the last dimension, each value on 1 to 32 neighbouring positions
- padding: int32 [2, 96, 128], P(None, ('dp', 'fsdp')), may hold values 0 or 1
- cotangent: bfloat16 [2, 96, 128, 768], P(None, ('dp', 'fsdp')), may hold values from -6 to 6
- step_table: bfloat16 [1000, 768], P(None, 'fsdp'), may hold values from -6 to 6
- triple_weight: bfloat16 [768, 2304], P('fsdp'), may hold values from -0.21875 to 0.21875
- query_bias: bfloat16 [768], P('fsdp'), may hold values from -3 to 3
- value_bias: bfloat16 [768], P('fsdp'), may hold values from -3 to 3
- output_weight: bfloat16 [768, 768], P('fsdp'), may hold values from -0.875 to 0.875
- output_bias: bfloat16 [768], P('fsdp'), may hold values from -3 to 3
- first_gain: bfloat16 [768], P('fsdp'), may hold values from 0.5 to 1.5
- first_shift: bfloat16 [768], P('fsdp'), may hold values from -3 to 3
- second_gain: bfloat16 [768], P('fsdp'), may hold values from 0.5 to 1.5
- second_shift: bfloat16 [768], P('fsdp'), may hold values from -3 to 3
- hidden_weight: bfloat16 [768, 3072], P('fsdp'), may hold values from -0.21875 to 0.21875
- hidden_bias: bfloat16 [3072], P('fsdp'), may hold values from -3 to 3
- down_weight: bfloat16 [3072, 768], P('fsdp'), may hold values from -0.109375 to 0.109375
- down_bias: bfloat16 [768], P('fsdp'), may hold values from -3 to 3
Outputs:
- result_rows: bfloat16 [2, 96, 128, 768], P(None, ('dp', 'fsdp'))
- input_grad: bfloat16 [2, 96, 128, 768], P(None, ('dp', 'fsdp'))
- table_grad: float32 [1000, 768], P(None, 'fsdp')
- triple_grad: float32 [768, 2304], P('fsdp')
- query_bias_grad: float32 [768], P('fsdp')
- value_bias_grad: float32 [768], P('fsdp')
- output_weight_grad: float32 [768, 768], P('fsdp')
- output_bias_grad: float32 [768], P('fsdp')
- first_gain_grad: float32 [768], P('fsdp')
- first_shift_grad: float32 [768], P('fsdp')
- second_gain_grad: float32 [768], P('fsdp')
- second_shift_grad: float32 [768], P('fsdp')
- hidden_weight_grad: float32 [768, 3072], P('fsdp')
- hidden_bias_grad: float32 [3072], P('fsdp')
- down_weight_grad: float32 [3072, 768], P('fsdp')
- down_bias_grad: float32 [768], P('fsdp')
Inputs may be any that keep to these rules, and one draw needn't show every extreme that they name: `segments`: within each row of 128 tokens the numbers never fall; each sentence holds 1 to 32 tokens. 1 marks a padding token.
All inputs are finite; a program needn't handle non-finite values. No bound on the sum of `padding` on one device may be relied on, other than what follows from the above.
Results may differ from a plain program's by a relative error of at most 0.012.
The roundings to bfloat16 on the way count: a program that leaves them out, or rounds other values in their place, can miss the bound.
Values may be sent and summed in bfloat16 or wider, within the bound.
No kernel may reach another device: no remote copies, remote signals or barrier semaphores. Data moves between devices by JAX's collectives and lax.ppermute only.
A program may use at most 192 MiB of HBM per device.

v0:
```python
import math

import jax
import jax.numpy as jnp
from jax import lax
from jax.sharding import PartitionSpec as P

HEADS = 12
HD = 64


highest = lax.Precision.HIGHEST
norm_eps = 1e-05
masked_score = -1e30


def layer_norm(values, gain, shift):
    average = jnp.mean(values, axis=-1, keepdims=True)
    centered = values - average
    variance = jnp.mean(centered * centered, axis=-1, keepdims=True)
    return centered * lax.rsqrt(variance + norm_eps) * gain + shift


def smooth_gate(values):
    return jax.nn.gelu(values, approximate=True)


def forward_pass(gathered, tokens_part, steps_part, segment_part, padding_part):
    (
        table_full,
        triple_full,
        query_add,
        value_add,
        output_full,
        output_add,
        first_scale,
        first_offset,
        second_scale,
        second_offset,
        hidden_full,
        hidden_add,
        down_full,
        down_add,
    ) = gathered
    row_count, length, model_width = tokens_part.shape
    token_count = row_count * length
    table_ids = lax.iota(jnp.int32, table_full.shape[0])
    onehot = (steps_part[:, None] == table_ids[None, :]).astype(jnp.bfloat16)
    row_embed = jnp.dot(onehot, table_full, preferred_element_type=jnp.float32)
    residual_in = (tokens_part.astype(jnp.float32) + row_embed[:, None, :]).reshape(
        token_count, model_width
    )
    normed = layer_norm(
        residual_in, first_scale.astype(jnp.float32), first_offset.astype(jnp.float32)
    )
    normed = normed.astype(jnp.bfloat16)
    triple = jnp.dot(normed, triple_full, preferred_element_type=jnp.float32)
    zero_keys = jnp.zeros((model_width,), jnp.float32)
    triple_add = jnp.concatenate(
        [query_add.astype(jnp.float32), zero_keys, value_add.astype(jnp.float32)]
    )
    heads = (triple + triple_add).astype(jnp.bfloat16).reshape(row_count, length, 3, HEADS, HD)
    queries = heads[:, :, 0]
    key_heads = heads[:, :, 1]
    values = heads[:, :, 2]
    positions = lax.iota(jnp.int32, length)
    diagonal = positions[:, None] == positions[None, :]
    same_segment = segment_part[:, :, None] == segment_part[:, None, :]
    allowed = same_segment & ((padding_part[:, None, :] == 0) | diagonal[None])
    score_scale = 1.0 / math.sqrt(HD)
    scores = (
        jnp.einsum("rqhd,rkhd->rhqk", queries, key_heads, preferred_element_type=jnp.float32)
        * score_scale
    )
    scores = jnp.where(allowed[:, None], scores, masked_score)
    largest = jnp.max(scores, axis=-1, keepdims=True)
    exponent = jnp.exp(scores - largest)
    attention = exponent / jnp.sum(exponent, axis=-1, keepdims=True)
    attention_low = attention.astype(jnp.bfloat16)
    attended = jnp.einsum(
        "rhqk,rkhd->rqhd", attention_low, values, preferred_element_type=jnp.float32
    )
    attended = attended.reshape(token_count, model_width).astype(jnp.bfloat16)
    branch = jnp.dot(attended, output_full, preferred_element_type=jnp.float32) + output_add.astype(
        jnp.float32
    )
    middle = residual_in + branch
    normed_two = layer_norm(
        middle, second_scale.astype(jnp.float32), second_offset.astype(jnp.float32)
    )
    normed_two = normed_two.astype(jnp.bfloat16)
    hidden = jnp.dot(
        normed_two, hidden_full, preferred_element_type=jnp.float32
    ) + hidden_add.astype(jnp.float32)
    active = smooth_gate(hidden).astype(jnp.bfloat16)
    down_part = jnp.dot(active, down_full, preferred_element_type=jnp.float32) + down_add.astype(
        jnp.float32
    )
    result = (middle + down_part).reshape(tokens_part.shape).astype(jnp.bfloat16)
    kept_values = (
        onehot,
        residual_in,
        normed,
        heads,
        attention,
        attention_low,
        attended,
        middle,
        normed_two,
        hidden,
        active,
    )
    return (result, kept_values)


def backward_pass(gathered, kept_values, cotangent_part):
    (
        table_full,
        triple_full,
        query_add,
        value_add,
        output_full,
        output_add,
        first_scale,
        first_offset,
        second_scale,
        second_offset,
        hidden_full,
        hidden_add,
        down_full,
        down_add,
    ) = gathered
    (
        onehot,
        residual_in,
        normed,
        heads,
        attention,
        attention_low,
        attended,
        middle,
        normed_two,
        hidden,
        active,
    ) = kept_values
    row_count, length, model_width = cotangent_part.shape
    token_count = row_count * length
    d_down = cotangent_part.reshape(token_count, model_width)
    down_bias_sum = jnp.sum(d_down.astype(jnp.float32), axis=0)
    down_grad = jnp.einsum("nf,nd->fd", active, d_down, preferred_element_type=jnp.float32)
    d_active = jnp.einsum("nd,fd->nf", d_down, down_full, preferred_element_type=jnp.float32)
    unused_gate, gate_pull = jax.vjp(smooth_gate, hidden)
    d_hidden = gate_pull(d_active)[0].astype(jnp.bfloat16)
    hidden_grad = jnp.einsum("nd,nf->df", normed_two, d_hidden, preferred_element_type=jnp.float32)
    hidden_bias_sum = jnp.sum(d_hidden.astype(jnp.float32), axis=0)
    d_normed_two = jnp.einsum(
        "nf,df->nd", d_hidden, hidden_full, preferred_element_type=jnp.float32
    )
    unused_second, second_pull = jax.vjp(
        layer_norm, middle, second_scale.astype(jnp.float32), second_offset.astype(jnp.float32)
    )
    d_middle_norm, second_gain_sum, second_shift_sum = second_pull(d_normed_two)
    d_middle = d_down.astype(jnp.float32) + d_middle_norm
    d_branch = d_middle.astype(jnp.bfloat16)
    output_grad = jnp.einsum("nc,nd->cd", attended, d_branch, preferred_element_type=jnp.float32)
    output_bias_sum = jnp.sum(d_branch.astype(jnp.float32), axis=0)
    d_attended = jnp.einsum("nd,cd->nc", d_branch, output_full, preferred_element_type=jnp.float32)
    d_attended = d_attended.astype(jnp.bfloat16).reshape(row_count, length, HEADS, HD)
    queries = heads[:, :, 0]
    key_heads = heads[:, :, 1]
    values = heads[:, :, 2]
    d_attention = jnp.einsum(
        "rqhd,rkhd->rhqk", d_attended, values, preferred_element_type=jnp.float32
    )
    d_values = jnp.einsum(
        "rhqk,rqhd->rkhd", attention_low, d_attended, preferred_element_type=jnp.float32
    )
    inner_sum = jnp.sum(attention * d_attention, axis=-1, keepdims=True)
    d_scores = (attention * (d_attention - inner_sum)).astype(jnp.bfloat16)
    score_scale = 1.0 / math.sqrt(HD)
    d_queries = (
        jnp.einsum("rhqk,rkhd->rqhd", d_scores, key_heads, preferred_element_type=jnp.float32)
        * score_scale
    )
    d_keys = (
        jnp.einsum("rhqk,rqhd->rkhd", d_scores, queries, preferred_element_type=jnp.float32)
        * score_scale
    )
    d_triple = jnp.stack([d_queries, d_keys, d_values], axis=2)
    d_triple = d_triple.reshape(token_count, 3 * model_width).astype(jnp.bfloat16)
    triple_grad = jnp.einsum("nd,ne->de", normed, d_triple, preferred_element_type=jnp.float32)
    triple_sums = jnp.sum(d_triple.astype(jnp.float32), axis=0)
    query_bias_sum = triple_sums[:model_width]
    value_bias_sum = triple_sums[2 * model_width :]
    d_normed = jnp.einsum("ne,de->nd", d_triple, triple_full, preferred_element_type=jnp.float32)
    unused_first, first_pull = jax.vjp(
        layer_norm, residual_in, first_scale.astype(jnp.float32), first_offset.astype(jnp.float32)
    )
    d_start_norm, first_gain_sum, first_shift_sum = first_pull(d_normed)
    d_start = d_middle + d_start_norm
    row_sums = jnp.sum(d_start.reshape(row_count, length, model_width), axis=1)
    input_grad = d_start.reshape(cotangent_part.shape).astype(jnp.bfloat16)
    grads = (
        triple_grad,
        query_bias_sum,
        value_bias_sum,
        output_grad,
        output_bias_sum,
        first_gain_sum,
        first_shift_sum,
        second_gain_sum,
        second_shift_sum,
        hidden_grad,
        hidden_bias_sum,
        down_grad,
        down_bias_sum,
    )
    return (input_grad, row_sums, grads)


def per_device(
    tokens,
    timesteps,
    segments,
    padding,
    cotangent,
    step_table,
    triple_weight,
    query_bias,
    value_bias,
    output_weight,
    output_bias,
    first_gain,
    first_shift,
    second_gain,
    second_shift,
    hidden_weight,
    hidden_bias,
    down_weight,
    down_bias,
):
    totals = None
    row_outputs = []
    input_grads = []
    for micro_index in range(tokens.shape[0]):
        gathered = (
            lax.all_gather(step_table, "fsdp", axis=1, tiled=True),
            lax.all_gather(triple_weight, "fsdp", axis=0, tiled=True),
            lax.all_gather(query_bias, "fsdp", axis=0, tiled=True),
            lax.all_gather(value_bias, "fsdp", axis=0, tiled=True),
            lax.all_gather(output_weight, "fsdp", axis=0, tiled=True),
            lax.all_gather(output_bias, "fsdp", axis=0, tiled=True),
            lax.all_gather(first_gain, "fsdp", axis=0, tiled=True),
            lax.all_gather(first_shift, "fsdp", axis=0, tiled=True),
            lax.all_gather(second_gain, "fsdp", axis=0, tiled=True),
            lax.all_gather(second_shift, "fsdp", axis=0, tiled=True),
            lax.all_gather(hidden_weight, "fsdp", axis=0, tiled=True),
            lax.all_gather(hidden_bias, "fsdp", axis=0, tiled=True),
            lax.all_gather(down_weight, "fsdp", axis=0, tiled=True),
            lax.all_gather(down_bias, "fsdp", axis=0, tiled=True),
        )
        result, kept_values = forward_pass(
            gathered,
            tokens[micro_index],
            timesteps[micro_index],
            segments[micro_index],
            padding[micro_index],
        )
        gathered = (
            lax.all_gather(step_table, "fsdp", axis=1, tiled=True),
            lax.all_gather(triple_weight, "fsdp", axis=0, tiled=True),
            lax.all_gather(query_bias, "fsdp", axis=0, tiled=True),
            lax.all_gather(value_bias, "fsdp", axis=0, tiled=True),
            lax.all_gather(output_weight, "fsdp", axis=0, tiled=True),
            lax.all_gather(output_bias, "fsdp", axis=0, tiled=True),
            lax.all_gather(first_gain, "fsdp", axis=0, tiled=True),
            lax.all_gather(first_shift, "fsdp", axis=0, tiled=True),
            lax.all_gather(second_gain, "fsdp", axis=0, tiled=True),
            lax.all_gather(second_shift, "fsdp", axis=0, tiled=True),
            lax.all_gather(hidden_weight, "fsdp", axis=0, tiled=True),
            lax.all_gather(hidden_bias, "fsdp", axis=0, tiled=True),
            lax.all_gather(down_weight, "fsdp", axis=0, tiled=True),
            lax.all_gather(down_bias, "fsdp", axis=0, tiled=True),
        )
        unused_result, kept_values = forward_pass(
            gathered,
            tokens[micro_index],
            timesteps[micro_index],
            segments[micro_index],
            padding[micro_index],
        )
        input_grad, row_sums, grads = backward_pass(gathered, kept_values, cotangent[micro_index])
        table_sum = jnp.einsum(
            "rt,rd->td", kept_values[0].astype(jnp.float32), row_sums, precision=highest
        )
        shares = (
            lax.psum_scatter(table_sum, "fsdp", scatter_dimension=1, tiled=True),
            lax.psum_scatter(grads[0], "fsdp", scatter_dimension=0, tiled=True),
            lax.psum_scatter(grads[1], "fsdp", scatter_dimension=0, tiled=True),
            lax.psum_scatter(grads[2], "fsdp", scatter_dimension=0, tiled=True),
            lax.psum_scatter(grads[3], "fsdp", scatter_dimension=0, tiled=True),
            lax.psum_scatter(grads[4], "fsdp", scatter_dimension=0, tiled=True),
            lax.psum_scatter(grads[5], "fsdp", scatter_dimension=0, tiled=True),
            lax.psum_scatter(grads[6], "fsdp", scatter_dimension=0, tiled=True),
            lax.psum_scatter(grads[7], "fsdp", scatter_dimension=0, tiled=True),
            lax.psum_scatter(grads[8], "fsdp", scatter_dimension=0, tiled=True),
            lax.psum_scatter(grads[9], "fsdp", scatter_dimension=0, tiled=True),
            lax.psum_scatter(grads[10], "fsdp", scatter_dimension=0, tiled=True),
            lax.psum_scatter(grads[11], "fsdp", scatter_dimension=0, tiled=True),
            lax.psum_scatter(grads[12], "fsdp", scatter_dimension=0, tiled=True),
        )
        totals = shares if totals is None else jax.tree.map(jnp.add, totals, shares)
        row_outputs.append(result)
        input_grads.append(input_grad)
    totals = lax.psum(
        (
            totals[0],
            totals[1],
            totals[2],
            totals[3],
            totals[4],
            totals[5],
            totals[6],
            totals[7],
            totals[8],
            totals[9],
            totals[10],
            totals[11],
            totals[12],
            totals[13],
        ),
        "dp",
    )
    return (
        jnp.stack(row_outputs),
        jnp.stack(input_grads),
        totals[0],
        totals[1],
        totals[2],
        totals[3],
        totals[4],
        totals[5],
        totals[6],
        totals[7],
        totals[8],
        totals[9],
        totals[10],
        totals[11],
        totals[12],
        totals[13],
    )


def solution(mesh):
    placed = (
        P(None, ("dp", "fsdp"), None, None),
        P(None, ("dp", "fsdp")),
        P(None, ("dp", "fsdp"), None),
        P(None, ("dp", "fsdp"), None),
        P(None, ("dp", "fsdp"), None, None),
        P(None, "fsdp"),
        P("fsdp", None),
        P("fsdp"),
        P("fsdp"),
        P("fsdp", None),
        P("fsdp"),
        P("fsdp"),
        P("fsdp"),
        P("fsdp"),
        P("fsdp"),
        P("fsdp", None),
        P("fsdp"),
        P("fsdp", None),
        P("fsdp"),
    )
    return jax.shard_map(
        per_device,
        mesh=mesh,
        in_specs=placed,
        out_specs=(
            P(None, ("dp", "fsdp"), None, None),
            P(None, ("dp", "fsdp"), None, None),
            P(None, "fsdp"),
            P("fsdp", None),
            P("fsdp"),
            P("fsdp"),
            P("fsdp", None),
            P("fsdp"),
            P("fsdp"),
            P("fsdp"),
            P("fsdp"),
            P("fsdp"),
            P("fsdp", None),
            P("fsdp"),
            P("fsdp", None),
            P("fsdp"),
        ),
        check_vma=False,
    )
```

profile of v0, /device:TPU:0, one launch (start us, length us, event | category | flops | bytes accessed | tf_op | source)
XLA Modules:
  0.0 736.8 jit_solution(1958575253571672371)
XLA Ops:
  14.0 30.5 %all-reduce.20 = (bf16[768]{0:T(1024)(128)(2,1)S(1)}, bf16[768]{0:T(1024)(128)(2,1)S(1)}, bf16[768]{0:T(1024)(128)(2,1)S(1)}, bf16[768]{0:T(1024)(128)(2,1)S(1)}...) all-reduce(bf16[768]{0:T(1024)(128)(2,1)S(1)} %dynamic-update-slice, ...), channel_id=1, replica_groups=mesh['dp'=4,'fsdp'=8] {'fsdp'}, use_global_device_ids=true, to_apply=%add.4 | all-reduce | flops 6144 | bytes 24576
  45.2 13.0 %all-gather = bf16[8,1,384]{2,1,0:T(2,128)(2,1)S(1)} all-gather(bf16[1,1,384]{2,1,0:T(2,128)(2,1)S(1)} %reshape.586), channel_id=1, replica_groups=mesh['dp'=4,'fsdp'=8] {'fsdp'}, dimensions={0}, use_global_device_ids=true | all-gather | bytes 6912 | tf_op jit(solution)/shard_map/all_gather | solution.py:258
  69.0 11.7 %all-gather.9.cloned.1.call-done = bf16[768,2304]{1,0:T(8,128)(2,1)} async-done(((bf16[96,2304]{1,0:T(8,128)(2,1)}), bf16[768,2304]{1,0:T(8,128)(2,1)}) %all-gather.9.cloned.1.call-update) | async-done | bytes 3538960 | tf_op jit(solution)/shard_map/all_gather | solution.py:248
  80.7 3.5 fusion.17
  84.2 4.9 reshape.615
  89.1 5.0 fusion.138
  110.8 6.4 reshape.614
  117.2 5.0 fusion.137
  129.5 3.7 fusion.148
  143.9 13.0 %all-gather.15.cloned.1.call-done = bf16[3072,768]{1,0:T(8,128)(2,1)} async-done(((bf16[384,768]{1,0:T(8,128)(2,1)}), bf16[3072,768]{1,0:T(8,128)(2,1)}) %all-gather.15.cloned.1.call-update) | async-done | bytes 4718608 | tf_op jit(solution)/shard_map/all_gather | solution.py:259
  156.9 6.9 fusion.156
  163.8 4.2 fusion.154
  168.0 41.0 %all-gather.13.cloned.1.call-done = bf16[768,3072]{1,0:T(8,128)(2,1)} async-done(((bf16[96,3072]{1,0:T(8,128)(2,1)}), bf16[768,3072]{1,0:T(8,128)(2,1)}) %all-gather.13.cloned.1.call-update) | async-done | bytes 4718608 | tf_op jit(solution)/shard_map/all_gather | solution.py:257
  209.0 10.6 %convert_reduce_fusion.1 = (f32[3072]{0:T(1024)}, bf16[384,3072]{1,0:T(8,128)(2,1)S(1)}, f32[384,3072]{1,0:T(8,128)}) fusion(f32[384,3072]{1,0:T(8,128)} %fusion.154, f32[3072]{0:T(1024)} %bitcast.333, bf16[768,3072]{1,0:T(8,128)(2,1)} %all-gather.13.cloned.1.call-done, f32[384,768]{1,0:T(8,128)S(1)} %get-tuple-element.133, f32[768]{0:T(1024)} %convert_element_type.342, ...), kind=kOutput, calls=%fused_computation.24 | convolution fusion | flops 1840542720 | bytes 17728512 | tf_op jit(solution)/shard_map/dot_general | solution.py:92
  222.8 8.1 %convert_reduce_fusion = (f32[3072]{0:T(1024)}, bf16[384,3072]{1,0:T(8,128)(2,1)S(1)}, f32[384,3072]{1,0:T(8,128)}) fusion(f32[384,3072]{1,0:T(8,128)S(1)} %copy-done.126, f32[3072]{0:T(1024)S(1)} %bitcast.334, bf16[768,3072]{1,0:T(8,128)(2,1)S(1)} %copy-done.117, f32[384,768]{1,0:T(8,128)S(1)} %get-tuple-element.129, f32[384]{0:T(512)S(1)} %copy-done.81, ...), kind=kOutput, calls=%fused_computation.23 | convolution fusion | flops 1840542720 | bytes 17728512 | tf_op jit(solution)/shard_map/dot_general | solution.py:92
  230.9 3.1 multiply_reduce_fusion.2
  261.0 3.1 copy.104
  297.8 3.3 convolution_add_fusion.7
  306.2 5.0 convolution_add_fusion
  311.9 4.7 fusion.127
  316.7 5.7 convolution_add_fusion.2
  323.4 5.3 fusion.128
  328.7 5.6 convolution_add_fusion.1
  334.4 5.9 reduce-scatter.6.cloned.1.call-done
  340.3 78.7 %reduce-scatter.8.cloned.1.call-done = f32[96,2304]{1,0:T(8,128)} async-done(((f32[768,2304]{1,0:T(8,128)}), f32[96,2304]{1,0:T(8,128)}) %reduce-scatter.8.cloned.1.call-update) | async-done | bytes 884752 | tf_op jit(solution)/shard_map/reduce_scatter | solution.py:298
  419.0 100.2 %reduce-scatter.12.cloned.1.call-done = f32[96,3072]{1,0:T(8,128)} async-done(((f32[768,3072]{1,0:T(8,128)}), f32[96,3072]{1,0:T(8,128)}) %reduce-scatter.12.cloned.1.call-update) | async-done | bytes 1179664 | tf_op jit(solution)/shard_map/reduce_scatter | solution.py:307
  519.2 100.0 %reduce-scatter.14.cloned.1.call-done = f32[384,768]{1,0:T(8,128)} async-done(((f32[3072,768]{1,0:T(8,128)}), f32[384,768]{1,0:T(8,128)}) %reduce-scatter.14.cloned.1.call-update) | async-done | bytes 1179664 | tf_op jit(solution)/shard_map/reduce_scatter | solution.py:309
  625.8 26.4 %all-reduce.17 = (f32[768]{0:T(1024)S(1)}, f32[768]{0:T(1024)S(1)}, f32[768]{0:T(1024)S(1)}, f32[768]{0:T(1024)S(1)}, f32[768]{0:T(1024)S(1)}, /*index=5*/f32[76...) all-reduce(f32[768]{0:T(1024)S(1)} %reshape.560, ...), channel_id=18, replica_groups=mesh['dp'=4,'fsdp'=8] {'fsdp'}, use_global_device_ids=true, to_apply=%region_31.32.clone | all-reduce | flops 9216 | bytes 73728
  652.9 10.9 %all-reduce.18 = (f32[96]{0:T(128)}, f32[96]{0:T(128)}, f32[96]{0:T(128)}, f32[96]{0:T(128)}, f32[96]{0:T(128)}, /*index=5*/f32[96]{0:T(128)}, f32[96]{0:T(128)}, f32[384]{0:T(512)}, f32[96]{0:T(128)}) all-reduce(f32[96]{0:T(128)S(1)} %dynamic-slice.9, f32[96]{0:T(128)S(1)} %dynamic-slice.11, ...), channel_id=1, replica_groups=mesh['dp'=4,'fsdp'=8] {'dp'}, use_global_device_ids=true, to_apply=%region_34.35 | all-reduce | flops 1152 | bytes 9216 | tf_op jit(solution)/shard_map/psum | solution.py:315
  663.8 6.7 fusion.35
  670.5 6.7 fusion.36
  680.1 42.4 %all-reduce.23.cloned.1.call-done = (f32[1000,96]{0,1:T(8,128)}, f32[96,2304]{1,0:T(8,128)}, f32[96,768]{1,0:T(8,128)}, f32[96,3072]{1,0:T(8,128)}, f32[384,768]{1,0:T(8,128)}) async-done(((f32[1000,96]{0,1:T(8,128)}, f32[96,2304]{1,0:T(8,128)}, f32[96,768]{1,0:T(8,128)}, f32[96,3072]{1,0:T(8,128)}, f32[384,768]{1,0:T(8,128)}), (f32[1000,96]{0,1:T(8,128)}, f32[96,2304]{1,0:T(8,128)}, f32[96,768]{1,0:T(8,128)}, ...) | async-done | bytes 3922960 | tf_op jit(solution)/shard_map/psum | solution.py:315
  (421 shorter events, 138.3 us)
Async XLA Ops:
  7.2 5.8 copy-start.122
  7.2 6.0 copy-start.123
  7.3 6.2 copy-start.124
  7.3 6.5 copy-start.125
  7.3 37.2 %copy-start.114 = (s32[2,3]{1,0:T(2,128)S(1)}, s32[2,3]{1,0:T(2,128)}, u32[]{:S(2)}) copy-start(s32[2,3]{1,0:T(2,128)} %param.20) | copy-start | bytes 76
  7.3 37.9 %copy-start.111 = (s32[2,3,128]{2,0,1:T(2,128)S(1)}, s32[2,3,128]{2,0,1:T(2,128)}, u32[]{:S(2)}) copy-start(s32[2,3,128]{2,0,1:T(2,128)} %param.21) | copy-start | bytes 9220
  7.3 37.9 %copy-start.112 = (s32[2,3,128]{2,0,1:T(2,128)S(1)}, s32[2,3,128]{2,0,1:T(2,128)}, u32[]{:S(2)}) copy-start(s32[2,3,128]{2,0,1:T(2,128)} %param.22) | copy-start | bytes 9220
  7.3 37.9 %copy-start.115 = (bf16[384]{0:T(512)(128)(2,1)S(1)}, bf16[384]{0:T(512)(128)(2,1)}, u32[]{:S(2)}) copy-start(bf16[384]{0:T(512)(128)(2,1)} %param.35) | copy-start | bytes 2308
  7.3 53.6 %copy-start.21 = (bf16[2,3,128,768]{3,2,1,0:T(8,128)(2,1)S(1)}, bf16[2,3,128,768]{3,2,1,0:T(8,128)(2,1)}, u32[]{:S(2)}) copy-start(bf16[2,3,128,768]{3,2,1,0:T(8,128)(2,1)} %param.23) | copy-start | bytes 3538948
  7.3 54.7 %all-gather.7.cloned.1.call-start = ((), (), s32[]{:S(2)}) async-start(), calls=%async_computation.5 | async-start | bytes 1769472 | tf_op jit(solution)/shard_map/all_gather | solution.py:247
  8.1 72.6 %all-gather.9.cloned.1.call-start = ((), (), s32[]{:S(2)}) async-start(), calls=%async_computation.6 | async-start | bytes 3981312 | tf_op jit(solution)/shard_map/all_gather | solution.py:248
  8.8 128.6 %all-gather.11.cloned.1.call-start = ((), (), s32[]{:S(2)}) async-start(), calls=%async_computation.7 | async-start | bytes 1327104 | tf_op jit(solution)/shard_map/all_gather | solution.py:251
  9.5 147.4 %all-gather.15.cloned.1.call-start = ((), (), s32[]{:S(2)}) async-start(), calls=%async_computation.9 | async-start | bytes 5308416 | tf_op jit(solution)/shard_map/all_gather | solution.py:259
  10.1 198.8 %all-gather.13.cloned.1.call-start = ((), (), s32[]{:S(2)}) async-start(), calls=%async_computation.8 | async-start | bytes 5308416 | tf_op jit(solution)/shard_map/all_gather | solution.py:257
  10.7 323.7 %reduce-scatter.10.cloned.1.call-start = ((), (), s32[]{:S(2)}) async-start(), calls=%async_computation.12 | async-start | bytes 2654208 | tf_op jit(solution)/shard_map/reduce_scatter | solution.py:301
  44.5 22.4 %copy-start.74 = (f32[768]{0:T(1024)}, f32[768]{0:T(1024)S(1)}, u32[]{:S(2)}) copy-start(f32[768]{0:T(1024)S(1)} %convert_element_type.331) | copy-start | bytes 9220
  44.5 22.4 %copy-start.57 = (f32[768]{0:T(1024)}, f32[768]{0:T(1024)S(1)}, u32[]{:S(2)}) copy-start(f32[768]{0:T(1024)S(1)} %convert_element_type.330) | copy-start | bytes 9220
  44.5 17.5 %copy-start.109 = (s32[3]{0:T(128)}, s32[3]{0:T(128)S(1)}, u32[]{:S(2)}) copy-start(s32[3]{0:T(128)S(1)} %get-tuple-element.122) | copy-start | bytes 40
  44.5 19.5 %copy-start.107 = (s32[3]{0:T(128)}, s32[3]{0:T(128)S(1)}, u32[]{:S(2)}) copy-start(s32[3]{0:T(128)S(1)} %get-tuple-element.123) | copy-start | bytes 40
  107.3 30.0 %copy-start.17 = (bf16[3,128,12,64]{1,0,3,2:T(4,128)(2,1)}, bf16[3,128,12,64]{1,0,3,2:T(4,128)(2,1)S(1)}, u32[]{:S(2)}) copy-start(bf16[3,128,12,64]{1,0,3,2:T(4,128)(2,1)S(1)} %copy.90) | copy-start | bytes 1769476
  156.9 6.9 copy-start.13
  156.9 6.9 copy-start.116
  209.0 10.7 %copy-start.117 = (bf16[768,3072]{1,0:T(8,128)(2,1)S(1)}, bf16[768,3072]{1,0:T(8,128)(2,1)}, u32[]{:S(2)}) copy-start(bf16[768,3072]{1,0:T(8,128)(2,1)} %all-gather.13.cloned.1.call-done) | copy-start | bytes 14155780
  222.8 8.1 %copy-start.60 = (f32[384]{0:T(512)S(1)}, f32[384]{0:T(512)}, u32[]{:S(2)}) copy-start(f32[384]{0:T(512)} %copy-done.59) | copy-start | bytes 4612
  222.8 8.1 %copy-start.71 = (f32[384]{0:T(512)S(1)}, f32[384]{0:T(512)}, u32[]{:S(2)}) copy-start(f32[384]{0:T(512)} %fusion.107) | copy-start | bytes 4612
  257.0 83.4 %reduce-scatter.6.cloned.1.call-start = ((), (), s32[]{:S(2)}) async-start(), calls=%async_computation.10 | async-start | bytes 3538944 | tf_op jit(solution)/shard_map/reduce_scatter | solution.py:297
  301.1 118.0 %reduce-scatter.8.cloned.1.call-start = ((), (), s32[]{:S(2)}) async-start(), calls=%async_computation.11 | async-start | bytes 7962624 | tf_op jit(solution)/shard_map/reduce_scatter | solution.py:298
  311.3 207.9 %reduce-scatter.12.cloned.1.call-start = ((), (), s32[]{:S(2)}) async-start(), calls=%async_computation.13 | async-start | bytes 10616832 | tf_op jit(solution)/shard_map/reduce_scatter | solution.py:307
  322.3 6.3 slice-start
  322.4 296.9 %reduce-scatter.14.cloned.1.call-start = ((), (), s32[]{:S(2)}) async-start(), calls=%async_computation.14 | async-start | bytes 10616832 | tf_op jit(solution)/shard_map/reduce_scatter | solution.py:309
  334.3 388.2 %all-reduce.23.cloned.1.call-start = ((), (), s32[]{:S(2)}) async-start(), calls=%async_computation.15 | async-start | bytes 7864320 | tf_op jit(solution)/shard_map/psum | solution.py:315
  663.8 6.7 copy-start.110
  (108 other events, 246.9 us)
Sparse Core Ops, SparseCore 0:
  9.8 27.9 all-gather.6
  39.5 41.1 all-gather.8
  82.3 21.5 all-gather.10
  105.4 51.4 all-gather.14
  158.4 50.5 all-gather.12
  257.1 34.9 reduce-scatter.9
  301.2 39.0 reduce-scatter.5
  342.7 76.3 reduce-scatter.7
  421.3 97.8 reduce-scatter.11
  521.4 97.8 reduce-scatter.13
  622.9 99.5 all-reduce.22
where the time goes:
time: 744 us; the launch traced here: 737 us
  waiting for transfers between devices  396 us (53%)
  matrix products  129 us (17%)
  blocking collectives  80.8 us (11%)
  local copies, waits for them, and re-layouts  78.9 us (11%)
  other arithmetic  34.4 us (5%)
  between operations  17.4 us (2%)
    reduce_scatter x1, waiting for transfers between devices, per_device(): lax.psum_scatter(grads[9], 'fsdp', scatter_dimension=0, tiled=True)  100 us
    reduce_scatter x1, waiting for transfers between devices, per_device(): lax.psum_scatter(grads[11], 'fsdp', scatter_dimension=0, tiled=True)  100 us
    reduce_scatter x1, waiting for transfers between devices, per_device(): lax.psum_scatter(grads[0], 'fsdp', scatter_dimension=0, tiled=True)  78.7 us
    unnamed x2, blocking collectives  56.9 us
    psum x1, waiting for transfers between devices, per_device(): lax.psum((totals[0], totals[1], totals[2], totals[3], totals[4], totals[5...  42.4 us
    all_gather x1, waiting for transfers between devices, per_device(): lax.all_gather(hidden_weight, 'fsdp', axis=0, tiled=True)  41 us
    unnamed x298, local copies, waits for them, and re-layouts  38.5 us
    dot_general x2, matrix products, forward_pass(): jnp.dot(normed_two, hidden_full, preferred_element_type=jnp.float32)  18.7 us
  transfers between devices with their start and end apart: 11, of which 8 were waited for; matrix products, arithmetic and copies ran while one was open for 24% of the time, Pallas kernels for 0%

commit v1 on v0

v1 whole, which is shorter than its diff:
```python
import functools
import math

import jax
import jax.numpy as jnp
from jax import lax
from jax.experimental import pallas as pl
from jax.experimental.pallas import tpu as pltpu
from jax.sharding import PartitionSpec as P

HEADS = 12
HD = 64
EPS = 1e-05
MASKED = -1e30
SCALE = 1.0 / math.sqrt(HD)
GELU_C = math.sqrt(2.0 / math.pi)
GELU_A = 0.044715
VMEM_LIMIT = 60 * 1024 * 1024
highest = lax.Precision.HIGHEST
f32 = jnp.float32
bf16 = jnp.bfloat16

NB = 8


def mm(a, b):
    return lax.dot_general(a, b, (((1,), (0,)), ((), ())), preferred_element_type=f32)


def mm_nt(a, b):
    return lax.dot_general(a, b, (((1,), (1,)), ((), ())), preferred_element_type=f32)


def mm_tn(a, b):
    return lax.dot_general(a, b, (((0,), (0,)), ((), ())), preferred_element_type=f32)


def moments(v):
    average = jnp.mean(v, axis=-1, keepdims=True)
    centered = v - average
    variance = jnp.mean(centered * centered, axis=-1, keepdims=True)
    inv = lax.rsqrt(variance + EPS)
    return centered * inv, inv


def ln_back(e, xhat, inv):
    return (e - jnp.mean(e, -1, keepdims=True) - xhat * jnp.mean(e * xhat, -1, keepdims=True)) * inv


def load_blocks(slots_ref, pieces, layout, w_ref, sem):
    copies = []
    for piece, first, count in layout:
        for t in range(count):
            i = len(copies)
            copies.append(
                pltpu.make_async_copy(pieces[piece].at[first + t], w_ref.at[slots_ref[i]], sem.at[i])
            )
    for cp in copies:
        cp.start()
    for cp in copies:
        cp.wait()


def square(w_ref, j):
    part = w_ref[NB * j : NB * (j + 1)]
    return part.reshape(part.shape[0] * part.shape[1], part.shape[2])


def put_pair(gpos_ref, at, keep_ref, send_ref, even, odd):
    idx = gpos_ref[at]
    side = gpos_ref[16]

    @pl.when(side == 0)
    def _():
        keep_ref[idx] = even
        send_ref[idx] = odd

    @pl.when(side != 0)
    def _():
        keep_ref[idx] = odd
        send_ref[idx] = even


def half_mask(rows, width):
    lane = lax.broadcasted_iota(jnp.int32, (rows, width), 1)
    return lane < HD


def both(x2, first):
    zero = jnp.zeros_like(x2)
    return jnp.concatenate([jnp.where(first, x2, zero), jnp.where(first, zero, x2)], axis=0)


def residual_of(tok_ref, emb_ref, step, rb, length):
    parts = []
    for r in range(rb):
        rows = tok_ref[r * length : (r + 1) * length].astype(f32)
        parts.append(rows + emb_ref[pl.ds(step * rb + r, 1), :])
    return jnp.concatenate(parts, axis=0) if rb > 1 else parts[0]


def f1_kernel(layout, rb, length, slots, tok_ref, emb_ref, seg_ref, pad_ref, vec_ref, *rest):
    n = max(l[0] for l in layout) + 1
    pieces = rest[:n]
    normed_ref, triple_ref, att_ref, attended_ref, middle_ref, n2_ref, w_ref, sem = rest[n:]
    step = pl.program_id(0)

    @pl.when(step == 0)
    def _():
        load_blocks(slots, pieces, layout, w_ref, sem)

    x = residual_of(tok_ref, emb_ref, step, rb, length)
    xhat, _inv = moments(x)
    normed = (xhat * vec_ref[3:4, :] + vec_ref[4:5, :]).astype(bf16)
    normed_ref[...] = normed
    width = normed.shape[1]
    for q, row in ((0, 0), (1, None), (2, 1)):
        t = mm(normed, square(w_ref, q))
        if row is not None:
            t = t + vec_ref[row : row + 1, :]
        triple_ref[q] = t.astype(bf16)
    eye = lax.broadcasted_iota(jnp.int32, (length, length), 0) == lax.broadcasted_iota(
        jnp.int32, (length, length), 1
    )
    first = half_mask(length, 2 * HD)
    for r in range(rb):
        seg = jnp.broadcast_to(seg_ref[pl.ds(step * rb + r, 1), :], (length, length))
        pad = jnp.broadcast_to(pad_ref[pl.ds(step * rb + r, 1), :], (length, length))
        same = seg == seg.T
        allowed = same & ((pad == 0.0) | eye)
        allowed = jnp.where(allowed, 1.0, 0.0)
        allowed = jnp.concatenate([allowed, allowed], axis=0) > 0.5
        rows = slice(r * length, (r + 1) * length)
        for hp in range(width // (2 * HD)):
            lanes = slice(hp * 2 * HD, (hp + 1) * 2 * HD)
            qs = both(triple_ref[0, rows, lanes], first)
            s = mm_nt(qs, triple_ref[1, rows, lanes]) * SCALE
            s = jnp.where(allowed, s, MASKED)
            top = jnp.max(s, axis=-1, keepdims=True)
            e = jnp.exp(s - top)
            p = (e / jnp.sum(e, axis=-1, keepdims=True)).astype(bf16)
            att_ref[r * (width // (2 * HD)) + hp] = p
            wide = jnp.concatenate([p[:length], p[length:]], axis=1)
            o = mm(wide, both(triple_ref[2, rows, lanes], first))
            attended_ref[rows, lanes] = o.astype(bf16)
    branch = mm(attended_ref[...], square(w_ref, 3)) + vec_ref[2:3, :]
    middle = x + branch
    middle_ref[...] = middle
    xhat2, _inv2 = moments(middle)
    n2_ref[...] = (xhat2 * vec_ref[5:6, :] + vec_ref[6:7, :]).astype(bf16)


def f2_kernel(layout, chunk, slots, gpos, n2_ref, cot_ref, hb_ref, *rest):
    n = max(l[0] for l in layout) + 1
    pieces = rest[:n]
    active_ref, gp_ref, keep_ref, send_ref, w_ref, h_ref, sem = rest[n:]
    j = pl.program_id(0)

    @pl.when(j == 0)
    def _():
        load_blocks(slots, pieces, layout, w_ref, sem)

    tokens, width = n2_ref.shape
    w = w_ref[pl.ds(j * NB, NB)].reshape(width, width)
    bias = hb_ref[pl.ds(j, 1), :]
    sub = 32
    for m in range(tokens // chunk):
        h_ref[...] = mm(n2_ref[m * chunk : (m + 1) * chunk], w)
        for s in range(chunk // sub):
            v = h_ref[s * sub : (s + 1) * sub] + bias
            v2 = v * v
            t = jnp.tanh((GELU_C * v) * (1.0 + GELU_A * v2))
            half = 0.5 * (1.0 + t)
            at = slice(m * chunk + s * sub, m * chunk + (s + 1) * sub)
            active_ref[at] = (v * half).astype(bf16)
            slope = half + (0.5 * GELU_C) * v * (1.0 - t * t) * (1.0 + (3.0 * GELU_A) * v2)
            gp_ref[at] = slope.astype(bf16)
    cot = cot_ref[...]
    hw = width // 2
    ev = mm_tn(active_ref[:, :hw], cot).astype(bf16)
    od = mm_tn(active_ref[:, hw:], cot).astype(bf16)
    b = width // NB
    for q in range(4):
        put_pair(gpos, q * 4 + j, keep_ref, send_ref, ev[q * b : (q + 1) * b], od[q * b : (q + 1) * b])


def b1_kernel(layout, chunk, slots, gpos, n2_ref, cot_ref, gp_ref, *rest):
    n = max(l[0] for l in layout) + 1
    pieces = rest[:n]
    dh_ref, hb_ref, db_ref, keep_ref, send_ref, w_ref, nt_ref, h_ref, sem = rest[n:]
    j = pl.program_id(0)
    tokens, width = n2_ref.shape

    @pl.when(j == 0)
    def _():
        load_blocks(slots, pieces, layout, w_ref, sem)
        nt_ref[...] = n2_ref[...].T
        db_ref[...] = jnp.zeros_like(db_ref)
        db_ref[0:1] = jnp.sum(cot_ref[...].astype(f32), axis=0, keepdims=True)
        hb_ref[...] = jnp.zeros_like(hb_ref)

    w = w_ref[pl.ds(j * NB, NB)].reshape(width, width)
    sub = 32
    total = jnp.zeros((8, width), f32)
    for m in range(tokens // chunk):
        h_ref[...] = mm_nt(cot_ref[m * chunk : (m + 1) * chunk], w)
        for s in range(chunk // sub):
            at = slice(m * chunk + s * sub, m * chunk + (s + 1) * sub)
            dh = (h_ref[s * sub : (s + 1) * sub] * gp_ref[at].astype(f32)).astype(bf16)
            dh_ref[at] = dh
            total = total + jnp.sum(dh.astype(f32).reshape(sub // 8, 8, width), axis=0)
    hb_ref[pl.ds(j, 1), :] = jnp.sum(total, axis=0, keepdims=True)
    b = width // NB
    dh_all = dh_ref[...]
    for zf in range(4):
        g = mm(nt_ref[zf * 2 * b : (zf + 1) * 2 * b], dh_all).astype(bf16)
        put_pair(gpos, j * 4 + zf, keep_ref, send_ref, g[:b], g[b:])


def b2_kernel(
    layout_a, layout_b, rb, length, slots_a, slots_b, gpos,
    dh_ref, cot_ref, middle_ref, triple_ref, att_ref, attended_ref, normed_ref, vec_ref, *rest
):
    na = max(l[0] for l in layout_a) + 1
    nb = max(l[0] for l in layout_b) + 1
    pieces_a, pieces_b, rest = rest[:na], rest[na : na + nb], rest[na + nb :]
    dmid_ref, dt_ref, sums_ref, keep_ref, send_ref, wa_ref, wb_ref, dbr_ref, dts_ref, sem_a, sem_b = rest
    step = pl.program_id(0)
    block = rb * length
    width = cot_ref.shape[1]

    @pl.when(step == 0)
    def _():
        load_blocks(slots_b, pieces_b, layout_b, wb_ref, sem_b)
        load_blocks(slots_a, pieces_a, layout_a, wa_ref, sem_a)
        sums_ref[...] = jnp.zeros_like(sums_ref)

    d_n2 = mm_nt(dh_ref[0], square(wb_ref, 0))
    for j in range(1, 4):
        d_n2 = d_n2 + mm_nt(dh_ref[j], square(wb_ref, j))
    xhat, inv = moments(middle_ref[...])
    sums_ref[0:1] += jnp.sum(d_n2 * xhat, axis=0, keepdims=True)
    sums_ref[1:2] += jnp.sum(d_n2, axis=0, keepdims=True)
    d_middle = cot_ref[...].astype(f32) + ln_back(d_n2 * vec_ref[5:6, :], xhat, inv)
    dmid_ref[...] = d_middle
    d_branch = d_middle.astype(bf16)
    base = pl.multiple_of(step * block, block)
    dbr_ref[pl.ds(base, block)] = d_branch
    sums_ref[2:3] += jnp.sum(d_branch.astype(f32), axis=0, keepdims=True)
    d_att = mm_nt(d_branch, square(wa_ref, 3)).astype(bf16)
    first = half_mask(length, 2 * HD)
    pairs = width // (2 * HD)
    for r in range(rb):
        rows = slice(r * length, (r + 1) * length)
        for hp in range(pairs):
            lanes = slice(hp * 2 * HD, (hp + 1) * 2 * HD)
            dos = both(d_att[rows, lanes], first)
            p_low = att_ref[r * pairs + hp]
            p = p_low.astype(f32)
            d_a = mm_nt(dos, triple_ref[2, rows, lanes])
            inner = jnp.sum(p * d_a, axis=-1, keepdims=True)
            ds = (p * (d_a - inner)).astype(bf16)
            wide = jnp.concatenate([ds[:length], ds[length:]], axis=1)
            dt_ref[0, rows, lanes] = (mm(wide, both(triple_ref[1, rows, lanes], first)) * SCALE).astype(bf16)
            dt_ref[1, rows, lanes] = (mm_tn(ds, both(triple_ref[0, rows, lanes], first)) * SCALE).astype(bf16)
            dt_ref[2, rows, lanes] = mm_tn(p_low, dos).astype(bf16)
    sums_ref[3:4] += jnp.sum(dt_ref[0].astype(f32), axis=0, keepdims=True)
    sums_ref[4:5] += jnp.sum(dt_ref[2].astype(f32), axis=0, keepdims=True)
    for q in range(3):
        dts_ref[q, pl.ds(base, block)] = dt_ref[q]

    @pl.when(step == pl.num_programs(0) - 1)
    def _():
        b = width // NB
        hw = width // 2
        for h in range(2):
            cols = slice(h * hw, (h + 1) * hw)
            for q in range(4):
                if q < 3:
                    g = mm_tn(normed_ref[:, cols], dts_ref[q])
                else:
                    g = mm_tn(attended_ref[:, cols], dbr_ref[...])
                g = g.astype(bf16)
                for zz in range(2):
                    put_pair(
                        gpos, q * 4 + 2 * h + zz, keep_ref, send_ref,
                        g[2 * zz * b : (2 * zz + 1) * b], g[(2 * zz + 1) * b : (2 * zz + 2) * b],
                    )


def b4_kernel(layout, rb, length, slots, tok_ref, emb_ref, dmid_ref, dt_ref, vec_ref, *rest):
    n = max(l[0] for l in layout) + 1
    pieces = rest[:n]
    ig_ref, rs_ref, sums_ref, w_ref, sem = rest[n:]
    step = pl.program_id(0)

    @pl.when(step == 0)
    def _():
        load_blocks(slots, pieces, layout, w_ref, sem)
        sums_ref[...] = jnp.zeros_like(sums_ref)
        rs_ref[...] = jnp.zeros_like(rs_ref)

    d_n = mm_nt(dt_ref[0], square(w_ref, 0))
    for q in range(1, 3):
        d_n = d_n + mm_nt(dt_ref[q], square(w_ref, q))
    xhat, inv = moments(residual_of(tok_ref, emb_ref, step, rb, length))
    sums_ref[0:1] += jnp.sum(d_n * xhat, axis=0, keepdims=True)
    sums_ref[1:2] += jnp.sum(d_n, axis=0, keepdims=True)
    d_start = dmid_ref[...] + ln_back(d_n * vec_ref[3:4, :], xhat, inv)
    ig_ref[...] = d_start.astype(bf16)
    for r in range(rb):
        rs_ref[pl.ds(step * rb + r, 1), :] = jnp.sum(d_start[r * length : (r + 1) * length], axis=0, keepdims=True)


def f3_kernel(layout, slots, act_ref, middle_ref, vec_ref, *rest):
    n = max(l[0] for l in layout) + 1
    pieces = rest[:n]
    out_ref, w_ref, sem = rest[n:]

    @pl.when(pl.program_id(0) == 0)
    def _():
        load_blocks(slots, pieces, layout, w_ref, sem)

    acc = mm(act_ref[0], square(w_ref, 0))
    for j in range(1, 4):
        acc = acc + mm(act_ref[j], square(w_ref, j))
    out_ref[...] = (middle_ref[...] + (acc + vec_ref[7:8, :])).astype(bf16)


def sds(shape, dtype):
    return jax.ShapeDtypeStruct(shape, dtype)


def full(shape):
    zeros = (0,) * len(shape)
    return pl.BlockSpec(shape, lambda i: zeros)


smem = pl.BlockSpec(memory_space=pltpu.SMEM)
hbm = pl.BlockSpec(memory_space=pl.ANY)


def call(kernel, grid, in_specs, out_shape, out_specs, scratch, flops, nbytes, args):
    return pl.pallas_call(
        kernel,
        grid=grid,
        in_specs=in_specs,
        out_shape=out_shape,
        out_specs=out_specs,
        scratch_shapes=scratch,
        compiler_params=pltpu.CompilerParams(
            dimension_semantics=("arbitrary",), vmem_limit_bytes=VMEM_LIMIT
        ),
        cost_estimate=pl.CostEstimate(flops=flops, bytes_accessed=nbytes, transcendentals=0),
    )(*args)


class Group:
    def __init__(self, arrays, layout, slots):
        self.arrays, self.layout, self.slots = arrays, layout, slots


def compute_f1(tok, emb, seg, pad, vecs, group, rows, length):
    n, width = tok.shape
    rb = 2 if rows % 2 == 0 else 1
    block = rb * length
    pairs = width // (2 * HD)
    b = width // NB
    return call(
        functools.partial(f1_kernel, group.layout, rb, length),
        (rows // rb,),
        [smem, pl.BlockSpec((block, width), lambda i: (i, 0)), full(emb.shape), full(seg.shape), full(pad.shape), full(vecs.shape)]
        + [hbm] * len(group.arrays),
        [sds((n, width), bf16), sds((3, n, width), bf16), sds((rows * pairs, 2 * length, length), bf16),
         sds((n, width), bf16), sds((n, width), f32), sds((n, width), bf16)],
        [pl.BlockSpec((block, width), lambda i: (i, 0)), pl.BlockSpec((3, block, width), lambda i: (0, i, 0)),
         pl.BlockSpec((rb * pairs, 2 * length, length), lambda i: (i, 0, 0)),
         pl.BlockSpec((block, width), lambda i: (i, 0)), pl.BlockSpec((block, width), lambda i: (i, 0)),
         pl.BlockSpec((block, width), lambda i: (i, 0))],
        [pltpu.VMEM((32, b, width), bf16), pltpu.SemaphoreType.DMA((32,))],
        2 * n * width * width * 4 * 3, 20 << 20,
        [group.slots, tok, emb, seg, pad, vecs, *group.arrays],
    )


def compute_f2(n2, cot, hb, group, gpos):
    n, width = n2.shape
    b = width // NB
    chunk = 256 if n % 256 == 0 else n
    return call(
        functools.partial(f2_kernel, group.layout, chunk),
        (4,),
        [smem, smem, full(n2.shape), full(cot.shape), full(hb.shape)] + [hbm] * len(group.arrays),
        [sds((4, n, width), bf16), sds((4, n, width), bf16), sds((16, b, width), bf16), sds((16, b, width), bf16)],
        [pl.BlockSpec((None, n, width), lambda i: (i, 0, 0)), pl.BlockSpec((None, n, width), lambda i: (i, 0, 0)),
         full((16, b, width)), full((16, b, width))],
        [pltpu.VMEM((32, b, width), bf16), pltpu.VMEM((chunk, width), f32), pltpu.SemaphoreType.DMA((32,))],
        2 * n * width * width * 8 * 2, 20 << 20,
        [group.slots, gpos, n2, cot, hb, *group.arrays],
    )


def compute_b1(n2, cot, gp, group, gpos):
    n, width = n2.shape
    b = width // NB
    chunk = 256 if n % 256 == 0 else n
    return call(
        functools.partial(b1_kernel, group.layout, chunk),
        (4,),
        [smem, smem, full(n2.shape), full(cot.shape), pl.BlockSpec((None, n, width), lambda i: (i, 0, 0))]
        + [hbm] * len(group.arrays),
        [sds((4, n, width), bf16), sds((8, width), f32), sds((8, width), f32), sds((16, b, width), bf16), sds((16, b, width), bf16)],
        [pl.BlockSpec((None, n, width), lambda i: (i, 0, 0)), full((8, width)), full((8, width)),
         full((16, b, width)), full((16, b, width))],
        [pltpu.VMEM((32, b, width), bf16), pltpu.VMEM((width, n), bf16), pltpu.VMEM((chunk, width), f32),
         pltpu.SemaphoreType.DMA((32,))],
        2 * n * width * width * 8 * 2, 20 << 20,
        [group.slots, gpos, n2, cot, gp, *group.arrays],
    )


def compute_b2(dh, cot, middle, triple, att, attended, normed, vecs, ga, gb, gpos, rows, length):
    n, width = cot.shape
    rb = 2 if rows % 2 == 0 else 1
    block = rb * length
    pairs = width // (2 * HD)
    b = width // NB
    return call(
        functools.partial(b2_kernel, ga.layout, gb.layout, rb, length),
        (rows // rb,),
        [smem, smem, smem, pl.BlockSpec((4, block, width), lambda i: (0, i, 0)), pl.BlockSpec((block, width), lambda i: (i, 0)),
         pl.BlockSpec((block, width), lambda i: (i, 0)), pl.BlockSpec((3, block, width), lambda i: (0, i, 0)),
         pl.BlockSpec((rb * pairs, 2 * length, length), lambda i: (i, 0, 0)), full(attended.shape), full(normed.shape),
         full(vecs.shape)] + [hbm] * (len(ga.arrays) + len(gb.arrays)),
        [sds((n, width), f32), sds((3, n, width), bf16), sds((8, width), f32), sds((16, b, width), bf16), sds((16, b, width), bf16)],
        [pl.BlockSpec((block, width), lambda i: (i, 0)), pl.BlockSpec((3, block, width), lambda i: (0, i, 0)), full((8, width)),
         full((16, b, width)), full((16, b, width))],
        [pltpu.VMEM((32, b, width), bf16), pltpu.VMEM((32, b, width), bf16), pltpu.VMEM((n, width), bf16),
         pltpu.VMEM((3, n, width), bf16), pltpu.SemaphoreType.DMA((32,)), pltpu.SemaphoreType.DMA((32,))],
        2 * n * width * width * 16, 40 << 20,
        [ga.slots, gb.slots, gpos, dh, cot, middle, triple, att, attended, normed, vecs, *ga.arrays, *gb.arrays],
    )


def compute_b4(tok, emb, dmid, dt, vecs, group, rows, length):
    n, width = tok.shape
    rb = 2 if rows % 2 == 0 else 1
    block = rb * length
    b = width // NB
    return call(
        functools.partial(b4_kernel, group.layout, rb, length),
        (rows // rb,),
        [smem, pl.BlockSpec((block, width), lambda i: (i, 0)), full(emb.shape), pl.BlockSpec((block, width), lambda i: (i, 0)),
         pl.BlockSpec((3, block, width), lambda i: (0, i, 0)), full(vecs.shape)] + [hbm] * len(group.arrays),
        [sds((n, width), bf16), sds((8 * ((rows + 7) // 8), width), f32), sds((8, width), f32)],
        [pl.BlockSpec((block, width), lambda i: (i, 0)), full((8 * ((rows + 7) // 8), width)), full((8, width))],
        [pltpu.VMEM((32, b, width), bf16), pltpu.SemaphoreType.DMA((32,))],
        2 * n * width * width * 3 * 2, 12 << 20,
        [group.slots, tok, emb, dmid, dt, vecs, *group.arrays],
    )


def compute_f3(active, middle, vecs, group):
    n, width = middle.shape
    b = width // NB
    block = 256 if n % 256 == 0 else n
    return call(
        functools.partial(f3_kernel, group.layout),
        (n // block,),
        [smem, pl.BlockSpec((4, block, width), lambda i: (0, i, 0)), pl.BlockSpec((block, width), lambda i: (i, 0)), full(vecs.shape)]
        + [hbm] * len(group.arrays),
        sds((n, width), bf16),
        pl.BlockSpec((block, width), lambda i: (i, 0)),
        [pltpu.VMEM((32, b, width), bf16), pltpu.SemaphoreType.DMA((32,))],
        2 * n * width * width * 4 * 2, 12 << 20,
        [group.slots, active, middle, vecs, *group.arrays],
    )


def plain_groups(own_a, own_b, own_c, small):
    width = own_a.shape[2]
    slots = jnp.arange(32, dtype=jnp.int32)

    def group(whole):
        return Group([whole.reshape(32, width // NB, width)], [(0, 0, 32)], slots)

    a = lax.all_gather(own_a, "fsdp", axis=1, tiled=True)
    b = lax.all_gather(own_b, "fsdp", axis=1, tiled=True)
    c = lax.all_gather(own_c, "fsdp", axis=0, tiled=True)
    vec = [lax.all_gather(v, "fsdp", axis=0, tiled=True) for v in small]
    return group(a), group(b), group(c), jnp.stack(vec[:8]).astype(f32), vec[8].astype(f32).reshape(4, width)


def plain_scatter(keep, send, rows_first):
    b, width = keep.shape[1:]
    g = jnp.stack([keep.reshape(4, 4, b, width), send.reshape(4, 4, b, width)], axis=2)
    if rows_first:
        g = g.transpose(1, 2, 0, 3, 4).reshape(32 * b, width)
        s = lax.psum_scatter(g.astype(f32), "fsdp", scatter_dimension=0, tiled=True)
        return lax.psum(s, "dp")
    g = g.reshape(4, NB * b, width)
    s = lax.psum_scatter(g.astype(f32), "fsdp", scatter_dimension=1, tiled=True)
    return lax.psum(s, "dp")


def pick(stacked, i):
    return lax.dynamic_index_in_dim(stacked, i, axis=0, keepdims=False)


def xor_perm(n, k):
    return [(i, i ^ k) for i in range(n)]


def core_swap(v):
    return lax.ppermute(v, "fsdp", xor_perm(8, 1))


def x_swap(v):
    return lax.ppermute(v, "dp", xor_perm(4, 1))


def y_swap(v):
    return lax.ppermute(v, "dp", xor_perm(4, 2))


def z_shift(v, k):
    return lax.ppermute(v, "fsdp", [(i, (i + 2 * k) % 8) for i in range(8)])


def fast_slots(d, z, c, rows_first):
    table = []

    def add(delta, k, e):
        q = d ^ delta
        f = 2 * lax.rem(z - k + 4, 4) + (c ^ e)
        table.append(f * 4 + q if rows_first else q * NB + f)

    for e in (0, 1):
        for delta in (0, 1, 2):
            for k in range(4):
                add(delta, k, e)
        for k in range(4):
            add(3, k, e)
    return jnp.stack(table).astype(jnp.int32)


def fast_gather(own, d, z, c, rows_first, extra=None):
    b = own.shape[0]
    sent = own if extra is None else jnp.concatenate([own, extra], axis=0)
    got = [sent] + [z_shift(sent, k) for k in (1, 2, 3)]
    s0 = jnp.stack([g[:b] for g in got])
    xs, ys = x_swap(s0), y_swap(s0)
    d1, d2 = y_swap(xs[:2]), x_swap(ys[2:])
    mine = [s0, xs, ys, d1, d2]
    arrays = mine + [core_swap(v) for v in mine]
    layout = []
    for e in range(2):
        layout += [(5 * e, 0, 4), (5 * e + 1, 0, 4), (5 * e + 2, 0, 4), (5 * e + 3, 0, 2), (5 * e + 4, 0, 2)]
    group = Group(arrays, layout, fast_slots(d, z, c, rows_first))
    if extra is None:
        return group
    e0 = jnp.stack([g[b:] for g in got])
    return group, e0, core_swap(e0)


def fast_small(e0, e1, z, c, width):
    pair = jnp.stack([jnp.where(c == 0, e0, e1), jnp.where(c == 0, e1, e0)], axis=1)[:, :, :2]
    rows = jnp.stack([pick(pair, lax.rem(z - i + 4, 4)) for i in range(4)])
    rows = rows.reshape(8, 2, width).astype(f32)
    vecs = rows[:, 0].reshape(8, 8, width // 8).transpose(1, 0, 2).reshape(8, width)
    hb = rows[:, 1, : width // 2].reshape(4, width)
    return vecs, hb


def fast_scatter(keep, send):
    b, width = keep.shape[1:]
    got = core_swap(send)

    def add(u, v):
        return (u.astype(f32) + v.astype(f32)).astype(bf16)

    keep = keep.reshape(4, 4, b, width)
    got = got.reshape(4, 4, b, width)

    def part(deltas, half):
        ks = slice(2 * half, 2 * half + 2)
        return jnp.stack([add(keep[dl, ks], got[dl, ks]) for dl in deltas])

    rx = x_swap(part((1, 3), 0))
    ry = y_swap(part((2, 3), 1))
    h2a = add(part((0, 2), 0), rx)
    h2b = add(part((0, 1), 1), ry)
    ra = y_swap(h2a[1])
    rb = x_swap(h2b[1])
    h3 = jnp.concatenate([add(h2a[0], ra), add(h2b[0], rb)], axis=0)
    parts = [h3[0]] + [z_shift(h3[k], k) for k in (1, 2, 3)]
    total = sum(p.astype(f32) for p in parts)
    return total.astype(bf16)


def fast_spread(mine, d):
    got = jnp.stack([mine, x_swap(mine), y_swap(mine), lax.ppermute(mine, "dp", xor_perm(4, 3))])
    return jnp.stack([pick(got, d ^ q) for q in range(4)]).astype(f32)


def per_device(
    fast, tokens, timesteps, segments, padding, cotangent, step_table,
    triple_weight, query_bias, value_bias, output_weight, output_bias,
    first_gain, first_shift, second_gain, second_shift,
    hidden_weight, hidden_bias, down_weight, down_bias,
):
    micro, local_rows, length, width = tokens.shape
    rows = micro * local_rows
    n = rows * length
    nd, nf = lax.axis_size("dp"), lax.axis_size("fsdp")
    d, f = lax.axis_index("dp"), lax.axis_index("fsdp")
    z, c = f // 2, lax.rem(f, 2)
    tok = tokens.reshape(n, width)
    cot = cotangent.reshape(n, width)
    seg = segments.reshape(rows, length).astype(f32)
    pad = padding.reshape(rows, length).astype(f32)

    ids = lax.all_gather(timesteps.reshape(1, rows), ("dp", "fsdp"), axis=0, tiled=True)
    here = lax.dynamic_slice_in_dim(ids, d * nf, nf, axis=0).reshape(nf * rows)
    steps = lax.iota(jnp.int32, step_table.shape[0])
    onehot = (here[:, None] == steps[None, :]).astype(bf16)
    looked = jnp.dot(onehot, step_table, preferred_element_type=f32).astype(bf16)
    looked = looked.reshape(nf, rows, width // nf)
    emb = lax.all_to_all(looked, "fsdp", 0, 0, tiled=True)
    emb = emb.transpose(1, 0, 2).reshape(rows, width).astype(f32)

    q4 = [triple_weight[:, i * width : (i + 1) * width] for i in range(3)] + [output_weight]
    h4 = [hidden_weight[:, i * width : (i + 1) * width] for i in range(4)]
    vec_args = (query_bias, value_bias, output_bias, first_gain, first_shift, second_gain, second_shift, down_bias)
    if fast:
        b = width // NB
        own_a = pick(jnp.stack(q4), d)
        own_b = pick(jnp.stack(h4), d)
        own_c = lax.dynamic_slice_in_dim(down_weight, d * b, b, axis=0)
        hb_row = jnp.concatenate([hidden_bias, jnp.zeros_like(hidden_bias)])
        small = jnp.stack([jnp.concatenate(vec_args), hb_row])
        small = jnp.concatenate([small, jnp.zeros((14, width), bf16)], axis=0)
        ga, e0, e1 = fast_gather(own_a, d, z, c, False, small)
        gb = fast_gather(own_b, d, z, c, False)
        gc = fast_gather(own_c, d, z, c, True)
        vecs, hb = fast_small(e0, e1, z, c, width)
        gpos = [(q ^ d) * 4 + lax.rem(zf - z + 4, 4) for q in range(4) for zf in range(4)] + [c]
        gpos = jnp.stack(gpos).astype(jnp.int32)
    else:
        ga, gb, gc, vecs, hb = plain_groups(
            jnp.stack(q4), jnp.stack(h4), down_weight, vec_args + (hidden_bias,)
        )
        gpos = jnp.concatenate([jnp.arange(16, dtype=jnp.int32), jnp.zeros((1,), jnp.int32)])

    normed, triple, att, attended, middle, n2 = compute_f1(tok, emb, seg, pad, vecs, ga, rows, length)
    active, gp, keep_c, send_c = compute_f2(n2, cot, hb, gb, gpos)
    dh, hb_sum, db_sum, keep_b, send_b = compute_b1(n2, cot, gp, gc, gpos)
    dmid, dt, sums2, keep_a, send_a = compute_b2(
        dh, cot, middle, triple, att, attended, normed, vecs, ga, gb, gpos, rows, length
    )
    result = compute_f3(active, middle, vecs, gc)
    input_grad, row_sums, sums4 = compute_b4(tok, emb, dmid, dt, vecs, ga, rows, length)
    row_sums = row_sums[:rows]

    if fast:
        out_c = fast_spread(fast_scatter(keep_c, send_c), d)
        out_b = fast_spread(fast_scatter(keep_b, send_b), d)
        out_a = fast_spread(fast_scatter(keep_a, send_a), d)
        down_grad = out_c.reshape(4 * b, width)
    else:
        out_b = plain_scatter(keep_b, send_b, False)
        out_a = plain_scatter(keep_a, send_a, False)
        down_grad = plain_scatter(keep_c, send_c, True)
    hidden_grad = jnp.concatenate([out_b[i] for i in range(4)], axis=1)
    triple_grad = jnp.concatenate([out_a[i] for i in range(3)], axis=1)
    output_grad = out_a[3]

    part = width // nf
    sums = jnp.concatenate(
        [row_sums, sums2[3:5], sums2[2:3], sums4[0:2], sums2[0:2], db_sum[0:1]], axis=0
    )
    lanes = sums.reshape(rows + 8, nf, part).transpose(1, 0, 2).reshape(nf, (rows + 8) * part)
    payload = jnp.concatenate([lanes, hb_sum[:4].reshape(nf, 4 * part)], axis=1)
    moved = lax.all_to_all(payload, "fsdp", 0, 0, tiled=True)
    moved = lax.all_gather(moved, "dp", axis=0, tiled=True)
    table_rows = moved[:, : rows * part].reshape(nd * nf * rows, part)
    all_hot = (steps[:, None] == ids.reshape(1, nd * nf * rows)).astype(f32)
    table_grad = jnp.dot(all_hot, table_rows, precision=highest)
    vec_sums = jnp.sum(moved[:, rows * part :], axis=0)
    v = [vec_sums[i * part : (i + 1) * part] for i in range(8)]
    hidden_bias_grad = vec_sums[8 * part :]
    shape = tokens.shape
    return (
        result.reshape(shape), input_grad.reshape(shape), table_grad, triple_grad, v[0], v[1], output_grad, v[2],
        v[3], v[4], v[5], v[6], hidden_grad, hidden_bias_grad, down_grad, v[7],
    )


def solution(mesh):
    fast = mesh.shape["dp"] == 4 and mesh.shape["fsdp"] == 8
    batch = ("dp", "fsdp")
    vec, mat, tab = P("fsdp"), P("fsdp", None), P(None, "fsdp")
    tokens_spec = P(None, batch, None, None)
    return jax.shard_map(
        functools.partial(per_device, fast),
        mesh=mesh,
        in_specs=(
            tokens_spec, P(None, batch), P(None, batch, None), P(None, batch, None), tokens_spec,
            tab, mat, vec, vec, mat, vec, vec, vec, vec, vec, mat, vec, mat, vec,
        ),
        out_specs=(
            tokens_spec, tokens_spec, tab, mat, vec, vec, mat, vec, vec, vec, vec, vec, mat, vec, mat, vec,
        ),
        check_vma=False,
    )
```

time: 744 us -> 390 us (0.52)
  waiting for transfers between devices: 396 us -> 95.6 us
  matrix products: 129 us -> 1.65 us
  Pallas kernels: 0 us -> 113 us
  starting transfers between devices: 0.44 us -> 83.8 us
  local copies, waits for them, and re-layouts: 78.9 us -> 21.4 us
  blocking collectives: 80.8 us -> 53.3 us
  other arithmetic: 34.4 us -> 14 us
  between operations: 17.4 us -> 2.52 us
    reduce_scatter x5 -> x0, waiting for transfers between devices: 285 us -> none  [the longest x1 100 us: per_device(): lax.psum_scatter(grads[9], 'fsdp', scatter_dimension=0, tiled=True)]
    dot_general x38 -> x2, matrix products: 122 us -> 1.65 us  [the longest x1 1.42 us: per_device(): table_grad = jnp.dot(all_hot, table_rows, precision=highest)]
    pallas_call x0 -> x6, Pallas kernels: none -> 113 us  [call(): pl.pallas_call(kernel, grid=grid, in_specs=in_specs, out_shape=out_shape,...]
    ppermute x0 -> x70, waiting for transfers between devices: none -> 95.6 us  [the longest x15 55.3 us: x_swap(): return lax.ppermute(v, 'dp', xor_perm(4, 1))]
    ppermute x0 -> x70, starting transfers between devices: none -> 76.7 us  [the longest x18 37.6 us: z_shift(): return lax.ppermute(v, 'fsdp', [(i, (i + 2 * k) % 8) for i in range(8)])]
    all_gather x5 -> x0, waiting for transfers between devices: 65.7 us -> none  [the longest x1 41 us: per_device(): lax.all_gather(hidden_weight, 'fsdp', axis=0, tiled=True)]
    unnamed x2 -> x0, blocking collectives: 56.9 us -> none
    psum x1 -> x0, waiting for transfers between devices: 42.4 us -> none  [per_device(): lax.psum((totals[0], totals[1], totals[2], totals[3], totals[4], totals[5...]
  transfers between devices with their start and end apart: 11 -> 72, of which waited for: 8 -> 25; matrix products, arithmetic and copies ran while one was open for 24% -> 8% of each run, Pallas kernels for 0% -> 14%
where the time goes in v1:
time: 390 us; the launch traced here: 385 us
  Pallas kernels  113 us (29%)
  waiting for transfers between devices  95.6 us (25%)
  starting transfers between devices  83.8 us (21%)
  blocking collectives  53.3 us (14%)
  local copies, waits for them, and re-layouts  21.4 us (5%)
  other arithmetic  14 us (4%)
    pallas_call x6, Pallas kernels, call(): pl.pallas_call(kernel, grid=grid, in_specs=in_specs, out_shape=out_shape,...  113 us
    ppermute x15, waiting for transfers between devices, x_swap(): return lax.ppermute(v, 'dp', xor_perm(4, 1))  55.3 us
    all_gather x1, blocking collectives, per_device(): lax.all_gather(timesteps.reshape(1, rows), ('dp', 'fsdp'), axis=0, tiled=...  44.9 us
    ppermute x18, starting transfers between devices, z_shift(): return lax.ppermute(v, 'fsdp', [(i, (i + 2 * k) % 8) for i in range(8)])  37.6 us
    ppermute x18, waiting for transfers between devices, z_shift(): return lax.ppermute(v, 'fsdp', [(i, (i + 2 * k) % 8) for i in range(8)])  24.3 us
    ppermute x15, starting transfers between devices, y_swap(): return lax.ppermute(v, 'dp', xor_perm(4, 2))  17.1 us
    ppermute x15, starting transfers between devices, x_swap(): return lax.ppermute(v, 'dp', xor_perm(4, 1))  13.4 us
    ppermute x15, waiting for transfers between devices, y_swap(): return lax.ppermute(v, 'dp', xor_perm(4, 2))  13.2 us
  transfers between devices with their start and end apart: 72, of which 25 were waited for; matrix products, arithmetic and copies ran while one was open for 8% of the time, Pallas kernels for 14%

profile of v1, /device:TPU:0, one launch (start us, length us, event | category | flops | bytes accessed | tf_op | source)
XLA Modules:
  0.0 385.1 jit_solution(2792391423971086273)
XLA Ops:
  2.2 5.1 %collective-permute-start.15 = (bf16[96,768]{1,0:T(8,128)(2,1)S(1)}, bf16[96,768]{1,0:T(8,128)(2,1)S(1)}, u32[]{:S(2)}, u32[]{:S(2)}) collective-permute-start(bf16[96,768]{1,0:T(8,128)(2,1)S(1)} %bitcast.261), channel_id=1, source_target_pairs={{0,6},{1,7},{2,0},{3,1},{4,2},{5,3},{6,4},{7,5},{8,14},{9,15},{10,... | collective-permute-start | bytes 442376 | tf_op jit(solution)/shard_map/ppermute | solution.py:527
  10.8 3.0 collective-permute-start.2
  13.9 44.9 %all-gather.1 = s32[32,1,6]{2,1,0:T(1,128)S(1)} all-gather(s32[1,1,6]{2,1,0:T(1,128)S(1)} %reshape.150), channel_id=1, replica_groups=mesh['dp'=4,'fsdp'=8] {'dp','fsdp'}, dimensions={0}, use_global_device_ids=true | all-gather | bytes 792 | tf_op jit(solution)/shard_map/all_gather | solution.py:623
  60.9 2.5 collective-permute-start
  65.1 12.8 %collective-permute-done.1 = bf16[112,768]{1,0:T(8,128)(2,1)S(1)} collective-permute-done((bf16[112,768]{1,0:T(8,128)(2,1)S(1)}, bf16[112,768]{1,0:T(8,128)(2,1)S(1)}, u32[]{:S(2)}, u32[]{:S(2)}) %collective-permute-start.1) | collective-permute-done | bytes 172064 | tf_op jit(solution)/shard_map/ppermute | solution.py:527
  81.6 3.1 collective-permute-done.27
  87.2 6.9 %collective-permute-done.16.rest_1_.rest_11_ = bf16[4,96,768]{2,1,0:T(8,128)(2,1)S(1)} collective-permute-done((bf16[4,96,768]{2,1,0:T(8,128)(2,1)S(1)}, bf16[4,96,768]{2,1,0:T(8,128)(2,1)S(1)}, u32[]{:S(2)}, u32[]{:S(2)}) %collective-permute-start.16) | collective-permute-done | bytes 589856 | tf_op jit(solution)/shard_map/ppermute | solution.py:519
  95.8 3.5 all-to-all-start
  103.7 3.1 collective-permute-done.4.rest_1_
  113.0 6.5 %collective-permute-done.28.rest_1_ = bf16[4,96,768]{2,1,0:T(8,128)(2,1)} collective-permute-done((bf16[4,96,768]{2,1,0:T(8,128)(2,1)S(1)}, bf16[4,96,768]{2,1,0:T(8,128)(2,1)}, u32[]{:S(2)}, u32[]{:S(2)}) %collective-permute-start.28) | collective-permute-done | bytes 589856 | tf_op jit(solution)/shard_map/ppermute | solution.py:519
  120.7 5.0 %collective-permute-done.19.rest_4_.rest_14_ = bf16[2,96,768]{2,1,0:T(8,128)(2,1)} collective-permute-done((bf16[2,96,768]{2,1,0:T(8,128)(2,1)S(1)}, bf16[2,96,768]{2,1,0:T(8,128)(2,1)}, u32[]{:S(2)}, u32[]{:S(2)}) %collective-permute-start.19) | collective-permute-done | bytes 294944 | tf_op jit(solution)/shard_map/ppermute | solution.py:519
  127.0 5.1 %collective-permute-done.7.rest_4_ = bf16[2,96,768]{2,1,0:T(8,128)(2,1)} collective-permute-done((bf16[2,96,768]{2,1,0:T(8,128)(2,1)S(1)}, bf16[2,96,768]{2,1,0:T(8,128)(2,1)}, u32[]{:S(2)}, u32[]{:S(2)}) %collective-permute-start.7) | collective-permute-done | bytes 294944 | tf_op jit(solution)/shard_map/ppermute | solution.py:519
  135.1 2.3 collective-permute-done.31.rest_4_
  139.8 15.5 %shard_map.306 = (bf16[768,768]{1,0:T(8,128)(2,1)}, bf16[3,768,768]{2,1,0:T(8,128)(2,1)}, bf16[36,256,128]{2,1,0:T(8,128)(2,1)}, bf16[768,768]{1,0:T(8,128)(2,1)...) custom-call(s32[32]{0:T(128)} %stack.584.slots.slots_a.slots_b, bf16[768,768]{1,0:T(8,128)(2,1)} %bitcast.291, ...), custom_call_target="tpu_custom_call" | custom-call | flops 10871635968 | bytes 20971520 | tf_op jit(solution)/shard_map/pallas_call | solution.py:344
  156.6 19.2 %shard_map.307 = (bf16[4,768,768]{2,1,0:T(8,128)(2,1)}, bf16[4,768,768]{2,1,0:T(8,128)(2,1)}, bf16[16,96,768]{2,1,0:T(8,128)(2,1)}, bf16[16,96,768]{2,1,0:T(8,128)(2,1)}) custom-call(s32[32]{0:T(128)} %stack.584.slots.slots_a.slots_b, s32[17]{0:T(128)} %stack.602.gpos, bf16[768,768]{1,0:T(8,128)(2,1)} %get-tuple-element.39.n2_ref, ...), custom_call_target="tpu_custom_call" | custom-call | flops 14495514624 | bytes 20971520 | tf_op jit(solution)/shard_map/pallas_call | solution.py:344
  177.2 19.8 %shard_map.309 = (bf16[4,768,768]{2,1,0:T(8,128)(2,1)}, f32[8,768]{1,0:T(8,128)}, f32[8,768]{1,0:T(8,128)}, bf16[16,96,768]{2,1,0:T(8,128)(2,1)}, bf16[16,96,768]{2,1,0:T(8,128)(2,1)}) custom-call(s32[32]{0:T(128)} %stack.551.slots, s32[17]{0:T(128)} %stack.602.gpos, bf16[768,768]{1,0:T(8,128)(2,1)} %get-tuple-element.39.n2_ref, bf16[768,768]{1,0:T(8,128)(2,1)} %bitcast.289, ...), custom_call_target="tpu_custom_call" | custom-call | flops 14495514624 | bytes 20971520 | tf_op jit(solution)/shard_map/pallas_call | solution.py:344
  197.0 38.8 %shard_map.310 = (f32[768,768]{1,0:T(8,128)}, bf16[3,768,768]{2,1,0:T(8,128)(2,1)}, f32[8,768]{1,0:T(8,128)}, bf16[16,96,768]{2,1,0:T(8,128)(2,1)}, bf16[16,96,768]{2,1,0:T(8,128)(2,1)}) custom-call(s32[32]{0:T(128)} %stack.584.slots.slots_a.slots_b, s32[32]{0:T(128)} %stack.584.slots.slots_a.slots_b, s32[17]{0:T(128)} %stack.602.gpos, ...), custom_call_target="tpu_custom_call" | custom-call | flops 14495514624 | bytes 41943040 | tf_op jit(solution)/shard_map/pallas_call | solution.py:344
  237.9 9.7 %shard_map.311 = (bf16[768,768]{1,0:T(8,128)(2,1)}, f32[8,768]{1,0:T(8,128)}, f32[8,768]{1,0:T(8,128)}) custom-call(s32[32]{0:T(128)} %stack.584.slots.slots_a.slots_b, bf16[768,768]{1,0:T(8,128)(2,1)} %bitcast.292, f32[6,768]{1,0:T(8,128)} %reshape.137.emb_ref, f32[768,768]{1,0:T(8,128)} %get-tuple-element.48.dmid_ref, ...), custom_call_target="tpu_custom_call" | custom-call | flops 5435817984 | bytes 12582912 | tf_op jit(solution)/shard_map/pallas_call | solution.py:344
  250.9 3.6 all-to-all-start.1
  255.0 9.8 %shard_map.308 = bf16[768,768]{1,0:T(8,128)(2,1)} custom-call(s32[32]{0:T(128)} %stack.551.slots, bf16[4,768,768]{2,1,0:T(8,128)(2,1)} %get-tuple-element.40.act_ref, f32[768,768]{1,0:T(8,128)} %get-tuple-element.41.middle_ref, f32[8,768]{1,0:T(8,128)} %reshape.123.vec_ref, bf16[4,96,768]{2,1,0:T(8,128)(2,1)} %copy-done.5, ...), custom_call_target="tpu_custom_call" | custom-call | flops 7247757312 | bytes 12582912 | tf_op jit(solution)/shard_map/pallas_call | solution.py:344
  264.8 8.4 %all-gather = f32[32,1,1728]{2,1,0:T(1,128)S(1)} all-gather(f32[8,1,1728]{2,1,0:T(1,128)S(1)} %all-to-all-done.1), channel_id=2, replica_groups=mesh['dp'=4,'fsdp'=8] {'dp'}, dimensions={0}, use_global_device_ids=true | all-gather | bytes 276480 | tf_op jit(solution)/shard_map/all_gather | solution.py:685
  280.6 2.3 add_convert_fusion.21
  288.7 6.0 %collective-permute-done.38 = bf16[2,2,96,768]{3,2,1,0:T(8,128)(2,1)S(1)} collective-permute-done((bf16[2,2,96,768]{3,2,1,0:T(8,128)(2,1)S(1)}, bf16[2,2,96,768]{3,2,1,0:T(8,128)(2,1)S(1)}, u32[]{:S(2)}, u32[]{:S(2)}) %collective-permute-start.38) | collective-permute-done | bytes 589856 | tf_op jit(solution)/shard_map/ppermute | solution.py:519
  297.2 10.2 %collective-permute-done.49 = bf16[2,2,96,768]{3,2,1,0:T(8,128)(2,1)S(1)} collective-permute-done((bf16[2,2,96,768]{3,2,1,0:T(8,128)(2,1)S(1)}, bf16[2,2,96,768]{3,2,1,0:T(8,128)(2,1)S(1)}, u32[]{:S(2)}, u32[]{:S(2)}) %collective-permute-start.49) | collective-permute-done | bytes 589856 | tf_op jit(solution)/shard_map/ppermute | solution.py:519
  309.8 10.2 %collective-permute-done.60 = bf16[2,2,96,768]{3,2,1,0:T(8,128)(2,1)S(1)} collective-permute-done((bf16[2,2,96,768]{3,2,1,0:T(8,128)(2,1)S(1)}, bf16[2,2,96,768]{3,2,1,0:T(8,128)(2,1)S(1)}, u32[]{:S(2)}, u32[]{:S(2)}) %collective-permute-start.60) | collective-permute-done | bytes 589856 | tf_op jit(solution)/shard_map/ppermute | solution.py:519
  322.5 5.0 %collective-permute-done.39 = bf16[2,96,768]{2,1,0:T(8,128)(2,1)S(1)} collective-permute-done((bf16[2,96,768]{2,1,0:T(8,128)(2,1)S(1)}, bf16[2,96,768]{2,1,0:T(8,128)(2,1)S(1)}, u32[]{:S(2)}, u32[]{:S(2)}) %collective-permute-start.39) | collective-permute-done | bytes 294944 | tf_op jit(solution)/shard_map/ppermute | solution.py:523
  330.4 3.2 collective-permute-done.50
  333.6 2.7 collective-permute-start.43
  342.9 3.3 collective-permute-done.43
  349.2 5.9 %collective-permute-start.65 = (bf16[96,768]{1,0:T(8,128)(2,1)S(1)}, bf16[96,768]{1,0:T(8,128)(2,1)S(1)}, u32[]{:S(2)}, u32[]{:S(2)}) collective-permute-start(bf16[96,768]{1,0:T(8,128)(2,1)S(1)} %get-tuple-element.113), channel_id=1, source_target_pairs={{0,4},{1,5},{2,6},{3,7},{4,0},{5,1},{6,2},{7,3},{8,12},{9,13},{10,... | collective-permute-start | bytes 442376 | tf_op jit(solution)/shard_map/ppermute | solution.py:527
  355.2 3.4 collective-permute-start.66
  358.6 3.1 collective-permute-done.54
  (327 shorter events, 98.6 us)
Async XLA Ops:
  2.2 56.7 %collective-permute-start.15 = (bf16[96,768]{1,0:T(8,128)(2,1)S(1)}, bf16[96,768]{1,0:T(8,128)(2,1)S(1)}, u32[]{:S(2)}, u32[]{:S(2)}) collective-permute-start(bf16[96,768]{1,0:T(8,128)(2,1)S(1)} %bitcast.261), channel_id=1, source_target_pairs={{0,6},{1,7},{2,0},{3,1},{4,2},{5,3},{6,4},{7,5},{8,14},{9,15},{10,... | collective-permute-start | bytes 442376 | tf_op jit(solution)/shard_map/ppermute | solution.py:527
  7.3 53.5 %collective-permute-start.14 = (bf16[96,768]{1,0:T(8,128)(2,1)S(1)}, bf16[96,768]{1,0:T(8,128)(2,1)S(1)}, u32[]{:S(2)}, u32[]{:S(2)}) collective-permute-start(bf16[96,768]{1,0:T(8,128)(2,1)S(1)} %bitcast.262), channel_id=1, source_target_pairs={{0,4},{1,5},{2,6},{3,7},{4,0},{5,1},{6,2},{7,3},{8,12},{9,13},{10,... | collective-permute-start | bytes 442376 | tf_op jit(solution)/shard_map/ppermute | solution.py:527
  7.4 53.5 %collective-permute-start.13 = (bf16[96,768]{1,0:T(8,128)(2,1)S(1)}, bf16[96,768]{1,0:T(8,128)(2,1)S(1)}, u32[]{:S(2)}, u32[]{:S(2)}) collective-permute-start(bf16[96,768]{1,0:T(8,128)(2,1)S(1)} %bitcast.263), channel_id=1, source_target_pairs={{0,2},{1,3},{2,4},{3,5},{4,6},{5,7},{6,0},{7,1},{8,10},{9,11},{10,... | collective-permute-start | bytes 442376 | tf_op jit(solution)/shard_map/ppermute | solution.py:527
  8.4 71.0 %collective-permute-start.26 = (bf16[96,768]{1,0:T(8,128)(2,1)S(1)}, bf16[96,768]{1,0:T(8,128)(2,1)S(1)}, u32[]{:S(2)}, u32[]{:S(2)}) collective-permute-start(bf16[96,768]{1,0:T(8,128)(2,1)S(1)} %constant_dynamic-slice_fusion.15), channel_id=1, source_target_pairs={{0,4},{1,5},{2,6},{3,7},{4,0},{5,1},{6,2},{7,3},{8,12},{9,13},{10,... | collective-permute-start | bytes 442376 | tf_op jit(solution)/shard_map/ppermute | solution.py:527
  10.8 52.7 %collective-permute-start.2 = (bf16[112,768]{1,0:T(8,128)(2,1)S(1)}, bf16[112,768]{1,0:T(8,128)(2,1)S(1)}, u32[]{:S(2)}, u32[]{:S(2)}) collective-permute-start(bf16[112,768]{1,0:T(8,128)(2,1)S(1)} %pad_maximum_fusion.15), channel_id=1, source_target_pairs={{0,6},{1,7},{2,0},{3,1},{4,2},{5,3},{6,4},{7,5},{8,14},{9,15},{10,... | collective-permute-start | bytes 516104 | tf_op jit(solution)/shard_map/ppermute | solution.py:527
  58.9 20.5 %collective-permute-start.25 = (bf16[96,768]{1,0:T(8,128)(2,1)S(1)}, bf16[96,768]{1,0:T(8,128)(2,1)S(1)}, u32[]{:S(2)}, u32[]{:S(2)}) collective-permute-start(bf16[96,768]{1,0:T(8,128)(2,1)S(1)} %constant_dynamic-slice_fusion.15), channel_id=1, source_target_pairs={{0,2},{1,3},{2,4},{3,5},{4,6},{5,7},{6,0},{7,1},{8,10},{9,11},{10,... | collective-permute-start | bytes 442376 | tf_op jit(solution)/shard_map/ppermute | solution.py:527
  63.5 22.7 %collective-permute-start.17 = (bf16[4,96,768]{2,1,0:T(8,128)(2,1)S(1)}, bf16[4,96,768]{2,1,0:T(8,128)(2,1)S(1)}, u32[]{:S(2)}, u32[]{:S(2)}) collective-permute-start(bf16[4,96,768]{2,1,0:T(8,128)(2,1)S(1)} %pad_maximum_fusion.3.rest_0_.rest_10_), channel_id=1, source_target_pairs={{0,16},{8,24},{16,0},{24,8},{1,17},{9,25},{17,1},{25,9},{2,18},{10... | collective-permute-start | bytes 1769480 | tf_op jit(solution)/shard_map/ppermute | solution.py:523
  79.5 27.4 %collective-permute-start.4 = (bf16[4,96,768]{2,1,0:T(8,128)(2,1)S(1)}, bf16[4,96,768]{2,1,0:T(8,128)(2,1)}, u32[]{:S(2)}, u32[]{:S(2)}) collective-permute-start(bf16[4,96,768]{2,1,0:T(8,128)(2,1)S(1)} %pad_maximum_fusion.2.rest_0_), channel_id=1, source_target_pairs={{0,8},{8,0},{16,24},{24,16},{1,9},{9,1},{17,25},{25,17},{2,10},{10... | collective-permute-start | bytes 1769480 | tf_op jit(solution)/shard_map/ppermute | solution.py:519
  86.0 23.7 %collective-permute-start.20 = (bf16[4,96,768]{2,1,0:T(8,128)(2,1)S(1)}, bf16[4,96,768]{2,1,0:T(8,128)(2,1)}, u32[]{:S(2)}, u32[]{:S(2)}) collective-permute-start(bf16[4,96,768]{2,1,0:T(8,128)(2,1)S(1)} %pad_maximum_fusion.3.rest_0_.rest_10_), channel_id=1, source_target_pairs={{0,1},{1,0},{2,3},{3,2},{4,5},{5,4},{6,7},{7,6},{8,9},{9,8},{10,11... | collective-permute-start | bytes 1769480 | tf_op jit(solution)/shard_map/ppermute | solution.py:515
  86.1 24.9 %collective-permute-start.29 = (bf16[4,96,768]{2,1,0:T(8,128)(2,1)S(1)}, bf16[4,96,768]{2,1,0:T(8,128)(2,1)}, u32[]{:S(2)}, u32[]{:S(2)}) collective-permute-start(bf16[4,96,768]{2,1,0:T(8,128)(2,1)S(1)} %pad_maximum_fusion.4.rest_0_), channel_id=1, source_target_pairs={{0,16},{8,24},{16,0},{24,8},{1,17},{9,25},{17,1},{25,9},{2,18},{10... | collective-permute-start | bytes 1769480 | tf_op jit(solution)/shard_map/ppermute | solution.py:523
  94.1 25.4 %collective-permute-start.28 = (bf16[4,96,768]{2,1,0:T(8,128)(2,1)S(1)}, bf16[4,96,768]{2,1,0:T(8,128)(2,1)}, u32[]{:S(2)}, u32[]{:S(2)}) collective-permute-start(bf16[4,96,768]{2,1,0:T(8,128)(2,1)S(1)} %pad_maximum_fusion.4.rest_0_), channel_id=1, source_target_pairs={{0,8},{8,0},{16,24},{24,16},{1,9},{9,1},{17,25},{25,17},{2,10},{10... | collective-permute-start | bytes 1769480 | tf_op jit(solution)/shard_map/ppermute | solution.py:519
  94.3 26.4 %collective-permute-start.8 = (bf16[4,96,768]{2,1,0:T(8,128)(2,1)S(1)}, bf16[4,96,768]{2,1,0:T(8,128)(2,1)}, u32[]{:S(2)}, u32[]{:S(2)}) collective-permute-start(bf16[4,96,768]{2,1,0:T(8,128)(2,1)S(1)} %pad_maximum_fusion.2.rest_0_), channel_id=1, source_target_pairs={{0,1},{1,0},{2,3},{3,2},{4,5},{5,4},{6,7},{7,6},{8,9},{9,8},{10,11... | collective-permute-start | bytes 1769480 | tf_op jit(solution)/shard_map/ppermute | solution.py:515
  106.8 19.0 %collective-permute-start.19 = (bf16[2,96,768]{2,1,0:T(8,128)(2,1)S(1)}, bf16[2,96,768]{2,1,0:T(8,128)(2,1)}, u32[]{:S(2)}, u32[]{:S(2)}) collective-permute-start(bf16[2,96,768]{2,1,0:T(8,128)(2,1)S(1)} %slice.491), channel_id=1, source_target_pairs={{0,8},{8,0},{16,24},{24,16},{1,9},{9,1},{17,25},{25,17},{2,10},{10... | collective-permute-start | bytes 884744 | tf_op jit(solution)/shard_map/ppermute | solution.py:519
  111.0 21.1 %collective-permute-start.7 = (bf16[2,96,768]{2,1,0:T(8,128)(2,1)S(1)}, bf16[2,96,768]{2,1,0:T(8,128)(2,1)}, u32[]{:S(2)}, u32[]{:S(2)}) collective-permute-start(bf16[2,96,768]{2,1,0:T(8,128)(2,1)S(1)} %slice.488), channel_id=1, source_target_pairs={{0,8},{8,0},{16,24},{24,16},{1,9},{9,1},{17,25},{25,17},{2,10},{10... | collective-permute-start | bytes 884744 | tf_op jit(solution)/shard_map/ppermute | solution.py:519
  155.3 20.5 %collective-permute-start.32 = (bf16[4,96,768]{2,1,0:T(8,128)(2,1)S(1)}, bf16[4,96,768]{2,1,0:T(8,128)(2,1)S(1)}, u32[]{:S(2)}, u32[]{:S(2)}) collective-permute-start(bf16[4,96,768]{2,1,0:T(8,128)(2,1)S(1)} %pad_maximum_fusion.4.rest_0_), channel_id=1, source_target_pairs={{0,1},{1,0},{2,3},{3,2},{4,5},{5,4},{6,7},{7,6},{8,9},{9,8},{10,11... | collective-permute-start | bytes 1769480 | tf_op jit(solution)/shard_map/ppermute | solution.py:515
  155.6 20.2 %collective-permute-start.34 = (bf16[4,96,768]{2,1,0:T(8,128)(2,1)}, bf16[4,96,768]{2,1,0:T(8,128)(2,1)S(1)}, u32[]{:S(2)}, u32[]{:S(2)}) collective-permute-start(bf16[4,96,768]{2,1,0:T(8,128)(2,1)} %collective-permute-done.29.rest_2_), channel_id=1, source_target_pairs={{0,1},{1,0},{2,3},{3,2},{4,5},{5,4},{6,7},{7,6},{8,9},{9,8},{10,11... | collective-permute-start | bytes 1769480 | tf_op jit(solution)/shard_map/ppermute | solution.py:515
  155.9 19.9 %collective-permute-start.33 = (bf16[4,96,768]{2,1,0:T(8,128)(2,1)}, bf16[4,96,768]{2,1,0:T(8,128)(2,1)S(1)}, u32[]{:S(2)}, u32[]{:S(2)}) collective-permute-start(bf16[4,96,768]{2,1,0:T(8,128)(2,1)} %collective-permute-done.28.rest_1_), channel_id=1, source_target_pairs={{0,1},{1,0},{2,3},{3,2},{4,5},{5,4},{6,7},{7,6},{8,9},{9,8},{10,11... | collective-permute-start | bytes 1769480 | tf_op jit(solution)/shard_map/ppermute | solution.py:515
  156.1 19.8 %collective-permute-start.36 = (bf16[2,96,768]{2,1,0:T(8,128)(2,1)}, bf16[2,96,768]{2,1,0:T(8,128)(2,1)S(1)}, u32[]{:S(2)}, u32[]{:S(2)}) collective-permute-start(bf16[2,96,768]{2,1,0:T(8,128)(2,1)} %collective-permute-done.31.rest_4_), channel_id=1, source_target_pairs={{0,1},{1,0},{2,3},{3,2},{4,5},{5,4},{6,7},{7,6},{8,9},{9,8},{10,11... | collective-permute-start | bytes 884744 | tf_op jit(solution)/shard_map/ppermute | solution.py:515
  156.4 19.5 %collective-permute-start.35 = (bf16[2,96,768]{2,1,0:T(8,128)(2,1)S(1)}, bf16[2,96,768]{2,1,0:T(8,128)(2,1)S(1)}, u32[]{:S(2)}, u32[]{:S(2)}) collective-permute-start(bf16[2,96,768]{2,1,0:T(8,128)(2,1)S(1)} %collective-permute-done.30.rest_3_), channel_id=1, source_target_pairs={{0,1},{1,0},{2,3},{3,2},{4,5},{5,4},{6,7},{7,6},{8,9},{9,8},{10,11... | collective-permute-start | bytes 884744 | tf_op jit(solution)/shard_map/ppermute | solution.py:515
  235.9 40.2 %collective-permute-start.37 = (bf16[16,96,768]{2,1,0:T(8,128)(2,1)}, bf16[16,96,768]{2,1,0:T(8,128)(2,1)}, u32[]{:S(2)}, u32[]{:S(2)}) collective-permute-start(bf16[16,96,768]{2,1,0:T(8,128)(2,1)} %get-tuple-element.57), channel_id=1, source_target_pairs={{0,1},{1,0},{2,3},{3,2},{4,5},{5,4},{6,7},{7,6},{8,9},{9,8},{10,11... | collective-permute-start | bytes 7077896 | tf_op jit(solution)/shard_map/ppermute | solution.py:515
  237.7 42.9 %collective-permute-start.48 = (bf16[16,96,768]{2,1,0:T(8,128)(2,1)}, bf16[16,96,768]{2,1,0:T(8,128)(2,1)}, u32[]{:S(2)}, u32[]{:S(2)}) collective-permute-start(bf16[16,96,768]{2,1,0:T(8,128)(2,1)} %get-tuple-element.59), channel_id=1, source_target_pairs={{0,1},{1,0},{2,3},{3,2},{4,5},{5,4},{6,7},{7,6},{8,9},{9,8},{10,11... | collective-permute-start | bytes 7077896 | tf_op jit(solution)/shard_map/ppermute | solution.py:515
  254.5 30.7 %collective-permute-start.59 = (bf16[16,96,768]{2,1,0:T(8,128)(2,1)}, bf16[16,96,768]{2,1,0:T(8,128)(2,1)}, u32[]{:S(2)}, u32[]{:S(2)}) collective-permute-start(bf16[16,96,768]{2,1,0:T(8,128)(2,1)} %get-tuple-element.61), channel_id=1, source_target_pairs={{0,1},{1,0},{2,3},{3,2},{4,5},{5,4},{6,7},{7,6},{8,9},{9,8},{10,11... | collective-permute-start | bytes 7077896 | tf_op jit(solution)/shard_map/ppermute | solution.py:515
  283.0 24.4 %collective-permute-start.49 = (bf16[2,2,96,768]{3,2,1,0:T(8,128)(2,1)S(1)}, bf16[2,2,96,768]{3,2,1,0:T(8,128)(2,1)S(1)}, u32[]{:S(2)}, u32[]{:S(2)}) collective-permute-start(bf16[2,2,96,768]{3,2,1,0:T(8,128)(2,1)S(1)} %pad_maximum_fusion.8), channel_id=1, source_target_pairs={{0,8},{8,0},{16,24},{24,16},{1,9},{9,1},{17,25},{25,17},{2,10},{10... | collective-permute-start | bytes 1769480 | tf_op jit(solution)/shard_map/ppermute | solution.py:519
  284.1 24.4 %collective-permute-start.52 = (bf16[2,2,96,768]{3,2,1,0:T(8,128)(2,1)S(1)}, bf16[2,2,96,768]{3,2,1,0:T(8,128)(2,1)S(1)}, u32[]{:S(2)}, u32[]{:S(2)}) collective-permute-start(bf16[2,2,96,768]{3,2,1,0:T(8,128)(2,1)S(1)} %pad_maximum_fusion.9), channel_id=1, source_target_pairs={{0,16},{8,24},{16,0},{24,8},{1,17},{9,25},{17,1},{25,9},{2,18},{10... | collective-permute-start | bytes 1769480 | tf_op jit(solution)/shard_map/ppermute | solution.py:523
  287.6 32.4 %collective-permute-start.60 = (bf16[2,2,96,768]{3,2,1,0:T(8,128)(2,1)S(1)}, bf16[2,2,96,768]{3,2,1,0:T(8,128)(2,1)S(1)}, u32[]{:S(2)}, u32[]{:S(2)}) collective-permute-start(bf16[2,2,96,768]{3,2,1,0:T(8,128)(2,1)S(1)} %pad_maximum_fusion.11), channel_id=1, source_target_pairs={{0,8},{8,0},{16,24},{24,16},{1,9},{9,1},{17,25},{25,17},{2,10},{10... | collective-permute-start | bytes 1769480 | tf_op jit(solution)/shard_map/ppermute | solution.py:519
  294.7 26.4 %collective-permute-start.63 = (bf16[2,2,96,768]{3,2,1,0:T(8,128)(2,1)S(1)}, bf16[2,2,96,768]{3,2,1,0:T(8,128)(2,1)S(1)}, u32[]{:S(2)}, u32[]{:S(2)}) collective-permute-start(bf16[2,2,96,768]{3,2,1,0:T(8,128)(2,1)S(1)} %pad_maximum_fusion.12), channel_id=1, source_target_pairs={{0,16},{8,24},{16,0},{24,8},{1,17},{9,25},{17,1},{25,9},{2,18},{10... | collective-permute-start | bytes 1769480 | tf_op jit(solution)/shard_map/ppermute | solution.py:523
  295.9 31.5 %collective-permute-start.39 = (bf16[2,96,768]{2,1,0:T(8,128)(2,1)S(1)}, bf16[2,96,768]{2,1,0:T(8,128)(2,1)S(1)}, u32[]{:S(2)}, u32[]{:S(2)}) collective-permute-start(bf16[2,96,768]{2,1,0:T(8,128)(2,1)S(1)} %slice_bitcast_fusion.18), channel_id=1, source_target_pairs={{0,16},{8,24},{16,0},{24,8},{1,17},{9,25},{17,1},{25,9},{2,18},{10... | collective-permute-start | bytes 884744 | tf_op jit(solution)/shard_map/ppermute | solution.py:523
  307.4 21.2 %collective-permute-start.42 = (bf16[2,96,768]{2,1,0:T(8,128)(2,1)S(1)}, bf16[2,96,768]{2,1,0:T(8,128)(2,1)S(1)}, u32[]{:S(2)}, u32[]{:S(2)}) collective-permute-start(bf16[2,96,768]{2,1,0:T(8,128)(2,1)S(1)} %slice_bitcast_fusion.16), channel_id=1, source_target_pairs={{0,8},{8,0},{16,24},{24,16},{1,9},{9,1},{17,25},{25,17},{2,10},{10... | collective-permute-start | bytes 884744 | tf_op jit(solution)/shard_map/ppermute | solution.py:519
  308.5 25.1 %collective-permute-start.50 = (bf16[2,96,768]{2,1,0:T(8,128)(2,1)S(1)}, bf16[2,96,768]{2,1,0:T(8,128)(2,1)S(1)}, u32[]{:S(2)}, u32[]{:S(2)}) collective-permute-start(bf16[2,96,768]{2,1,0:T(8,128)(2,1)S(1)} %slice_bitcast_fusion.10), channel_id=1, source_target_pairs={{0,16},{8,24},{16,0},{24,8},{1,17},{9,25},{17,1},{25,9},{2,18},{10... | collective-permute-start | bytes 884744 | tf_op jit(solution)/shard_map/ppermute | solution.py:523
  338.8 22.9 %collective-permute-start.54 = (bf16[96,768]{1,0:T(8,128)(2,1)S(1)}, bf16[96,768]{1,0:T(8,128)(2,1)S(1)}, u32[]{:S(2)}, u32[]{:S(2)}) collective-permute-start(bf16[96,768]{1,0:T(8,128)(2,1)S(1)} %get-tuple-element.115), channel_id=1, source_target_pairs={{0,4},{1,5},{2,6},{3,7},{4,0},{5,1},{6,2},{7,3},{8,12},{9,13},{10,... | collective-permute-start | bytes 442376 | tf_op jit(solution)/shard_map/ppermute | solution.py:527
  340.6 22.5 %collective-permute-start.55 = (bf16[96,768]{1,0:T(8,128)(2,1)S(1)}, bf16[96,768]{1,0:T(8,128)(2,1)S(1)}, u32[]{:S(2)}, u32[]{:S(2)}) collective-permute-start(bf16[96,768]{1,0:T(8,128)(2,1)S(1)} %get-tuple-element.116), channel_id=1, source_target_pairs={{0,6},{1,7},{2,0},{3,1},{4,2},{5,3},{6,4},{7,5},{8,14},{9,15},{10,... | collective-permute-start | bytes 442376 | tf_op jit(solution)/shard_map/ppermute | solution.py:527
  346.1 18.1 %collective-permute-start.62 = (bf16[96,768]{1,0:T(8,128)(2,1)S(1)}, bf16[96,768]{1,0:T(8,128)(2,1)S(1)}, u32[]{:S(2)}, u32[]{:S(2)}) collective-permute-start(bf16[96,768]{1,0:T(8,128)(2,1)S(1)} %slice_bitcast_fusion.22), channel_id=1, source_target_pairs={{0,2},{1,3},{2,4},{3,5},{4,6},{5,7},{6,0},{7,1},{8,10},{9,11},{10,... | collective-permute-start | bytes 442376 | tf_op jit(solution)/shard_map/ppermute | solution.py:527
  (79 other events, 967.4 us)

commit v2 on v1

--- a/solution.py
+++ b/solution.py
@@ -47,18 +47,26 @@
     return (e - jnp.mean(e, -1, keepdims=True) - xhat * jnp.mean(e * xhat, -1, keepdims=True)) * inv
 
 
-def load_blocks(slots_ref, pieces, layout, w_ref, sem):
-    copies = []
+def start_blocks(slots_ref, pieces, layout, w_ref, sem):
+    i = 0
     for piece, first, count in layout:
         for t in range(count):
-            i = len(copies)
-            copies.append(
-                pltpu.make_async_copy(pieces[piece].at[first + t], w_ref.at[slots_ref[i]], sem.at[i])
-            )
-    for cp in copies:
-        cp.start()
-    for cp in copies:
-        cp.wait()
+            slot = slots_ref[i]
+            pltpu.make_async_copy(pieces[piece].at[first + t], w_ref.at[slot], sem.at[slot]).start()
+            i += 1
+
+
+def wait_blocks(w_ref, sem, first, count):
+    def one(t, carry):
+        pltpu.make_async_copy(w_ref.at[first + t], w_ref.at[first + t], sem.at[first + t]).wait()
+        return carry
+
+    lax.fori_loop(0, count, one, 0)
+
+
+def load_blocks(slots_ref, pieces, layout, w_ref, sem):
+    start_blocks(slots_ref, pieces, layout, w_ref, sem)
+    wait_blocks(w_ref, sem, 0, 32)
 
 
 def square(w_ref, j):
@@ -158,8 +166,9 @@
 
     @pl.when(j == 0)
     def _():
-        load_blocks(slots, pieces, layout, w_ref, sem)
-
+        start_blocks(slots, pieces, layout, w_ref, sem)
+
+    wait_blocks(w_ref, sem, j * NB, NB)
     tokens, width = n2_ref.shape
     w = w_ref[pl.ds(j * NB, NB)].reshape(width, width)
     bias = hb_ref[pl.ds(j, 1), :]
@@ -193,12 +202,13 @@
 
     @pl.when(j == 0)
     def _():
-        load_blocks(slots, pieces, layout, w_ref, sem)
+        start_blocks(slots, pieces, layout, w_ref, sem)
         nt_ref[...] = n2_ref[...].T
         db_ref[...] = jnp.zeros_like(db_ref)
         db_ref[0:1] = jnp.sum(cot_ref[...].astype(f32), axis=0, keepdims=True)
         hb_ref[...] = jnp.zeros_like(hb_ref)
 
+    wait_blocks(w_ref, sem, j * NB, NB)
     w = w_ref[pl.ds(j * NB, NB)].reshape(width, width)
     sub = 32
     total = jnp.zeros((8, width), f32)
@@ -217,23 +227,18 @@
         put_pair(gpos, j * 4 + zf, keep_ref, send_ref, g[:b], g[b:])
 
 
-def b2_kernel(
-    layout_a, layout_b, rb, length, slots_a, slots_b, gpos,
-    dh_ref, cot_ref, middle_ref, triple_ref, att_ref, attended_ref, normed_ref, vec_ref, *rest
-):
+def b2_kernel(layout_a, layout_b, slots_a, slots_b, dh_ref, cot_ref, middle_ref, vec_ref, *rest):
     na = max(l[0] for l in layout_a) + 1
     nb = max(l[0] for l in layout_b) + 1
     pieces_a, pieces_b, rest = rest[:na], rest[na : na + nb], rest[na + nb :]
-    dmid_ref, dt_ref, sums_ref, keep_ref, send_ref, wa_ref, wb_ref, dbr_ref, dts_ref, sem_a, sem_b = rest
-    step = pl.program_id(0)
-    block = rb * length
-    width = cot_ref.shape[1]
-
-    @pl.when(step == 0)
-    def _():
-        load_blocks(slots_b, pieces_b, layout_b, wb_ref, sem_b)
-        load_blocks(slots_a, pieces_a, layout_a, wa_ref, sem_a)
+    dmid_ref, dbr_ref, datt_ref, sums_ref, wa_ref, wb_ref, sem_a, sem_b = rest
+
+    @pl.when(pl.program_id(0) == 0)
+    def _():
+        start_blocks(slots_b, pieces_b, layout_b, wb_ref, sem_b)
+        start_blocks(slots_a, pieces_a, layout_a, wa_ref, sem_a)
         sums_ref[...] = jnp.zeros_like(sums_ref)
+        wait_blocks(wb_ref, sem_b, 0, 32)
 
     d_n2 = mm_nt(dh_ref[0], square(wb_ref, 0))
     for j in range(1, 4):
@@ -244,17 +249,30 @@
     d_middle = cot_ref[...].astype(f32) + ln_back(d_n2 * vec_ref[5:6, :], xhat, inv)
     dmid_ref[...] = d_middle
     d_branch = d_middle.astype(bf16)
-    base = pl.multiple_of(step * block, block)
-    dbr_ref[pl.ds(base, block)] = d_branch
+    dbr_ref[...] = d_branch
     sums_ref[2:3] += jnp.sum(d_branch.astype(f32), axis=0, keepdims=True)
-    d_att = mm_nt(d_branch, square(wa_ref, 3)).astype(bf16)
+
+    @pl.when(pl.program_id(0) == 0)
+    def _():
+        wait_blocks(wa_ref, sem_a, 0, 32)
+
+    datt_ref[...] = mm_nt(d_branch, square(wa_ref, 3)).astype(bf16)
+
+
+def b3_kernel(rb, length, datt_ref, triple_ref, att_ref, dt_ref, sums_ref):
+    width = datt_ref.shape[1]
+
+    @pl.when(pl.program_id(0) == 0)
+    def _():
+        sums_ref[...] = jnp.zeros_like(sums_ref)
+
     first = half_mask(length, 2 * HD)
     pairs = width // (2 * HD)
     for r in range(rb):
         rows = slice(r * length, (r + 1) * length)
         for hp in range(pairs):
             lanes = slice(hp * 2 * HD, (hp + 1) * 2 * HD)
-            dos = both(d_att[rows, lanes], first)
+            dos = both(datt_ref[rows, lanes], first)
             p_low = att_ref[r * pairs + hp]
             p = p_low.astype(f32)
             d_a = mm_nt(dos, triple_ref[2, rows, lanes])
@@ -264,28 +282,35 @@
             dt_ref[0, rows, lanes] = (mm(wide, both(triple_ref[1, rows, lanes], first)) * SCALE).astype(bf16)
             dt_ref[1, rows, lanes] = (mm_tn(ds, both(triple_ref[0, rows, lanes], first)) * SCALE).astype(bf16)
             dt_ref[2, rows, lanes] = mm_tn(p_low, dos).astype(bf16)
-    sums_ref[3:4] += jnp.sum(dt_ref[0].astype(f32), axis=0, keepdims=True)
-    sums_ref[4:5] += jnp.sum(dt_ref[2].astype(f32), axis=0, keepdims=True)
-    for q in range(3):
-        dts_ref[q, pl.ds(base, block)] = dt_ref[q]
-
-    @pl.when(step == pl.num_programs(0) - 1)
-    def _():
-        b = width // NB
-        hw = width // 2
-        for h in range(2):
-            cols = slice(h * hw, (h + 1) * hw)
-            for q in range(4):
-                if q < 3:
-                    g = mm_tn(normed_ref[:, cols], dts_ref[q])
-                else:
-                    g = mm_tn(attended_ref[:, cols], dbr_ref[...])
-                g = g.astype(bf16)
-                for zz in range(2):
-                    put_pair(
-                        gpos, q * 4 + 2 * h + zz, keep_ref, send_ref,
-                        g[2 * zz * b : (2 * zz + 1) * b], g[(2 * zz + 1) * b : (2 * zz + 2) * b],
-                    )
+    sums_ref[0:1] += jnp.sum(dt_ref[0].astype(f32), axis=0, keepdims=True)
+    sums_ref[1:2] += jnp.sum(dt_ref[2].astype(f32), axis=0, keepdims=True)
+
+
+def ga_kernel(gpos, normed_ref, attended_ref, dt_ref, dbr_ref, keep_ref, send_ref, nt_ref):
+    j = pl.program_id(0)
+    width = normed_ref.shape[1]
+    b = width // NB
+
+    @pl.when(j == 0)
+    def _():
+        nt_ref[...] = normed_ref[...].T
+
+    @pl.when(j == 3)
+    def _():
+        nt_ref[...] = attended_ref[...].T
+
+    def block(rhs):
+        for zf in range(4):
+            g = mm(nt_ref[2 * zf * b : 2 * (zf + 1) * b], rhs).astype(bf16)
+            put_pair(gpos, j * 4 + zf, keep_ref, send_ref, g[:b], g[b:])
+
+    @pl.when(j < 3)
+    def _():
+        block(dt_ref[...])
+
+    @pl.when(j == 3)
+    def _():
+        block(dbr_ref[...])
 
 
 def b4_kernel(layout, rb, length, slots, tok_ref, emb_ref, dmid_ref, dt_ref, vec_ref, *rest):
@@ -419,26 +444,57 @@
     )
 
 
-def compute_b2(dh, cot, middle, triple, att, attended, normed, vecs, ga, gb, gpos, rows, length):
+def compute_b2(dh, cot, middle, vecs, ga, gb):
     n, width = cot.shape
+    b = width // NB
+    block = 256 if n % 256 == 0 else n
+    tile = pl.BlockSpec((block, width), lambda i: (i, 0))
+    return call(
+        functools.partial(b2_kernel, ga.layout, gb.layout),
+        (n // block,),
+        [smem, smem, pl.BlockSpec((4, block, width), lambda i: (0, i, 0)), tile, tile, full(vecs.shape)]
+        + [hbm] * (len(ga.arrays) + len(gb.arrays)),
+        [sds((n, width), f32), sds((n, width), bf16), sds((n, width), bf16), sds((8, width), f32)],
+        [tile, tile, tile, full((8, width))],
+        [pltpu.VMEM((32, b, width), bf16), pltpu.VMEM((32, b, width), bf16),
+         pltpu.SemaphoreType.DMA((32,)), pltpu.SemaphoreType.DMA((32,))],
+        2 * n * width * width * 5 * 2, 20 << 20,
+        [ga.slots, gb.slots, dh, cot, middle, vecs, *ga.arrays, *gb.arrays],
+    )
+
+
+def compute_b3(datt, triple, att, rows, length):
+    n, width = datt.shape
     rb = 2 if rows % 2 == 0 else 1
     block = rb * length
     pairs = width // (2 * HD)
-    b = width // NB
+    wide = pl.BlockSpec((3, block, width), lambda i: (0, i, 0))
     return call(
-        functools.partial(b2_kernel, ga.layout, gb.layout, rb, length),
+        functools.partial(b3_kernel, rb, length),
         (rows // rb,),
-        [smem, smem, smem, pl.BlockSpec((4, block, width), lambda i: (0, i, 0)), pl.BlockSpec((block, width), lambda i: (i, 0)),
-         pl.BlockSpec((block, width), lambda i: (i, 0)), pl.BlockSpec((3, block, width), lambda i: (0, i, 0)),
-         pl.BlockSpec((rb * pairs, 2 * length, length), lambda i: (i, 0, 0)), full(attended.shape), full(normed.shape),
-         full(vecs.shape)] + [hbm] * (len(ga.arrays) + len(gb.arrays)),
-        [sds((n, width), f32), sds((3, n, width), bf16), sds((8, width), f32), sds((16, b, width), bf16), sds((16, b, width), bf16)],
-        [pl.BlockSpec((block, width), lambda i: (i, 0)), pl.BlockSpec((3, block, width), lambda i: (0, i, 0)), full((8, width)),
-         full((16, b, width)), full((16, b, width))],
-        [pltpu.VMEM((32, b, width), bf16), pltpu.VMEM((32, b, width), bf16), pltpu.VMEM((n, width), bf16),
-         pltpu.VMEM((3, n, width), bf16), pltpu.SemaphoreType.DMA((32,)), pltpu.SemaphoreType.DMA((32,))],
-        2 * n * width * width * 16, 40 << 20,
-        [ga.slots, gb.slots, gpos, dh, cot, middle, triple, att, attended, normed, vecs, *ga.arrays, *gb.arrays],
+        [pl.BlockSpec((block, width), lambda i: (i, 0)), wide,
+         pl.BlockSpec((rb * pairs, 2 * length, length), lambda i: (i, 0, 0))],
+        [sds((3, n, width), bf16), sds((8, width), f32)],
+        [wide, full((8, width))],
+        [],
+        2 * n * width * width * 5 * 2, 20 << 20,
+        [datt, triple, att],
+    )
+
+
+def compute_ga(normed, attended, dt, dbr, gpos):
+    n, width = normed.shape
+    b = width // NB
+    return call(
+        ga_kernel,
+        (4,),
+        [smem, full(normed.shape), full(attended.shape),
+         pl.BlockSpec((None, n, width), lambda i: (jnp.minimum(i, 2), 0, 0)), full(dbr.shape)],
+        [sds((16, b, width), bf16), sds((16, b, width), bf16)],
+        [full((16, b, width)), full((16, b, width))],
+        [pltpu.VMEM((width, n), bf16)],
+        2 * n * width * width * 4 * 2, 12 << 20,
+        [gpos, normed, attended, dt, dbr],
     )
 
 
@@ -523,84 +579,91 @@
     return lax.ppermute(v, "dp", xor_perm(4, 2))
 
 
+def diagonal_swap(v):
+    return lax.ppermute(v, "dp", xor_perm(4, 3))
+
+
 def z_shift(v, k):
     return lax.ppermute(v, "fsdp", [(i, (i + 2 * k) % 8) for i in range(8)])
 
 
-def fast_slots(d, z, c, rows_first):
+def tie(values, after):
+    return lax.optimization_barrier((values, after))[0]
+
+
+def columns(v):
+    return lax.all_to_all(jnp.broadcast_to(v[None], (4,) + v.shape), "dp", 0, 0, tiled=True)
+
+
+def fast_slots(z, c):
     table = []
-
-    def add(delta, k, e):
-        q = d ^ delta
-        f = 2 * lax.rem(z - k + 4, 4) + (c ^ e)
-        table.append(f * 4 + q if rows_first else q * NB + f)
-
     for e in (0, 1):
-        for delta in (0, 1, 2):
+        for q in range(4):
             for k in range(4):
-                add(delta, k, e)
-        for k in range(4):
-            add(3, k, e)
+                table.append(q * NB + 2 * lax.rem(z - k + 4, 4) + (c ^ e))
     return jnp.stack(table).astype(jnp.int32)
 
 
-def fast_gather(own, d, z, c, rows_first, extra=None):
-    b = own.shape[0]
-    sent = own if extra is None else jnp.concatenate([own, extra], axis=0)
-    got = [sent] + [z_shift(sent, k) for k in (1, 2, 3)]
-    s0 = jnp.stack([g[:b] for g in got])
-    xs, ys = x_swap(s0), y_swap(s0)
-    d1, d2 = y_swap(xs[:2]), x_swap(ys[2:])
-    mine = [s0, xs, ys, d1, d2]
-    arrays = mine + [core_swap(v) for v in mine]
-    layout = []
-    for e in range(2):
-        layout += [(5 * e, 0, 4), (5 * e + 1, 0, 4), (5 * e + 2, 0, 4), (5 * e + 3, 0, 2), (5 * e + 4, 0, 2)]
-    group = Group(arrays, layout, fast_slots(d, z, c, rows_first))
-    if extra is None:
-        return group
-    e0 = jnp.stack([g[b:] for g in got])
-    return group, e0, core_swap(e0)
-
-
-def fast_small(e0, e1, z, c, width):
-    pair = jnp.stack([jnp.where(c == 0, e0, e1), jnp.where(c == 0, e1, e0)], axis=1)[:, :, :2]
-    rows = jnp.stack([pick(pair, lax.rem(z - i + 4, 4)) for i in range(4)])
-    rows = rows.reshape(8, 2, width).astype(f32)
-    vecs = rows[:, 0].reshape(8, 8, width // 8).transpose(1, 0, 2).reshape(8, width)
-    hb = rows[:, 1, : width // 2].reshape(4, width)
-    return vecs, hb
-
-
-def fast_scatter(keep, send):
-    b, width = keep.shape[1:]
-    got = core_swap(send)
-
-    def add(u, v):
-        return (u.astype(f32) + v.astype(f32)).astype(bf16)
-
-    keep = keep.reshape(4, 4, b, width)
-    got = got.reshape(4, 4, b, width)
-
-    def part(deltas, half):
-        ks = slice(2 * half, 2 * half + 2)
-        return jnp.stack([add(keep[dl, ks], got[dl, ks]) for dl in deltas])
-
-    rx = x_swap(part((1, 3), 0))
-    ry = y_swap(part((2, 3), 1))
-    h2a = add(part((0, 2), 0), rx)
-    h2b = add(part((0, 1), 1), ry)
-    ra = y_swap(h2a[1])
-    rb = x_swap(h2b[1])
-    h3 = jnp.concatenate([add(h2a[0], ra), add(h2b[0], rb)], axis=0)
-    parts = [h3[0]] + [z_shift(h3[k], k) for k in (1, 2, 3)]
-    total = sum(p.astype(f32) for p in parts)
-    return total.astype(bf16)
-
-
-def fast_spread(mine, d):
-    got = jnp.stack([mine, x_swap(mine), y_swap(mine), lax.ppermute(mine, "dp", xor_perm(4, 3))])
-    return jnp.stack([pick(got, d ^ q) for q in range(4)]).astype(f32)
+def along_z(v):
+    return [v] + [z_shift(v, k) for k in (1, 2, 3)]
+
+
+def rows_of(got, first, count):
+    return jnp.stack([g[first : first + count] for g in got])
+
+
+def down_slots(z, c, quarters_in):
+    table = []
+    for e in (0, 1):
+        for part in quarters_in:
+            for k in range(4):
+                table += [8 * lax.rem(z - k + 4, 4) + 4 * (c ^ e) + q for q in part]
+    return jnp.stack(table).astype(jnp.int32)
+
+
+def fast_small(e0, e1, z, c, width, rows):
+    pair = jnp.stack([jnp.where(c == 0, e0, e1), jnp.where(c == 0, e1, e0)], axis=1)
+    got = jnp.stack([pick(pair, lax.rem(z - i + 4, 4)) for i in range(4)])
+    got = got.reshape(8, 16, width).astype(f32)
+    vecs = got[:, :8, : width // 8].transpose(1, 0, 2).reshape(8, width)
+    hb = got[:, 8, : width // 2].reshape(4, width)
+    ids = (got[:, 9, :rows] * 32.0 + got[:, 10, :rows]).astype(jnp.int32)
+    return vecs, hb, ids
+
+
+def add(u, v):
+    return (u.astype(f32) + v.astype(f32)).astype(bf16)
+
+
+class Scatter:
+    def __init__(self, keep, send):
+        b, width = keep.shape[1:]
+        self.keep = keep.reshape(4, 4, b, width)
+        self.got = core_swap(send).reshape(4, 4, b, width)
+
+    def split(self):
+        def part(deltas, half):
+            ks = slice(2 * half, 2 * half + 2)
+            return jnp.stack([add(self.keep[dl, ks], self.got[dl, ks]) for dl in deltas])
+
+        self.out = [part((1, 3), 0), part((2, 3), 1)]
+        self.own = [part((0, 2), 0), part((0, 1), 1)]
+
+    def one(self):
+        self.r1 = [x_swap(self.out[0]), y_swap(self.out[1])]
+
+    def two(self):
+        h = [add(self.own[i], self.r1[i]) for i in range(2)]
+        self.h = h
+        self.r2 = [y_swap(h[0][1]), x_swap(h[1][1])]
+
+    def three(self):
+        h3 = [add(self.h[i][0], self.r2[i]) for i in range(2)]
+        h3 = [h3[0][0], h3[0][1], h3[1][0], h3[1][1]]
+        self.r3 = [h3[0]] + [z_shift(h3[k], k) for k in (1, 2, 3)]
+
+    def total(self):
+        return sum(p.astype(f32) for p in self.r3).astype(bf16)
 
 
 def per_device(
@@ -620,15 +683,8 @@
     seg = segments.reshape(rows, length).astype(f32)
     pad = padding.reshape(rows, length).astype(f32)
 
-    ids = lax.all_gather(timesteps.reshape(1, rows), ("dp", "fsdp"), axis=0, tiled=True)
-    here = lax.dynamic_slice_in_dim(ids, d * nf, nf, axis=0).reshape(nf * rows)
+    ids = timesteps.reshape(rows)
     steps = lax.iota(jnp.int32, step_table.shape[0])
-    onehot = (here[:, None] == steps[None, :]).astype(bf16)
-    looked = jnp.dot(onehot, step_table, preferred_element_type=f32).astype(bf16)
-    looked = looked.reshape(nf, rows, width // nf)
-    emb = lax.all_to_all(looked, "fsdp", 0, 0, tiled=True)
-    emb = emb.transpose(1, 0, 2).reshape(rows, width).astype(f32)
-
     q4 = [triple_weight[:, i * width : (i + 1) * width] for i in range(3)] + [output_weight]
     h4 = [hidden_weight[:, i * width : (i + 1) * width] for i in range(4)]
     vec_args = (query_bias, value_bias, output_bias, first_gain, first_shift, second_gain, second_shift, down_bias)
@@ -636,14 +692,18 @@
         b = width // NB
         own_a = pick(jnp.stack(q4), d)
         own_b = pick(jnp.stack(h4), d)
-        own_c = lax.dynamic_slice_in_dim(down_weight, d * b, b, axis=0)
-        hb_row = jnp.concatenate([hidden_bias, jnp.zeros_like(hidden_bias)])
-        small = jnp.stack([jnp.concatenate(vec_args), hb_row])
-        small = jnp.concatenate([small, jnp.zeros((14, width), bf16)], axis=0)
-        ga, e0, e1 = fast_gather(own_a, d, z, c, False, small)
-        gb = fast_gather(own_b, d, z, c, False)
-        gc = fast_gather(own_c, d, z, c, True)
-        vecs, hb = fast_small(e0, e1, z, c, width)
+        small = jnp.zeros((16, width), bf16)
+        small = small.at[:8, : width // nf].set(jnp.stack(vec_args))
+        small = small.at[8, : 4 * width // nf].set(hidden_bias)
+        small = small.at[9:11, :rows].set(jnp.stack([ids // 32, lax.rem(ids, 32)]).astype(bf16))
+        got = along_z(jnp.concatenate([own_a, small], axis=0))
+        s0 = rows_of(got, 0, b)
+        e0 = rows_of(got, b, 16)
+        e1 = core_swap(e0)
+        own_c = [down_weight[i * b : (i + 1) * b] for i in range(4)]
+        mine_a = columns(s0)
+        got1 = along_z(tie(jnp.concatenate([own_b, own_c[0]], axis=0), got))
+        vecs, hb, here = fast_small(e0, e1, z, c, width, rows)
         gpos = [(q ^ d) * 4 + lax.rem(zf - z + 4, 4) for q in range(4) for zf in range(4)] + [c]
         gpos = jnp.stack(gpos).astype(jnp.int32)
     else:
@@ -651,22 +711,104 @@
             jnp.stack(q4), jnp.stack(h4), down_weight, vec_args + (hidden_bias,)
         )
         gpos = jnp.concatenate([jnp.arange(16, dtype=jnp.int32), jnp.zeros((1,), jnp.int32)])
-
-    normed, triple, att, attended, middle, n2 = compute_f1(tok, emb, seg, pad, vecs, ga, rows, length)
+        here = lax.all_gather(ids, "fsdp", axis=0, tiled=True)
+
+    onehot = (here.reshape(nf * rows)[:, None] == steps[None, :]).astype(bf16)
+    looked = jnp.dot(onehot, step_table, preferred_element_type=f32).astype(bf16)
+    looked = looked.reshape(nf, rows, width // nf)
+    if fast:
+        (mine_a, looked), got1 = lax.optimization_barrier(((mine_a, looked), got1))
+    emb = lax.all_to_all(looked, "fsdp", 0, 0, tiled=True)
+    emb = emb.transpose(1, 0, 2).reshape(rows, width).astype(f32)
+
+    if fast:
+        flat = (16, b, width)
+        mine_a = mine_a.reshape(flat)
+        core_a = core_swap(mine_a)
+        s0 = rows_of(got1, 0, b)
+        c0 = rows_of(got1, b, b)
+        ga = Group([mine_a, core_a], [(0, 0, 16), (1, 0, 16)], fast_slots(z, c))
+        tok_in, s0, own_c12 = tie((tok, s0, jnp.concatenate(own_c[1:3], axis=0)), (core_a, emb, c0))
+        mine_b = columns(s0)
+        got2 = along_z(own_c12)
+    else:
+        tok_in = tok
+    normed, triple, att, attended, middle, n2 = compute_f1(tok_in, emb, seg, pad, vecs, ga, rows, length)
+    if fast:
+        mine_b, got2, n2 = lax.optimization_barrier((mine_b, got2, n2))
+        mine_b = mine_b.reshape(flat)
+        core_b = core_swap(mine_b)
+        gb = Group([mine_b, core_b], [(0, 0, 16), (1, 0, 16)], fast_slots(z, c))
+        n2, c0, c12, c3 = tie((n2, c0, got2, own_c[3]), core_b)
+        c12 = jnp.stack(c12).reshape(8, b, width)
+        got3 = along_z(c3)
+        c0x, c12x = core_swap(c0), core_swap(c12)
     active, gp, keep_c, send_c = compute_f2(n2, cot, hb, gb, gpos)
+    if fast:
+        got3, c0x, c12x, gp, keep_c, send_c = lax.optimization_barrier((got3, c0x, c12x, gp, keep_c, send_c))
+        c3 = jnp.stack(got3)
+        c3x = core_swap(c3)
+        gc = Group(
+            [c0, c12, c3, c0x, c12x, c3x],
+            [(0, 0, 4), (1, 0, 8), (2, 0, 4), (3, 0, 4), (4, 0, 8), (5, 0, 4)],
+            down_slots(z, c, ((0,), (1, 2), (3,))),
+        )
+        sc = Scatter(keep_c, send_c)
+        sc.split()
+        gp, sc.out = lax.optimization_barrier((gp, sc.out))
+        sc.one()
     dh, hb_sum, db_sum, keep_b, send_b = compute_b1(n2, cot, gp, gc, gpos)
-    dmid, dt, sums2, keep_a, send_a = compute_b2(
-        dh, cot, middle, triple, att, attended, normed, vecs, ga, gb, gpos, rows, length
-    )
-    result = compute_f3(active, middle, vecs, gc)
+    if fast:
+        dh, keep_b, send_b, sc.r1 = lax.optimization_barrier((dh, keep_b, send_b, sc.r1))
+        sc.two()
+        sb = Scatter(keep_b, send_b)
+        sb.split()
+        dh, sb.out, sc.r2 = lax.optimization_barrier((dh, sb.out, sc.r2))
+        sb.one()
+        sc.three()
+    dmid, dbr, datt, sums2 = compute_b2(dh, cot, middle, vecs, ga, gb)
+    if fast:
+        datt, sb.r1, sc.r3 = lax.optimization_barrier((datt, sb.r1, sc.r3))
+        sb.two()
+        out_c = columns(sc.total())
+    dt, sums3 = compute_b3(datt, triple, att, rows, length)
+    if fast:
+        dt, sb.r2, out_c = lax.optimization_barrier((dt, sb.r2, out_c))
+        sb.three()
+    keep_a, send_a = compute_ga(normed, attended, dt, dbr, gpos)
+    if fast:
+        keep_a, send_a, sb.r3 = lax.optimization_barrier((keep_a, send_a, sb.r3))
+        sa = Scatter(keep_a, send_a)
+        sa.split()
+        dt, sa.out = lax.optimization_barrier((dt, sa.out))
+        sa.one()
     input_grad, row_sums, sums4 = compute_b4(tok, emb, dmid, dt, vecs, ga, rows, length)
     row_sums = row_sums[:rows]
 
-    if fast:
-        out_c = fast_spread(fast_scatter(keep_c, send_c), d)
-        out_b = fast_spread(fast_scatter(keep_b, send_b), d)
-        out_a = fast_spread(fast_scatter(keep_a, send_a), d)
-        down_grad = out_c.reshape(4 * b, width)
+    part = width // nf
+    sums = jnp.concatenate(
+        [row_sums, sums3[0:2], sums2[2:3], sums4[0:2], sums2[0:2], db_sum[0:1]], axis=0
+    )
+    lanes = sums.reshape(rows + 8, nf, part).transpose(1, 0, 2).reshape(nf, (rows + 8) * part)
+    marks = jnp.broadcast_to(ids.astype(f32)[None, :], (nf, rows))
+    payload = jnp.concatenate([lanes, hb_sum[:4].reshape(nf, 4 * part), marks], axis=1)
+    moved = lax.all_to_all(payload, "fsdp", 0, 0, tiled=True)
+    if fast:
+        sa.r1, moved, active = lax.optimization_barrier((sa.r1, moved, active))
+        sa.two()
+        moved = columns(moved).reshape(nd * nf, payload.shape[1])
+    else:
+        moved = lax.all_gather(moved, "dp", axis=0, tiled=True)
+    result = compute_f3(active, middle, vecs, gc)
+    if fast:
+        sa.r2, moved, tb = lax.optimization_barrier((sa.r2, moved, sb.r3))
+        sa.three()
+        sb.r3 = tb
+        out_b = columns(sb.total())
+        sa.r3, out_b = lax.optimization_barrier((sa.r3, out_b))
+        out_a = columns(sa.total()).astype(f32)
+        out_b = out_b.astype(f32)
+        down_grad = out_c.astype(f32).reshape(4 * b, width)
     else:
         out_b = plain_scatter(keep_b, send_b, False)
         out_a = plain_scatter(keep_a, send_a, False)
@@ -674,19 +816,11 @@
     hidden_grad = jnp.concatenate([out_b[i] for i in range(4)], axis=1)
     triple_grad = jnp.concatenate([out_a[i] for i in range(3)], axis=1)
     output_grad = out_a[3]
-
-    part = width // nf
-    sums = jnp.concatenate(
-        [row_sums, sums2[3:5], sums2[2:3], sums4[0:2], sums2[0:2], db_sum[0:1]], axis=0
-    )
-    lanes = sums.reshape(rows + 8, nf, part).transpose(1, 0, 2).reshape(nf, (rows + 8) * part)
-    payload = jnp.concatenate([lanes, hb_sum[:4].reshape(nf, 4 * part)], axis=1)
-    moved = lax.all_to_all(payload, "fsdp", 0, 0, tiled=True)
-    moved = lax.all_gather(moved, "dp", axis=0, tiled=True)
     table_rows = moved[:, : rows * part].reshape(nd * nf * rows, part)
-    all_hot = (steps[:, None] == ids.reshape(1, nd * nf * rows)).astype(f32)
+    all_ids = moved[:, (rows + 12) * part :].astype(jnp.int32).reshape(1, nd * nf * rows)
+    all_hot = (steps[:, None] == all_ids).astype(f32)
     table_grad = jnp.dot(all_hot, table_rows, precision=highest)
-    vec_sums = jnp.sum(moved[:, rows * part :], axis=0)
+    vec_sums = jnp.sum(moved[:, rows * part : (rows + 12) * part], axis=0)
     v = [vec_sums[i * part : (i + 1) * part] for i in range(8)]
     hidden_bias_grad = vec_sums[8 * part :]
     shape = tokens.shape

time: 390 us -> 340 us (0.87)
  blocking collectives: 53.3 us -> 0 us
  local copies, waits for them, and re-layouts: 21.4 us -> 46.2 us
  waiting for transfers between devices: 95.6 us -> 70.9 us
  Pallas kernels: 113 us -> 117 us
    all_gather x2 -> x0, blocking collectives: 53.3 us -> none  [the longest x1 44.9 us: per_device(): lax.all_gather(timesteps.reshape(1, rows), ('dp', 'fsdp'), axis=0, tiled=...]
    ppermute x15 -> x6, waiting for transfers between devices: 55.3 us -> 3.25 us  [x_swap(): return lax.ppermute(v, 'dp', xor_perm(4, 1))]
    all_to_all x0 -> x6, starting transfers between devices: none -> 24.3 us  [columns(): lax.all_to_all(jnp.broadcast_to(v[None], (4,) + v.shape), 'dp', 0, 0, til...]
    ppermute x18 -> x21, waiting for transfers between devices: 24.3 us -> 44.5 us  [z_shift(): return lax.ppermute(v, 'fsdp', [(i, (i + 2 * k) % 8) for i in range(8)])]
    ppermute x15 -> x6, waiting for transfers between devices: 13.2 us -> 0.53 us  [y_swap(): return lax.ppermute(v, 'dp', xor_perm(4, 2))]
    ppermute x15 -> x6, starting transfers between devices: 17.1 us -> 5.4 us  [y_swap(): return lax.ppermute(v, 'dp', xor_perm(4, 2))]
    ppermute x18 -> x21, starting transfers between devices: 37.6 us -> 29.7 us  [z_shift(): return lax.ppermute(v, 'fsdp', [(i, (i + 2 * k) % 8) for i in range(8)])]
    ppermute x19 -> x9, waiting for transfers between devices: 1.26 us -> 8.46 us  [core_swap(): return lax.ppermute(v, 'fsdp', xor_perm(8, 1))]
  transfers between devices with their start and end apart: 72 -> 50, of which waited for: 25 -> 15; matrix products, arithmetic and copies ran while one was open for 8% -> 13% of each run, Pallas kernels for 14% -> 35%
where the time goes in v2:
time: 340 us; the launch traced here: 337 us
  Pallas kernels  117 us (34%)
  starting transfers between devices  82.3 us (24%)
  waiting for transfers between devices  70.9 us (21%)
  local copies, waits for them, and re-layouts  46.2 us (14%)
  other arithmetic  17.8 us (5%)
    pallas_call x8, Pallas kernels, call(): pl.pallas_call(kernel, grid=grid, in_specs=in_specs, out_shape=out_shape,...  117 us
    ppermute x21, waiting for transfers between devices, z_shift(): return lax.ppermute(v, 'fsdp', [(i, (i + 2 * k) % 8) for i in range(8)])  44.5 us
    ppermute x21, starting transfers between devices, z_shift(): return lax.ppermute(v, 'fsdp', [(i, (i + 2 * k) % 8) for i in range(8)])  29.7 us
    all_to_all x6, starting transfers between devices, columns(): lax.all_to_all(jnp.broadcast_to(v[None], (4,) + v.shape), 'dp', 0, 0, til...  24.3 us
    ppermute x6, starting transfers between devices, x_swap(): return lax.ppermute(v, 'dp', xor_perm(4, 1))  8.64 us
    all_to_all x1, starting transfers between devices, per_device(): emb = lax.all_to_all(looked, 'fsdp', 0, 0, tiled=True)  8.48 us
    ppermute x9, waiting for transfers between devices, core_swap(): return lax.ppermute(v, 'fsdp', xor_perm(8, 1))  8.46 us
    convert_element_type x15, other arithmetic, add(): return (u.astype(f32) + v.astype(f32)).astype(bf16)  7.25 us
  transfers between devices with their start and end apart: 50, of which 15 were waited for; matrix products, arithmetic and copies ran while one was open for 13% of the time, Pallas kernels for 35%

profile of v2, /device:TPU:0, one launch (start us, length us, event | category | flops | bytes accessed | tf_op | source)
XLA Modules:
  0.0 337.1 jit_solution(12861633632542146296)
XLA Ops:
  4.9 5.1 %collective-permute-start.2 = (bf16[112,768]{1,0:T(8,128)(2,1)S(1)}, bf16[112,768]{1,0:T(8,128)(2,1)S(1)}, u32[]{:S(2)}, u32[]{:S(2)}) collective-permute-start(bf16[112,768]{1,0:T(8,128)(2,1)S(1)} %pad_maximum_fusion.14), channel_id=1, source_target_pairs={{0,6},{1,7},{2,0},{3,1},{4,2},{5,3},{6,4},{7,5},{8,14},{9,15},{10,... | collective-permute-start | bytes 516104 | tf_op jit(solution)/shard_map/ppermute | solution.py:587
  11.8 3.1 collective-permute-done.2
  15.5 9.1 %collective-permute-done.1 = bf16[112,768]{1,0:T(8,128)(2,1)S(1)} collective-permute-done((bf16[112,768]{1,0:T(8,128)(2,1)S(1)}, bf16[112,768]{1,0:T(8,128)(2,1)S(1)}, u32[]{:S(2)}, u32[]{:S(2)}) %collective-permute-start.1) | collective-permute-done | bytes 172064 | tf_op jit(solution)/shard_map/ppermute | solution.py:587
  26.4 4.6 %all-to-all-start = ((bf16[4,4,96,768]{3,2,1,0:T(8,128)(2,1)}), bf16[4,4,96,768]{3,2,1,0:T(8,128)(2,1)S(1)}, u32[]{:S(2)}, u32[]{:S(2)}) async-start(bf16[4,4,96,768]{3,2,1,0:T(8,128)(2,1)} %broadcast_in_dim.14), calls=%async_computation | async-start | bytes 4718592 | tf_op jit(solution)/shard_map/all_to_all | solution.py:595
  36.4 2.8 collective-permute-start.6
  41.1 4.2 %collective-permute-done.4 = bf16[192,768]{1,0:T(8,128)(2,1)S(1)} collective-permute-done((bf16[192,768]{1,0:T(8,128)(2,1)S(1)}, bf16[192,768]{1,0:T(8,128)(2,1)S(1)}, u32[]{:S(2)}, u32[]{:S(2)}) %collective-permute-start.4) | collective-permute-done | bytes 294944 | tf_op jit(solution)/shard_map/ppermute | solution.py:587
  45.3 12.2 %collective-permute-done.5 = bf16[192,768]{1,0:T(8,128)(2,1)S(1)} collective-permute-done((bf16[192,768]{1,0:T(8,128)(2,1)S(1)}, bf16[192,768]{1,0:T(8,128)(2,1)S(1)}, u32[]{:S(2)}, u32[]{:S(2)}) %collective-permute-start.5) | collective-permute-done | bytes 294944 | tf_op jit(solution)/shard_map/ppermute | solution.py:587
  59.8 8.5 %all-to-all-start.1 = ((bf16[8,6,96]{2,1,0:T(8,128)(2,1)}), bf16[8,6,96]{2,1,0:T(8,128)(2,1)S(1)}, u32[]{:S(2)}, u32[]{:S(2)}) async-start(bf16[8,6,96]{2,1,0:T(8,128)(2,1)} %reshape.327), calls=%async_computation.1 | async-start | bytes 32768 | tf_op jit(solution)/shard_map/all_to_all | solution.py:721
  76.2 4.3 %all-to-all-start.2 = ((bf16[4,4,96,768]{3,2,1,0:T(8,128)(2,1)}), bf16[4,4,96,768]{3,2,1,0:T(8,128)(2,1)S(1)}, u32[]{:S(2)}, u32[]{:S(2)}) async-start(bf16[4,4,96,768]{3,2,1,0:T(8,128)(2,1)} %broadcast_in_dim.15), calls=%async_computation.2 | async-start | bytes 4718592 | tf_op jit(solution)/shard_map/all_to_all | solution.py:595
  86.5 15.5 %shard_map.306 = (bf16[768,768]{1,0:T(8,128)(2,1)}, bf16[3,768,768]{2,1,0:T(8,128)(2,1)}, bf16[36,256,128]{2,1,0:T(8,128)(2,1)}, bf16[768,768]{1,0:T(8,128)(2,1)...) custom-call(s32[32]{0:T(128)} %stack.577.slots.slots_a.slots_b, bf16[768,768]{1,0:T(8,128)(2,1)} %bitcast.305, ...), custom_call_target="tpu_custom_call" | custom-call | flops 10871635968 | bytes 20971520 | tf_op jit(solution)/shard_map/pallas_call | solution.py:369
  102.0 9.5 %collective-permute-done.9 = bf16[192,768]{1,0:T(8,128)(2,1)} collective-permute-done((bf16[192,768]{1,0:T(8,128)(2,1)S(1)}, bf16[192,768]{1,0:T(8,128)(2,1)}, u32[]{:S(2)}, u32[]{:S(2)}) %collective-permute-start.9) | collective-permute-done | bytes 294944 | tf_op jit(solution)/shard_map/ppermute | solution.py:587
  116.1 3.2 collective-permute-start.13
  122.9 18.7 %shard_map.307 = (bf16[4,768,768]{2,1,0:T(8,128)(2,1)}, bf16[4,768,768]{2,1,0:T(8,128)(2,1)}, bf16[16,96,768]{2,1,0:T(8,128)(2,1)}, bf16[16,96,768]{2,1,0:T(8,128)(2,1)}) custom-call(s32[32]{0:T(128)} %stack.577.slots.slots_a.slots_b, s32[17]{0:T(128)} %stack.595.gpos, bf16[768,768]{1,0:T(8,128)(2,1)} %get-tuple-element.176.n2_ref, ...), custom_call_target="tpu_custom_call" | custom-call | flops 14495514624 | bytes 20971520 | tf_op jit(solution)/shard_map/pallas_call | solution.py:369
  144.9 2.6 collective-permute-done.17
  153.3 19.5 %shard_map.308 = (bf16[4,768,768]{2,1,0:T(8,128)(2,1)}, f32[8,768]{1,0:T(8,128)}, f32[8,768]{1,0:T(8,128)}, bf16[16,96,768]{2,1,0:T(8,128)(2,1)}, bf16[16,96,768]{2,1,0:T(8,128)(2,1)}) custom-call(s32[32]{0:T(128)} %stack.544.slots, s32[17]{0:T(128)} %stack.595.gpos, bf16[768,768]{1,0:T(8,128)(2,1)} %get-tuple-element.176.n2_ref, ...), custom_call_target="tpu_custom_call" | custom-call | flops 14495514624 | bytes 20971520 | tf_op jit(solution)/shard_map/pallas_call | solution.py:369
  174.2 3.5 %collective-permute-done.21 = bf16[16,96,768]{2,1,0:T(8,128)(2,1)S(1)} collective-permute-done((bf16[16,96,768]{2,1,0:T(8,128)(2,1)}, bf16[16,96,768]{2,1,0:T(8,128)(2,1)S(1)}, u32[]{:S(2)}, u32[]{:S(2)}) %collective-permute-start.21) | collective-permute-done | bytes 2359328 | tf_op jit(solution)/shard_map/ppermute | solution.py:571
  179.3 3.2 collective-permute-done.23
  190.7 15.7 %shard_map.309 = (f32[768,768]{1,0:T(8,128)}, bf16[768,768]{1,0:T(8,128)(2,1)}, bf16[768,768]{1,0:T(8,128)(2,1)}, f32[8,768]{1,0:T(8,128)}) custom-call(s32[32]{0:T(128)} %stack.577.slots.slots_a.slots_b, s32[32]{0:T(128)} %stack.577.slots.slots_a.slots_b, bf16[4,768,768]{2,1,0:T(8,128)(2,1)} %get-tuple-element.206.dh_ref, bf16[768,768]{1,0:T(8,128)(2,1)} %bitcast.304, ...), custom_call_target="tpu_custom_call" | custom-call | flops 9059696640 | bytes 20971520 | tf_op jit(solution)/shard_map/pallas_call | solution.py:369
  207.4 3.7 %all-to-all-start.3 = ((bf16[4,96,768]{2,1,0:T(8,128)(2,1)}), bf16[4,96,768]{2,1,0:T(8,128)(2,1)S(1)}, u32[]{:S(2)}, u32[]{:S(2)}) async-start(bf16[4,96,768]{2,1,0:T(8,128)(2,1)} %broadcast_in_dim.16), calls=%async_computation.3 | async-start | bytes 1179648 | tf_op jit(solution)/shard_map/all_to_all | solution.py:595
  215.0 14.3 %shard_map.310 = (bf16[3,768,768]{2,1,0:T(8,128)(2,1)}, f32[8,768]{1,0:T(8,128)}) custom-call(bf16[768,768]{1,0:T(8,128)(2,1)} %get-tuple-element.213.datt_ref, bf16[3,768,768]{2,1,0:T(8,128)(2,1)} %get-tuple-element.214.triple_ref, bf16[36,256,128]{2,1,0:T(8,128)(2,1)} %get-tuple-element.215.att_ref), custom_call_target="tpu_custom_call" | custom-call | flops 9059696640 | bytes 20971520 | tf_op jit(solution)/shard_map/pallas_call | solution.py:369
  230.4 2.7 collective-permute-start.33
  234.4 13.4 %shard_map.311 = (bf16[16,96,768]{2,1,0:T(8,128)(2,1)}, bf16[16,96,768]{2,1,0:T(8,128)(2,1)}) custom-call(s32[17]{0:T(128)} %stack.595.gpos, bf16[768,768]{1,0:T(8,128)(2,1)} %get-tuple-element.224.normed_ref, bf16[768,768]{1,0:T(8,128)(2,1)} %get-tuple-element.225.attended_ref, bf16[3,768,768]{2,1,0:T(8,128)(2,1)} %get-tuple-element.236.dt_ref, ...), custom_call_target="tpu_custom_call" | custom-call | flops 7247757312 | bytes 12582912 | tf_op jit(solution)/shard_map/pallas_call | solution.py:369
  254.0 3.0 add_convert_fusion.7
  258.5 9.7 %shard_map.312 = (bf16[768,768]{1,0:T(8,128)(2,1)}, f32[8,768]{1,0:T(8,128)}, f32[8,768]{1,0:T(8,128)}) custom-call(s32[32]{0:T(128)} %stack.577.slots.slots_a.slots_b, bf16[768,768]{1,0:T(8,128)(2,1)} %bitcast.306, f32[6,768]{1,0:T(8,128)} %reshape.349.emb_ref, f32[768,768]{1,0:T(8,128)} %get-tuple-element.235.dmid_ref, ...), custom_call_target="tpu_custom_call" | custom-call | flops 5435817984 | bytes 12582912 | tf_op jit(solution)/shard_map/pallas_call | solution.py:369
  275.8 4.6 %all-to-all-start.4 = ((f32[8,1,1734]{2,1,0:T(1,128)}), f32[8,1,1734]{2,1,0:T(1,128)}, u32[]{:S(2)}, u32[]{:S(2)}) async-start(f32[8,1,1734]{2,1,0:T(1,128)} %copy.50), calls=%async_computation.4 | async-start | bytes 114688 | tf_op jit(solution)/shard_map/all_to_all | solution.py:795
  281.5 4.8 %all-to-all-done.4 = f32[8,1,1734]{2,1,0:T(1,128)} async-done(((f32[8,1,1734]{2,1,0:T(1,128)}), f32[8,1,1734]{2,1,0:T(1,128)}, u32[]{:S(2)}, u32[]{:S(2)}) %all-to-all-start.4) | async-done | bytes 55520 | tf_op jit(solution)/shard_map/all_to_all | solution.py:795
  291.8 3.6 %all-to-all-start.5 = ((f32[4,8,1734]{2,1,0:T(8,128)}), f32[4,8,1734]{2,1,0:T(8,128)S(1)}, u32[]{:S(2)}, u32[]{:S(2)}) async-start(f32[4,8,1734]{2,1,0:T(8,128)} %broadcast_in_dim.18), calls=%async_computation.5 | async-start | bytes 458752 | tf_op jit(solution)/shard_map/all_to_all | solution.py:595
  295.5 9.8 %shard_map.313 = bf16[768,768]{1,0:T(8,128)(2,1)} custom-call(s32[32]{0:T(128)} %stack.544.slots, bf16[4,768,768]{2,1,0:T(8,128)(2,1)} %get-tuple-element.244.act_ref, f32[768,768]{1,0:T(8,128)} %get-tuple-element.207.middle_ref, f32[8,768]{1,0:T(8,128)} %reshape.329.vec_ref, bf16[4,96,768]{2,1,0:T(8,128)(2,1)} %pad_maximum_fusion.5.rest_0_, ...), custom_call_target="tpu_custom_call" | custom-call | flops 7247757312 | bytes 12582912 | tf_op jit(solution)/shard_map/pallas_call | solution.py:369
  306.6 3.8 %all-to-all-start.6 = ((bf16[4,96,768]{2,1,0:T(8,128)(2,1)}), bf16[4,96,768]{2,1,0:T(8,128)(2,1)S(1)}, u32[]{:S(2)}, u32[]{:S(2)}) async-start(bf16[4,96,768]{2,1,0:T(8,128)(2,1)} %broadcast_in_dim.19), calls=%async_computation.6 | async-start | bytes 1179648 | tf_op jit(solution)/shard_map/all_to_all | solution.py:595
  316.6 6.4 %collective-permute-done.40 = bf16[96,768]{1,0:T(8,128)(2,1)S(1)} collective-permute-done((bf16[96,768]{1,0:T(8,128)(2,1)S(1)}, bf16[96,768]{1,0:T(8,128)(2,1)S(1)}, u32[]{:S(2)}, u32[]{:S(2)}) %collective-permute-start.40) | collective-permute-done | bytes 147488 | tf_op jit(solution)/shard_map/ppermute | solution.py:587
  324.0 4.2 %all-to-all-start.7 = ((bf16[4,96,768]{2,1,0:T(8,128)(2,1)}), bf16[4,96,768]{2,1,0:T(8,128)(2,1)S(1)}, u32[]{:S(2)}, u32[]{:S(2)}) async-start(bf16[4,96,768]{2,1,0:T(8,128)(2,1)} %broadcast_in_dim.20), calls=%async_computation.7 | async-start | bytes 1179648 | tf_op jit(solution)/shard_map/all_to_all | solution.py:595
  329.5 5.8 %all-to-all-done.7 = bf16[4,96,768]{2,1,0:T(8,128)(2,1)S(1)} async-done(((bf16[4,96,768]{2,1,0:T(8,128)(2,1)}), bf16[4,96,768]{2,1,0:T(8,128)(2,1)S(1)}, u32[]{:S(2)}, u32[]{:S(2)}) %all-to-all-start.7) | async-done | bytes 589856 | tf_op jit(solution)/shard_map/all_to_all | solution.py:595
  (273 shorter events, 100.1 us)
Async XLA Ops:
  10.0 14.6 %collective-permute-start.1 = (bf16[112,768]{1,0:T(8,128)(2,1)S(1)}, bf16[112,768]{1,0:T(8,128)(2,1)S(1)}, u32[]{:S(2)}, u32[]{:S(2)}) collective-permute-start(bf16[112,768]{1,0:T(8,128)(2,1)S(1)} %pad_maximum_fusion.14), channel_id=1, source_target_pairs={{0,4},{1,5},{2,6},{3,7},{4,0},{5,1},{6,2},{7,3},{8,12},{9,13},{10,... | collective-permute-start | bytes 516104 | tf_op jit(solution)/shard_map/ppermute | solution.py:587
  10.0 14.6 %collective-permute-start = (bf16[112,768]{1,0:T(8,128)(2,1)S(1)}, bf16[112,768]{1,0:T(8,128)(2,1)S(1)}, u32[]{:S(2)}, u32[]{:S(2)}) collective-permute-start(bf16[112,768]{1,0:T(8,128)(2,1)S(1)} %pad_maximum_fusion.14), channel_id=1, source_target_pairs={{0,2},{1,3},{2,4},{3,5},{4,6},{5,7},{6,0},{7,1},{8,10},{9,11},{10,... | collective-permute-start | bytes 516104 | tf_op jit(solution)/shard_map/ppermute | solution.py:587
  26.4 32.2 %all-to-all-start = ((bf16[4,4,96,768]{3,2,1,0:T(8,128)(2,1)}), bf16[4,4,96,768]{3,2,1,0:T(8,128)(2,1)S(1)}, u32[]{:S(2)}, u32[]{:S(2)}) async-start(bf16[4,4,96,768]{3,2,1,0:T(8,128)(2,1)} %broadcast_in_dim.14), calls=%async_computation | async-start | bytes 4718592 | tf_op jit(solution)/shard_map/all_to_all | solution.py:595
  34.4 23.1 %collective-permute-start.5 = (bf16[192,768]{1,0:T(8,128)(2,1)S(1)}, bf16[192,768]{1,0:T(8,128)(2,1)S(1)}, u32[]{:S(2)}, u32[]{:S(2)}) collective-permute-start(bf16[192,768]{1,0:T(8,128)(2,1)S(1)} %pad_maximum_fusion.13), channel_id=1, source_target_pairs={{0,4},{1,5},{2,6},{3,7},{4,0},{5,1},{6,2},{7,3},{8,12},{9,13},{10,... | collective-permute-start | bytes 884744 | tf_op jit(solution)/shard_map/ppermute | solution.py:587
  36.4 21.1 %collective-permute-start.6 = (bf16[192,768]{1,0:T(8,128)(2,1)S(1)}, bf16[192,768]{1,0:T(8,128)(2,1)}, u32[]{:S(2)}, u32[]{:S(2)}) collective-permute-start(bf16[192,768]{1,0:T(8,128)(2,1)S(1)} %pad_maximum_fusion.13), channel_id=1, source_target_pairs={{0,6},{1,7},{2,0},{3,1},{4,2},{5,3},{6,4},{7,5},{8,14},{9,15},{10,... | collective-permute-start | bytes 884744 | tf_op jit(solution)/shard_map/ppermute | solution.py:587
  58.5 16.1 %collective-permute-start.7 = (bf16[16,96,768]{2,1,0:T(8,128)(2,1)S(1)}, bf16[16,96,768]{2,1,0:T(8,128)(2,1)}, u32[]{:S(2)}, u32[]{:S(2)}) collective-permute-start(bf16[16,96,768]{2,1,0:T(8,128)(2,1)S(1)} %bitcast.268), channel_id=1, source_target_pairs={{0,1},{1,0},{2,3},{3,2},{4,5},{5,4},{6,7},{7,6},{8,9},{9,8},{10,11... | collective-permute-start | bytes 7077896 | tf_op jit(solution)/shard_map/ppermute | solution.py:571
  76.2 35.3 %all-to-all-start.2 = ((bf16[4,4,96,768]{3,2,1,0:T(8,128)(2,1)}), bf16[4,4,96,768]{3,2,1,0:T(8,128)(2,1)S(1)}, u32[]{:S(2)}, u32[]{:S(2)}) async-start(bf16[4,4,96,768]{3,2,1,0:T(8,128)(2,1)} %broadcast_in_dim.15), calls=%async_computation.2 | async-start | bytes 4718592 | tf_op jit(solution)/shard_map/all_to_all | solution.py:595
  83.9 18.0 %collective-permute-start.10 = (bf16[192,768]{1,0:T(8,128)(2,1)S(1)}, bf16[192,768]{1,0:T(8,128)(2,1)}, u32[]{:S(2)}, u32[]{:S(2)}) collective-permute-start(bf16[192,768]{1,0:T(8,128)(2,1)S(1)} %concatenate.29), channel_id=1, source_target_pairs={{0,6},{1,7},{2,0},{3,1},{4,2},{5,3},{6,4},{7,5},{8,14},{9,15},{10,... | collective-permute-start | bytes 884744 | tf_op jit(solution)/shard_map/ppermute | solution.py:587
  85.2 16.8 %collective-permute-start.8 = (bf16[192,768]{1,0:T(8,128)(2,1)S(1)}, bf16[192,768]{1,0:T(8,128)(2,1)}, u32[]{:S(2)}, u32[]{:S(2)}) collective-permute-start(bf16[192,768]{1,0:T(8,128)(2,1)S(1)} %concatenate.29), channel_id=1, source_target_pairs={{0,2},{1,3},{2,4},{3,5},{4,6},{5,7},{6,0},{7,1},{8,10},{9,11},{10,... | collective-permute-start | bytes 884744 | tf_op jit(solution)/shard_map/ppermute | solution.py:587
  86.0 25.5 %collective-permute-start.9 = (bf16[192,768]{1,0:T(8,128)(2,1)S(1)}, bf16[192,768]{1,0:T(8,128)(2,1)}, u32[]{:S(2)}, u32[]{:S(2)}) collective-permute-start(bf16[192,768]{1,0:T(8,128)(2,1)S(1)} %concatenate.29), channel_id=1, source_target_pairs={{0,4},{1,5},{2,6},{3,7},{4,0},{5,1},{6,2},{7,3},{8,12},{9,13},{10,... | collective-permute-start | bytes 884744 | tf_op jit(solution)/shard_map/ppermute | solution.py:587
  116.1 25.4 %collective-permute-start.12 = (bf16[96,768]{1,0:T(8,128)(2,1)S(1)}, bf16[96,768]{1,0:T(8,128)(2,1)S(1)}, u32[]{:S(2)}, u32[]{:S(2)}) collective-permute-start(bf16[96,768]{1,0:T(8,128)(2,1)S(1)} %copy-done.7), channel_id=1, source_target_pairs={{0,2},{1,3},{2,4},{3,5},{4,6},{5,7},{6,0},{7,1},{8,10},{9,11},{10,... | collective-permute-start | bytes 442376 | tf_op jit(solution)/shard_map/ppermute | solution.py:587
  116.1 25.4 %collective-permute-start.13 = (bf16[96,768]{1,0:T(8,128)(2,1)S(1)}, bf16[96,768]{1,0:T(8,128)(2,1)S(1)}, u32[]{:S(2)}, u32[]{:S(2)}) collective-permute-start(bf16[96,768]{1,0:T(8,128)(2,1)S(1)} %copy-done.7), channel_id=1, source_target_pairs={{0,4},{1,5},{2,6},{3,7},{4,0},{5,1},{6,2},{7,3},{8,12},{9,13},{10,... | collective-permute-start | bytes 442376 | tf_op jit(solution)/shard_map/ppermute | solution.py:587
  119.4 22.3 %collective-permute-start.14 = (bf16[96,768]{1,0:T(8,128)(2,1)S(1)}, bf16[96,768]{1,0:T(8,128)(2,1)S(1)}, u32[]{:S(2)}, u32[]{:S(2)}) collective-permute-start(bf16[96,768]{1,0:T(8,128)(2,1)S(1)} %copy-done.7), channel_id=1, source_target_pairs={{0,6},{1,7},{2,0},{3,1},{4,2},{5,3},{6,4},{7,5},{8,14},{9,15},{10,... | collective-permute-start | bytes 442376 | tf_op jit(solution)/shard_map/ppermute | solution.py:587
  122.4 19.3 %collective-permute-start.16 = (bf16[8,96,768]{2,1,0:T(8,128)(2,1)}, bf16[8,96,768]{2,1,0:T(8,128)(2,1)S(1)}, u32[]{:S(2)}, u32[]{:S(2)}) collective-permute-start(bf16[8,96,768]{2,1,0:T(8,128)(2,1)} %bitcast.127.rest_1_), channel_id=1, source_target_pairs={{0,1},{1,0},{2,3},{3,2},{4,5},{5,4},{6,7},{7,6},{8,9},{9,8},{10,11... | collective-permute-start | bytes 3538952 | tf_op jit(solution)/shard_map/ppermute | solution.py:571
  122.4 19.3 %collective-permute-start.15 = (bf16[4,96,768]{2,1,0:T(8,128)(2,1)S(1)}, bf16[4,96,768]{2,1,0:T(8,128)(2,1)S(1)}, u32[]{:S(2)}, u32[]{:S(2)}) collective-permute-start(bf16[4,96,768]{2,1,0:T(8,128)(2,1)S(1)} %copy-done.10), channel_id=1, source_target_pairs={{0,1},{1,0},{2,3},{3,2},{4,5},{5,4},{6,7},{7,6},{8,9},{9,8},{10,11... | collective-permute-start | bytes 1769480 | tf_op jit(solution)/shard_map/ppermute | solution.py:571
  150.0 22.8 %collective-permute-start.19 = (bf16[2,2,96,768]{3,2,1,0:T(8,128)(2,1)S(1)}, bf16[2,2,96,768]{3,2,1,0:T(8,128)(2,1)S(1)}, u32[]{:S(2)}, u32[]{:S(2)}) collective-permute-start(bf16[2,2,96,768]{3,2,1,0:T(8,128)(2,1)S(1)} %pad_maximum_fusion.6), channel_id=1, source_target_pairs={{0,8},{8,0},{16,24},{24,16},{1,9},{9,1},{17,25},{25,17},{2,10},{10... | collective-permute-start | bytes 1769480 | tf_op jit(solution)/shard_map/ppermute | solution.py:575
  151.9 20.9 %collective-permute-start.20 = (bf16[2,2,96,768]{3,2,1,0:T(8,128)(2,1)S(1)}, bf16[2,2,96,768]{3,2,1,0:T(8,128)(2,1)S(1)}, u32[]{:S(2)}, u32[]{:S(2)}) collective-permute-start(bf16[2,2,96,768]{3,2,1,0:T(8,128)(2,1)S(1)} %pad_maximum_fusion.7), channel_id=1, source_target_pairs={{0,16},{8,24},{16,0},{24,8},{1,17},{9,25},{17,1},{25,9},{2,18},{10... | collective-permute-start | bytes 1769480 | tf_op jit(solution)/shard_map/ppermute | solution.py:579
  183.8 22.6 %collective-permute-start.27 = (bf16[96,768]{1,0:T(8,128)(2,1)}, bf16[96,768]{1,0:T(8,128)(2,1)S(1)}, u32[]{:S(2)}, u32[]{:S(2)}) collective-permute-start(bf16[96,768]{1,0:T(8,128)(2,1)} %get-tuple-element.316), channel_id=1, source_target_pairs={{0,4},{1,5},{2,6},{3,7},{4,0},{5,1},{6,2},{7,3},{8,12},{9,13},{10,... | collective-permute-start | bytes 442376 | tf_op jit(solution)/shard_map/ppermute | solution.py:587
  185.9 20.5 %collective-permute-start.28 = (bf16[96,768]{1,0:T(8,128)(2,1)S(1)}, bf16[96,768]{1,0:T(8,128)(2,1)S(1)}, u32[]{:S(2)}, u32[]{:S(2)}) collective-permute-start(bf16[96,768]{1,0:T(8,128)(2,1)S(1)} %get-tuple-element.315), channel_id=1, source_target_pairs={{0,6},{1,7},{2,0},{3,1},{4,2},{5,3},{6,4},{7,5},{8,14},{9,15},{10,... | collective-permute-start | bytes 442376 | tf_op jit(solution)/shard_map/ppermute | solution.py:587
  188.4 18.0 %collective-permute-start.26 = (bf16[96,768]{1,0:T(8,128)(2,1)}, bf16[96,768]{1,0:T(8,128)(2,1)S(1)}, u32[]{:S(2)}, u32[]{:S(2)}) collective-permute-start(bf16[96,768]{1,0:T(8,128)(2,1)} %get-tuple-element.317), channel_id=1, source_target_pairs={{0,2},{1,3},{2,4},{3,5},{4,6},{5,7},{6,0},{7,1},{8,10},{9,11},{10,... | collective-permute-start | bytes 442376 | tf_op jit(solution)/shard_map/ppermute | solution.py:587
  188.7 17.7 %collective-permute-start.24 = (bf16[2,2,96,768]{3,2,1,0:T(8,128)(2,1)}, bf16[2,2,96,768]{3,2,1,0:T(8,128)(2,1)S(1)}, u32[]{:S(2)}, u32[]{:S(2)}) collective-permute-start(bf16[2,2,96,768]{3,2,1,0:T(8,128)(2,1)} %pad_maximum_fusion.9), channel_id=1, source_target_pairs={{0,8},{8,0},{16,24},{24,16},{1,9},{9,1},{17,25},{25,17},{2,10},{10... | collective-permute-start | bytes 1769480 | tf_op jit(solution)/shard_map/ppermute | solution.py:575
  190.2 16.3 %collective-permute-start.25 = (bf16[2,2,96,768]{3,2,1,0:T(8,128)(2,1)S(1)}, bf16[2,2,96,768]{3,2,1,0:T(8,128)(2,1)S(1)}, u32[]{:S(2)}, u32[]{:S(2)}) collective-permute-start(bf16[2,2,96,768]{3,2,1,0:T(8,128)(2,1)S(1)} %pad_maximum_fusion.10), channel_id=1, source_target_pairs={{0,16},{8,24},{16,0},{24,8},{1,17},{9,25},{17,1},{25,9},{2,18},{10... | collective-permute-start | bytes 1769480 | tf_op jit(solution)/shard_map/ppermute | solution.py:579
  207.4 22.0 %all-to-all-start.3 = ((bf16[4,96,768]{2,1,0:T(8,128)(2,1)}), bf16[4,96,768]{2,1,0:T(8,128)(2,1)S(1)}, u32[]{:S(2)}, u32[]{:S(2)}) async-start(bf16[4,96,768]{2,1,0:T(8,128)(2,1)} %broadcast_in_dim.16), calls=%async_computation.3 | async-start | bytes 1179648 | tf_op jit(solution)/shard_map/all_to_all | solution.py:595
  211.3 18.1 %collective-permute-start.30 = (bf16[2,96,768]{2,1,0:T(8,128)(2,1)S(1)}, bf16[2,96,768]{2,1,0:T(8,128)(2,1)S(1)}, u32[]{:S(2)}, u32[]{:S(2)}) collective-permute-start(bf16[2,96,768]{2,1,0:T(8,128)(2,1)S(1)} %slice_bitcast_fusion.14), channel_id=1, source_target_pairs={{0,8},{8,0},{16,24},{24,16},{1,9},{9,1},{17,25},{25,17},{2,10},{10... | collective-permute-start | bytes 884744 | tf_op jit(solution)/shard_map/ppermute | solution.py:575
  213.5 15.9 %collective-permute-start.29 = (bf16[2,96,768]{2,1,0:T(8,128)(2,1)S(1)}, bf16[2,96,768]{2,1,0:T(8,128)(2,1)S(1)}, u32[]{:S(2)}, u32[]{:S(2)}) collective-permute-start(bf16[2,96,768]{2,1,0:T(8,128)(2,1)S(1)} %slice_bitcast_fusion.15), channel_id=1, source_target_pairs={{0,16},{8,24},{16,0},{24,8},{1,17},{9,25},{17,1},{25,9},{2,18},{10... | collective-permute-start | bytes 884744 | tf_op jit(solution)/shard_map/ppermute | solution.py:579
  229.5 18.3 %collective-permute-start.32 = (bf16[96,768]{1,0:T(8,128)(2,1)S(1)}, bf16[96,768]{1,0:T(8,128)(2,1)S(1)}, u32[]{:S(2)}, u32[]{:S(2)}) collective-permute-start(bf16[96,768]{1,0:T(8,128)(2,1)S(1)} %get-tuple-element.312), channel_id=1, source_target_pairs={{0,4},{1,5},{2,6},{3,7},{4,0},{5,1},{6,2},{7,3},{8,12},{9,13},{10,... | collective-permute-start | bytes 442376 | tf_op jit(solution)/shard_map/ppermute | solution.py:587
  230.4 17.4 %collective-permute-start.33 = (bf16[96,768]{1,0:T(8,128)(2,1)S(1)}, bf16[96,768]{1,0:T(8,128)(2,1)S(1)}, u32[]{:S(2)}, u32[]{:S(2)}) collective-permute-start(bf16[96,768]{1,0:T(8,128)(2,1)S(1)} %get-tuple-element.311), channel_id=1, source_target_pairs={{0,6},{1,7},{2,0},{3,1},{4,2},{5,3},{6,4},{7,5},{8,14},{9,15},{10,... | collective-permute-start | bytes 442376 | tf_op jit(solution)/shard_map/ppermute | solution.py:587
  257.9 29.2 %collective-permute-start.35 = (bf16[2,2,96,768]{3,2,1,0:T(8,128)(2,1)}, bf16[2,2,96,768]{3,2,1,0:T(8,128)(2,1)S(1)}, u32[]{:S(2)}, u32[]{:S(2)}) collective-permute-start(bf16[2,2,96,768]{3,2,1,0:T(8,128)(2,1)} %pad_maximum_fusion.11), channel_id=1, source_target_pairs={{0,8},{8,0},{16,24},{24,16},{1,9},{9,1},{17,25},{25,17},{2,10},{10... | collective-permute-start | bytes 1769480 | tf_op jit(solution)/shard_map/ppermute | solution.py:575
  258.5 28.7 %collective-permute-start.36 = (bf16[2,2,96,768]{3,2,1,0:T(8,128)(2,1)S(1)}, bf16[2,2,96,768]{3,2,1,0:T(8,128)(2,1)S(1)}, u32[]{:S(2)}, u32[]{:S(2)}) collective-permute-start(bf16[2,2,96,768]{3,2,1,0:T(8,128)(2,1)S(1)} %pad_maximum_fusion.12), channel_id=1, source_target_pairs={{0,16},{8,24},{16,0},{24,8},{1,17},{9,25},{17,1},{25,9},{2,18},{10... | collective-permute-start | bytes 1769480 | tf_op jit(solution)/shard_map/ppermute | solution.py:579
  287.4 18.0 %collective-permute-start.38 = (bf16[2,96,768]{2,1,0:T(8,128)(2,1)S(1)}, bf16[2,96,768]{2,1,0:T(8,128)(2,1)S(1)}, u32[]{:S(2)}, u32[]{:S(2)}) collective-permute-start(bf16[2,96,768]{2,1,0:T(8,128)(2,1)S(1)} %slice_bitcast_fusion.10), channel_id=1, source_target_pairs={{0,8},{8,0},{16,24},{24,16},{1,9},{9,1},{17,25},{25,17},{2,10},{10... | collective-permute-start | bytes 884744 | tf_op jit(solution)/shard_map/ppermute | solution.py:575
  289.6 15.8 %collective-permute-start.37 = (bf16[2,96,768]{2,1,0:T(8,128)(2,1)S(1)}, bf16[2,96,768]{2,1,0:T(8,128)(2,1)S(1)}, u32[]{:S(2)}, u32[]{:S(2)}) collective-permute-start(bf16[2,96,768]{2,1,0:T(8,128)(2,1)S(1)} %slice_bitcast_fusion.11), channel_id=1, source_target_pairs={{0,16},{8,24},{16,0},{24,8},{1,17},{9,25},{17,1},{25,9},{2,18},{10... | collective-permute-start | bytes 884744 | tf_op jit(solution)/shard_map/ppermute | solution.py:579
  306.6 16.4 %all-to-all-start.6 = ((bf16[4,96,768]{2,1,0:T(8,128)(2,1)}), bf16[4,96,768]{2,1,0:T(8,128)(2,1)S(1)}, u32[]{:S(2)}, u32[]{:S(2)}) async-start(bf16[4,96,768]{2,1,0:T(8,128)(2,1)} %broadcast_in_dim.19), calls=%async_computation.6 | async-start | bytes 1179648 | tf_op jit(solution)/shard_map/all_to_all | solution.py:595
  (52 other events, 464.5 us)

commit v3 on v2

--- a/solution.py
+++ b/solution.py
@@ -621,10 +621,14 @@
     return jnp.stack(table).astype(jnp.int32)
 
 
-def fast_small(e0, e1, z, c, width, rows):
+def shard_order(e0, e1, z, c):
     pair = jnp.stack([jnp.where(c == 0, e0, e1), jnp.where(c == 0, e1, e0)], axis=1)
     got = jnp.stack([pick(pair, lax.rem(z - i + 4, 4)) for i in range(4)])
-    got = got.reshape(8, 16, width).astype(f32)
+    return got.reshape((8,) + got.shape[2:])
+
+
+def fast_small(got, width, rows):
+    got = got.astype(f32)
     vecs = got[:, :8, : width // 8].transpose(1, 0, 2).reshape(8, width)
     hb = got[:, 8, : width // 2].reshape(4, width)
     ids = (got[:, 9, :rows] * 32.0 + got[:, 10, :rows]).astype(jnp.int32)
@@ -664,6 +668,15 @@
 
     def total(self):
         return sum(p.astype(f32) for p in self.r3).astype(bf16)
+
+
+def spread(mine):
+    return [mine, x_swap(mine), y_swap(mine), diagonal_swap(mine)]
+
+
+def quarters(got, d):
+    got = jnp.stack(got)
+    return [pick(got, d ^ q).astype(f32) for q in range(4)]
 
 
 def per_device(
@@ -699,13 +712,13 @@
         got = along_z(jnp.concatenate([own_a, small], axis=0))
         s0 = rows_of(got, 0, b)
         e0 = rows_of(got, b, 16)
-        e1 = core_swap(e0)
-        own_c = [down_weight[i * b : (i + 1) * b] for i in range(4)]
         mine_a = columns(s0)
-        got1 = along_z(tie(jnp.concatenate([own_b, own_c[0]], axis=0), got))
-        vecs, hb, here = fast_small(e0, e1, z, c, width, rows)
+        got1 = along_z(tie(jnp.concatenate([own_b, down_weight[:b]], axis=0), got))
+        vecs, hb, here = fast_small(shard_order(e0, core_swap(e0), z, c), width, rows)
         gpos = [(q ^ d) * 4 + lax.rem(zf - z + 4, 4) for q in range(4) for zf in range(4)] + [c]
         gpos = jnp.stack(gpos).astype(jnp.int32)
+        slots = fast_slots(z, c)
+        slots_c = down_slots(z, c, ((0,), (1, 2), (3,)))
     else:
         ga, gb, gc, vecs, hb = plain_groups(
             jnp.stack(q4), jnp.stack(h4), down_weight, vec_args + (hidden_bias,)
@@ -715,43 +728,47 @@
 
     onehot = (here.reshape(nf * rows)[:, None] == steps[None, :]).astype(bf16)
     looked = jnp.dot(onehot, step_table, preferred_element_type=f32).astype(bf16)
-    looked = looked.reshape(nf, rows, width // nf)
-    if fast:
-        (mine_a, looked), got1 = lax.optimization_barrier(((mine_a, looked), got1))
-    emb = lax.all_to_all(looked, "fsdp", 0, 0, tiled=True)
+    if fast:
+        looked, seg, pad, vecs, hb, gpos, slots, slots_c = lax.optimization_barrier(
+            (looked.reshape(rows, width), seg, pad, vecs, hb, gpos, slots, slots_c)
+        )
+        sent = jnp.pad(looked, ((0, 16 - rows), (0, 0)))
+        got_e = jnp.stack(along_z(sent))
+        mine_a, got1, got_e = lax.optimization_barrier((mine_a, got1, got_e))
+        emb = shard_order(got_e, core_swap(got_e), z, c)[:, :rows].reshape(nf, nf, rows, width // nf)
+        emb = pick(emb.transpose(1, 0, 2, 3), f)
+    else:
+        emb = lax.all_to_all(looked.reshape(nf, rows, width // nf), "fsdp", 0, 0, tiled=True)
     emb = emb.transpose(1, 0, 2).reshape(rows, width).astype(f32)
 
     if fast:
         flat = (16, b, width)
         mine_a = mine_a.reshape(flat)
         core_a = core_swap(mine_a)
-        s0 = rows_of(got1, 0, b)
+        ga = Group([mine_a, core_a], [(0, 0, 16), (1, 0, 16)], slots)
+        mine_b = columns(rows_of(got1, 0, b))
         c0 = rows_of(got1, b, b)
-        ga = Group([mine_a, core_a], [(0, 0, 16), (1, 0, 16)], fast_slots(z, c))
-        tok_in, s0, own_c12 = tie((tok, s0, jnp.concatenate(own_c[1:3], axis=0)), (core_a, emb, c0))
-        mine_b = columns(s0)
-        got2 = along_z(own_c12)
+        got2 = along_z(tie(down_weight[b : 3 * b], got1))
+        tok_in = tie(tok, (core_a, emb))
     else:
         tok_in = tok
     normed, triple, att, attended, middle, n2 = compute_f1(tok_in, emb, seg, pad, vecs, ga, rows, length)
     if fast:
-        mine_b, got2, n2 = lax.optimization_barrier((mine_b, got2, n2))
-        mine_b = mine_b.reshape(flat)
+        mine_b, n2, got2 = lax.optimization_barrier((mine_b.reshape(flat), n2, got2))
         core_b = core_swap(mine_b)
-        gb = Group([mine_b, core_b], [(0, 0, 16), (1, 0, 16)], fast_slots(z, c))
-        n2, c0, c12, c3 = tie((n2, c0, got2, own_c[3]), core_b)
-        c12 = jnp.stack(c12).reshape(8, b, width)
-        got3 = along_z(c3)
+        gb = Group([mine_b, core_b], [(0, 0, 16), (1, 0, 16)], slots)
+        n2, c0, got2, own_c3 = tie((n2, c0, got2, down_weight[3 * b :]), core_b)
+        got3 = along_z(own_c3)
+        c12 = jnp.stack(got2).reshape(8, b, width)
         c0x, c12x = core_swap(c0), core_swap(c12)
     active, gp, keep_c, send_c = compute_f2(n2, cot, hb, gb, gpos)
     if fast:
         got3, c0x, c12x, gp, keep_c, send_c = lax.optimization_barrier((got3, c0x, c12x, gp, keep_c, send_c))
         c3 = jnp.stack(got3)
-        c3x = core_swap(c3)
         gc = Group(
-            [c0, c12, c3, c0x, c12x, c3x],
+            [c0, c12, c3, c0x, c12x, core_swap(c3)],
             [(0, 0, 4), (1, 0, 8), (2, 0, 4), (3, 0, 4), (4, 0, 8), (5, 0, 4)],
-            down_slots(z, c, ((0,), (1, 2), (3,))),
+            slots_c,
         )
         sc = Scatter(keep_c, send_c)
         sc.split()
@@ -763,52 +780,58 @@
         sc.two()
         sb = Scatter(keep_b, send_b)
         sb.split()
-        dh, sb.out, sc.r2 = lax.optimization_barrier((dh, sb.out, sc.r2))
+        dh, sb.out = lax.optimization_barrier((dh, sb.out))
         sb.one()
+    dmid, dbr, datt, sums2 = compute_b2(dh, cot, middle, vecs, ga, gb)
+    if fast:
+        datt, sb.r1, sc.r2 = lax.optimization_barrier((datt, sb.r1, sc.r2))
+        sb.two()
         sc.three()
-    dmid, dbr, datt, sums2 = compute_b2(dh, cot, middle, vecs, ga, gb)
-    if fast:
-        datt, sb.r1, sc.r3 = lax.optimization_barrier((datt, sb.r1, sc.r3))
-        sb.two()
-        out_c = columns(sc.total())
     dt, sums3 = compute_b3(datt, triple, att, rows, length)
     if fast:
-        dt, sb.r2, out_c = lax.optimization_barrier((dt, sb.r2, out_c))
+        dt, sb.r2, sc.r3 = lax.optimization_barrier((dt, sb.r2, sc.r3))
         sb.three()
+        mine_c = sc.total()
     keep_a, send_a = compute_ga(normed, attended, dt, dbr, gpos)
     if fast:
-        keep_a, send_a, sb.r3 = lax.optimization_barrier((keep_a, send_a, sb.r3))
+        keep_a, send_a, sb.r3, mine_c, dt = lax.optimization_barrier((keep_a, send_a, sb.r3, mine_c, dt))
         sa = Scatter(keep_a, send_a)
         sa.split()
-        dt, sa.out = lax.optimization_barrier((dt, sa.out))
+        dt, sa.out, active = lax.optimization_barrier((dt, sa.out, active))
         sa.one()
+        out_c = spread(mine_c)
+        mine_b = sb.total()
     input_grad, row_sums, sums4 = compute_b4(tok, emb, dmid, dt, vecs, ga, rows, length)
-    row_sums = row_sums[:rows]
+    if fast:
+        result = compute_f3(active, middle, vecs, gc)
+        sa.r1, row_sums, sums4, result, out_c = lax.optimization_barrier((sa.r1, row_sums, sums4, result, out_c))
 
     part = width // nf
-    sums = jnp.concatenate(
-        [row_sums, sums3[0:2], sums2[2:3], sums4[0:2], sums2[0:2], db_sum[0:1]], axis=0
-    )
-    lanes = sums.reshape(rows + 8, nf, part).transpose(1, 0, 2).reshape(nf, (rows + 8) * part)
+    every = [row_sums, sums3, sums2, sums4, db_sum, hb_sum]
+    lines = row_sums.shape[0] + 32
     marks = jnp.broadcast_to(ids.astype(f32)[None, :], (nf, rows))
+    lanes = jnp.concatenate(every[:5], axis=0).reshape(lines, nf, part).transpose(1, 0, 2).reshape(nf, lines * part)
     payload = jnp.concatenate([lanes, hb_sum[:4].reshape(nf, 4 * part), marks], axis=1)
+    nt, end = rows * part, payload.shape[1] - rows
+    if fast:
+        sa.two()
+        out_b = spread(mine_b)
     moved = lax.all_to_all(payload, "fsdp", 0, 0, tiled=True)
     if fast:
-        sa.r1, moved, active = lax.optimization_barrier((sa.r1, moved, active))
-        sa.two()
+        sa.r2, moved, out_b = lax.optimization_barrier((sa.r2, moved, out_b))
+        sa.three()
         moved = columns(moved).reshape(nd * nf, payload.shape[1])
+        moved, sa.r3 = lax.optimization_barrier((moved, sa.r3))
     else:
         moved = lax.all_gather(moved, "dp", axis=0, tiled=True)
-    result = compute_f3(active, middle, vecs, gc)
-    if fast:
-        sa.r2, moved, tb = lax.optimization_barrier((sa.r2, moved, sb.r3))
-        sa.three()
-        sb.r3 = tb
-        out_b = columns(sb.total())
-        sa.r3, out_b = lax.optimization_barrier((sa.r3, out_b))
-        out_a = columns(sa.total()).astype(f32)
-        out_b = out_b.astype(f32)
-        down_grad = out_c.astype(f32).reshape(4 * b, width)
+    table_rows = moved[:, :nt].reshape(nd * nf * rows, part)
+    all_ids = moved[:, end:].astype(jnp.int32).reshape(1, nd * nf * rows)
+    vec_sums = jnp.sum(moved[:, nt:end], axis=0)
+    if not fast:
+        result = compute_f3(active, middle, vecs, gc)
+    if fast:
+        out_a, out_b, out_c = (quarters(v, d) for v in (spread(sa.total()), out_b, out_c))
+        down_grad = jnp.concatenate(out_c, axis=0)
     else:
         out_b = plain_scatter(keep_b, send_b, False)
         out_a = plain_scatter(keep_a, send_a, False)
@@ -816,13 +839,11 @@
     hidden_grad = jnp.concatenate([out_b[i] for i in range(4)], axis=1)
     triple_grad = jnp.concatenate([out_a[i] for i in range(3)], axis=1)
     output_grad = out_a[3]
-    table_rows = moved[:, : rows * part].reshape(nd * nf * rows, part)
-    all_ids = moved[:, (rows + 12) * part :].astype(jnp.int32).reshape(1, nd * nf * rows)
     all_hot = (steps[:, None] == all_ids).astype(f32)
     table_grad = jnp.dot(all_hot, table_rows, precision=highest)
-    vec_sums = jnp.sum(moved[:, rows * part : (rows + 12) * part], axis=0)
-    v = [vec_sums[i * part : (i + 1) * part] for i in range(8)]
-    hidden_bias_grad = vec_sums[8 * part :]
+    kept = vec_sums[(lines - 32 - rows) * part : (lines - rows) * part].reshape(32, part)
+    v = [kept[i] for i in (0, 1, 10, 16, 17, 8, 9, 24)]
+    hidden_bias_grad = vec_sums[(lines - rows) * part :]
     shape = tokens.shape
     return (
         result.reshape(shape), input_grad.reshape(shape), table_grad, triple_grad, v[0], v[1], output_grad, v[2],

time: 340 us -> 320 us (0.941)
  local copies, waits for them, and re-layouts: 46.2 us -> 33.7 us
  waiting for transfers between devices: 70.9 us -> 62.5 us
  other arithmetic: 17.8 us -> 21.4 us
    all_to_all x6 -> x3, starting transfers between devices: 24.3 us -> 12.7 us  [columns(): lax.all_to_all(jnp.broadcast_to(v[None], (4,) + v.shape), 'dp', 0, 0, til...]
    ppermute x21 -> x24, waiting for transfers between devices: 44.5 us -> 33.2 us  [z_shift(): return lax.ppermute(v, 'fsdp', [(i, (i + 2 * k) % 8) for i in range(8)])]
    ppermute x21 -> x24, starting transfers between devices: 29.7 us -> 39.8 us  [z_shift(): return lax.ppermute(v, 'fsdp', [(i, (i + 2 * k) % 8) for i in range(8)])]
    all_to_all x1 -> x0, starting transfers between devices: 8.48 us -> none  [per_device(): emb = lax.all_to_all(looked, 'fsdp', 0, 0, tiled=True)]
    ppermute x6 -> x9, waiting for transfers between devices: 0.53 us -> 6.79 us  [y_swap(): return lax.ppermute(v, 'dp', xor_perm(4, 2))]
    all_to_all x1, waiting for transfers between devices: 4.85 us -> 0.01 us  [per_device(): moved = lax.all_to_all(payload, 'fsdp', 0, 0, tiled=True)]
    ppermute x0 -> x3, starting transfers between devices: none -> 4.73 us  [diagonal_swap(): return lax.ppermute(v, 'dp', xor_perm(4, 3))]
    slice x9 -> x6, local copies, waits for them, and re-layouts: 7.35 us -> 2.94 us  [the longest x1 0.98 us: per_device(): got2 = along_z(tie(down_weight[b:3 * b], got1))]
  transfers between devices with their start and end apart: 50 -> 59, of which waited for: 15 -> 15; matrix products, arithmetic and copies ran while one was open for 13% -> 13% of each run, Pallas kernels for 35% -> 37%
where the time goes in v3:
time: 320 us; the launch traced here: 319 us
  Pallas kernels  116 us (36%)
  starting transfers between devices  81.1 us (25%)
  waiting for transfers between devices  62.5 us (20%)
  local copies, waits for them, and re-layouts  33.7 us (11%)
  other arithmetic  21.4 us (7%)
    pallas_call x8, Pallas kernels, call(): pl.pallas_call(kernel, grid=grid, in_specs=in_specs, out_shape=out_shape,...  116 us
    ppermute x24, starting transfers between devices, z_shift(): return lax.ppermute(v, 'fsdp', [(i, (i + 2 * k) % 8) for i in range(8)])  39.8 us
    ppermute x24, waiting for transfers between devices, z_shift(): return lax.ppermute(v, 'fsdp', [(i, (i + 2 * k) % 8) for i in range(8)])  33.2 us
    all_to_all x3, starting transfers between devices, columns(): lax.all_to_all(jnp.broadcast_to(v[None], (4,) + v.shape), 'dp', 0, 0, til...  12.7 us
    ppermute x10, waiting for transfers between devices, core_swap(): return lax.ppermute(v, 'fsdp', xor_perm(8, 1))  11.9 us
    ppermute x9, starting transfers between devices, y_swap(): return lax.ppermute(v, 'dp', xor_perm(4, 2))  8.97 us
    ppermute x9, starting transfers between devices, x_swap(): return lax.ppermute(v, 'dp', xor_perm(4, 1))  8.57 us
    convert_element_type x15, other arithmetic, add(): return (u.astype(f32) + v.astype(f32)).astype(bf16)  8.38 us
  transfers between devices with their start and end apart: 59, of which 15 were waited for; matrix products, arithmetic and copies ran while one was open for 13% of the time, Pallas kernels for 37%

profile of v3, /device:TPU:0, one launch (start us, length us, event | category | flops | bytes accessed | tf_op | source)
XLA Modules:
  0.0 318.6 jit_solution(3139193934639743526)
XLA Ops:
  5.0 5.1 %collective-permute-start.2 = (bf16[112,768]{1,0:T(8,128)(2,1)S(1)}, bf16[112,768]{1,0:T(8,128)(2,1)S(1)}, u32[]{:S(2)}, u32[]{:S(2)}) collective-permute-start(bf16[112,768]{1,0:T(8,128)(2,1)S(1)} %pad_maximum_fusion.16), channel_id=1, source_target_pairs={{0,6},{1,7},{2,0},{3,1},{4,2},{5,3},{6,4},{7,5},{8,14},{9,15},{10,... | collective-permute-start | bytes 516104 | tf_op jit(solution)/shard_map/ppermute | solution.py:587
  15.1 9.5 %collective-permute-done.1 = bf16[112,768]{1,0:T(8,128)(2,1)S(1)} collective-permute-done((bf16[112,768]{1,0:T(8,128)(2,1)S(1)}, bf16[112,768]{1,0:T(8,128)(2,1)S(1)}, u32[]{:S(2)}, u32[]{:S(2)}) %collective-permute-start.1) | collective-permute-done | bytes 172064 | tf_op jit(solution)/shard_map/ppermute | solution.py:587
  26.4 4.7 %all-to-all-start = ((bf16[4,4,96,768]{3,2,1,0:T(8,128)(2,1)}), bf16[4,4,96,768]{3,2,1,0:T(8,128)(2,1)S(1)}, u32[]{:S(2)}, u32[]{:S(2)}) async-start(bf16[4,4,96,768]{3,2,1,0:T(8,128)(2,1)} %broadcast_in_dim.8), calls=%async_computation | async-start | bytes 4718592 | tf_op jit(solution)/shard_map/all_to_all | solution.py:595
  35.7 2.8 collective-permute-start.6
  45.0 12.7 %collective-permute-done.7 = bf16[16,768]{1,0:T(8,128)(2,1)S(1)} collective-permute-done((bf16[16,768]{1,0:T(8,128)(2,1)S(1)}, bf16[16,768]{1,0:T(8,128)(2,1)S(1)}, u32[]{:S(2)}, u32[]{:S(2)}) %collective-permute-start.7) | collective-permute-done | bytes 24608 | tf_op jit(solution)/shard_map/ppermute | solution.py:587
  57.7 6.6 %collective-permute-done.8 = bf16[16,768]{1,0:T(8,128)(2,1)S(1)} collective-permute-done((bf16[16,768]{1,0:T(8,128)(2,1)S(1)}, bf16[16,768]{1,0:T(8,128)(2,1)S(1)}, u32[]{:S(2)}, u32[]{:S(2)}) %collective-permute-start.8) | collective-permute-done | bytes 24608 | tf_op jit(solution)/shard_map/ppermute | solution.py:587
  71.6 4.5 %all-to-all-start.1 = ((bf16[4,4,96,768]{3,2,1,0:T(8,128)(2,1)}), bf16[4,4,96,768]{3,2,1,0:T(8,128)(2,1)}, u32[]{:S(2)}, u32[]{:S(2)}) async-start(bf16[4,4,96,768]{3,2,1,0:T(8,128)(2,1)} %broadcast_in_dim.9), calls=%async_computation.1 | async-start | bytes 4718592 | tf_op jit(solution)/shard_map/all_to_all | solution.py:595
  77.3 2.5 collective-permute-start.12
  81.4 2.8 collective-permute-start.14
  86.2 15.5 %shard_map.306 = (bf16[768,768]{1,0:T(8,128)(2,1)}, bf16[3,768,768]{2,1,0:T(8,128)(2,1)}, bf16[36,256,128]{2,1,0:T(8,128)(2,1)}, bf16[768,768]{1,0:T(8,128)(2,1)...) custom-call(s32[32]{0:T(128)} %stack.629.slots.slots_a.slots_b, bf16[768,768]{1,0:T(8,128)(2,1)} %bitcast.343, ...), custom_call_target="tpu_custom_call" | custom-call | flops 10871635968 | bytes 20971520 | tf_op jit(solution)/shard_map/pallas_call | solution.py:369
  101.7 3.1 all-to-all-done.1
  104.9 4.6 %collective-permute-done.15.rest_1_.rest_3_ = bf16[16,96,768]{2,1,0:T(8,128)(2,1)S(1)} collective-permute-done((bf16[16,96,768]{2,1,0:T(8,128)(2,1)}, bf16[16,96,768]{2,1,0:T(8,128)(2,1)S(1)}, u32[]{:S(2)}, u32[]{:S(2)}) %collective-permute-start.15) | collective-permute-done | bytes 2359328 | tf_op jit(solution)/shard_map/ppermute | solution.py:571
  109.5 3.3 %collective-permute-start.16 = (bf16[96,768]{1,0:T(8,128)(2,1)S(1)}, bf16[96,768]{1,0:T(8,128)(2,1)S(1)}, u32[]{:S(2)}, u32[]{:S(2)}) collective-permute-start(bf16[96,768]{1,0:T(8,128)(2,1)S(1)} %get-tuple-element.213), channel_id=1, source_target_pairs={{0,2},{1,3},{2,4},{3,5},{4,6},{5,7},{6,0},{7,1},{8,10},{9,11},{10,... | collective-permute-start | bytes 442376 | tf_op jit(solution)/shard_map/ppermute | solution.py:587
  112.8 3.0 collective-permute-start.17
  118.3 18.7 %shard_map.307 = (bf16[4,768,768]{2,1,0:T(8,128)(2,1)}, bf16[4,768,768]{2,1,0:T(8,128)(2,1)}, bf16[16,96,768]{2,1,0:T(8,128)(2,1)}, bf16[16,96,768]{2,1,0:T(8,128)(2,1)}) custom-call(s32[32]{0:T(128)} %stack.629.slots.slots_a.slots_b, s32[17]{0:T(128)} %stack.596.gpos, bf16[768,768]{1,0:T(8,128)(2,1)} %get-tuple-element.198.n2_ref, ...), custom_call_target="tpu_custom_call" | custom-call | flops 14495514624 | bytes 20971520 | tf_op jit(solution)/shard_map/pallas_call | solution.py:369
  137.8 4.9 %collective-permute-done.21 = bf16[16,96,768]{2,1,0:T(8,128)(2,1)S(1)} collective-permute-done((bf16[16,96,768]{2,1,0:T(8,128)(2,1)}, bf16[16,96,768]{2,1,0:T(8,128)(2,1)S(1)}, u32[]{:S(2)}, u32[]{:S(2)}) %collective-permute-start.21) | collective-permute-done | bytes 2359328 | tf_op jit(solution)/shard_map/ppermute | solution.py:571
  142.7 2.3 add_convert_fusion.19
  148.9 19.5 %shard_map.308 = (bf16[4,768,768]{2,1,0:T(8,128)(2,1)}, f32[8,768]{1,0:T(8,128)}, f32[8,768]{1,0:T(8,128)}, bf16[16,96,768]{2,1,0:T(8,128)(2,1)}, bf16[16,96,768]{2,1,0:T(8,128)(2,1)}) custom-call(s32[32]{0:T(128)} %stack.662.slots, s32[17]{0:T(128)} %stack.596.gpos, bf16[768,768]{1,0:T(8,128)(2,1)} %get-tuple-element.198.n2_ref, ...), custom_call_target="tpu_custom_call" | custom-call | flops 14495514624 | bytes 20971520 | tf_op jit(solution)/shard_map/pallas_call | solution.py:369
  176.0 15.7 %shard_map.309 = (f32[768,768]{1,0:T(8,128)}, bf16[768,768]{1,0:T(8,128)(2,1)}, bf16[768,768]{1,0:T(8,128)(2,1)}, f32[8,768]{1,0:T(8,128)}) custom-call(s32[32]{0:T(128)} %stack.629.slots.slots_a.slots_b, s32[32]{0:T(128)} %stack.629.slots.slots_a.slots_b, bf16[4,768,768]{2,1,0:T(8,128)(2,1)} %get-tuple-element.227.dh_ref, bf16[768,768]{1,0:T(8,128)(2,1)} %bitcast.342, ...), custom_call_target="tpu_custom_call" | custom-call | flops 9059696640 | bytes 20971520 | tf_op jit(solution)/shard_map/pallas_call | solution.py:369
  196.0 3.0 collective-permute-start.34
  203.3 14.4 %shard_map.310 = (bf16[3,768,768]{2,1,0:T(8,128)(2,1)}, f32[8,768]{1,0:T(8,128)}) custom-call(bf16[768,768]{1,0:T(8,128)(2,1)} %get-tuple-element.234.datt_ref, bf16[3,768,768]{2,1,0:T(8,128)(2,1)} %get-tuple-element.235.triple_ref, bf16[36,256,128]{2,1,0:T(8,128)(2,1)} %get-tuple-element.236.att_ref), custom_call_target="tpu_custom_call" | custom-call | flops 9059696640 | bytes 20971520 | tf_op jit(solution)/shard_map/pallas_call | solution.py:369
  218.4 3.3 %collective-permute-start.37 = (bf16[96,768]{1,0:T(8,128)(2,1)S(1)}, bf16[96,768]{1,0:T(8,128)(2,1)S(1)}, u32[]{:S(2)}, u32[]{:S(2)}) collective-permute-start(bf16[96,768]{1,0:T(8,128)(2,1)S(1)} %get-tuple-element.343), channel_id=1, source_target_pairs={{0,6},{1,7},{2,0},{3,1},{4,2},{5,3},{6,4},{7,5},{8,14},{9,15},{10,... | collective-permute-start | bytes 442376 | tf_op jit(solution)/shard_map/ppermute | solution.py:587
  223.0 13.2 %shard_map.311 = (bf16[16,96,768]{2,1,0:T(8,128)(2,1)}, bf16[16,96,768]{2,1,0:T(8,128)(2,1)}) custom-call(s32[17]{0:T(128)} %stack.596.gpos, bf16[768,768]{1,0:T(8,128)(2,1)} %get-tuple-element.183.normed_ref, bf16[768,768]{1,0:T(8,128)(2,1)} %get-tuple-element.184.attended_ref, bf16[3,768,768]{2,1,0:T(8,128)(2,1)} %get-tuple-element.259.dt_ref, ...), custom_call_target="tpu_custom_call" | custom-call | flops 7247757312 | bytes 12582912 | tf_op jit(solution)/shard_map/pallas_call | solution.py:369
  246.9 9.7 %shard_map.313 = bf16[768,768]{1,0:T(8,128)(2,1)} custom-call(s32[32]{0:T(128)} %stack.662.slots, bf16[4,768,768]{2,1,0:T(8,128)(2,1)} %get-tuple-element.262.act_ref, f32[768,768]{1,0:T(8,128)} %get-tuple-element.228.middle_ref, f32[8,768]{1,0:T(8,128)} %reshape.369.vec_ref, bf16[4,96,768]{2,1,0:T(8,128)(2,1)} %copy-done.8, bf16[8,96,768]{2,1,0:T(8,128)(2,1)} %bitcast.310, ...), custom_call_target="tpu_custom_call" | custom-call | flops 7247757312 | bytes 12582912 | tf_op jit(solution)/shard_map/pallas_call | solution.py:369
  256.7 9.7 %shard_map.312 = (bf16[768,768]{1,0:T(8,128)(2,1)}, f32[8,768]{1,0:T(8,128)}, f32[8,768]{1,0:T(8,128)}) custom-call(s32[32]{0:T(128)} %stack.629.slots.slots_a.slots_b, bf16[768,768]{1,0:T(8,128)(2,1)} %bitcast.344, f32[6,768]{1,0:T(8,128)} %reshape.391.emb_ref, f32[768,768]{1,0:T(8,128)} %get-tuple-element.258.dmid_ref, ...), custom_call_target="tpu_custom_call" | custom-call | flops 5435817984 | bytes 12582912 | tf_op jit(solution)/shard_map/pallas_call | solution.py:369
  269.1 4.7 %all-to-all-start.2 = ((f32[8,1,4230]{2,1,0:T(1,128)}), f32[8,1,4230]{2,1,0:T(1,128)}, u32[]{:S(2)}, u32[]{:S(2)}) async-start(f32[8,1,4230]{2,1,0:T(1,128)} %copy.51), calls=%async_computation.2 | async-start | bytes 278528 | tf_op jit(solution)/shard_map/all_to_all | solution.py:819
  282.2 4.7 %collective-permute-done.46 = bf16[96,768]{1,0:T(8,128)(2,1)S(1)} collective-permute-done((bf16[96,768]{1,0:T(8,128)(2,1)S(1)}, bf16[96,768]{1,0:T(8,128)(2,1)S(1)}, u32[]{:S(2)}, u32[]{:S(2)}) %collective-permute-start.46) | collective-permute-done | bytes 147488 | tf_op jit(solution)/shard_map/ppermute | solution.py:575
  286.9 4.1 %collective-permute-done.47 = bf16[96,768]{1,0:T(8,128)(2,1)S(1)} collective-permute-done((bf16[96,768]{1,0:T(8,128)(2,1)S(1)}, bf16[96,768]{1,0:T(8,128)(2,1)S(1)}, u32[]{:S(2)}, u32[]{:S(2)}) %collective-permute-start.47) | collective-permute-done | bytes 147488 | tf_op jit(solution)/shard_map/ppermute | solution.py:579
  291.2 2.6 collective-permute-start.50
  296.9 3.5 %all-to-all-start.3 = ((f32[4,8,4230]{2,1,0:T(8,128)}), f32[4,8,4230]{2,1,0:T(8,128)S(1)}, u32[]{:S(2)}, u32[]{:S(2)}) async-start(f32[4,8,4230]{2,1,0:T(8,128)} %broadcast_in_dim.11), calls=%async_computation.3 | async-start | bytes 1114112 | tf_op jit(solution)/shard_map/all_to_all | solution.py:595
  301.6 2.9 collective-permute-done.50
  304.5 2.8 all-to-all-done.3
  (296 shorter events, 96.2 us)
Async XLA Ops:
  26.4 39.3 %all-to-all-start = ((bf16[4,4,96,768]{3,2,1,0:T(8,128)(2,1)}), bf16[4,4,96,768]{3,2,1,0:T(8,128)(2,1)S(1)}, u32[]{:S(2)}, u32[]{:S(2)}) async-start(bf16[4,4,96,768]{3,2,1,0:T(8,128)(2,1)} %broadcast_in_dim.8), calls=%async_computation | async-start | bytes 4718592 | tf_op jit(solution)/shard_map/all_to_all | solution.py:595
  32.8 32.9 %collective-permute-start.4 = (bf16[192,768]{1,0:T(8,128)(2,1)S(1)}, bf16[192,768]{1,0:T(8,128)(2,1)}, u32[]{:S(2)}, u32[]{:S(2)}) collective-permute-start(bf16[192,768]{1,0:T(8,128)(2,1)S(1)} %pad_maximum_fusion.14), channel_id=1, source_target_pairs={{0,2},{1,3},{2,4},{3,5},{4,6},{5,7},{6,0},{7,1},{8,10},{9,11},{10,... | collective-permute-start | bytes 884744 | tf_op jit(solution)/shard_map/ppermute | solution.py:587
  33.7 32.0 %collective-permute-start.5 = (bf16[192,768]{1,0:T(8,128)(2,1)S(1)}, bf16[192,768]{1,0:T(8,128)(2,1)}, u32[]{:S(2)}, u32[]{:S(2)}) collective-permute-start(bf16[192,768]{1,0:T(8,128)(2,1)S(1)} %pad_maximum_fusion.14), channel_id=1, source_target_pairs={{0,4},{1,5},{2,6},{3,7},{4,0},{5,1},{6,2},{7,3},{8,12},{9,13},{10,... | collective-permute-start | bytes 884744 | tf_op jit(solution)/shard_map/ppermute | solution.py:587
  35.7 30.0 %collective-permute-start.6 = (bf16[192,768]{1,0:T(8,128)(2,1)S(1)}, bf16[192,768]{1,0:T(8,128)(2,1)}, u32[]{:S(2)}, u32[]{:S(2)}) collective-permute-start(bf16[192,768]{1,0:T(8,128)(2,1)S(1)} %pad_maximum_fusion.14), channel_id=1, source_target_pairs={{0,6},{1,7},{2,0},{3,1},{4,2},{5,3},{6,4},{7,5},{8,14},{9,15},{10,... | collective-permute-start | bytes 884744 | tf_op jit(solution)/shard_map/ppermute | solution.py:587
  44.4 19.8 %collective-permute-start.8 = (bf16[16,768]{1,0:T(8,128)(2,1)S(1)}, bf16[16,768]{1,0:T(8,128)(2,1)S(1)}, u32[]{:S(2)}, u32[]{:S(2)}) collective-permute-start(bf16[16,768]{1,0:T(8,128)(2,1)S(1)} %get-tuple-element.380), channel_id=1, source_target_pairs={{0,4},{1,5},{2,6},{3,7},{4,0},{5,1},{6,2},{7,3},{8,12},{9,13},{10,... | collective-permute-start | bytes 73736 | tf_op jit(solution)/shard_map/ppermute | solution.py:587
  65.8 20.4 %collective-permute-start.10 = (bf16[16,96,768]{2,1,0:T(8,128)(2,1)S(1)}, bf16[16,96,768]{2,1,0:T(8,128)(2,1)}, u32[]{:S(2)}, u32[]{:S(2)}) collective-permute-start(bf16[16,96,768]{2,1,0:T(8,128)(2,1)S(1)} %bitcast.299), channel_id=1, source_target_pairs={{0,1},{1,0},{2,3},{3,2},{4,5},{5,4},{6,7},{7,6},{8,9},{9,8},{10,11... | collective-permute-start | bytes 7077896 | tf_op jit(solution)/shard_map/ppermute | solution.py:571
  71.6 33.2 %all-to-all-start.1 = ((bf16[4,4,96,768]{3,2,1,0:T(8,128)(2,1)}), bf16[4,4,96,768]{3,2,1,0:T(8,128)(2,1)}, u32[]{:S(2)}, u32[]{:S(2)}) async-start(bf16[4,4,96,768]{3,2,1,0:T(8,128)(2,1)} %broadcast_in_dim.9), calls=%async_computation.1 | async-start | bytes 4718592 | tf_op jit(solution)/shard_map/all_to_all | solution.py:595
  77.3 24.4 %collective-permute-start.12 = (bf16[192,768]{1,0:T(8,128)(2,1)S(1)}, bf16[192,768]{1,0:T(8,128)(2,1)}, u32[]{:S(2)}, u32[]{:S(2)}) collective-permute-start(bf16[192,768]{1,0:T(8,128)(2,1)S(1)} %slice.444), channel_id=1, source_target_pairs={{0,2},{1,3},{2,4},{3,5},{4,6},{5,7},{6,0},{7,1},{8,10},{9,11},{10,... | collective-permute-start | bytes 884744 | tf_op jit(solution)/shard_map/ppermute | solution.py:587
  79.8 21.8 %collective-permute-start.13 = (bf16[192,768]{1,0:T(8,128)(2,1)S(1)}, bf16[192,768]{1,0:T(8,128)(2,1)}, u32[]{:S(2)}, u32[]{:S(2)}) collective-permute-start(bf16[192,768]{1,0:T(8,128)(2,1)S(1)} %slice.444), channel_id=1, source_target_pairs={{0,4},{1,5},{2,6},{3,7},{4,0},{5,1},{6,2},{7,3},{8,12},{9,13},{10,... | collective-permute-start | bytes 884744 | tf_op jit(solution)/shard_map/ppermute | solution.py:587
  81.4 20.3 %collective-permute-start.14 = (bf16[192,768]{1,0:T(8,128)(2,1)S(1)}, bf16[192,768]{1,0:T(8,128)(2,1)}, u32[]{:S(2)}, u32[]{:S(2)}) collective-permute-start(bf16[192,768]{1,0:T(8,128)(2,1)S(1)} %slice.444), channel_id=1, source_target_pairs={{0,6},{1,7},{2,0},{3,1},{4,2},{5,3},{6,4},{7,5},{8,14},{9,15},{10,... | collective-permute-start | bytes 884744 | tf_op jit(solution)/shard_map/ppermute | solution.py:587
  109.5 27.5 %collective-permute-start.16 = (bf16[96,768]{1,0:T(8,128)(2,1)S(1)}, bf16[96,768]{1,0:T(8,128)(2,1)S(1)}, u32[]{:S(2)}, u32[]{:S(2)}) collective-permute-start(bf16[96,768]{1,0:T(8,128)(2,1)S(1)} %get-tuple-element.213), channel_id=1, source_target_pairs={{0,2},{1,3},{2,4},{3,5},{4,6},{5,7},{6,0},{7,1},{8,10},{9,11},{10,... | collective-permute-start | bytes 442376 | tf_op jit(solution)/shard_map/ppermute | solution.py:587
  112.8 24.2 %collective-permute-start.17 = (bf16[96,768]{1,0:T(8,128)(2,1)S(1)}, bf16[96,768]{1,0:T(8,128)(2,1)S(1)}, u32[]{:S(2)}, u32[]{:S(2)}) collective-permute-start(bf16[96,768]{1,0:T(8,128)(2,1)S(1)} %get-tuple-element.213), channel_id=1, source_target_pairs={{0,4},{1,5},{2,6},{3,7},{4,0},{5,1},{6,2},{7,3},{8,12},{9,13},{10,... | collective-permute-start | bytes 442376 | tf_op jit(solution)/shard_map/ppermute | solution.py:587
  115.9 21.2 %collective-permute-start.18 = (bf16[96,768]{1,0:T(8,128)(2,1)S(1)}, bf16[96,768]{1,0:T(8,128)(2,1)S(1)}, u32[]{:S(2)}, u32[]{:S(2)}) collective-permute-start(bf16[96,768]{1,0:T(8,128)(2,1)S(1)} %get-tuple-element.213), channel_id=1, source_target_pairs={{0,6},{1,7},{2,0},{3,1},{4,2},{5,3},{6,4},{7,5},{8,14},{9,15},{10,... | collective-permute-start | bytes 442376 | tf_op jit(solution)/shard_map/ppermute | solution.py:587
  117.7 19.4 %collective-permute-start.20 = (bf16[8,96,768]{2,1,0:T(8,128)(2,1)S(1)}, bf16[8,96,768]{2,1,0:T(8,128)(2,1)S(1)}, u32[]{:S(2)}, u32[]{:S(2)}) collective-permute-start(bf16[8,96,768]{2,1,0:T(8,128)(2,1)S(1)} %bitcast.308), channel_id=1, source_target_pairs={{0,1},{1,0},{2,3},{3,2},{4,5},{5,4},{6,7},{7,6},{8,9},{9,8},{10,11... | collective-permute-start | bytes 3538952 | tf_op jit(solution)/shard_map/ppermute | solution.py:571
  117.8 19.3 %collective-permute-start.19 = (bf16[4,96,768]{2,1,0:T(8,128)(2,1)S(1)}, bf16[4,96,768]{2,1,0:T(8,128)(2,1)}, u32[]{:S(2)}, u32[]{:S(2)}) collective-permute-start(bf16[4,96,768]{2,1,0:T(8,128)(2,1)S(1)} %pad_maximum_fusion.3.rest_0_), channel_id=1, source_target_pairs={{0,1},{1,0},{2,3},{3,2},{4,5},{5,4},{6,7},{7,6},{8,9},{9,8},{10,11... | collective-permute-start | bytes 1769480 | tf_op jit(solution)/shard_map/ppermute | solution.py:571
  146.0 22.4 %collective-permute-start.23 = (bf16[2,2,96,768]{3,2,1,0:T(8,128)(2,1)}, bf16[2,2,96,768]{3,2,1,0:T(8,128)(2,1)S(1)}, u32[]{:S(2)}, u32[]{:S(2)}) collective-permute-start(bf16[2,2,96,768]{3,2,1,0:T(8,128)(2,1)} %pad_maximum_fusion.4), channel_id=1, source_target_pairs={{0,8},{8,0},{16,24},{24,16},{1,9},{9,1},{17,25},{25,17},{2,10},{10... | collective-permute-start | bytes 1769480 | tf_op jit(solution)/shard_map/ppermute | solution.py:575
  147.5 20.9 %collective-permute-start.24 = (bf16[2,2,96,768]{3,2,1,0:T(8,128)(2,1)S(1)}, bf16[2,2,96,768]{3,2,1,0:T(8,128)(2,1)S(1)}, u32[]{:S(2)}, u32[]{:S(2)}) collective-permute-start(bf16[2,2,96,768]{3,2,1,0:T(8,128)(2,1)S(1)} %pad_maximum_fusion.5), channel_id=1, source_target_pairs={{0,16},{8,24},{16,0},{24,8},{1,17},{9,25},{17,1},{25,9},{2,18},{10... | collective-permute-start | bytes 1769480 | tf_op jit(solution)/shard_map/ppermute | solution.py:579
  169.4 22.3 %collective-permute-start.29 = (bf16[2,96,768]{2,1,0:T(8,128)(2,1)}, bf16[2,96,768]{2,1,0:T(8,128)(2,1)}, u32[]{:S(2)}, u32[]{:S(2)}) collective-permute-start(bf16[2,96,768]{2,1,0:T(8,128)(2,1)} %slice_bitcast_fusion.10), channel_id=1, source_target_pairs={{0,8},{8,0},{16,24},{24,16},{1,9},{9,1},{17,25},{25,17},{2,10},{10... | collective-permute-start | bytes 884744 | tf_op jit(solution)/shard_map/ppermute | solution.py:575
  170.8 20.9 %collective-permute-start.28 = (bf16[2,96,768]{2,1,0:T(8,128)(2,1)}, bf16[2,96,768]{2,1,0:T(8,128)(2,1)}, u32[]{:S(2)}, u32[]{:S(2)}) collective-permute-start(bf16[2,96,768]{2,1,0:T(8,128)(2,1)} %slice_bitcast_fusion.11), channel_id=1, source_target_pairs={{0,16},{8,24},{16,0},{24,8},{1,17},{9,25},{17,1},{25,9},{2,18},{10... | collective-permute-start | bytes 884744 | tf_op jit(solution)/shard_map/ppermute | solution.py:579
  175.4 17.3 %collective-permute-start.27 = (bf16[2,2,96,768]{3,2,1,0:T(8,128)(2,1)S(1)}, bf16[2,2,96,768]{3,2,1,0:T(8,128)(2,1)S(1)}, u32[]{:S(2)}, u32[]{:S(2)}) collective-permute-start(bf16[2,2,96,768]{3,2,1,0:T(8,128)(2,1)S(1)} %pad_maximum_fusion.8), channel_id=1, source_target_pairs={{0,16},{8,24},{16,0},{24,8},{1,17},{9,25},{17,1},{25,9},{2,18},{10... | collective-permute-start | bytes 1769480 | tf_op jit(solution)/shard_map/ppermute | solution.py:579
  194.5 23.1 %collective-permute-start.33 = (bf16[96,768]{1,0:T(8,128)(2,1)}, bf16[96,768]{1,0:T(8,128)(2,1)S(1)}, u32[]{:S(2)}, u32[]{:S(2)}) collective-permute-start(bf16[96,768]{1,0:T(8,128)(2,1)} %get-tuple-element.348), channel_id=1, source_target_pairs={{0,4},{1,5},{2,6},{3,7},{4,0},{5,1},{6,2},{7,3},{8,12},{9,13},{10,... | collective-permute-start | bytes 442376 | tf_op jit(solution)/shard_map/ppermute | solution.py:587
  196.0 21.7 %collective-permute-start.34 = (bf16[96,768]{1,0:T(8,128)(2,1)}, bf16[96,768]{1,0:T(8,128)(2,1)S(1)}, u32[]{:S(2)}, u32[]{:S(2)}) collective-permute-start(bf16[96,768]{1,0:T(8,128)(2,1)} %get-tuple-element.347), channel_id=1, source_target_pairs={{0,6},{1,7},{2,0},{3,1},{4,2},{5,3},{6,4},{7,5},{8,14},{9,15},{10,... | collective-permute-start | bytes 442376 | tf_op jit(solution)/shard_map/ppermute | solution.py:587
  200.7 17.0 %collective-permute-start.32 = (bf16[96,768]{1,0:T(8,128)(2,1)}, bf16[96,768]{1,0:T(8,128)(2,1)S(1)}, u32[]{:S(2)}, u32[]{:S(2)}) collective-permute-start(bf16[96,768]{1,0:T(8,128)(2,1)} %get-tuple-element.349), channel_id=1, source_target_pairs={{0,2},{1,3},{2,4},{3,5},{4,6},{5,7},{6,0},{7,1},{8,10},{9,11},{10,... | collective-permute-start | bytes 442376 | tf_op jit(solution)/shard_map/ppermute | solution.py:587
  200.9 16.8 %collective-permute-start.31 = (bf16[2,96,768]{2,1,0:T(8,128)(2,1)S(1)}, bf16[2,96,768]{2,1,0:T(8,128)(2,1)S(1)}, u32[]{:S(2)}, u32[]{:S(2)}) collective-permute-start(bf16[2,96,768]{2,1,0:T(8,128)(2,1)S(1)} %slice_bitcast_fusion.8), channel_id=1, source_target_pairs={{0,8},{8,0},{16,24},{24,16},{1,9},{9,1},{17,25},{25,17},{2,10},{10... | collective-permute-start | bytes 884744 | tf_op jit(solution)/shard_map/ppermute | solution.py:575
  217.8 19.2 %collective-permute-start.36 = (bf16[96,768]{1,0:T(8,128)(2,1)S(1)}, bf16[96,768]{1,0:T(8,128)(2,1)S(1)}, u32[]{:S(2)}, u32[]{:S(2)}) collective-permute-start(bf16[96,768]{1,0:T(8,128)(2,1)S(1)} %get-tuple-element.344), channel_id=1, source_target_pairs={{0,4},{1,5},{2,6},{3,7},{4,0},{5,1},{6,2},{7,3},{8,12},{9,13},{10,... | collective-permute-start | bytes 442376 | tf_op jit(solution)/shard_map/ppermute | solution.py:587
  218.4 18.6 %collective-permute-start.37 = (bf16[96,768]{1,0:T(8,128)(2,1)S(1)}, bf16[96,768]{1,0:T(8,128)(2,1)S(1)}, u32[]{:S(2)}, u32[]{:S(2)}) collective-permute-start(bf16[96,768]{1,0:T(8,128)(2,1)S(1)} %get-tuple-element.343), channel_id=1, source_target_pairs={{0,6},{1,7},{2,0},{3,1},{4,2},{5,3},{6,4},{7,5},{8,14},{9,15},{10,... | collective-permute-start | bytes 442376 | tf_op jit(solution)/shard_map/ppermute | solution.py:587
  238.5 27.9 %collective-permute-start.41 = (bf16[96,768]{1,0:T(8,128)(2,1)}, bf16[96,768]{1,0:T(8,128)(2,1)}, u32[]{:S(2)}, u32[]{:S(2)}) collective-permute-start(bf16[96,768]{1,0:T(8,128)(2,1)} %add_convert_fusion.32), channel_id=1, source_target_pairs={{0,8},{8,0},{16,24},{24,16},{1,9},{9,1},{17,25},{25,17},{2,10},{10... | collective-permute-start | bytes 442376 | tf_op jit(solution)/shard_map/ppermute | solution.py:575
  238.9 27.5 %collective-permute-start.42 = (bf16[96,768]{1,0:T(8,128)(2,1)}, bf16[96,768]{1,0:T(8,128)(2,1)}, u32[]{:S(2)}, u32[]{:S(2)}) collective-permute-start(bf16[96,768]{1,0:T(8,128)(2,1)} %add_convert_fusion.32), channel_id=1, source_target_pairs={{0,16},{8,24},{16,0},{24,8},{1,17},{9,25},{17,1},{25,9},{2,18},{10... | collective-permute-start | bytes 442376 | tf_op jit(solution)/shard_map/ppermute | solution.py:579
  240.5 25.9 %collective-permute-start.43 = (bf16[96,768]{1,0:T(8,128)(2,1)}, bf16[96,768]{1,0:T(8,128)(2,1)}, u32[]{:S(2)}, u32[]{:S(2)}) collective-permute-start(bf16[96,768]{1,0:T(8,128)(2,1)} %add_convert_fusion.32), channel_id=1, source_target_pairs={{0,24},{8,16},{16,8},{24,0},{1,25},{9,17},{17,9},{25,1},{2,26},{10... | collective-permute-start | bytes 442376 | tf_op jit(solution)/shard_map/ppermute | solution.py:583
  244.9 21.5 %collective-permute-start.39 = (bf16[2,2,96,768]{3,2,1,0:T(8,128)(2,1)S(1)}, bf16[2,2,96,768]{3,2,1,0:T(8,128)(2,1)S(1)}, u32[]{:S(2)}, u32[]{:S(2)}) collective-permute-start(bf16[2,2,96,768]{3,2,1,0:T(8,128)(2,1)S(1)} %pad_maximum_fusion.9), channel_id=1, source_target_pairs={{0,8},{8,0},{16,24},{24,16},{1,9},{9,1},{17,25},{25,17},{2,10},{10... | collective-permute-start | bytes 1769480 | tf_op jit(solution)/shard_map/ppermute | solution.py:575
  245.3 21.1 %collective-permute-start.40 = (bf16[2,2,96,768]{3,2,1,0:T(8,128)(2,1)S(1)}, bf16[2,2,96,768]{3,2,1,0:T(8,128)(2,1)S(1)}, u32[]{:S(2)}, u32[]{:S(2)}) collective-permute-start(bf16[2,2,96,768]{3,2,1,0:T(8,128)(2,1)S(1)} %pad_maximum_fusion.10), channel_id=1, source_target_pairs={{0,16},{8,24},{16,0},{24,8},{1,17},{9,25},{17,1},{25,9},{2,18},{10... | collective-permute-start | bytes 1769480 | tf_op jit(solution)/shard_map/ppermute | solution.py:579
  273.9 17.2 %collective-permute-start.45 = (bf16[2,96,768]{2,1,0:T(8,128)(2,1)S(1)}, bf16[2,96,768]{2,1,0:T(8,128)(2,1)S(1)}, u32[]{:S(2)}, u32[]{:S(2)}) collective-permute-start(bf16[2,96,768]{2,1,0:T(8,128)(2,1)S(1)} %slice_bitcast_fusion.2), channel_id=1, source_target_pairs={{0,8},{8,0},{16,24},{24,16},{1,9},{9,1},{17,25},{25,17},{2,10},{10... | collective-permute-start | bytes 884744 | tf_op jit(solution)/shard_map/ppermute | solution.py:575
  (60 other events, 563.6 us)

commit v4 on v3

--- a/solution.py
+++ b/solution.py
@@ -47,12 +47,20 @@
     return (e - jnp.mean(e, -1, keepdims=True) - xhat * jnp.mean(e * xhat, -1, keepdims=True)) * inv
 
 
-def start_blocks(slots_ref, pieces, layout, w_ref, sem):
+def start_blocks(slots_ref, pieces, layout, w_ref, sem, low=None):
     i = 0
     for piece, first, count in layout:
         for t in range(count):
             slot = slots_ref[i]
-            pltpu.make_async_copy(pieces[piece].at[first + t], w_ref.at[slot], sem.at[slot]).start()
+            if low is None:
+                pltpu.make_async_copy(pieces[piece].at[first + t], w_ref.at[slot], sem.at[slot]).start()
+            else:
+
+                @pl.when(slot >= low)
+                def _(piece=piece, at=first + t, slot=slot):
+                    place = slot - low
+                    pltpu.make_async_copy(pieces[piece].at[at], w_ref.at[place], sem.at[place]).start()
+
             i += 1
 
 
@@ -74,19 +82,30 @@
     return part.reshape(part.shape[0] * part.shape[1], part.shape[2])
 
 
-def put_pair(gpos_ref, at, keep_ref, send_ref, even, odd):
-    idx = gpos_ref[at]
-    side = gpos_ref[16]
-
-    @pl.when(side == 0)
-    def _():
-        keep_ref[idx] = even
-        send_ref[idx] = odd
-
-    @pl.when(side != 0)
-    def _():
-        keep_ref[idx] = odd
-        send_ref[idx] = even
+def block_copies(gpos_ref, spots, buf_ref, even_rows, odd_rows, b, keep_ref, send_ref, sem):
+    for side in range(2):
+        first, second = (keep_ref, send_ref) if side == 0 else (send_ref, keep_ref)
+        copies = []
+        for t, at in enumerate(spots):
+            idx = gpos_ref[at]
+            copies.append(pltpu.make_async_copy(buf_ref.at[pl.ds(even_rows[t], b)], first.at[idx], sem.at[2 * t]))
+            copies.append(pltpu.make_async_copy(buf_ref.at[pl.ds(odd_rows[t], b)], second.at[idx], sem.at[2 * t + 1]))
+        yield side, copies
+
+
+def send_blocks(gpos_ref, spots, buf_ref, even_rows, odd_rows, b, keep_ref, send_ref, sem):
+    core = gpos_ref[16]
+    for side, copies in block_copies(gpos_ref, spots, buf_ref, even_rows, odd_rows, b, keep_ref, send_ref, sem):
+
+        @pl.when(core == side)
+        def _(copies=copies):
+            for cp in copies:
+                cp.start()
+
+
+def drain_blocks(buf_ref, b, sem):
+    for t in range(8):
+        pltpu.make_async_copy(buf_ref.at[pl.ds(0, b)], buf_ref.at[pl.ds(0, b)], sem.at[t]).wait()
 
 
 def half_mask(rows, width):
@@ -131,26 +150,31 @@
         jnp.int32, (length, length), 1
     )
     first = half_mask(length, 2 * HD)
+    masks = []
     for r in range(rb):
         seg = jnp.broadcast_to(seg_ref[pl.ds(step * rb + r, 1), :], (length, length))
         pad = jnp.broadcast_to(pad_ref[pl.ds(step * rb + r, 1), :], (length, length))
-        same = seg == seg.T
-        allowed = same & ((pad == 0.0) | eye)
+        allowed = (seg == seg.T) & ((pad == 0.0) | eye)
         allowed = jnp.where(allowed, 1.0, 0.0)
-        allowed = jnp.concatenate([allowed, allowed], axis=0) > 0.5
-        rows = slice(r * length, (r + 1) * length)
-        for hp in range(width // (2 * HD)):
+        masks.append(jnp.concatenate([allowed, allowed], axis=0) > 0.5)
+    pairs = width // (2 * HD)
+    every = [(r, hp) for r in range(rb) for hp in range(pairs)]
+    for start in range(0, len(every), 12):
+        some = []
+        for r, hp in every[start : start + 12]:
+            rows = slice(r * length, (r + 1) * length)
             lanes = slice(hp * 2 * HD, (hp + 1) * 2 * HD)
-            qs = both(triple_ref[0, rows, lanes], first)
-            s = mm_nt(qs, triple_ref[1, rows, lanes]) * SCALE
-            s = jnp.where(allowed, s, MASKED)
-            top = jnp.max(s, axis=-1, keepdims=True)
-            e = jnp.exp(s - top)
+            s = mm_nt(both(triple_ref[0, rows, lanes], first), triple_ref[1, rows, lanes]) * SCALE
+            some.append((r, hp, rows, lanes, jnp.where(masks[r], s, MASKED)))
+        done = []
+        for r, hp, rows, lanes, s in some:
+            e = jnp.exp(s - jnp.max(s, axis=-1, keepdims=True))
             p = (e / jnp.sum(e, axis=-1, keepdims=True)).astype(bf16)
-            att_ref[r * (width // (2 * HD)) + hp] = p
+            att_ref[r * pairs + hp] = p
+            done.append((rows, lanes, p))
+        for rows, lanes, p in done:
             wide = jnp.concatenate([p[:length], p[length:]], axis=1)
-            o = mm(wide, both(triple_ref[2, rows, lanes], first))
-            attended_ref[rows, lanes] = o.astype(bf16)
+            attended_ref[rows, lanes] = mm(wide, both(triple_ref[2, rows, lanes], first)).astype(bf16)
     branch = mm(attended_ref[...], square(w_ref, 3)) + vec_ref[2:3, :]
     middle = x + branch
     middle_ref[...] = middle
@@ -158,52 +182,77 @@
     n2_ref[...] = (xhat2 * vec_ref[5:6, :] + vec_ref[6:7, :]).astype(bf16)
 
 
-def f2_kernel(layout, chunk, slots, gpos, n2_ref, cot_ref, hb_ref, *rest):
+def gelu_rows(h_ref, bias, active_ref, gp_ref, first, count):
+    sub = 32
+    for m in range(count // sub):
+        at = slice(first + m * sub, first + (m + 1) * sub)
+        v = h_ref[at] + bias
+        v2 = v * v
+        w = GELU_C * v
+        cubic = w * v2
+        t = jnp.tanh(w + cubic * GELU_A)
+        half = 0.5 * t + 0.5
+        active_ref[at] = (v * half).astype(bf16)
+        steep = w + cubic * (3.0 * GELU_A)
+        gp_ref[at] = (half + (half - half * t) * steep).astype(bf16)
+
+
+def f2_kernel(layout, slots, gpos, n2_ref, cot_hbm, hb_ref, *rest):
     n = max(l[0] for l in layout) + 1
     pieces = rest[:n]
-    active_ref, gp_ref, keep_ref, send_ref, w_ref, h_ref, sem = rest[n:]
+    active_ref, gp_ref, keep_ref, send_ref, w_ref, h_ref, g_ref, cot_ref, sem, cot_sem, out_sem = rest[n:]
     j = pl.program_id(0)
+    load = pltpu.make_async_copy(cot_hbm, cot_ref, cot_sem)
 
     @pl.when(j == 0)
     def _():
         start_blocks(slots, pieces, layout, w_ref, sem)
+        load.start()
 
     wait_blocks(w_ref, sem, j * NB, NB)
     tokens, width = n2_ref.shape
-    w = w_ref[pl.ds(j * NB, NB)].reshape(width, width)
+    b = width // NB
     bias = hb_ref[pl.ds(j, 1), :]
-    sub = 32
-    for m in range(tokens // chunk):
-        h_ref[...] = mm(n2_ref[m * chunk : (m + 1) * chunk], w)
-        for s in range(chunk // sub):
-            v = h_ref[s * sub : (s + 1) * sub] + bias
-            v2 = v * v
-            t = jnp.tanh((GELU_C * v) * (1.0 + GELU_A * v2))
-            half = 0.5 * (1.0 + t)
-            at = slice(m * chunk + s * sub, m * chunk + (s + 1) * sub)
-            active_ref[at] = (v * half).astype(bf16)
-            slope = half + (0.5 * GELU_C) * v * (1.0 - t * t) * (1.0 + (3.0 * GELU_A) * v2)
-            gp_ref[at] = slope.astype(bf16)
-    cot = cot_ref[...]
-    hw = width // 2
-    ev = mm_tn(active_ref[:, :hw], cot).astype(bf16)
-    od = mm_tn(active_ref[:, hw:], cot).astype(bf16)
-    b = width // NB
-    for q in range(4):
-        put_pair(gpos, q * 4 + j, keep_ref, send_ref, ev[q * b : (q + 1) * b], od[q * b : (q + 1) * b])
+    slot = lax.rem(j, 2)
+
+    @pl.when(j >= 2)
+    def _():
+        drain_blocks(g_ref.at[slot], b, out_sem.at[slot])
+
+    part = w_ref[pl.ds(j * NB, NB)].reshape(width, width)
+    half = tokens // 2
+    h_ref[:half] = mm(n2_ref[:half], part)
+    h_ref[half:] = mm(n2_ref[half:], part)
+    gelu_rows(h_ref, bias, active_ref, gp_ref, 0, half)
+    gelu_rows(h_ref, bias, active_ref, gp_ref, half, half)
+
+    @pl.when(j == 0)
+    def _():
+        load.wait()
+
+    g_ref[slot] = mm_tn(active_ref[...], cot_ref[...]).astype(bf16)
+    spots = [q * 4 + j for q in range(4)]
+    even_rows, odd_rows = [q * b for q in range(4)], [(4 + q) * b for q in range(4)]
+    send_blocks(gpos, spots, g_ref.at[slot], even_rows, odd_rows, b, keep_ref, send_ref, out_sem.at[slot])
+
+    @pl.when(j == 3)
+    def _():
+        drain_blocks(g_ref.at[0], b, out_sem.at[0])
+        drain_blocks(g_ref.at[1], b, out_sem.at[1])
 
 
 def b1_kernel(layout, chunk, slots, gpos, n2_ref, cot_ref, gp_ref, *rest):
     n = max(l[0] for l in layout) + 1
     pieces = rest[:n]
-    dh_ref, hb_ref, db_ref, keep_ref, send_ref, w_ref, nt_ref, h_ref, sem = rest[n:]
+    dh_ref, hb_ref, db_ref, keep_ref, send_ref, w_ref, h_ref, g_ref, sem, out_sem = rest[n:]
     j = pl.program_id(0)
     tokens, width = n2_ref.shape
+    b = width // NB
+    slot = lax.rem(j, 2)
 
     @pl.when(j == 0)
     def _():
         start_blocks(slots, pieces, layout, w_ref, sem)
-        nt_ref[...] = n2_ref[...].T
         db_ref[...] = jnp.zeros_like(db_ref)
         db_ref[0:1] = jnp.sum(cot_ref[...].astype(f32), axis=0, keepdims=True)
         hb_ref[...] = jnp.zeros_like(hb_ref)
@@ -213,36 +262,55 @@
     sub = 32
     total = jnp.zeros((8, width), f32)
     for m in range(tokens // chunk):
-        h_ref[...] = mm_nt(cot_ref[m * chunk : (m + 1) * chunk], w)
+        h_ref[m] = mm_nt(cot_ref[m * chunk : (m + 1) * chunk], w)
+    for m in range(tokens // chunk):
         for s in range(chunk // sub):
             at = slice(m * chunk + s * sub, m * chunk + (s + 1) * sub)
-            dh = (h_ref[s * sub : (s + 1) * sub] * gp_ref[at].astype(f32)).astype(bf16)
+            dh = (h_ref[m, s * sub : (s + 1) * sub] * gp_ref[at].astype(f32)).astype(bf16)
             dh_ref[at] = dh
             total = total + jnp.sum(dh.astype(f32).reshape(sub // 8, 8, width), axis=0)
     hb_ref[pl.ds(j, 1), :] = jnp.sum(total, axis=0, keepdims=True)
-    b = width // NB
-    dh_all = dh_ref[...]
-    for zf in range(4):
-        g = mm(nt_ref[zf * 2 * b : (zf + 1) * 2 * b], dh_all).astype(bf16)
-        put_pair(gpos, j * 4 + zf, keep_ref, send_ref, g[:b], g[b:])
-
-
-def b2_kernel(layout_a, layout_b, slots_a, slots_b, dh_ref, cot_ref, middle_ref, vec_ref, *rest):
+
+    @pl.when(j >= 2)
+    def _():
+        drain_blocks(g_ref.at[slot], b, out_sem.at[slot])
+
+    g_ref[slot] = mm_tn(n2_ref[...], dh_ref[...]).astype(bf16)
+    spots = [j * 4 + zf for zf in range(4)]
+    even_rows, odd_rows = [2 * zf * b for zf in range(4)], [(2 * zf + 1) * b for zf in range(4)]
+    send_blocks(gpos, spots, g_ref.at[slot], even_rows, odd_rows, b, keep_ref, send_ref, out_sem.at[slot])
+
+    @pl.when(j == 3)
+    def _():
+        drain_blocks(g_ref.at[0], b, out_sem.at[0])
+        drain_blocks(g_ref.at[1], b, out_sem.at[1])
+
+
+def b2_kernel(
+    layout_a, layout_b, rb, length, slots_a, slots_b,
+    dh_ref, cot_ref, middle_ref, vec_ref, triple_ref, att_ref, *rest
+):
     na = max(l[0] for l in layout_a) + 1
     nb = max(l[0] for l in layout_b) + 1
     pieces_a, pieces_b, rest = rest[:na], rest[na : na + nb], rest[na + nb :]
-    dmid_ref, dbr_ref, datt_ref, sums_ref, wa_ref, wb_ref, sem_a, sem_b = rest
+    dmid_ref, dbr_ref, dt_ref, sums_ref, wo_ref, wb_ref, datt_ref, sem_a, sem_b = rest
+    width = cot_ref.shape[1]
+    b = width // NB
 
     @pl.when(pl.program_id(0) == 0)
     def _():
         start_blocks(slots_b, pieces_b, layout_b, wb_ref, sem_b)
-        start_blocks(slots_a, pieces_a, layout_a, wa_ref, sem_a)
+        start_blocks(slots_a, pieces_a, layout_a, wo_ref, sem_a, 3 * NB)
         sums_ref[...] = jnp.zeros_like(sums_ref)
         wait_blocks(wb_ref, sem_b, 0, 32)
-
-    d_n2 = mm_nt(dh_ref[0], square(wb_ref, 0))
+        wait_blocks(wo_ref, sem_a, 0, NB)
+
+    def slope(j):
+        return mm_nt(dh_ref[:, j * width : (j + 1) * width], square(wb_ref, j))
+
+    d_n2 = slope(0)
     for j in range(1, 4):
-        d_n2 = d_n2 + mm_nt(dh_ref[j], square(wb_ref, j))
+        d_n2 = d_n2 + slope(j)
     xhat, inv = moments(middle_ref[...])
     sums_ref[0:1] += jnp.sum(d_n2 * xhat, axis=0, keepdims=True)
     sums_ref[1:2] += jnp.sum(d_n2, axis=0, keepdims=True)
@@ -252,65 +320,70 @@
     dbr_ref[...] = d_branch
     sums_ref[2:3] += jnp.sum(d_branch.astype(f32), axis=0, keepdims=True)
 
-    @pl.when(pl.program_id(0) == 0)
-    def _():
-        wait_blocks(wa_ref, sem_a, 0, 32)
-
-    datt_ref[...] = mm_nt(d_branch, square(wa_ref, 3)).astype(bf16)
-
-
-def b3_kernel(rb, length, datt_ref, triple_ref, att_ref, dt_ref, sums_ref):
-    width = datt_ref.shape[1]
-
-    @pl.when(pl.program_id(0) == 0)
-    def _():
-        sums_ref[...] = jnp.zeros_like(sums_ref)
-
+    datt_ref[...] = mm_nt(d_branch, wo_ref[...].reshape(width, width)).astype(bf16)
     first = half_mask(length, 2 * HD)
     pairs = width // (2 * HD)
-    for r in range(rb):
-        rows = slice(r * length, (r + 1) * length)
-        for hp in range(pairs):
+    every = [(r, hp) for r in range(rb) for hp in range(pairs)]
+    for start in range(0, len(every), 6):
+        some = []
+        for r, hp in every[start : start + 6]:
+            rows = slice(r * length, (r + 1) * length)
             lanes = slice(hp * 2 * HD, (hp + 1) * 2 * HD)
             dos = both(datt_ref[rows, lanes], first)
-            p_low = att_ref[r * pairs + hp]
+            some.append((rows, lanes, dos, att_ref[r * pairs + hp], mm_nt(dos, triple_ref[2, rows, lanes])))
+        slopes = []
+        for rows, lanes, dos, p_low, d_a in some:
+            dt_ref[2, rows, lanes] = mm_tn(p_low, dos).astype(bf16)
             p = p_low.astype(f32)
-            d_a = mm_nt(dos, triple_ref[2, rows, lanes])
             inner = jnp.sum(p * d_a, axis=-1, keepdims=True)
-            ds = (p * (d_a - inner)).astype(bf16)
+            slopes.append((p * (d_a - inner)).astype(bf16))
+        for (rows, lanes, dos, p_low, d_a), ds in zip(some, slopes):
             wide = jnp.concatenate([ds[:length], ds[length:]], axis=1)
             dt_ref[0, rows, lanes] = (mm(wide, both(triple_ref[1, rows, lanes], first)) * SCALE).astype(bf16)
             dt_ref[1, rows, lanes] = (mm_tn(ds, both(triple_ref[0, rows, lanes], first)) * SCALE).astype(bf16)
-            dt_ref[2, rows, lanes] = mm_tn(p_low, dos).astype(bf16)
-    sums_ref[0:1] += jnp.sum(dt_ref[0].astype(f32), axis=0, keepdims=True)
-    sums_ref[1:2] += jnp.sum(dt_ref[2].astype(f32), axis=0, keepdims=True)
-
-
-def ga_kernel(gpos, normed_ref, attended_ref, dt_ref, dbr_ref, keep_ref, send_ref, nt_ref):
+    sums_ref[3:4] += jnp.sum(dt_ref[0].astype(f32), axis=0, keepdims=True)
+    sums_ref[4:5] += jnp.sum(dt_ref[2].astype(f32), axis=0, keepdims=True)
+
+
+def ga_kernel(
+    gpos, normed_ref, dt_ref, attended_hbm, dbr_hbm, keep_ref, send_ref, attended_ref, dbr_ref, g_ref, in_sem, out_sem
+):
     j = pl.program_id(0)
     width = normed_ref.shape[1]
     b = width // NB
+    slot = lax.rem(j, 2)
+    loads = [
+        pltpu.make_async_copy(attended_hbm, attended_ref, in_sem.at[0]),
+        pltpu.make_async_copy(dbr_hbm, dbr_ref, in_sem.at[1]),
+    ]
 
     @pl.when(j == 0)
     def _():
-        nt_ref[...] = normed_ref[...].T
+        for cp in loads:
+            cp.start()
+
+    @pl.when(j >= 2)
+    def _():
+        drain_blocks(g_ref.at[slot], b, out_sem.at[slot])
+
+    @pl.when(j < 3)
+    def _():
+        g_ref[slot] = mm_tn(normed_ref[...], dt_ref[...]).astype(bf16)
 
     @pl.when(j == 3)
     def _():
-        nt_ref[...] = attended_ref[...].T
-
-    def block(rhs):
-        for zf in range(4):
-            g = mm(nt_ref[2 * zf * b : 2 * (zf + 1) * b], rhs).astype(bf16)
-            put_pair(gpos, j * 4 + zf, keep_ref, send_ref, g[:b], g[b:])
-
-    @pl.when(j < 3)
-    def _():
-        block(dt_ref[...])
+        for cp in loads:
+            cp.wait()
+        g_ref[slot] = mm_tn(attended_ref[...], dbr_ref[...]).astype(bf16)
+
+    spots = [j * 4 + zf for zf in range(4)]
+    even_rows, odd_rows = [2 * zf * b for zf in range(4)], [(2 * zf + 1) * b for zf in range(4)]
+    send_blocks(gpos, spots, g_ref.at[slot], even_rows, odd_rows, b, keep_ref, send_ref, out_sem.at[slot])
 
     @pl.when(j == 3)
     def _():
-        block(dbr_ref[...])
+        drain_blocks(g_ref.at[0], b, out_sem.at[0])
+        drain_blocks(g_ref.at[1], b, out_sem.at[1])
 
 
 def b4_kernel(layout, rb, length, slots, tok_ref, emb_ref, dmid_ref, dt_ref, vec_ref, *rest):
@@ -346,9 +419,8 @@
     def _():
         load_blocks(slots, pieces, layout, w_ref, sem)
 
-    acc = mm(act_ref[0], square(w_ref, 0))
-    for j in range(1, 4):
-        acc = acc + mm(act_ref[j], square(w_ref, j))
+    width = middle_ref.shape[1]
+    acc = mm(act_ref[...], w_ref[...].reshape(4 * width, width))
     out_ref[...] = (middle_ref[...] + (acc + vec_ref[7:8, :])).astype(bf16)
 
 
@@ -411,15 +483,15 @@
 def compute_f2(n2, cot, hb, group, gpos):
     n, width = n2.shape
     b = width // NB
-    chunk = 256 if n % 256 == 0 else n
+    column = pl.BlockSpec((n, width), lambda i: (0, i))
     return call(
-        functools.partial(f2_kernel, group.layout, chunk),
+        functools.partial(f2_kernel, group.layout),
         (4,),
-        [smem, smem, full(n2.shape), full(cot.shape), full(hb.shape)] + [hbm] * len(group.arrays),
-        [sds((4, n, width), bf16), sds((4, n, width), bf16), sds((16, b, width), bf16), sds((16, b, width), bf16)],
-        [pl.BlockSpec((None, n, width), lambda i: (i, 0, 0)), pl.BlockSpec((None, n, width), lambda i: (i, 0, 0)),
-         full((16, b, width)), full((16, b, width))],
-        [pltpu.VMEM((32, b, width), bf16), pltpu.VMEM((chunk, width), f32), pltpu.SemaphoreType.DMA((32,))],
+        [smem, smem, full(n2.shape), hbm, full(hb.shape)] + [hbm] * len(group.arrays),
+        [sds((n, 4 * width), bf16), sds((n, 4 * width), bf16), sds((16, b, width), bf16), sds((16, b, width), bf16)],
+        [column, column, hbm, hbm],
+        [pltpu.VMEM((32, b, width), bf16), pltpu.VMEM((n, width), f32), pltpu.VMEM((2, width, width), bf16), pltpu.VMEM((n, width), bf16),
+         pltpu.SemaphoreType.DMA((32,)), pltpu.SemaphoreType.DMA(()), pltpu.SemaphoreType.DMA((2, 8))],
         2 * n * width * width * 8 * 2, 20 << 20,
         [group.slots, gpos, n2, cot, hb, *group.arrays],
     )
@@ -429,56 +501,40 @@
     n, width = n2.shape
     b = width // NB
     chunk = 256 if n % 256 == 0 else n
+    column = pl.BlockSpec((n, width), lambda i: (0, i))
     return call(
         functools.partial(b1_kernel, group.layout, chunk),
         (4,),
-        [smem, smem, full(n2.shape), full(cot.shape), pl.BlockSpec((None, n, width), lambda i: (i, 0, 0))]
-        + [hbm] * len(group.arrays),
-        [sds((4, n, width), bf16), sds((8, width), f32), sds((8, width), f32), sds((16, b, width), bf16), sds((16, b, width), bf16)],
-        [pl.BlockSpec((None, n, width), lambda i: (i, 0, 0)), full((8, width)), full((8, width)),
-         full((16, b, width)), full((16, b, width))],
-        [pltpu.VMEM((32, b, width), bf16), pltpu.VMEM((width, n), bf16), pltpu.VMEM((chunk, width), f32),
-         pltpu.SemaphoreType.DMA((32,))],
+        [smem, smem, full(n2.shape), full(cot.shape), column] + [hbm] * len(group.arrays),
+        [sds((n, 4 * width), bf16), sds((8, width), f32), sds((8, width), f32), sds((16, b, width), bf16), sds((16, b, width), bf16)],
+        [column, full((8, width)), full((8, width)), hbm, hbm],
+        [pltpu.VMEM((32, b, width), bf16), pltpu.VMEM((n // chunk, chunk, width), f32), pltpu.VMEM((2, width, width), bf16),
+         pltpu.SemaphoreType.DMA((32,)), pltpu.SemaphoreType.DMA((2, 8))],
         2 * n * width * width * 8 * 2, 20 << 20,
         [group.slots, gpos, n2, cot, gp, *group.arrays],
     )
 
 
-def compute_b2(dh, cot, middle, vecs, ga, gb):
+def compute_b2(dh, cot, middle, vecs, triple, att, ga, gb, rows, length):
     n, width = cot.shape
-    b = width // NB
-    block = 256 if n % 256 == 0 else n
-    tile = pl.BlockSpec((block, width), lambda i: (i, 0))
-    return call(
-        functools.partial(b2_kernel, ga.layout, gb.layout),
-        (n // block,),
-        [smem, smem, pl.BlockSpec((4, block, width), lambda i: (0, i, 0)), tile, tile, full(vecs.shape)]
-        + [hbm] * (len(ga.arrays) + len(gb.arrays)),
-        [sds((n, width), f32), sds((n, width), bf16), sds((n, width), bf16), sds((8, width), f32)],
-        [tile, tile, tile, full((8, width))],
-        [pltpu.VMEM((32, b, width), bf16), pltpu.VMEM((32, b, width), bf16),
-         pltpu.SemaphoreType.DMA((32,)), pltpu.SemaphoreType.DMA((32,))],
-        2 * n * width * width * 5 * 2, 20 << 20,
-        [ga.slots, gb.slots, dh, cot, middle, vecs, *ga.arrays, *gb.arrays],
-    )
-
-
-def compute_b3(datt, triple, att, rows, length):
-    n, width = datt.shape
     rb = 2 if rows % 2 == 0 else 1
     block = rb * length
     pairs = width // (2 * HD)
+    b = width // NB
+    tile = pl.BlockSpec((block, width), lambda i: (i, 0))
     wide = pl.BlockSpec((3, block, width), lambda i: (0, i, 0))
     return call(
-        functools.partial(b3_kernel, rb, length),
+        functools.partial(b2_kernel, ga.layout, gb.layout, rb, length),
         (rows // rb,),
-        [pl.BlockSpec((block, width), lambda i: (i, 0)), wide,
-         pl.BlockSpec((rb * pairs, 2 * length, length), lambda i: (i, 0, 0))],
-        [sds((3, n, width), bf16), sds((8, width), f32)],
-        [wide, full((8, width))],
-        [],
-        2 * n * width * width * 5 * 2, 20 << 20,
-        [datt, triple, att],
+        [smem, smem, pl.BlockSpec((block, 4 * width), lambda i: (i, 0)), tile, tile, full(vecs.shape), wide,
+         pl.BlockSpec((rb * pairs, 2 * length, length), lambda i: (i, 0, 0))]
+        + [hbm] * (len(ga.arrays) + len(gb.arrays)),
+        [sds((n, width), f32), sds((n, width), bf16), sds((3, n, width), bf16), sds((8, width), f32)],
+        [tile, tile, wide, full((8, width))],
+        [pltpu.VMEM((NB, b, width), bf16), pltpu.VMEM((32, b, width), bf16), pltpu.VMEM((block, width), bf16),
+         pltpu.SemaphoreType.DMA((NB,)), pltpu.SemaphoreType.DMA((32,))],
+        2 * n * width * width * 10, 30 << 20,
+        [ga.slots, gb.slots, dh, cot, middle, vecs, triple, att, *ga.arrays, *gb.arrays],
     )
 
 
@@ -488,13 +544,13 @@
     return call(
         ga_kernel,
         (4,),
-        [smem, full(normed.shape), full(attended.shape),
-         pl.BlockSpec((None, n, width), lambda i: (jnp.minimum(i, 2), 0, 0)), full(dbr.shape)],
+        [smem, full(normed.shape), pl.BlockSpec((None, n, width), lambda i: (jnp.minimum(i, 2), 0, 0)), hbm, hbm],
         [sds((16, b, width), bf16), sds((16, b, width), bf16)],
-        [full((16, b, width)), full((16, b, width))],
-        [pltpu.VMEM((width, n), bf16)],
+        [hbm, hbm],
+        [pltpu.VMEM((n, width), bf16), pltpu.VMEM((n, width), bf16), pltpu.VMEM((2, width, width), bf16),
+         pltpu.SemaphoreType.DMA((2,)), pltpu.SemaphoreType.DMA((2, 8))],
         2 * n * width * width * 4 * 2, 12 << 20,
-        [gpos, normed, attended, dt, dbr],
+        [gpos, normed, dt, attended, dbr],
     )
 
 
@@ -523,7 +579,7 @@
     return call(
         functools.partial(f3_kernel, group.layout),
         (n // block,),
-        [smem, pl.BlockSpec((4, block, width), lambda i: (0, i, 0)), pl.BlockSpec((block, width), lambda i: (i, 0)), full(vecs.shape)]
+        [smem, pl.BlockSpec((block, 4 * width), lambda i: (i, 0)), pl.BlockSpec((block, width), lambda i: (i, 0)), full(vecs.shape)]
         + [hbm] * len(group.arrays),
         sds((n, width), bf16),
         pl.BlockSpec((block, width), lambda i: (i, 0)),
@@ -595,10 +651,13 @@
     return lax.all_to_all(jnp.broadcast_to(v[None], (4,) + v.shape), "dp", 0, 0, tiled=True)
 
 
+quarter_major = [(e, 4 * q, 4) for q in range(4) for e in (0, 1)]
+
+
 def fast_slots(z, c):
     table = []
-    for e in (0, 1):
-        for q in range(4):
+    for q in range(4):
+        for e in (0, 1):
             for k in range(4):
                 table.append(q * NB + 2 * lax.rem(z - k + 4, 4) + (c ^ e))
     return jnp.stack(table).astype(jnp.int32)
@@ -656,15 +715,21 @@
     def one(self):
         self.r1 = [x_swap(self.out[0]), y_swap(self.out[1])]
 
+    def add_two(self):
+        self.on = [add(self.own[i][1], self.r1[i][1]) for i in range(2)]
+
+    def send_two(self):
+        self.r2 = [y_swap(self.on[0]), x_swap(self.on[1])]
+
     def two(self):
-        h = [add(self.own[i], self.r1[i]) for i in range(2)]
-        self.h = h
-        self.r2 = [y_swap(h[0][1]), x_swap(h[1][1])]
+        self.add_two()
+        self.send_two()
 
     def three(self):
-        h3 = [add(self.h[i][0], self.r2[i]) for i in range(2)]
-        h3 = [h3[0][0], h3[0][1], h3[1][0], h3[1][1]]
-        self.r3 = [h3[0]] + [z_shift(h3[k], k) for k in (1, 2, 3)]
+        first = [self.own[i][0].astype(f32) + self.r1[i][0].astype(f32) for i in range(2)]
+        both_halves = [(first[i] + self.r2[i].astype(f32)).astype(bf16) for i in range(2)]
+        self.h3 = [both_halves[k // 2][k % 2] for k in range(4)]
+        self.r3 = [self.h3[0]] + [z_shift(self.h3[k], k) for k in (1, 2, 3)]
 
     def total(self):
         return sum(p.astype(f32) for p in self.r3).astype(bf16)
@@ -745,7 +810,7 @@
         flat = (16, b, width)
         mine_a = mine_a.reshape(flat)
         core_a = core_swap(mine_a)
-        ga = Group([mine_a, core_a], [(0, 0, 16), (1, 0, 16)], slots)
+        ga = Group([mine_a, core_a], quarter_major, slots)
         mine_b = columns(rows_of(got1, 0, b))
         c0 = rows_of(got1, b, b)
         got2 = along_z(tie(down_weight[b : 3 * b], got1))
@@ -756,10 +821,10 @@
     if fast:
         mine_b, n2, got2 = lax.optimization_barrier((mine_b.reshape(flat), n2, got2))
         core_b = core_swap(mine_b)
-        gb = Group([mine_b, core_b], [(0, 0, 16), (1, 0, 16)], slots)
-        n2, c0, got2, own_c3 = tie((n2, c0, got2, down_weight[3 * b :]), core_b)
-        got3 = along_z(own_c3)
+        gb = Group([mine_b, core_b], quarter_major, slots)
+        got3 = along_z(tie(down_weight[3 * b :], got2))
         c12 = jnp.stack(got2).reshape(8, b, width)
+        n2, c12 = tie((n2, c12), core_b)
         c0x, c12x = core_swap(c0), core_swap(c12)
     active, gp, keep_c, send_c = compute_f2(n2, cot, hb, gb, gpos)
     if fast:
@@ -782,47 +847,47 @@
         sb.split()
         dh, sb.out = lax.optimization_barrier((dh, sb.out))
         sb.one()
-    dmid, dbr, datt, sums2 = compute_b2(dh, cot, middle, vecs, ga, gb)
-    if fast:
-        datt, sb.r1, sc.r2 = lax.optimization_barrier((datt, sb.r1, sc.r2))
+    part = width // nf
+    hb_lanes = hb_sum[:4].reshape(nf, 4 * part)
+    marks = jnp.broadcast_to(ids.astype(f32)[None, :], (nf, rows))
+    dmid, dbr, dt, sums2 = compute_b2(dh, cot, middle, vecs, triple, att, ga, gb, rows, length)
+    if fast:
+        dt, sb.r1, sc.r2, hb_lanes, marks = lax.optimization_barrier((dt, sb.r1, sc.r2, hb_lanes, marks))
         sb.two()
         sc.three()
-    dt, sums3 = compute_b3(datt, triple, att, rows, length)
-    if fast:
-        dt, sb.r2, sc.r3 = lax.optimization_barrier((dt, sb.r2, sc.r3))
+    keep_a, send_a = compute_ga(normed, attended, dt, dbr, gpos)
+    if fast:
+        keep_a, send_a, sc.r3, sb.r2, dt = lax.optimization_barrier((keep_a, send_a, sc.r3, sb.r2, dt))
         sb.three()
-        mine_c = sc.total()
-    keep_a, send_a = compute_ga(normed, attended, dt, dbr, gpos)
-    if fast:
-        keep_a, send_a, sb.r3, mine_c, dt = lax.optimization_barrier((keep_a, send_a, sb.r3, mine_c, dt))
         sa = Scatter(keep_a, send_a)
         sa.split()
         dt, sa.out, active = lax.optimization_barrier((dt, sa.out, active))
         sa.one()
-        out_c = spread(mine_c)
+        mine_c = sc.total()
+    input_grad, row_sums, sums4 = compute_b4(tok, emb, dmid, dt, vecs, ga, rows, length)
+    if fast:
+        sa.r1, row_sums, sums4, active, sb.r3, mine_c = lax.optimization_barrier(
+            (sa.r1, row_sums, sums4, active, sb.r3, mine_c)
+        )
+        sa.add_two()
+        row_sums, sums4, active = tie((row_sums, sums4, active), sa.on)
+        result = compute_f3(active, middle, vecs, gc)
+
+    lines = row_sums.shape[0] + 24
+    lanes = jnp.concatenate([row_sums, sums2, sums4, db_sum], axis=0).reshape(lines, nf, part).transpose(1, 0, 2).reshape(nf, lines * part)
+    payload = jnp.concatenate([lanes, hb_lanes, marks], axis=1)
+    nt, end = rows * part, payload.shape[1] - rows
+    if fast:
+        sa.send_two()
+        everyone = jnp.broadcast_to(payload[None], (nd,) + payload.shape).reshape(nd * nf, payload.shape[1])
+        moved = lax.all_to_all(everyone, ("dp", "fsdp"), 0, 0, tiled=True)
         mine_b = sb.total()
-    input_grad, row_sums, sums4 = compute_b4(tok, emb, dmid, dt, vecs, ga, rows, length)
-    if fast:
-        result = compute_f3(active, middle, vecs, gc)
-        sa.r1, row_sums, sums4, result, out_c = lax.optimization_barrier((sa.r1, row_sums, sums4, result, out_c))
-
-    part = width // nf
-    every = [row_sums, sums3, sums2, sums4, db_sum, hb_sum]
-    lines = row_sums.shape[0] + 32
-    marks = jnp.broadcast_to(ids.astype(f32)[None, :], (nf, rows))
-    lanes = jnp.concatenate(every[:5], axis=0).reshape(lines, nf, part).transpose(1, 0, 2).reshape(nf, lines * part)
-    payload = jnp.concatenate([lanes, hb_sum[:4].reshape(nf, 4 * part), marks], axis=1)
-    nt, end = rows * part, payload.shape[1] - rows
-    if fast:
-        sa.two()
-        out_b = spread(mine_b)
-    moved = lax.all_to_all(payload, "fsdp", 0, 0, tiled=True)
-    if fast:
-        sa.r2, moved, out_b = lax.optimization_barrier((sa.r2, moved, out_b))
+        sa.r2, moved, mine_b, mine_c, result = lax.optimization_barrier((sa.r2, moved, mine_b, mine_c, result))
         sa.three()
-        moved = columns(moved).reshape(nd * nf, payload.shape[1])
-        moved, sa.r3 = lax.optimization_barrier((moved, sa.r3))
+        mine_b, mine_c = tie((mine_b, mine_c), sa.h3)
+        out_bc = columns(jnp.concatenate([mine_b, mine_c], axis=0))
     else:
+        moved = lax.all_to_all(payload, "fsdp", 0, 0, tiled=True)
         moved = lax.all_gather(moved, "dp", axis=0, tiled=True)
     table_rows = moved[:, :nt].reshape(nd * nf * rows, part)
     all_ids = moved[:, end:].astype(jnp.int32).reshape(1, nd * nf * rows)
@@ -830,8 +895,10 @@
     if not fast:
         result = compute_f3(active, middle, vecs, gc)
     if fast:
-        out_a, out_b, out_c = (quarters(v, d) for v in (spread(sa.total()), out_b, out_c))
-        down_grad = jnp.concatenate(out_c, axis=0)
+        sa.r3, out_bc, moved = lax.optimization_barrier((sa.r3, out_bc, moved))
+        out_a = quarters(spread(sa.total()), d)
+        out_b = out_bc[:, :b].astype(f32)
+        down_grad = out_bc[:, b:].astype(f32).reshape(4 * b, width)
     else:
         out_b = plain_scatter(keep_b, send_b, False)
         out_a = plain_scatter(keep_a, send_a, False)
@@ -841,8 +908,8 @@
     output_grad = out_a[3]
     all_hot = (steps[:, None] == all_ids).astype(f32)
     table_grad = jnp.dot(all_hot, table_rows, precision=highest)
-    kept = vec_sums[(lines - 32 - rows) * part : (lines - rows) * part].reshape(32, part)
-    v = [kept[i] for i in (0, 1, 10, 16, 17, 8, 9, 24)]
+    kept = vec_sums[(lines - 24 - rows) * part : (lines - rows) * part].reshape(24, part)
+    v = [kept[i] for i in (3, 4, 2, 8, 9, 0, 1, 16)]
     hidden_bias_grad = vec_sums[(lines - rows) * part :]
     shape = tokens.shape
     return (

time: 320 us -> 295 us (0.922)
  Pallas kernels: 116 us -> 96.3 us
  other arithmetic: 21.4 us -> 32.3 us
  waiting for transfers between devices: 62.5 us -> 55.1 us
  local copies, waits for them, and re-layouts: 33.7 us -> 28.9 us
  starting transfers between devices: 81.1 us -> 77.6 us
    pallas_call x8 -> x7, Pallas kernels: 116 us -> 96.3 us  [call(): pl.pallas_call(kernel, grid=grid, in_specs=in_specs, out_shape=out_shape,...]
    ppermute x10, waiting for transfers between devices: 11.9 us -> 5.74 us  [core_swap(): return lax.ppermute(v, 'fsdp', xor_perm(8, 1))]
    convert_element_type x0 -> x3, other arithmetic: none -> 5.18 us  [three(): (first[i] + self.r2[i].astype(f32)).astype(bf16)]
    ppermute x24, starting transfers between devices: 39.8 us -> 44.3 us  [z_shift(): return lax.ppermute(v, 'fsdp', [(i, (i + 2 * k) % 8) for i in range(8)])]
    all_to_all x1, waiting for transfers between devices: 0.01 us -> 4.33 us  [per_device(): moved = lax.all_to_all(everyone, ('dp', 'fsdp'), 0, 0, tiled=True)]
    ppermute x9 -> x7, waiting for transfers between devices: 6.79 us -> 2.64 us  [y_swap(): return lax.ppermute(v, 'dp', xor_perm(4, 2))]
    ppermute x9 -> x7, waiting for transfers between devices: 4.71 us -> 0.77 us  [x_swap(): return lax.ppermute(v, 'dp', xor_perm(4, 1))]
    another operation x6, other arithmetic: 1.98 us -> 5.49 us  [part(): jnp.stack([add(self.keep[dl, ks], self.got[dl, ks]) for dl in deltas])]
  transfers between devices with their start and end apart: 59 -> 53, of which waited for: 15 -> 15; matrix products, arithmetic and copies ran while one was open for 13% -> 15% of each run, Pallas kernels for 37% -> 33%
where the time goes in v4:
time: 295 us; the launch traced here: 294 us
  Pallas kernels  96.3 us (33%)
  starting transfers between devices  77.6 us (26%)
  waiting for transfers between devices  55.1 us (19%)
  other arithmetic  32.3 us (11%)
  local copies, waits for them, and re-layouts  28.9 us (10%)
    pallas_call x7, Pallas kernels, call(): pl.pallas_call(kernel, grid=grid, in_specs=in_specs, out_shape=out_shape,...  96.3 us
    ppermute x24, starting transfers between devices, z_shift(): return lax.ppermute(v, 'fsdp', [(i, (i + 2 * k) % 8) for i in range(8)])  44.3 us
    ppermute x24, waiting for transfers between devices, z_shift(): return lax.ppermute(v, 'fsdp', [(i, (i + 2 * k) % 8) for i in range(8)])  35.4 us
    all_to_all x3, starting transfers between devices, columns(): lax.all_to_all(jnp.broadcast_to(v[None], (4,) + v.shape), 'dp', 0, 0, til...  12.6 us
    convert_element_type x6, other arithmetic, add(): return (u.astype(f32) + v.astype(f32)).astype(bf16)  10.9 us
    ppermute x7, starting transfers between devices, y_swap(): return lax.ppermute(v, 'dp', xor_perm(4, 2))  8.47 us
    ppermute x7, starting transfers between devices, x_swap(): return lax.ppermute(v, 'dp', xor_perm(4, 1))  6.54 us
  transfers between devices with their start and end apart: 53, of which 15 were waited for; matrix products, arithmetic and copies ran while one was open for 15% of the time, Pallas kernels for 33%

profile of v4, /device:TPU:0, one launch (start us, length us, event | category | flops | bytes accessed | tf_op | source)
XLA Modules:
  0.0 293.6 jit_solution(11228305289063951585)
XLA Ops:
  4.9 5.1 %collective-permute-start.2 = (bf16[112,768]{1,0:T(8,128)(2,1)S(1)}, bf16[112,768]{1,0:T(8,128)(2,1)S(1)}, u32[]{:S(2)}, u32[]{:S(2)}) collective-permute-start(bf16[112,768]{1,0:T(8,128)(2,1)S(1)} %pad_maximum_fusion.16), channel_id=1, source_target_pairs={{0,6},{1,7},{2,0},{3,1},{4,2},{5,3},{6,4},{7,5},{8,14},{9,15},{10,... | collective-permute-start | bytes 516104 | tf_op jit(solution)/shard_map/ppermute | solution.py:643
  15.1 9.5 %collective-permute-done.1 = bf16[112,768]{1,0:T(8,128)(2,1)S(1)} collective-permute-done((bf16[112,768]{1,0:T(8,128)(2,1)S(1)}, bf16[112,768]{1,0:T(8,128)(2,1)S(1)}, u32[]{:S(2)}, u32[]{:S(2)}) %collective-permute-start.1) | collective-permute-done | bytes 172064 | tf_op jit(solution)/shard_map/ppermute | solution.py:643
  26.4 4.6 %all-to-all-start = ((bf16[4,4,96,768]{3,2,1,0:T(8,128)(2,1)}), bf16[4,4,96,768]{3,2,1,0:T(8,128)(2,1)S(1)}, u32[]{:S(2)}, u32[]{:S(2)}) async-start(bf16[4,4,96,768]{3,2,1,0:T(8,128)(2,1)} %broadcast_in_dim.10), calls=%async_computation | async-start | bytes 4718592 | tf_op jit(solution)/shard_map/all_to_all | solution.py:651
  32.0 2.0 collective-permute-start.5
  34.0 2.8 collective-permute-start.6
  39.5 15.8 %collective-permute-done.9 = bf16[16,768]{1,0:T(8,128)(2,1)S(1)} collective-permute-done((bf16[16,768]{1,0:T(8,128)(2,1)S(1)}, bf16[16,768]{1,0:T(8,128)(2,1)S(1)}, u32[]{:S(2)}, u32[]{:S(2)}) %collective-permute-start.9) | collective-permute-done | bytes 24608 | tf_op jit(solution)/shard_map/ppermute | solution.py:643
  55.2 8.3 %collective-permute-start.7 = (bf16[16,768]{1,0:T(8,128)(2,1)S(1)}, bf16[16,768]{1,0:T(8,128)(2,1)S(1)}, u32[]{:S(2)}, u32[]{:S(2)}) collective-permute-start(bf16[16,768]{1,0:T(8,128)(2,1)S(1)} %get-tuple-element.368), channel_id=1, source_target_pairs={{0,2},{1,3},{2,4},{3,5},{4,6},{5,7},{6,0},{7,1},{8,10},{9,11},{10,... | collective-permute-start | bytes 73736 | tf_op jit(solution)/shard_map/ppermute | solution.py:643
  69.9 4.5 %all-to-all-start.1 = ((bf16[4,4,96,768]{3,2,1,0:T(8,128)(2,1)}), bf16[4,4,96,768]{3,2,1,0:T(8,128)(2,1)}, u32[]{:S(2)}, u32[]{:S(2)}) async-start(bf16[4,4,96,768]{3,2,1,0:T(8,128)(2,1)} %broadcast_in_dim.11), calls=%async_computation.1 | async-start | bytes 4718592 | tf_op jit(solution)/shard_map/all_to_all | solution.py:651
  75.4 2.4 collective-permute-start.12
  77.8 2.4 collective-permute-start.14
  83.5 14.5 %shard_map.306 = (bf16[768,768]{1,0:T(8,128)(2,1)}, bf16[3,768,768]{2,1,0:T(8,128)(2,1)}, bf16[36,256,128]{2,1,0:T(8,128)(2,1)}, bf16[768,768]{1,0:T(8,128)(2,1)...) custom-call(s32[32]{0:T(128)} %stack.569.slots.slots_a.slots_b, bf16[768,768]{1,0:T(8,128)(2,1)} %bitcast.328, ...), custom_call_target="tpu_custom_call" | custom-call | flops 10871635968 | bytes 20971520 | tf_op jit(solution)/shard_map/pallas_call | solution.py:441
  99.5 3.1 %all-to-all-done.1 = bf16[4,4,96,768]{3,2,1,0:T(8,128)(2,1)} async-done(((bf16[4,4,96,768]{3,2,1,0:T(8,128)(2,1)}), bf16[4,4,96,768]{3,2,1,0:T(8,128)(2,1)}, u32[]{:S(2)}, u32[]{:S(2)}) %all-to-all-start.1) | async-done | bytes 2359328 | tf_op jit(solution)/shard_map/all_to_all | solution.py:651
  103.3 3.7 %collective-permute-start.16 = (bf16[96,768]{1,0:T(8,128)(2,1)S(1)}, bf16[96,768]{1,0:T(8,128)(2,1)S(1)}, u32[]{:S(2)}, u32[]{:S(2)}) collective-permute-start(bf16[96,768]{1,0:T(8,128)(2,1)S(1)} %copy-done.10), channel_id=1, source_target_pairs={{0,2},{1,3},{2,4},{3,5},{4,6},{5,7},{6,0},{7,1},{8,10},{9,11},{10,... | collective-permute-start | bytes 442376 | tf_op jit(solution)/shard_map/ppermute | solution.py:643
  112.2 17.5 %shard_map.307 = (bf16[768,3072]{1,0:T(8,128)(2,1)}, bf16[768,3072]{1,0:T(8,128)(2,1)}, bf16[16,96,768]{2,1,0:T(8,128)(2,1)}, bf16[16,96,768]{2,1,0:T(8,128)(2,1)}) custom-call(s32[32]{0:T(128)} %stack.569.slots.slots_a.slots_b, s32[17]{0:T(128)} %stack.536.gpos, bf16[768,768]{1,0:T(8,128)(2,1)} %get-tuple-element.192.n2_ref, bf16[768,768]{1,0:T(8,128)(2,1)} %bitcast.325, ...), custom_call_target="tpu_custom_call" | custom-call | flops 14495514624 | bytes 20971520 | tf_op jit(solution)/shard_map/pallas_call | solution.py:441
  130.5 5.0 %collective-permute-done.21 = bf16[16,96,768]{2,1,0:T(8,128)(2,1)S(1)} collective-permute-done((bf16[16,96,768]{2,1,0:T(8,128)(2,1)}, bf16[16,96,768]{2,1,0:T(8,128)(2,1)S(1)}, u32[]{:S(2)}, u32[]{:S(2)}) %collective-permute-start.21) | collective-permute-done | bytes 2359328 | tf_op jit(solution)/shard_map/ppermute | solution.py:627
  135.6 2.4 add_convert_fusion.27
  139.7 2.0 collective-permute-start.23
  144.1 17.2 %shard_map.308 = (bf16[768,3072]{1,0:T(8,128)(2,1)}, f32[8,768]{1,0:T(8,128)}, f32[8,768]{1,0:T(8,128)}, bf16[16,96,768]{2,1,0:T(8,128)(2,1)}, bf16[16,96,768]{2,1,0:T(8,128)(2,1)}) custom-call(s32[32]{0:T(128)} %stack.602.slots, s32[17]{0:T(128)} %stack.536.gpos, bf16[768,768]{1,0:T(8,128)(2,1)} %get-tuple-element.192.n2_ref, bf16[768,768]{1,0:T(8,128)(2,1)} %bitcast.326, ...), custom_call_target="tpu_custom_call" | custom-call | flops 14495514624 | bytes 20971520 | tf_op jit(solution)/shard_map/pallas_call | solution.py:441
  162.6 2.3 fusion.9
  172.3 19.3 %shard_map.309 = (f32[768,768]{1,0:T(8,128)}, bf16[768,768]{1,0:T(8,128)(2,1)}, bf16[3,768,768]{2,1,0:T(8,128)(2,1)}, f32[8,768]{1,0:T(8,128)}) custom-call(s32[32]{0:T(128)} %stack.569.slots.slots_a.slots_b, s32[32]{0:T(128)} %stack.569.slots.slots_a.slots_b, bf16[768,3072]{1,0:T(8,128)(2,1)} %get-tuple-element.217.dh_ref, bf16[768,768]{1,0:T(8,128)(2,1)} %bitcast.327, ...), custom_call_target="tpu_custom_call" | custom-call | flops 9059696640 | bytes 31457280 | tf_op jit(solution)/shard_map/pallas_call | solution.py:441
  195.6 1.9 collective-permute-start.31
  198.6 2.2 fusion.11
  202.1 8.2 %shard_map.310 = (bf16[16,96,768]{2,1,0:T(8,128)(2,1)}, bf16[16,96,768]{2,1,0:T(8,128)(2,1)}) custom-call(s32[17]{0:T(128)} %stack.536.gpos, bf16[768,768]{1,0:T(8,128)(2,1)} %get-tuple-element.178.normed_ref, bf16[3,768,768]{2,1,0:T(8,128)(2,1)} %get-tuple-element.243.dt_ref, bf16[768,768]{1,0:T(8,128)(2,1)} %get-tuple-element.228.attended_hbm, ...), custom_call_target="tpu_custom_call" | custom-call | flops 7247757312 | bytes 12582912 | tf_op jit(solution)/shard_map/pallas_call | solution.py:441
  215.6 2.9 collective-permute-start.40
  225.4 9.7 %shard_map.311 = (bf16[768,768]{1,0:T(8,128)(2,1)}, f32[8,768]{1,0:T(8,128)}, f32[8,768]{1,0:T(8,128)}) custom-call(s32[32]{0:T(128)} %stack.569.slots.slots_a.slots_b, bf16[768,768]{1,0:T(8,128)(2,1)} %bitcast.329, f32[6,768]{1,0:T(8,128)} %reshape.466.emb_ref, f32[768,768]{1,0:T(8,128)} %get-tuple-element.242.dmid_ref, ...), custom_call_target="tpu_custom_call" | custom-call | flops 5435817984 | bytes 12582912 | tf_op jit(solution)/shard_map/pallas_call | solution.py:441
  237.0 2.2 fusion.13
  242.9 2.6 all-to-all-start.2
  245.5 9.8 %shard_map.312 = bf16[768,768]{1,0:T(8,128)(2,1)} custom-call(s32[32]{0:T(128)} %stack.602.slots, bf16[768,3072]{1,0:T(8,128)(2,1)} %get-tuple-element.269.act_ref, f32[768,768]{1,0:T(8,128)} %get-tuple-element.218.middle_ref, f32[8,768]{1,0:T(8,128)} %reshape.443.vec_ref, bf16[4,96,768]{2,1,0:T(8,128)(2,1)} %copy-done.13, bf16[8,96,768]{2,1,0:T(8,128)(2,1)} %bitcast.297, ...), custom_call_target="tpu_custom_call" | custom-call | flops 7247757312 | bytes 12582912 | tf_op jit(solution)/shard_map/pallas_call | solution.py:441
  256.1 4.3 %all-to-all-done.2 = f32[32,1,3462]{2,1,0:T(1,128)S(1)} async-done(((f32[32,1,3462]{2,1,0:T(1,128)}), f32[32,1,3462]{2,1,0:T(1,128)S(1)}, u32[]{:S(2)}, u32[]{:S(2)}) %all-to-all-start.2) | async-done | bytes 443168 | tf_op jit(solution)/shard_map/all_to_all | solution.py:883
  263.5 3.5 %all-to-all-start.3 = ((bf16[4,192,768]{2,1,0:T(8,128)(2,1)}), bf16[4,192,768]{2,1,0:T(8,128)(2,1)S(1)}, u32[]{:S(2)}, u32[]{:S(2)}) async-start(bf16[4,192,768]{2,1,0:T(8,128)(2,1)} %broadcast_in_dim.14), calls=%async_computation.3 | async-start | bytes 2359296 | tf_op jit(solution)/shard_map/all_to_all | solution.py:651
  267.6 3.3 %collective-permute-start.45 = (bf16[96,768]{1,0:T(8,128)(2,1)S(1)}, bf16[96,768]{1,0:T(8,128)(2,1)S(1)}, u32[]{:S(2)}, u32[]{:S(2)}) collective-permute-start(bf16[96,768]{1,0:T(8,128)(2,1)S(1)} %get-tuple-element.327), channel_id=1, source_target_pairs={{0,6},{1,7},{2,0},{3,1},{4,2},{5,3},{6,4},{7,5},{8,14},{9,15},{10,... | collective-permute-start | bytes 442376 | tf_op jit(solution)/shard_map/ppermute | solution.py:643
  275.7 5.4 %collective-permute-done.44 = bf16[96,768]{1,0:T(8,128)(2,1)S(1)} collective-permute-done((bf16[96,768]{1,0:T(8,128)(2,1)S(1)}, bf16[96,768]{1,0:T(8,128)(2,1)S(1)}, u32[]{:S(2)}, u32[]{:S(2)}) %collective-permute-start.44) | collective-permute-done | bytes 147488 | tf_op jit(solution)/shard_map/ppermute | solution.py:643
  (270 shorter events, 91.2 us)
Async XLA Ops:
  26.4 38.7 %all-to-all-start = ((bf16[4,4,96,768]{3,2,1,0:T(8,128)(2,1)}), bf16[4,4,96,768]{3,2,1,0:T(8,128)(2,1)S(1)}, u32[]{:S(2)}, u32[]{:S(2)}) async-start(bf16[4,4,96,768]{3,2,1,0:T(8,128)(2,1)} %broadcast_in_dim.10), calls=%async_computation | async-start | bytes 4718592 | tf_op jit(solution)/shard_map/all_to_all | solution.py:651
  31.1 33.9 %collective-permute-start.4 = (bf16[192,768]{1,0:T(8,128)(2,1)S(1)}, bf16[192,768]{1,0:T(8,128)(2,1)}, u32[]{:S(2)}, u32[]{:S(2)}) collective-permute-start(bf16[192,768]{1,0:T(8,128)(2,1)S(1)} %pad_maximum_fusion.13), channel_id=1, source_target_pairs={{0,2},{1,3},{2,4},{3,5},{4,6},{5,7},{6,0},{7,1},{8,10},{9,11},{10,... | collective-permute-start | bytes 884744 | tf_op jit(solution)/shard_map/ppermute | solution.py:643
  32.0 33.0 %collective-permute-start.5 = (bf16[192,768]{1,0:T(8,128)(2,1)S(1)}, bf16[192,768]{1,0:T(8,128)(2,1)}, u32[]{:S(2)}, u32[]{:S(2)}) collective-permute-start(bf16[192,768]{1,0:T(8,128)(2,1)S(1)} %pad_maximum_fusion.13), channel_id=1, source_target_pairs={{0,4},{1,5},{2,6},{3,7},{4,0},{5,1},{6,2},{7,3},{8,12},{9,13},{10,... | collective-permute-start | bytes 884744 | tf_op jit(solution)/shard_map/ppermute | solution.py:643
  34.0 31.0 %collective-permute-start.6 = (bf16[192,768]{1,0:T(8,128)(2,1)S(1)}, bf16[192,768]{1,0:T(8,128)(2,1)}, u32[]{:S(2)}, u32[]{:S(2)}) collective-permute-start(bf16[192,768]{1,0:T(8,128)(2,1)S(1)} %pad_maximum_fusion.13), channel_id=1, source_target_pairs={{0,6},{1,7},{2,0},{3,1},{4,2},{5,3},{6,4},{7,5},{8,14},{9,15},{10,... | collective-permute-start | bytes 884744 | tf_op jit(solution)/shard_map/ppermute | solution.py:643
  38.8 16.4 %collective-permute-start.9 = (bf16[16,768]{1,0:T(8,128)(2,1)S(1)}, bf16[16,768]{1,0:T(8,128)(2,1)S(1)}, u32[]{:S(2)}, u32[]{:S(2)}) collective-permute-start(bf16[16,768]{1,0:T(8,128)(2,1)S(1)} %get-tuple-element.368), channel_id=1, source_target_pairs={{0,6},{1,7},{2,0},{3,1},{4,2},{5,3},{6,4},{7,5},{8,14},{9,15},{10,... | collective-permute-start | bytes 73736 | tf_op jit(solution)/shard_map/ppermute | solution.py:643
  38.8 24.7 %collective-permute-start.8 = (bf16[16,768]{1,0:T(8,128)(2,1)S(1)}, bf16[16,768]{1,0:T(8,128)(2,1)S(1)}, u32[]{:S(2)}, u32[]{:S(2)}) collective-permute-start(bf16[16,768]{1,0:T(8,128)(2,1)S(1)} %get-tuple-element.368), channel_id=1, source_target_pairs={{0,4},{1,5},{2,6},{3,7},{4,0},{5,1},{6,2},{7,3},{8,12},{9,13},{10,... | collective-permute-start | bytes 73736 | tf_op jit(solution)/shard_map/ppermute | solution.py:643
  65.1 18.4 %collective-permute-start.10 = (bf16[16,96,768]{2,1,0:T(8,128)(2,1)S(1)}, bf16[16,96,768]{2,1,0:T(8,128)(2,1)}, u32[]{:S(2)}, u32[]{:S(2)}) collective-permute-start(bf16[16,96,768]{2,1,0:T(8,128)(2,1)S(1)} %bitcast.271), channel_id=1, source_target_pairs={{0,1},{1,0},{2,3},{3,2},{4,5},{5,4},{6,7},{7,6},{8,9},{9,8},{10,11... | collective-permute-start | bytes 7077896 | tf_op jit(solution)/shard_map/ppermute | solution.py:627
  69.9 32.8 %all-to-all-start.1 = ((bf16[4,4,96,768]{3,2,1,0:T(8,128)(2,1)}), bf16[4,4,96,768]{3,2,1,0:T(8,128)(2,1)}, u32[]{:S(2)}, u32[]{:S(2)}) async-start(bf16[4,4,96,768]{3,2,1,0:T(8,128)(2,1)} %broadcast_in_dim.11), calls=%async_computation.1 | async-start | bytes 4718592 | tf_op jit(solution)/shard_map/all_to_all | solution.py:651
  75.4 22.6 %collective-permute-start.12 = (bf16[192,768]{1,0:T(8,128)(2,1)S(1)}, bf16[192,768]{1,0:T(8,128)(2,1)}, u32[]{:S(2)}, u32[]{:S(2)}) collective-permute-start(bf16[192,768]{1,0:T(8,128)(2,1)S(1)} %slice.462), channel_id=1, source_target_pairs={{0,2},{1,3},{2,4},{3,5},{4,6},{5,7},{6,0},{7,1},{8,10},{9,11},{10,... | collective-permute-start | bytes 884744 | tf_op jit(solution)/shard_map/ppermute | solution.py:643
  77.8 21.8 %collective-permute-start.13 = (bf16[192,768]{1,0:T(8,128)(2,1)S(1)}, bf16[192,768]{1,0:T(8,128)(2,1)}, u32[]{:S(2)}, u32[]{:S(2)}) collective-permute-start(bf16[192,768]{1,0:T(8,128)(2,1)S(1)} %slice.462), channel_id=1, source_target_pairs={{0,4},{1,5},{2,6},{3,7},{4,0},{5,1},{6,2},{7,3},{8,12},{9,13},{10,... | collective-permute-start | bytes 884744 | tf_op jit(solution)/shard_map/ppermute | solution.py:643
  77.8 21.8 %collective-permute-start.14 = (bf16[192,768]{1,0:T(8,128)(2,1)S(1)}, bf16[192,768]{1,0:T(8,128)(2,1)}, u32[]{:S(2)}, u32[]{:S(2)}) collective-permute-start(bf16[192,768]{1,0:T(8,128)(2,1)S(1)} %slice.462), channel_id=1, source_target_pairs={{0,6},{1,7},{2,0},{3,1},{4,2},{5,3},{6,4},{7,5},{8,14},{9,15},{10,... | collective-permute-start | bytes 884744 | tf_op jit(solution)/shard_map/ppermute | solution.py:643
  102.7 27.0 %collective-permute-start.19 = (bf16[4,96,768]{2,1,0:T(8,128)(2,1)S(1)}, bf16[4,96,768]{2,1,0:T(8,128)(2,1)}, u32[]{:S(2)}, u32[]{:S(2)}) collective-permute-start(bf16[4,96,768]{2,1,0:T(8,128)(2,1)S(1)} %pad_maximum_fusion.4.rest_0_), channel_id=1, source_target_pairs={{0,1},{1,0},{2,3},{3,2},{4,5},{5,4},{6,7},{7,6},{8,9},{9,8},{10,11... | collective-permute-start | bytes 1769480 | tf_op jit(solution)/shard_map/ppermute | solution.py:627
  103.3 26.4 %collective-permute-start.16 = (bf16[96,768]{1,0:T(8,128)(2,1)S(1)}, bf16[96,768]{1,0:T(8,128)(2,1)S(1)}, u32[]{:S(2)}, u32[]{:S(2)}) collective-permute-start(bf16[96,768]{1,0:T(8,128)(2,1)S(1)} %copy-done.10), channel_id=1, source_target_pairs={{0,2},{1,3},{2,4},{3,5},{4,6},{5,7},{6,0},{7,1},{8,10},{9,11},{10,... | collective-permute-start | bytes 442376 | tf_op jit(solution)/shard_map/ppermute | solution.py:643
  107.0 22.7 %collective-permute-start.17 = (bf16[96,768]{1,0:T(8,128)(2,1)S(1)}, bf16[96,768]{1,0:T(8,128)(2,1)S(1)}, u32[]{:S(2)}, u32[]{:S(2)}) collective-permute-start(bf16[96,768]{1,0:T(8,128)(2,1)S(1)} %copy-done.10), channel_id=1, source_target_pairs={{0,4},{1,5},{2,6},{3,7},{4,0},{5,1},{6,2},{7,3},{8,12},{9,13},{10,... | collective-permute-start | bytes 442376 | tf_op jit(solution)/shard_map/ppermute | solution.py:643
  108.1 21.6 %collective-permute-start.18 = (bf16[96,768]{1,0:T(8,128)(2,1)S(1)}, bf16[96,768]{1,0:T(8,128)(2,1)S(1)}, u32[]{:S(2)}, u32[]{:S(2)}) collective-permute-start(bf16[96,768]{1,0:T(8,128)(2,1)S(1)} %copy-done.10), channel_id=1, source_target_pairs={{0,6},{1,7},{2,0},{3,1},{4,2},{5,3},{6,4},{7,5},{8,14},{9,15},{10,... | collective-permute-start | bytes 442376 | tf_op jit(solution)/shard_map/ppermute | solution.py:643
  112.2 17.6 %collective-permute-start.20 = (bf16[8,96,768]{2,1,0:T(8,128)(2,1)S(1)}, bf16[8,96,768]{2,1,0:T(8,128)(2,1)S(1)}, u32[]{:S(2)}, u32[]{:S(2)}) collective-permute-start(bf16[8,96,768]{2,1,0:T(8,128)(2,1)S(1)} %bitcast.295), channel_id=1, source_target_pairs={{0,1},{1,0},{2,3},{3,2},{4,5},{5,4},{6,7},{7,6},{8,9},{9,8},{10,11... | collective-permute-start | bytes 3538952 | tf_op jit(solution)/shard_map/ppermute | solution.py:627
  139.7 21.6 %collective-permute-start.23 = (bf16[2,2,96,768]{3,2,1,0:T(8,128)(2,1)}, bf16[2,2,96,768]{3,2,1,0:T(8,128)(2,1)S(1)}, u32[]{:S(2)}, u32[]{:S(2)}) collective-permute-start(bf16[2,2,96,768]{3,2,1,0:T(8,128)(2,1)} %pad_maximum_fusion.5), channel_id=1, source_target_pairs={{0,8},{8,0},{16,24},{24,16},{1,9},{9,1},{17,25},{25,17},{2,10},{10... | collective-permute-start | bytes 1769480 | tf_op jit(solution)/shard_map/ppermute | solution.py:631
  141.8 19.5 %collective-permute-start.24 = (bf16[2,2,96,768]{3,2,1,0:T(8,128)(2,1)}, bf16[2,2,96,768]{3,2,1,0:T(8,128)(2,1)}, u32[]{:S(2)}, u32[]{:S(2)}) collective-permute-start(bf16[2,2,96,768]{3,2,1,0:T(8,128)(2,1)} %pad_maximum_fusion.6), channel_id=1, source_target_pairs={{0,16},{8,24},{16,0},{24,8},{1,17},{9,25},{17,1},{25,9},{2,18},{10... | collective-permute-start | bytes 1769480 | tf_op jit(solution)/shard_map/ppermute | solution.py:635
  164.9 26.7 %collective-permute-start.28 = (bf16[2,96,768]{2,1,0:T(8,128)(2,1)}, bf16[2,96,768]{2,1,0:T(8,128)(2,1)S(1)}, u32[]{:S(2)}, u32[]{:S(2)}) collective-permute-start(bf16[2,96,768]{2,1,0:T(8,128)(2,1)} %get-tuple-element.299), channel_id=1, source_target_pairs={{0,16},{8,24},{16,0},{24,8},{1,17},{9,25},{17,1},{25,9},{2,18},{10... | collective-permute-start | bytes 884744 | tf_op jit(solution)/shard_map/ppermute | solution.py:635
  165.5 26.1 %collective-permute-start.29 = (bf16[2,96,768]{2,1,0:T(8,128)(2,1)}, bf16[2,96,768]{2,1,0:T(8,128)(2,1)S(1)}, u32[]{:S(2)}, u32[]{:S(2)}) collective-permute-start(bf16[2,96,768]{2,1,0:T(8,128)(2,1)} %get-tuple-element.298), channel_id=1, source_target_pairs={{0,8},{8,0},{16,24},{24,16},{1,9},{9,1},{17,25},{25,17},{2,10},{10... | collective-permute-start | bytes 884744 | tf_op jit(solution)/shard_map/ppermute | solution.py:631
  169.5 22.1 %collective-permute-start.26 = (bf16[2,2,96,768]{3,2,1,0:T(8,128)(2,1)}, bf16[2,2,96,768]{3,2,1,0:T(8,128)(2,1)S(1)}, u32[]{:S(2)}, u32[]{:S(2)}) collective-permute-start(bf16[2,2,96,768]{3,2,1,0:T(8,128)(2,1)} %pad_maximum_fusion.8), channel_id=1, source_target_pairs={{0,8},{8,0},{16,24},{24,16},{1,9},{9,1},{17,25},{25,17},{2,10},{10... | collective-permute-start | bytes 1769480 | tf_op jit(solution)/shard_map/ppermute | solution.py:631
  170.8 20.8 %collective-permute-start.27 = (bf16[2,2,96,768]{3,2,1,0:T(8,128)(2,1)}, bf16[2,2,96,768]{3,2,1,0:T(8,128)(2,1)}, u32[]{:S(2)}, u32[]{:S(2)}) collective-permute-start(bf16[2,2,96,768]{3,2,1,0:T(8,128)(2,1)} %pad_maximum_fusion.9), channel_id=1, source_target_pairs={{0,16},{8,24},{16,0},{24,8},{1,17},{9,25},{17,1},{25,9},{2,18},{10... | collective-permute-start | bytes 1769480 | tf_op jit(solution)/shard_map/ppermute | solution.py:635
  194.0 16.3 %collective-permute-start.30 = (bf16[96,768]{1,0:T(8,128)(2,1)}, bf16[96,768]{1,0:T(8,128)(2,1)S(1)}, u32[]{:S(2)}, u32[]{:S(2)}) collective-permute-start(bf16[96,768]{1,0:T(8,128)(2,1)} %get-tuple-element.337), channel_id=1, source_target_pairs={{0,2},{1,3},{2,4},{3,5},{4,6},{5,7},{6,0},{7,1},{8,10},{9,11},{10,... | collective-permute-start | bytes 442376 | tf_op jit(solution)/shard_map/ppermute | solution.py:643
  212.9 22.3 %collective-permute-start.38 = (bf16[96,768]{1,0:T(8,128)(2,1)}, bf16[96,768]{1,0:T(8,128)(2,1)S(1)}, u32[]{:S(2)}, u32[]{:S(2)}) collective-permute-start(bf16[96,768]{1,0:T(8,128)(2,1)} %get-tuple-element.333), channel_id=1, source_target_pairs={{0,2},{1,3},{2,4},{3,5},{4,6},{5,7},{6,0},{7,1},{8,10},{9,11},{10,... | collective-permute-start | bytes 442376 | tf_op jit(solution)/shard_map/ppermute | solution.py:643
  214.6 20.6 %collective-permute-start.39 = (bf16[96,768]{1,0:T(8,128)(2,1)}, bf16[96,768]{1,0:T(8,128)(2,1)S(1)}, u32[]{:S(2)}, u32[]{:S(2)}) collective-permute-start(bf16[96,768]{1,0:T(8,128)(2,1)} %get-tuple-element.332), channel_id=1, source_target_pairs={{0,4},{1,5},{2,6},{3,7},{4,0},{5,1},{6,2},{7,3},{8,12},{9,13},{10,... | collective-permute-start | bytes 442376 | tf_op jit(solution)/shard_map/ppermute | solution.py:643
  215.6 19.5 %collective-permute-start.40 = (bf16[96,768]{1,0:T(8,128)(2,1)}, bf16[96,768]{1,0:T(8,128)(2,1)S(1)}, u32[]{:S(2)}, u32[]{:S(2)}) collective-permute-start(bf16[96,768]{1,0:T(8,128)(2,1)} %get-tuple-element.331), channel_id=1, source_target_pairs={{0,6},{1,7},{2,0},{3,1},{4,2},{5,3},{6,4},{7,5},{8,14},{9,15},{10,... | collective-permute-start | bytes 442376 | tf_op jit(solution)/shard_map/ppermute | solution.py:643
  221.0 15.0 %collective-permute-start.36 = (bf16[2,2,96,768]{3,2,1,0:T(8,128)(2,1)}, bf16[2,2,96,768]{3,2,1,0:T(8,128)(2,1)S(1)}, u32[]{:S(2)}, u32[]{:S(2)}) collective-permute-start(bf16[2,2,96,768]{3,2,1,0:T(8,128)(2,1)} %pad_maximum_fusion.10), channel_id=1, source_target_pairs={{0,8},{8,0},{16,24},{24,16},{1,9},{9,1},{17,25},{25,17},{2,10},{10... | collective-permute-start | bytes 1769480 | tf_op jit(solution)/shard_map/ppermute | solution.py:631
  222.2 14.8 %collective-permute-start.37 = (bf16[2,2,96,768]{3,2,1,0:T(8,128)(2,1)}, bf16[2,2,96,768]{3,2,1,0:T(8,128)(2,1)}, u32[]{:S(2)}, u32[]{:S(2)}) collective-permute-start(bf16[2,2,96,768]{3,2,1,0:T(8,128)(2,1)} %pad_maximum_fusion.11), channel_id=1, source_target_pairs={{0,16},{8,24},{16,0},{24,8},{1,17},{9,25},{17,1},{25,9},{2,18},{10... | collective-permute-start | bytes 1769480 | tf_op jit(solution)/shard_map/ppermute | solution.py:635
  239.2 21.3 %collective-permute-start.41 = (bf16[2,96,768]{2,1,0:T(8,128)(2,1)}, bf16[2,96,768]{2,1,0:T(8,128)(2,1)}, u32[]{:S(2)}, u32[]{:S(2)}) collective-permute-start(bf16[2,96,768]{2,1,0:T(8,128)(2,1)} %get-tuple-element.287), channel_id=1, source_target_pairs={{0,16},{8,24},{16,0},{24,8},{1,17},{9,25},{17,1},{25,9},{2,18},{10... | collective-permute-start | bytes 884744 | tf_op jit(solution)/shard_map/ppermute | solution.py:635
  240.6 19.9 %collective-permute-start.42 = (bf16[2,96,768]{2,1,0:T(8,128)(2,1)}, bf16[2,96,768]{2,1,0:T(8,128)(2,1)}, u32[]{:S(2)}, u32[]{:S(2)}) collective-permute-start(bf16[2,96,768]{2,1,0:T(8,128)(2,1)} %get-tuple-element.286), channel_id=1, source_target_pairs={{0,8},{8,0},{16,24},{24,16},{1,9},{9,1},{17,25},{25,17},{2,10},{10... | collective-permute-start | bytes 884744 | tf_op jit(solution)/shard_map/ppermute | solution.py:631
  242.9 17.6 %all-to-all-start.2 = ((f32[32,1,3462]{2,1,0:T(1,128)}), f32[32,1,3462]{2,1,0:T(1,128)S(1)}, u32[]{:S(2)}, u32[]{:S(2)}) async-start(f32[32,1,3462]{2,1,0:T(1,128)} %all_to_all.19), calls=%async_computation.2 | async-start | bytes 917504 | tf_op jit(solution)/shard_map/all_to_all | solution.py:883
  263.5 19.1 %all-to-all-start.3 = ((bf16[4,192,768]{2,1,0:T(8,128)(2,1)}), bf16[4,192,768]{2,1,0:T(8,128)(2,1)S(1)}, u32[]{:S(2)}, u32[]{:S(2)}) async-start(bf16[4,192,768]{2,1,0:T(8,128)(2,1)} %broadcast_in_dim.14), calls=%async_computation.3 | async-start | bytes 2359296 | tf_op jit(solution)/shard_map/all_to_all | solution.py:651
  (56 other events, 519.2 us)

commit v5 on v4

--- a/solution.py
+++ b/solution.py
@@ -15,7 +15,7 @@
 SCALE = 1.0 / math.sqrt(HD)
 GELU_C = math.sqrt(2.0 / math.pi)
 GELU_A = 0.044715
-VMEM_LIMIT = 60 * 1024 * 1024
+VMEM_LIMIT = 55 * 1024 * 1024
 highest = lax.Precision.HIGHEST
 f32 = jnp.float32
 bf16 = jnp.bfloat16
@@ -82,25 +82,22 @@
     return part.reshape(part.shape[0] * part.shape[1], part.shape[2])
 
 
-def block_copies(gpos_ref, spots, buf_ref, even_rows, odd_rows, b, keep_ref, send_ref, sem):
-    for side in range(2):
-        first, second = (keep_ref, send_ref) if side == 0 else (send_ref, keep_ref)
-        copies = []
-        for t, at in enumerate(spots):
-            idx = gpos_ref[at]
-            copies.append(pltpu.make_async_copy(buf_ref.at[pl.ds(even_rows[t], b)], first.at[idx], sem.at[2 * t]))
-            copies.append(pltpu.make_async_copy(buf_ref.at[pl.ds(odd_rows[t], b)], second.at[idx], sem.at[2 * t + 1]))
-        yield side, copies
-
-
-def send_blocks(gpos_ref, spots, buf_ref, even_rows, odd_rows, b, keep_ref, send_ref, sem):
+def send_blocks(gpos_ref, spots, buf_ref, even_rows, odd_rows, b, outs, sem):
     core = gpos_ref[16]
-    for side, copies in block_copies(gpos_ref, spots, buf_ref, even_rows, odd_rows, b, keep_ref, send_ref, sem):
-
-        @pl.when(core == side)
-        def _(copies=copies):
-            for cp in copies:
-                cp.start()
+    keep_out, keep_own, send_out, send_own = outs
+    for t, at in enumerate(spots):
+        place = gpos_ref[at]
+        idx = lax.rem(place, 8)
+        for parity, row in ((0, even_rows[t]), (1, odd_rows[t])):
+            for kept in (True, False):
+                for low in (True, False):
+                    ref = (keep_out if low else keep_own) if kept else (send_out if low else send_own)
+                    mine = (core == parity) if kept else (core != parity)
+                    region = (place < 8) if low else (place >= 8)
+
+                    @pl.when(mine & region)
+                    def _(ref=ref, row=row, idx=idx, which=2 * t + parity):
+                        pltpu.make_async_copy(buf_ref.at[pl.ds(row, b)], ref.at[idx], sem.at[which]).start()
 
 
 def drain_blocks(buf_ref, b, sem):
@@ -200,7 +197,9 @@
 def f2_kernel(layout, slots, gpos, n2_ref, cot_hbm, hb_ref, *rest):
     n = max(l[0] for l in layout) + 1
     pieces = rest[:n]
-    active_ref, gp_ref, keep_ref, send_ref, w_ref, h_ref, g_ref, cot_ref, sem, cot_sem, out_sem = rest[n:]
+    active_ref, gp_ref = rest[n : n + 2]
+    outs = rest[n + 2 : n + 6]
+    w_ref, h_ref, g_ref, cot_ref, sem, cot_sem, out_sem = rest[n + 6 :]
     j = pl.program_id(0)
     load = pltpu.make_async_copy(cot_hbm, cot_ref, cot_sem)
 
@@ -233,7 +232,7 @@
     g_ref[slot] = mm_tn(active_ref[...], cot_ref[...]).astype(bf16)
     spots = [q * 4 + j for q in range(4)]
     even_rows, odd_rows = [q * b for q in range(4)], [(4 + q) * b for q in range(4)]
-    send_blocks(gpos, spots, g_ref.at[slot], even_rows, odd_rows, b, keep_ref, send_ref, out_sem.at[slot])
+    send_blocks(gpos, spots, g_ref.at[slot], even_rows, odd_rows, b, outs, out_sem.at[slot])
 
     @pl.when(j == 3)
     def _():
@@ -244,7 +243,9 @@
 def b1_kernel(layout, chunk, slots, gpos, n2_ref, cot_ref, gp_ref, *rest):
     n = max(l[0] for l in layout) + 1
     pieces = rest[:n]
-    dh_ref, hb_ref, db_ref, keep_ref, send_ref, w_ref, h_ref, g_ref, sem, out_sem = rest[n:]
+    dh_ref, hb_ref, db_ref = rest[n : n + 3]
+    outs = rest[n + 3 : n + 7]
+    w_ref, h_ref, g_ref, sem, out_sem = rest[n + 7 :]
     j = pl.program_id(0)
     tokens, width = n2_ref.shape
     b = width // NB
@@ -278,7 +279,7 @@
     g_ref[slot] = mm_tn(n2_ref[...], dh_ref[...]).astype(bf16)
     spots = [j * 4 + zf for zf in range(4)]
     even_rows, odd_rows = [2 * zf * b for zf in range(4)], [(2 * zf + 1) * b for zf in range(4)]
-    send_blocks(gpos, spots, g_ref.at[slot], even_rows, odd_rows, b, keep_ref, send_ref, out_sem.at[slot])
+    send_blocks(gpos, spots, g_ref.at[slot], even_rows, odd_rows, b, outs, out_sem.at[slot])
 
     @pl.when(j == 3)
     def _():
@@ -345,9 +346,9 @@
     sums_ref[4:5] += jnp.sum(dt_ref[2].astype(f32), axis=0, keepdims=True)
 
 
-def ga_kernel(
-    gpos, normed_ref, dt_ref, attended_hbm, dbr_hbm, keep_ref, send_ref, attended_ref, dbr_ref, g_ref, in_sem, out_sem
-):
+def ga_kernel(gpos, normed_ref, dt_ref, attended_hbm, dbr_hbm, *rest):
+    outs = rest[:4]
+    attended_ref, dbr_ref, g_ref, in_sem, out_sem = rest[4:]
     j = pl.program_id(0)
     width = normed_ref.shape[1]
     b = width // NB
@@ -378,7 +379,7 @@
 
     spots = [j * 4 + zf for zf in range(4)]
     even_rows, odd_rows = [2 * zf * b for zf in range(4)], [(2 * zf + 1) * b for zf in range(4)]
-    send_blocks(gpos, spots, g_ref.at[slot], even_rows, odd_rows, b, keep_ref, send_ref, out_sem.at[slot])
+    send_blocks(gpos, spots, g_ref.at[slot], even_rows, odd_rows, b, outs, out_sem.at[slot])
 
     @pl.when(j == 3)
     def _():
@@ -386,28 +387,30 @@
         drain_blocks(g_ref.at[1], b, out_sem.at[1])
 
 
-def b4_kernel(layout, rb, length, slots, tok_ref, emb_ref, dmid_ref, dt_ref, vec_ref, *rest):
+def b4_kernel(layout, rb, length, slots, tok_ref, emb_ref, dmid_ref, dt_ref, vec_ref, sums2_ref, db_ref, *rest):
     n = max(l[0] for l in layout) + 1
     pieces = rest[:n]
-    ig_ref, rs_ref, sums_ref, w_ref, sem = rest[n:]
+    ig_ref, sums_ref, w_ref, sem = rest[n:]
+    base = pl.num_programs(0) * rb
     step = pl.program_id(0)
 
     @pl.when(step == 0)
     def _():
         load_blocks(slots, pieces, layout, w_ref, sem)
         sums_ref[...] = jnp.zeros_like(sums_ref)
-        rs_ref[...] = jnp.zeros_like(rs_ref)
+        sums_ref[pl.ds(base + 2, 5)] = sums2_ref[0:5]
+        sums_ref[pl.ds(base + 7, 1)] = db_ref[0:1]
 
     d_n = mm_nt(dt_ref[0], square(w_ref, 0))
     for q in range(1, 3):
         d_n = d_n + mm_nt(dt_ref[q], square(w_ref, q))
     xhat, inv = moments(residual_of(tok_ref, emb_ref, step, rb, length))
-    sums_ref[0:1] += jnp.sum(d_n * xhat, axis=0, keepdims=True)
-    sums_ref[1:2] += jnp.sum(d_n, axis=0, keepdims=True)
+    sums_ref[pl.ds(base, 1)] += jnp.sum(d_n * xhat, axis=0, keepdims=True)
+    sums_ref[pl.ds(base + 1, 1)] += jnp.sum(d_n, axis=0, keepdims=True)
     d_start = dmid_ref[...] + ln_back(d_n * vec_ref[3:4, :], xhat, inv)
     ig_ref[...] = d_start.astype(bf16)
     for r in range(rb):
-        rs_ref[pl.ds(step * rb + r, 1), :] = jnp.sum(d_start[r * length : (r + 1) * length], axis=0, keepdims=True)
+        sums_ref[pl.ds(step * rb + r, 1), :] = jnp.sum(d_start[r * length : (r + 1) * length], axis=0, keepdims=True)
 
 
 def f3_kernel(layout, slots, act_ref, middle_ref, vec_ref, *rest):
@@ -488,8 +491,8 @@
         functools.partial(f2_kernel, group.layout),
         (4,),
         [smem, smem, full(n2.shape), hbm, full(hb.shape)] + [hbm] * len(group.arrays),
-        [sds((n, 4 * width), bf16), sds((n, 4 * width), bf16), sds((16, b, width), bf16), sds((16, b, width), bf16)],
-        [column, column, hbm, hbm],
+        [sds((n, 4 * width), bf16), sds((n, 4 * width), bf16), *[sds((8, b, width), bf16)] * 4],
+        [column, column, hbm, hbm, hbm, hbm],
         [pltpu.VMEM((32, b, width), bf16), pltpu.VMEM((n, width), f32), pltpu.VMEM((2, width, width), bf16), pltpu.VMEM((n, width), bf16),
          pltpu.SemaphoreType.DMA((32,)), pltpu.SemaphoreType.DMA(()), pltpu.SemaphoreType.DMA((2, 8))],
         2 * n * width * width * 8 * 2, 20 << 20,
@@ -506,8 +509,8 @@
         functools.partial(b1_kernel, group.layout, chunk),
         (4,),
         [smem, smem, full(n2.shape), full(cot.shape), column] + [hbm] * len(group.arrays),
-        [sds((n, 4 * width), bf16), sds((8, width), f32), sds((8, width), f32), sds((16, b, width), bf16), sds((16, b, width), bf16)],
-        [column, full((8, width)), full((8, width)), hbm, hbm],
+        [sds((n, 4 * width), bf16), sds((4, width), f32), sds((8, width), f32), *[sds((8, b, width), bf16)] * 4],
+        [column, full((4, width)), full((8, width)), hbm, hbm, hbm, hbm],
         [pltpu.VMEM((32, b, width), bf16), pltpu.VMEM((n // chunk, chunk, width), f32), pltpu.VMEM((2, width, width), bf16),
          pltpu.SemaphoreType.DMA((32,)), pltpu.SemaphoreType.DMA((2, 8))],
         2 * n * width * width * 8 * 2, 20 << 20,
@@ -545,8 +548,8 @@
         ga_kernel,
         (4,),
         [smem, full(normed.shape), pl.BlockSpec((None, n, width), lambda i: (jnp.minimum(i, 2), 0, 0)), hbm, hbm],
-        [sds((16, b, width), bf16), sds((16, b, width), bf16)],
-        [hbm, hbm],
+        [*[sds((8, b, width), bf16)] * 4],
+        [hbm, hbm, hbm, hbm],
         [pltpu.VMEM((n, width), bf16), pltpu.VMEM((n, width), bf16), pltpu.VMEM((2, width, width), bf16),
          pltpu.SemaphoreType.DMA((2,)), pltpu.SemaphoreType.DMA((2, 8))],
         2 * n * width * width * 4 * 2, 12 << 20,
@@ -554,21 +557,23 @@
     )
 
 
-def compute_b4(tok, emb, dmid, dt, vecs, group, rows, length):
+def compute_b4(tok, emb, dmid, dt, vecs, sums2, db_sum, group, rows, length):
     n, width = tok.shape
     rb = 2 if rows % 2 == 0 else 1
     block = rb * length
     b = width // NB
+    lines = 8 * ((rows + 8 + 7) // 8)
     return call(
         functools.partial(b4_kernel, group.layout, rb, length),
         (rows // rb,),
         [smem, pl.BlockSpec((block, width), lambda i: (i, 0)), full(emb.shape), pl.BlockSpec((block, width), lambda i: (i, 0)),
-         pl.BlockSpec((3, block, width), lambda i: (0, i, 0)), full(vecs.shape)] + [hbm] * len(group.arrays),
-        [sds((n, width), bf16), sds((8 * ((rows + 7) // 8), width), f32), sds((8, width), f32)],
-        [pl.BlockSpec((block, width), lambda i: (i, 0)), full((8 * ((rows + 7) // 8), width)), full((8, width))],
+         pl.BlockSpec((3, block, width), lambda i: (0, i, 0)), full(vecs.shape), full(sums2.shape), full(db_sum.shape)]
+        + [hbm] * len(group.arrays),
+        [sds((n, width), bf16), sds((lines, width), f32)],
+        [pl.BlockSpec((block, width), lambda i: (i, 0)), full((lines, width))],
         [pltpu.VMEM((32, b, width), bf16), pltpu.SemaphoreType.DMA((32,))],
         2 * n * width * width * 3 * 2, 12 << 20,
-        [group.slots, tok, emb, dmid, dt, vecs, *group.arrays],
+        [group.slots, tok, emb, dmid, dt, vecs, sums2, db_sum, *group.arrays],
     )
 
 
@@ -603,16 +608,15 @@
     return group(a), group(b), group(c), jnp.stack(vec[:8]).astype(f32), vec[8].astype(f32).reshape(4, width)
 
 
-def plain_scatter(keep, send, rows_first):
-    b, width = keep.shape[1:]
-    g = jnp.stack([keep.reshape(4, 4, b, width), send.reshape(4, 4, b, width)], axis=2)
+def plain_scatter(keep_out, keep_own, send_out, send_own, rows_first=False):
+    b, width = keep_out.shape[1:]
+    g = [jnp.concatenate(v, axis=0).reshape(4, 4, b, width) for v in ((keep_out, keep_own), (send_out, send_own))]
+    g = jnp.stack(g, axis=2).astype(f32)
     if rows_first:
         g = g.transpose(1, 2, 0, 3, 4).reshape(32 * b, width)
-        s = lax.psum_scatter(g.astype(f32), "fsdp", scatter_dimension=0, tiled=True)
-        return lax.psum(s, "dp")
+        return lax.psum(lax.psum_scatter(g, "fsdp", scatter_dimension=0, tiled=True), "dp")
     g = g.reshape(4, NB * b, width)
-    s = lax.psum_scatter(g.astype(f32), "fsdp", scatter_dimension=1, tiled=True)
-    return lax.psum(s, "dp")
+    return lax.psum(lax.psum_scatter(g, "fsdp", scatter_dimension=1, tiled=True), "dp")
 
 
 def pick(stacked, i):
@@ -652,6 +656,12 @@
 
 
 quarter_major = [(e, 4 * q, 4) for q in range(4) for e in (0, 1)]
+
+
+def grad_place(delta, k):
+    half, high, low = k // 2, delta // 2, lax.rem(delta, 2)
+    leaves, other = jnp.where(half == 0, low, high), jnp.where(half == 0, high, low)
+    return (1 - leaves) * 8 + half * 4 + other * 2 + lax.rem(k, 2)
 
 
 def fast_slots(z, c):
@@ -694,29 +704,24 @@
     return vecs, hb, ids
 
 
-def add(u, v):
-    return (u.astype(f32) + v.astype(f32)).astype(bf16)
+def plus(*values):
+    return sum(v.astype(f32) for v in values).astype(bf16)
 
 
 class Scatter:
-    def __init__(self, keep, send):
-        b, width = keep.shape[1:]
-        self.keep = keep.reshape(4, 4, b, width)
-        self.got = core_swap(send).reshape(4, 4, b, width)
+    def __init__(self, keep_out, keep_own, send_out, send_own):
+        self.keep = (keep_out, keep_own)
+        self.got = (core_swap(send_out), core_swap(send_own))
 
     def split(self):
-        def part(deltas, half):
-            ks = slice(2 * half, 2 * half + 2)
-            return jnp.stack([add(self.keep[dl, ks], self.got[dl, ks]) for dl in deltas])
-
-        self.out = [part((1, 3), 0), part((2, 3), 1)]
-        self.own = [part((0, 2), 0), part((0, 1), 1)]
+        self.out = [plus(self.keep[0][4 * i : 4 * i + 4], self.got[0][4 * i : 4 * i + 4]) for i in range(2)]
 
     def one(self):
         self.r1 = [x_swap(self.out[0]), y_swap(self.out[1])]
 
     def add_two(self):
-        self.on = [add(self.own[i][1], self.r1[i][1]) for i in range(2)]
+        at = [slice(4 * i + 2, 4 * i + 4) for i in range(2)]
+        self.on = [plus(self.keep[1][at[i]], self.got[1][at[i]], self.r1[i][2:]) for i in range(2)]
 
     def send_two(self):
         self.r2 = [y_swap(self.on[0]), x_swap(self.on[1])]
@@ -726,9 +731,9 @@
         self.send_two()
 
     def three(self):
-        first = [self.own[i][0].astype(f32) + self.r1[i][0].astype(f32) for i in range(2)]
-        both_halves = [(first[i] + self.r2[i].astype(f32)).astype(bf16) for i in range(2)]
-        self.h3 = [both_halves[k // 2][k % 2] for k in range(4)]
+        at = [slice(4 * i, 4 * i + 2) for i in range(2)]
+        halves = [plus(self.keep[1][at[i]], self.got[1][at[i]], self.r1[i][:2], self.r2[i]) for i in range(2)]
+        self.h3 = [halves[k // 2][k % 2] for k in range(4)]
         self.r3 = [self.h3[0]] + [z_shift(self.h3[k], k) for k in (1, 2, 3)]
 
     def total(self):
@@ -762,6 +767,7 @@
     pad = padding.reshape(rows, length).astype(f32)
 
     ids = timesteps.reshape(rows)
+    marks = jnp.broadcast_to(ids.astype(f32)[None, :], (nf, rows))
     steps = lax.iota(jnp.int32, step_table.shape[0])
     q4 = [triple_weight[:, i * width : (i + 1) * width] for i in range(3)] + [output_weight]
     h4 = [hidden_weight[:, i * width : (i + 1) * width] for i in range(4)]
@@ -780,7 +786,7 @@
         mine_a = columns(s0)
         got1 = along_z(tie(jnp.concatenate([own_b, down_weight[:b]], axis=0), got))
         vecs, hb, here = fast_small(shard_order(e0, core_swap(e0), z, c), width, rows)
-        gpos = [(q ^ d) * 4 + lax.rem(zf - z + 4, 4) for q in range(4) for zf in range(4)] + [c]
+        gpos = [grad_place(q ^ d, lax.rem(zf - z + 4, 4)) for q in range(4) for zf in range(4)] + [c]
         gpos = jnp.stack(gpos).astype(jnp.int32)
         slots = fast_slots(z, c)
         slots_c = down_slots(z, c, ((0,), (1, 2), (3,)))
@@ -794,8 +800,8 @@
     onehot = (here.reshape(nf * rows)[:, None] == steps[None, :]).astype(bf16)
     looked = jnp.dot(onehot, step_table, preferred_element_type=f32).astype(bf16)
     if fast:
-        looked, seg, pad, vecs, hb, gpos, slots, slots_c = lax.optimization_barrier(
-            (looked.reshape(rows, width), seg, pad, vecs, hb, gpos, slots, slots_c)
+        looked, seg, pad, vecs, hb, gpos, slots, slots_c, marks = lax.optimization_barrier(
+            (looked.reshape(rows, width), seg, pad, vecs, hb, gpos, slots, slots_c, marks)
         )
         sent = jnp.pad(looked, ((0, 16 - rows), (0, 0)))
         got_e = jnp.stack(along_z(sent))
@@ -812,7 +818,6 @@
         core_a = core_swap(mine_a)
         ga = Group([mine_a, core_a], quarter_major, slots)
         mine_b = columns(rows_of(got1, 0, b))
-        c0 = rows_of(got1, b, b)
         got2 = along_z(tie(down_weight[b : 3 * b], got1))
         tok_in = tie(tok, (core_a, emb))
     else:
@@ -823,58 +828,60 @@
         core_b = core_swap(mine_b)
         gb = Group([mine_b, core_b], quarter_major, slots)
         got3 = along_z(tie(down_weight[3 * b :], got2))
+        c0 = rows_of(tie(got1, n2), b, b)
         c12 = jnp.stack(got2).reshape(8, b, width)
         n2, c12 = tie((n2, c12), core_b)
         c0x, c12x = core_swap(c0), core_swap(c12)
-    active, gp, keep_c, send_c = compute_f2(n2, cot, hb, gb, gpos)
-    if fast:
-        got3, c0x, c12x, gp, keep_c, send_c = lax.optimization_barrier((got3, c0x, c12x, gp, keep_c, send_c))
+    active, gp, *grads_c = compute_f2(n2, cot, hb, gb, gpos)
+    if fast:
+        got3, c0x, c12x, gp, grads_c = lax.optimization_barrier((got3, c0x, c12x, gp, grads_c))
         c3 = jnp.stack(got3)
         gc = Group(
             [c0, c12, c3, c0x, c12x, core_swap(c3)],
             [(0, 0, 4), (1, 0, 8), (2, 0, 4), (3, 0, 4), (4, 0, 8), (5, 0, 4)],
             slots_c,
         )
-        sc = Scatter(keep_c, send_c)
+        sc = Scatter(*grads_c)
         sc.split()
         gp, sc.out = lax.optimization_barrier((gp, sc.out))
         sc.one()
-    dh, hb_sum, db_sum, keep_b, send_b = compute_b1(n2, cot, gp, gc, gpos)
-    if fast:
-        dh, keep_b, send_b, sc.r1 = lax.optimization_barrier((dh, keep_b, send_b, sc.r1))
+    dh, hb_sum, db_sum, *grads_b = compute_b1(n2, cot, gp, gc, gpos)
+    if fast:
+        dh, grads_b, sc.r1, sc.got = lax.optimization_barrier((dh, grads_b, sc.r1, sc.got))
         sc.two()
-        sb = Scatter(keep_b, send_b)
+        sb = Scatter(*grads_b)
         sb.split()
         dh, sb.out = lax.optimization_barrier((dh, sb.out))
         sb.one()
     part = width // nf
-    hb_lanes = hb_sum[:4].reshape(nf, 4 * part)
-    marks = jnp.broadcast_to(ids.astype(f32)[None, :], (nf, rows))
     dmid, dbr, dt, sums2 = compute_b2(dh, cot, middle, vecs, triple, att, ga, gb, rows, length)
     if fast:
-        dt, sb.r1, sc.r2, hb_lanes, marks = lax.optimization_barrier((dt, sb.r1, sc.r2, hb_lanes, marks))
+        dt, sb.r1, sc.r2, hb_sum = lax.optimization_barrier((dt, sb.r1, sc.r2, hb_sum))
         sb.two()
         sc.three()
-    keep_a, send_a = compute_ga(normed, attended, dt, dbr, gpos)
-    if fast:
-        keep_a, send_a, sc.r3, sb.r2, dt = lax.optimization_barrier((keep_a, send_a, sc.r3, sb.r2, dt))
+    grads_a = compute_ga(normed, attended, dt, dbr, gpos)
+    if fast:
+        grads_a, sc.r3, sb.r2, dt = lax.optimization_barrier((grads_a, sc.r3, sb.r2, dt))
         sb.three()
-        sa = Scatter(keep_a, send_a)
+        sa = Scatter(*grads_a)
         sa.split()
         dt, sa.out, active = lax.optimization_barrier((dt, sa.out, active))
         sa.one()
         mine_c = sc.total()
-    input_grad, row_sums, sums4 = compute_b4(tok, emb, dmid, dt, vecs, ga, rows, length)
-    if fast:
-        sa.r1, row_sums, sums4, active, sb.r3, mine_c = lax.optimization_barrier(
-            (sa.r1, row_sums, sums4, active, sb.r3, mine_c)
+    input_grad, sums = compute_b4(tok, emb, dmid, dt, vecs, sums2, db_sum, ga, rows, length)
+    if fast:
+        hb_lanes = tie(hb_sum, sa.out).reshape(nf, 4 * part)
+        sa.r1, sums, active, mine_c, hb_lanes, sb.r3 = lax.optimization_barrier(
+            (sa.r1, sums, active, mine_c, hb_lanes, sb.r3)
         )
         sa.add_two()
-        row_sums, sums4, active = tie((row_sums, sums4, active), sa.on)
+        sums, active = tie((sums, active), sa.on)
         result = compute_f3(active, middle, vecs, gc)
 
-    lines = row_sums.shape[0] + 24
-    lanes = jnp.concatenate([row_sums, sums2, sums4, db_sum], axis=0).reshape(lines, nf, part).transpose(1, 0, 2).reshape(nf, lines * part)
+    lines = sums.shape[0]
+    if not fast:
+        hb_lanes = hb_sum.reshape(nf, 4 * part)
+    lanes = sums.reshape(lines, nf, part).transpose(1, 0, 2).reshape(nf, lines * part)
     payload = jnp.concatenate([lanes, hb_lanes, marks], axis=1)
     nt, end = rows * part, payload.shape[1] - rows
     if fast:
@@ -900,16 +907,15 @@
         out_b = out_bc[:, :b].astype(f32)
         down_grad = out_bc[:, b:].astype(f32).reshape(4 * b, width)
     else:
-        out_b = plain_scatter(keep_b, send_b, False)
-        out_a = plain_scatter(keep_a, send_a, False)
-        down_grad = plain_scatter(keep_c, send_c, True)
+        out_b = plain_scatter(*grads_b)
+        out_a = plain_scatter(*grads_a)
+        down_grad = plain_scatter(*grads_c, rows_first=True)
     hidden_grad = jnp.concatenate([out_b[i] for i in range(4)], axis=1)
     triple_grad = jnp.concatenate([out_a[i] for i in range(3)], axis=1)
     output_grad = out_a[3]
     all_hot = (steps[:, None] == all_ids).astype(f32)
     table_grad = jnp.dot(all_hot, table_rows, precision=highest)
-    kept = vec_sums[(lines - 24 - rows) * part : (lines - rows) * part].reshape(24, part)
-    v = [kept[i] for i in (3, 4, 2, 8, 9, 0, 1, 16)]
+    v = [vec_sums[i * part : (i + 1) * part] for i in (5, 6, 4, 0, 1, 2, 3, 7)]
     hidden_bias_grad = vec_sums[(lines - rows) * part :]
     shape = tokens.shape
     return (

time: 295 us -> 277 us (0.939)
  other arithmetic: 32.3 us -> 15.4 us
  starting transfers between devices: 77.6 us -> 72 us
    ppermute x24, waiting for transfers between devices: 35.4 us -> 48 us  [z_shift(): return lax.ppermute(v, 'fsdp', [(i, (i + 2 * k) % 8) for i in range(8)])]
    convert_element_type x9, other arithmetic: 16.1 us -> 6.35 us  [plus(): return sum((v.astype(f32) for v in values)).astype(bf16)]
    ppermute x24, starting transfers between devices: 44.3 us -> 37.4 us  [z_shift(): return lax.ppermute(v, 'fsdp', [(i, (i + 2 * k) % 8) for i in range(8)])]
    another operation x7 -> x1, other arithmetic: 5.5 us -> 0.01 us  [the longest x6 5.49 us: part(): jnp.stack([add(self.keep[dl, ks], self.got[dl, ks]) for dl in deltas])]
    all_to_all x3, waiting for transfers between devices: 4.58 us -> 0.02 us  [columns(): lax.all_to_all(jnp.broadcast_to(v[None], (4,) + v.shape), 'dp', 0, 0, til...]
    all_to_all x1, waiting for transfers between devices: 4.33 us -> 0.01 us  [per_device(): moved = lax.all_to_all(everyone, ('dp', 'fsdp'), 0, 0, tiled=True)]
  transfers between devices with their start and end apart: 53 -> 56, of which waited for: 15 -> 14; matrix products, arithmetic and copies ran while one was open for 15% -> 11% of each run, Pallas kernels for 33% -> 35%
where the time goes in v5:
time: 277 us; the launch traced here: 276 us
  Pallas kernels  96.4 us (35%)
  starting transfers between devices  72 us (26%)
  waiting for transfers between devices  57.3 us (21%)
  local copies, waits for them, and re-layouts  30.4 us (11%)
  other arithmetic  15.4 us (6%)
    pallas_call x7, Pallas kernels, call(): pl.pallas_call(kernel, grid=grid, in_specs=in_specs, out_shape=out_shape,...  96.4 us
    ppermute x24, waiting for transfers between devices, z_shift(): return lax.ppermute(v, 'fsdp', [(i, (i + 2 * k) % 8) for i in range(8)])  48 us
    ppermute x24, starting transfers between devices, z_shift(): return lax.ppermute(v, 'fsdp', [(i, (i + 2 * k) % 8) for i in range(8)])  37.4 us
    all_to_all x3, starting transfers between devices, columns(): lax.all_to_all(jnp.broadcast_to(v[None], (4,) + v.shape), 'dp', 0, 0, til...  13 us
    ppermute x7, starting transfers between devices, x_swap(): return lax.ppermute(v, 'dp', xor_perm(4, 1))  7.11 us
    ppermute x7, starting transfers between devices, y_swap(): return lax.ppermute(v, 'dp', xor_perm(4, 2))  6.63 us
    convert_element_type x9, other arithmetic, plus(): return sum((v.astype(f32) for v in values)).astype(bf16)  6.35 us
    another operation x12, local copies, waits for them, and re-layouts, rows_of(): return jnp.stack([g[first:first + count] for g in got])  5.67 us
  transfers between devices with their start and end apart: 56, of which 14 were waited for; matrix products, arithmetic and copies ran while one was open for 11% of the time, Pallas kernels for 35%

profile of v5, /device:TPU:0, one launch (start us, length us, event | category | flops | bytes accessed | tf_op | source)
XLA Modules:
  0.0 275.6 jit_solution(5575036105817505015)
XLA Ops:
  5.0 5.1 %collective-permute-start.2 = (bf16[112,768]{1,0:T(8,128)(2,1)S(1)}, bf16[112,768]{1,0:T(8,128)(2,1)S(1)}, u32[]{:S(2)}, u32[]{:S(2)}) collective-permute-start(bf16[112,768]{1,0:T(8,128)(2,1)S(1)} %pad_maximum_fusion.10), channel_id=1, source_target_pairs={{0,6},{1,7},{2,0},{3,1},{4,2},{5,3},{6,4},{7,5},{8,14},{9,15},{10,... | collective-permute-start | bytes 516104 | tf_op jit(solution)/shard_map/ppermute | solution.py:647
  15.3 9.4 %collective-permute-done.1 = bf16[112,768]{1,0:T(8,128)(2,1)S(1)} collective-permute-done((bf16[112,768]{1,0:T(8,128)(2,1)S(1)}, bf16[112,768]{1,0:T(8,128)(2,1)S(1)}, u32[]{:S(2)}, u32[]{:S(2)}) %collective-permute-start.1) | collective-permute-done | bytes 172064 | tf_op jit(solution)/shard_map/ppermute | solution.py:647
  26.4 4.6 %all-to-all-start = ((bf16[4,4,96,768]{3,2,1,0:T(8,128)(2,1)}), bf16[4,4,96,768]{3,2,1,0:T(8,128)(2,1)S(1)}, u32[]{:S(2)}, u32[]{:S(2)}) async-start(bf16[4,4,96,768]{3,2,1,0:T(8,128)(2,1)} %broadcast_in_dim.11), calls=%async_computation | async-start | bytes 4718592 | tf_op jit(solution)/shard_map/all_to_all | solution.py:655
  32.8 1.9 collective-permute-start.5
  34.8 1.9 collective-permute-start.4
  42.2 2.3 collective-permute-start.7
  44.4 18.5 %collective-permute-done.8 = bf16[16,768]{1,0:T(8,128)(2,1)S(1)} collective-permute-done((bf16[16,768]{1,0:T(8,128)(2,1)S(1)}, bf16[16,768]{1,0:T(8,128)(2,1)S(1)}, u32[]{:S(2)}, u32[]{:S(2)}) %collective-permute-start.8) | collective-permute-done | bytes 24608 | tf_op jit(solution)/shard_map/ppermute | solution.py:647
  64.2 2.5 collective-permute-done.9
  70.7 4.5 %all-to-all-start.1 = ((bf16[4,4,96,768]{3,2,1,0:T(8,128)(2,1)}), bf16[4,4,96,768]{3,2,1,0:T(8,128)(2,1)}, u32[]{:S(2)}, u32[]{:S(2)}) async-start(bf16[4,4,96,768]{3,2,1,0:T(8,128)(2,1)} %broadcast_in_dim.12), calls=%async_computation.1 | async-start | bytes 4718592 | tf_op jit(solution)/shard_map/all_to_all | solution.py:655
  76.6 3.1 %collective-permute-start.14 = (bf16[192,768]{1,0:T(8,128)(2,1)S(1)}, bf16[192,768]{1,0:T(8,128)(2,1)}, u32[]{:S(2)}, u32[]{:S(2)}) collective-permute-start(bf16[192,768]{1,0:T(8,128)(2,1)S(1)} %slice.406), channel_id=1, source_target_pairs={{0,6},{1,7},{2,0},{3,1},{4,2},{5,3},{6,4},{7,5},{8,14},{9,15},{10,... | collective-permute-start | bytes 884744 | tf_op jit(solution)/shard_map/ppermute | solution.py:647
  81.4 14.5 %shard_map.306 = (bf16[768,768]{1,0:T(8,128)(2,1)}, bf16[3,768,768]{2,1,0:T(8,128)(2,1)}, bf16[36,256,128]{2,1,0:T(8,128)(2,1)}, bf16[768,768]{1,0:T(8,128)(2,1)...) custom-call(s32[32]{0:T(128)} %stack.539.slots.slots_a.slots_b, bf16[768,768]{1,0:T(8,128)(2,1)} %bitcast.268, ...), custom_call_target="tpu_custom_call" | custom-call | flops 10871635968 | bytes 20971520 | tf_op jit(solution)/shard_map/pallas_call | solution.py:444
  95.9 8.1 %collective-permute-done.13 = bf16[192,768]{1,0:T(8,128)(2,1)} collective-permute-done((bf16[192,768]{1,0:T(8,128)(2,1)S(1)}, bf16[192,768]{1,0:T(8,128)(2,1)}, u32[]{:S(2)}, u32[]{:S(2)}) %collective-permute-start.13) | collective-permute-done | bytes 294944 | tf_op jit(solution)/shard_map/ppermute | solution.py:647
  104.0 3.1 %collective-permute-start.18 = (bf16[96,768]{1,0:T(8,128)(2,1)S(1)}, bf16[96,768]{1,0:T(8,128)(2,1)S(1)}, u32[]{:S(2)}, u32[]{:S(2)}) collective-permute-start(bf16[96,768]{1,0:T(8,128)(2,1)S(1)} %get-tuple-element.225), channel_id=1, source_target_pairs={{0,6},{1,7},{2,0},{3,1},{4,2},{5,3},{6,4},{7,5},{8,14},{9,15},{10,... | collective-permute-start | bytes 442376 | tf_op jit(solution)/shard_map/ppermute | solution.py:647
  108.1 2.0 collective-permute-start.16
  115.9 17.5 %shard_map.307 = (bf16[768,3072]{1,0:T(8,128)(2,1)}, bf16[768,3072]{1,0:T(8,128)(2,1)}, bf16[8,96,768]{2,1,0:T(8,128)(2,1)}, bf16[8,96,768]{2,1,0:T(8,128)(2,1)}...) custom-call(s32[32]{0:T(128)} %stack.539.slots.slots_a.slots_b, s32[17]{0:T(128)} %stack.506.gpos, ...), custom_call_target="tpu_custom_call" | custom-call | flops 14495514624 | bytes 20971520 | tf_op jit(solution)/shard_map/pallas_call | solution.py:444
  134.6 2.0 collective-permute-done.21
  137.0 2.1 collective-permute-start.23
  141.4 17.2 %shard_map.308 = (bf16[768,3072]{1,0:T(8,128)(2,1)}, f32[4,768]{1,0:T(4,128)}, f32[8,768]{1,0:T(8,128)}, bf16[8,96,768]{2,1,0:T(8,128)(2,1)}, bf16[8,96,768]{2,1...) custom-call(s32[32]{0:T(128)} %stack.572.slots, s32[17]{0:T(128)} %stack.506.gpos, ...), custom_call_target="tpu_custom_call" | custom-call | flops 14495514624 | bytes 20971520 | tf_op jit(solution)/shard_map/pallas_call | solution.py:444
  163.5 19.3 %shard_map.309 = (f32[768,768]{1,0:T(8,128)}, bf16[768,768]{1,0:T(8,128)(2,1)}, bf16[3,768,768]{2,1,0:T(8,128)(2,1)}, f32[8,768]{1,0:T(8,128)}) custom-call(s32[32]{0:T(128)} %stack.539.slots.slots_a.slots_b, s32[32]{0:T(128)} %stack.539.slots.slots_a.slots_b, bf16[768,3072]{1,0:T(8,128)(2,1)} %get-tuple-element.242.dh_ref, bf16[768,768]{1,0:T(8,128)(2,1)} %bitcast.267, ...), custom_call_target="tpu_custom_call" | custom-call | flops 9059696640 | bytes 31457280 | tf_op jit(solution)/shard_map/pallas_call | solution.py:444
  183.2 2.3 collective-permute-start.33
  189.3 8.2 %shard_map.310 = (bf16[8,96,768]{2,1,0:T(8,128)(2,1)}, bf16[8,96,768]{2,1,0:T(8,128)(2,1)}, bf16[8,96,768]{2,1,0:T(8,128)(2,1)}, bf16[8,96,768]{2,1,0:T(8,128)(2,1)}) custom-call(s32[17]{0:T(128)} %stack.506.gpos, bf16[768,768]{1,0:T(8,128)(2,1)} %get-tuple-element.194.normed_ref, bf16[3,768,768]{2,1,0:T(8,128)(2,1)} %get-tuple-element.276.dt_ref, ...), custom_call_target="tpu_custom_call" | custom-call | flops 7247757312 | bytes 12582912 | tf_op jit(solution)/shard_map/pallas_call | solution.py:444
  199.3 2.5 collective-permute-start.43
  209.0 9.8 %shard_map.311 = (bf16[768,768]{1,0:T(8,128)(2,1)}, f32[16,768]{1,0:T(8,128)}) custom-call(s32[32]{0:T(128)} %stack.539.slots.slots_a.slots_b, bf16[768,768]{1,0:T(8,128)(2,1)} %bitcast.269, f32[6,768]{1,0:T(8,128)} %reshape.329.emb_ref, f32[768,768]{1,0:T(8,128)} %get-tuple-element.275.dmid_ref, bf16[3,768,768]{2,1,0:T(8,128)(2,1)} %get-tuple-element.276.dt_ref, ...), custom_call_target="tpu_custom_call" | custom-call | flops 5435817984 | bytes 12582912 | tf_op jit(solution)/shard_map/pallas_call | solution.py:444
  218.9 2.0 collective-permute-done.39
  221.3 2.0 add_convert_fusion.8
  226.6 3.1 %all-to-all-start.2 = ((f32[32,1,1926]{2,1,0:T(1,128)}), f32[32,1,1926]{2,1,0:T(1,128)S(1)}, u32[]{:S(2)}, u32[]{:S(2)}) async-start(f32[32,1,1926]{2,1,0:T(1,128)} %all_to_all.19), calls=%async_computation.2 | async-start | bytes 524288 | tf_op jit(solution)/shard_map/all_to_all | solution.py:890
  229.7 9.8 %shard_map.312 = bf16[768,768]{1,0:T(8,128)(2,1)} custom-call(s32[32]{0:T(128)} %stack.572.slots, bf16[768,3072]{1,0:T(8,128)(2,1)} %get-tuple-element.301.act_ref, f32[768,768]{1,0:T(8,128)} %get-tuple-element.243.middle_ref, f32[8,768]{1,0:T(8,128)} %reshape.312.vec_ref, bf16[4,96,768]{2,1,0:T(8,128)(2,1)} %copy-done.12, bf16[8,96,768]{2,1,0:T(8,128)(2,1)} %bitcast.237, ...), custom_call_target="tpu_custom_call" | custom-call | flops 7247757312 | bytes 12582912 | tf_op jit(solution)/shard_map/pallas_call | solution.py:444
  244.0 3.9 %all-to-all-start.3 = ((bf16[4,192,768]{2,1,0:T(8,128)(2,1)}), bf16[4,192,768]{2,1,0:T(8,128)(2,1)S(1)}, u32[]{:S(2)}, u32[]{:S(2)}) async-start(bf16[4,192,768]{2,1,0:T(8,128)(2,1)} %broadcast_in_dim.14), calls=%async_computation.3 | async-start | bytes 2359296 | tf_op jit(solution)/shard_map/all_to_all | solution.py:655
  247.9 3.4 %collective-permute-start.48 = (bf16[96,768]{1,0:T(8,128)(2,1)S(1)}, bf16[96,768]{1,0:T(8,128)(2,1)S(1)}, u32[]{:S(2)}, u32[]{:S(2)}) collective-permute-start(bf16[96,768]{1,0:T(8,128)(2,1)S(1)} %get-tuple-element.353), channel_id=1, source_target_pairs={{0,6},{1,7},{2,0},{3,1},{4,2},{5,3},{6,4},{7,5},{8,14},{9,15},{10,... | collective-permute-start | bytes 442376 | tf_op jit(solution)/shard_map/ppermute | solution.py:647
  255.6 8.5 %collective-permute-done.47 = bf16[96,768]{1,0:T(8,128)(2,1)S(1)} collective-permute-done((bf16[96,768]{1,0:T(8,128)(2,1)S(1)}, bf16[96,768]{1,0:T(8,128)(2,1)S(1)}, u32[]{:S(2)}, u32[]{:S(2)}) %collective-permute-start.47) | collective-permute-done | bytes 147488 | tf_op jit(solution)/shard_map/ppermute | solution.py:647
  264.3 2.6 collective-permute-start.51
  271.2 2.5 collective-permute-done.50
  (268 shorter events, 72.8 us)
Async XLA Ops:
  10.1 14.6 %collective-permute-start = (bf16[112,768]{1,0:T(8,128)(2,1)S(1)}, bf16[112,768]{1,0:T(8,128)(2,1)S(1)}, u32[]{:S(2)}, u32[]{:S(2)}) collective-permute-start(bf16[112,768]{1,0:T(8,128)(2,1)S(1)} %pad_maximum_fusion.10), channel_id=1, source_target_pairs={{0,2},{1,3},{2,4},{3,5},{4,6},{5,7},{6,0},{7,1},{8,10},{9,11},{10,... | collective-permute-start | bytes 516104 | tf_op jit(solution)/shard_map/ppermute | solution.py:647
  26.4 40.4 %all-to-all-start = ((bf16[4,4,96,768]{3,2,1,0:T(8,128)(2,1)}), bf16[4,4,96,768]{3,2,1,0:T(8,128)(2,1)S(1)}, u32[]{:S(2)}, u32[]{:S(2)}) async-start(bf16[4,4,96,768]{3,2,1,0:T(8,128)(2,1)} %broadcast_in_dim.11), calls=%async_computation | async-start | bytes 4718592 | tf_op jit(solution)/shard_map/all_to_all | solution.py:655
  31.9 34.9 %collective-permute-start.6 = (bf16[192,768]{1,0:T(8,128)(2,1)S(1)}, bf16[192,768]{1,0:T(8,128)(2,1)}, u32[]{:S(2)}, u32[]{:S(2)}) collective-permute-start(bf16[192,768]{1,0:T(8,128)(2,1)S(1)} %pad_maximum_fusion.7), channel_id=1, source_target_pairs={{0,6},{1,7},{2,0},{3,1},{4,2},{5,3},{6,4},{7,5},{8,14},{9,15},{10,... | collective-permute-start | bytes 884744 | tf_op jit(solution)/shard_map/ppermute | solution.py:647
  32.8 33.9 %collective-permute-start.5 = (bf16[192,768]{1,0:T(8,128)(2,1)S(1)}, bf16[192,768]{1,0:T(8,128)(2,1)}, u32[]{:S(2)}, u32[]{:S(2)}) collective-permute-start(bf16[192,768]{1,0:T(8,128)(2,1)S(1)} %pad_maximum_fusion.7), channel_id=1, source_target_pairs={{0,4},{1,5},{2,6},{3,7},{4,0},{5,1},{6,2},{7,3},{8,12},{9,13},{10,... | collective-permute-start | bytes 884744 | tf_op jit(solution)/shard_map/ppermute | solution.py:647
  34.8 32.0 %collective-permute-start.4 = (bf16[192,768]{1,0:T(8,128)(2,1)S(1)}, bf16[192,768]{1,0:T(8,128)(2,1)}, u32[]{:S(2)}, u32[]{:S(2)}) collective-permute-start(bf16[192,768]{1,0:T(8,128)(2,1)S(1)} %pad_maximum_fusion.7), channel_id=1, source_target_pairs={{0,2},{1,3},{2,4},{3,5},{4,6},{5,7},{6,0},{7,1},{8,10},{9,11},{10,... | collective-permute-start | bytes 884744 | tf_op jit(solution)/shard_map/ppermute | solution.py:647
  41.9 21.0 %collective-permute-start.8 = (bf16[16,768]{1,0:T(8,128)(2,1)S(1)}, bf16[16,768]{1,0:T(8,128)(2,1)S(1)}, u32[]{:S(2)}, u32[]{:S(2)}) collective-permute-start(bf16[16,768]{1,0:T(8,128)(2,1)S(1)} %get-tuple-element.378), channel_id=1, source_target_pairs={{0,4},{1,5},{2,6},{3,7},{4,0},{5,1},{6,2},{7,3},{8,12},{9,13},{10,... | collective-permute-start | bytes 73736 | tf_op jit(solution)/shard_map/ppermute | solution.py:647
  42.2 22.1 %collective-permute-start.7 = (bf16[16,768]{1,0:T(8,128)(2,1)S(1)}, bf16[16,768]{1,0:T(8,128)(2,1)S(1)}, u32[]{:S(2)}, u32[]{:S(2)}) collective-permute-start(bf16[16,768]{1,0:T(8,128)(2,1)S(1)} %get-tuple-element.378), channel_id=1, source_target_pairs={{0,2},{1,3},{2,4},{3,5},{4,6},{5,7},{6,0},{7,1},{8,10},{9,11},{10,... | collective-permute-start | bytes 73736 | tf_op jit(solution)/shard_map/ppermute | solution.py:647
  66.8 14.6 %collective-permute-start.10 = (bf16[16,96,768]{2,1,0:T(8,128)(2,1)S(1)}, bf16[16,96,768]{2,1,0:T(8,128)(2,1)}, u32[]{:S(2)}, u32[]{:S(2)}) collective-permute-start(bf16[16,96,768]{2,1,0:T(8,128)(2,1)S(1)} %bitcast.229), channel_id=1, source_target_pairs={{0,1},{1,0},{2,3},{3,2},{4,5},{5,4},{6,7},{7,6},{8,9},{9,8},{10,11... | collective-permute-start | bytes 7077896 | tf_op jit(solution)/shard_map/ppermute | solution.py:631
  70.7 33.3 %all-to-all-start.1 = ((bf16[4,4,96,768]{3,2,1,0:T(8,128)(2,1)}), bf16[4,4,96,768]{3,2,1,0:T(8,128)(2,1)}, u32[]{:S(2)}, u32[]{:S(2)}) async-start(bf16[4,4,96,768]{3,2,1,0:T(8,128)(2,1)} %broadcast_in_dim.12), calls=%async_computation.1 | async-start | bytes 4718592 | tf_op jit(solution)/shard_map/all_to_all | solution.py:655
  76.6 19.4 %collective-permute-start.14 = (bf16[192,768]{1,0:T(8,128)(2,1)S(1)}, bf16[192,768]{1,0:T(8,128)(2,1)}, u32[]{:S(2)}, u32[]{:S(2)}) collective-permute-start(bf16[192,768]{1,0:T(8,128)(2,1)S(1)} %slice.406), channel_id=1, source_target_pairs={{0,6},{1,7},{2,0},{3,1},{4,2},{5,3},{6,4},{7,5},{8,14},{9,15},{10,... | collective-permute-start | bytes 884744 | tf_op jit(solution)/shard_map/ppermute | solution.py:647
  79.7 24.3 %collective-permute-start.13 = (bf16[192,768]{1,0:T(8,128)(2,1)S(1)}, bf16[192,768]{1,0:T(8,128)(2,1)}, u32[]{:S(2)}, u32[]{:S(2)}) collective-permute-start(bf16[192,768]{1,0:T(8,128)(2,1)S(1)} %slice.406), channel_id=1, source_target_pairs={{0,4},{1,5},{2,6},{3,7},{4,0},{5,1},{6,2},{7,3},{8,12},{9,13},{10,... | collective-permute-start | bytes 884744 | tf_op jit(solution)/shard_map/ppermute | solution.py:647
  79.7 24.3 %collective-permute-start.12 = (bf16[192,768]{1,0:T(8,128)(2,1)S(1)}, bf16[192,768]{1,0:T(8,128)(2,1)}, u32[]{:S(2)}, u32[]{:S(2)}) collective-permute-start(bf16[192,768]{1,0:T(8,128)(2,1)S(1)} %slice.406), channel_id=1, source_target_pairs={{0,2},{1,3},{2,4},{3,5},{4,6},{5,7},{6,0},{7,1},{8,10},{9,11},{10,... | collective-permute-start | bytes 884744 | tf_op jit(solution)/shard_map/ppermute | solution.py:647
  104.0 29.4 %collective-permute-start.18 = (bf16[96,768]{1,0:T(8,128)(2,1)S(1)}, bf16[96,768]{1,0:T(8,128)(2,1)S(1)}, u32[]{:S(2)}, u32[]{:S(2)}) collective-permute-start(bf16[96,768]{1,0:T(8,128)(2,1)S(1)} %get-tuple-element.225), channel_id=1, source_target_pairs={{0,6},{1,7},{2,0},{3,1},{4,2},{5,3},{6,4},{7,5},{8,14},{9,15},{10,... | collective-permute-start | bytes 442376 | tf_op jit(solution)/shard_map/ppermute | solution.py:647
  107.1 26.3 %collective-permute-start.17 = (bf16[96,768]{1,0:T(8,128)(2,1)S(1)}, bf16[96,768]{1,0:T(8,128)(2,1)S(1)}, u32[]{:S(2)}, u32[]{:S(2)}) collective-permute-start(bf16[96,768]{1,0:T(8,128)(2,1)S(1)} %get-tuple-element.225), channel_id=1, source_target_pairs={{0,4},{1,5},{2,6},{3,7},{4,0},{5,1},{6,2},{7,3},{8,12},{9,13},{10,... | collective-permute-start | bytes 442376 | tf_op jit(solution)/shard_map/ppermute | solution.py:647
  108.1 25.4 %collective-permute-start.16 = (bf16[96,768]{1,0:T(8,128)(2,1)S(1)}, bf16[96,768]{1,0:T(8,128)(2,1)S(1)}, u32[]{:S(2)}, u32[]{:S(2)}) collective-permute-start(bf16[96,768]{1,0:T(8,128)(2,1)S(1)} %get-tuple-element.225), channel_id=1, source_target_pairs={{0,2},{1,3},{2,4},{3,5},{4,6},{5,7},{6,0},{7,1},{8,10},{9,11},{10,... | collective-permute-start | bytes 442376 | tf_op jit(solution)/shard_map/ppermute | solution.py:647
  112.9 20.5 %collective-permute-start.19 = (bf16[4,96,768]{2,1,0:T(8,128)(2,1)S(1)}, bf16[4,96,768]{2,1,0:T(8,128)(2,1)S(1)}, u32[]{:S(2)}, u32[]{:S(2)}) collective-permute-start(bf16[4,96,768]{2,1,0:T(8,128)(2,1)S(1)} %pad_maximum_fusion.4.rest_0_), channel_id=1, source_target_pairs={{0,1},{1,0},{2,3},{3,2},{4,5},{5,4},{6,7},{7,6},{8,9},{9,8},{10,11... | collective-permute-start | bytes 1769480 | tf_op jit(solution)/shard_map/ppermute | solution.py:631
  114.5 19.0 %collective-permute-start.20 = (bf16[8,96,768]{2,1,0:T(8,128)(2,1)S(1)}, bf16[8,96,768]{2,1,0:T(8,128)(2,1)S(1)}, u32[]{:S(2)}, u32[]{:S(2)}) collective-permute-start(bf16[8,96,768]{2,1,0:T(8,128)(2,1)S(1)} %bitcast.235), channel_id=1, source_target_pairs={{0,1},{1,0},{2,3},{3,2},{4,5},{5,4},{6,7},{7,6},{8,9},{9,8},{10,11... | collective-permute-start | bytes 3538952 | tf_op jit(solution)/shard_map/ppermute | solution.py:631
  134.3 24.4 %collective-permute-start.25 = (bf16[8,96,768]{2,1,0:T(8,128)(2,1)}, bf16[8,96,768]{2,1,0:T(8,128)(2,1)S(1)}, u32[]{:S(2)}, u32[]{:S(2)}) collective-permute-start(bf16[8,96,768]{2,1,0:T(8,128)(2,1)} %get-tuple-element.238), channel_id=1, source_target_pairs={{0,1},{1,0},{2,3},{3,2},{4,5},{5,4},{6,7},{7,6},{8,9},{9,8},{10,11... | collective-permute-start | bytes 3538952 | tf_op jit(solution)/shard_map/ppermute | solution.py:631
  137.0 21.7 %collective-permute-start.23 = (bf16[4,96,768]{2,1,0:T(8,128)(2,1)S(1)}, bf16[4,96,768]{2,1,0:T(8,128)(2,1)S(1)}, u32[]{:S(2)}, u32[]{:S(2)}) collective-permute-start(bf16[4,96,768]{2,1,0:T(8,128)(2,1)S(1)} %get-tuple-element.236), channel_id=1, source_target_pairs={{0,8},{8,0},{16,24},{24,16},{1,9},{9,1},{17,25},{25,17},{2,10},{10... | collective-permute-start | bytes 1769480 | tf_op jit(solution)/shard_map/ppermute | solution.py:635
  139.1 19.6 %collective-permute-start.24 = (bf16[4,96,768]{2,1,0:T(8,128)(2,1)S(1)}, bf16[4,96,768]{2,1,0:T(8,128)(2,1)S(1)}, u32[]{:S(2)}, u32[]{:S(2)}) collective-permute-start(bf16[4,96,768]{2,1,0:T(8,128)(2,1)S(1)} %get-tuple-element.237), channel_id=1, source_target_pairs={{0,16},{8,24},{16,0},{24,8},{1,17},{9,25},{17,1},{25,9},{2,18},{10... | collective-permute-start | bytes 1769480 | tf_op jit(solution)/shard_map/ppermute | solution.py:639
  159.0 23.8 %collective-permute-start.30 = (bf16[2,96,768]{2,1,0:T(8,128)(2,1)S(1)}, bf16[2,96,768]{2,1,0:T(8,128)(2,1)S(1)}, u32[]{:S(2)}, u32[]{:S(2)}) collective-permute-start(bf16[2,96,768]{2,1,0:T(8,128)(2,1)S(1)} %get-tuple-element.328), channel_id=1, source_target_pairs={{0,8},{8,0},{16,24},{24,16},{1,9},{9,1},{17,25},{25,17},{2,10},{10... | collective-permute-start | bytes 884744 | tf_op jit(solution)/shard_map/ppermute | solution.py:635
  159.6 23.2 %collective-permute-start.29 = (bf16[2,96,768]{2,1,0:T(8,128)(2,1)S(1)}, bf16[2,96,768]{2,1,0:T(8,128)(2,1)S(1)}, u32[]{:S(2)}, u32[]{:S(2)}) collective-permute-start(bf16[2,96,768]{2,1,0:T(8,128)(2,1)S(1)} %get-tuple-element.329), channel_id=1, source_target_pairs={{0,16},{8,24},{16,0},{24,8},{1,17},{9,25},{17,1},{25,9},{2,18},{10... | collective-permute-start | bytes 884744 | tf_op jit(solution)/shard_map/ppermute | solution.py:639
  160.5 25.7 %collective-permute-start.34 = (bf16[8,96,768]{2,1,0:T(8,128)(2,1)}, bf16[8,96,768]{2,1,0:T(8,128)(2,1)S(1)}, u32[]{:S(2)}, u32[]{:S(2)}) collective-permute-start(bf16[8,96,768]{2,1,0:T(8,128)(2,1)} %get-tuple-element.264), channel_id=1, source_target_pairs={{0,1},{1,0},{2,3},{3,2},{4,5},{5,4},{6,7},{7,6},{8,9},{9,8},{10,11... | collective-permute-start | bytes 3538952 | tf_op jit(solution)/shard_map/ppermute | solution.py:631
  162.1 20.7 %collective-permute-start.27 = (bf16[4,96,768]{2,1,0:T(8,128)(2,1)S(1)}, bf16[4,96,768]{2,1,0:T(8,128)(2,1)S(1)}, u32[]{:S(2)}, u32[]{:S(2)}) collective-permute-start(bf16[4,96,768]{2,1,0:T(8,128)(2,1)S(1)} %get-tuple-element.247), channel_id=1, source_target_pairs={{0,8},{8,0},{16,24},{24,16},{1,9},{9,1},{17,25},{25,17},{2,10},{10... | collective-permute-start | bytes 1769480 | tf_op jit(solution)/shard_map/ppermute | solution.py:635
  162.8 20.1 %collective-permute-start.28 = (bf16[4,96,768]{2,1,0:T(8,128)(2,1)S(1)}, bf16[4,96,768]{2,1,0:T(8,128)(2,1)S(1)}, u32[]{:S(2)}, u32[]{:S(2)}) collective-permute-start(bf16[4,96,768]{2,1,0:T(8,128)(2,1)S(1)} %get-tuple-element.248), channel_id=1, source_target_pairs={{0,16},{8,24},{16,0},{24,8},{1,17},{9,25},{17,1},{25,9},{2,18},{10... | collective-permute-start | bytes 1769480 | tf_op jit(solution)/shard_map/ppermute | solution.py:639
  201.8 17.1 %collective-permute-start.42 = (bf16[96,768]{1,0:T(8,128)(2,1)}, bf16[96,768]{1,0:T(8,128)(2,1)S(1)}, u32[]{:S(2)}, u32[]{:S(2)}) collective-permute-start(bf16[96,768]{1,0:T(8,128)(2,1)} %get-tuple-element.358), channel_id=1, source_target_pairs={{0,4},{1,5},{2,6},{3,7},{4,0},{5,1},{6,2},{7,3},{8,12},{9,13},{10,... | collective-permute-start | bytes 442376 | tf_op jit(solution)/shard_map/ppermute | solution.py:647
  202.9 18.4 %collective-permute-start.37 = (bf16[8,96,768]{2,1,0:T(8,128)(2,1)}, bf16[8,96,768]{2,1,0:T(8,128)(2,1)S(1)}, u32[]{:S(2)}, u32[]{:S(2)}) collective-permute-start(bf16[8,96,768]{2,1,0:T(8,128)(2,1)} %get-tuple-element.268), channel_id=1, source_target_pairs={{0,1},{1,0},{2,3},{3,2},{4,5},{5,4},{6,7},{7,6},{8,9},{9,8},{10,11... | collective-permute-start | bytes 3538952 | tf_op jit(solution)/shard_map/ppermute | solution.py:631
  204.9 16.0 %collective-permute-start.39 = (bf16[4,96,768]{2,1,0:T(8,128)(2,1)}, bf16[4,96,768]{2,1,0:T(8,128)(2,1)S(1)}, u32[]{:S(2)}, u32[]{:S(2)}) collective-permute-start(bf16[4,96,768]{2,1,0:T(8,128)(2,1)} %get-tuple-element.273), channel_id=1, source_target_pairs={{0,8},{8,0},{16,24},{24,16},{1,9},{9,1},{17,25},{25,17},{2,10},{10... | collective-permute-start | bytes 1769480 | tf_op jit(solution)/shard_map/ppermute | solution.py:635
  205.5 15.8 %collective-permute-start.40 = (bf16[4,96,768]{2,1,0:T(8,128)(2,1)}, bf16[4,96,768]{2,1,0:T(8,128)(2,1)}, u32[]{:S(2)}, u32[]{:S(2)}) collective-permute-start(bf16[4,96,768]{2,1,0:T(8,128)(2,1)} %get-tuple-element.274), channel_id=1, source_target_pairs={{0,16},{8,24},{16,0},{24,8},{1,17},{9,25},{17,1},{25,9},{2,18},{10... | collective-permute-start | bytes 1769480 | tf_op jit(solution)/shard_map/ppermute | solution.py:639
  223.3 17.1 %collective-permute-start.45 = (bf16[2,96,768]{2,1,0:T(8,128)(2,1)}, bf16[2,96,768]{2,1,0:T(8,128)(2,1)}, u32[]{:S(2)}, u32[]{:S(2)}) collective-permute-start(bf16[2,96,768]{2,1,0:T(8,128)(2,1)} %get-tuple-element.318), channel_id=1, source_target_pairs={{0,8},{8,0},{16,24},{24,16},{1,9},{9,1},{17,25},{25,17},{2,10},{10... | collective-permute-start | bytes 884744 | tf_op jit(solution)/shard_map/ppermute | solution.py:635
  224.8 15.7 %collective-permute-start.44 = (bf16[2,96,768]{2,1,0:T(8,128)(2,1)}, bf16[2,96,768]{2,1,0:T(8,128)(2,1)}, u32[]{:S(2)}, u32[]{:S(2)}) collective-permute-start(bf16[2,96,768]{2,1,0:T(8,128)(2,1)} %get-tuple-element.319), channel_id=1, source_target_pairs={{0,16},{8,24},{16,0},{24,8},{1,17},{9,25},{17,1},{25,9},{2,18},{10... | collective-permute-start | bytes 884744 | tf_op jit(solution)/shard_map/ppermute | solution.py:639
  244.0 20.2 %all-to-all-start.3 = ((bf16[4,192,768]{2,1,0:T(8,128)(2,1)}), bf16[4,192,768]{2,1,0:T(8,128)(2,1)S(1)}, u32[]{:S(2)}, u32[]{:S(2)}) async-start(bf16[4,192,768]{2,1,0:T(8,128)(2,1)} %broadcast_in_dim.14), calls=%async_computation.3 | async-start | bytes 2359296 | tf_op jit(solution)/shard_map/all_to_all | solution.py:655
  (57 other events, 456.9 us)

commit v6 on v5

--- a/solution.py
+++ b/solution.py
@@ -62,6 +62,28 @@
                     pltpu.make_async_copy(pieces[piece].at[at], w_ref.at[place], sem.at[place]).start()
 
             i += 1
+
+
+def start_wide(slots_ref, pieces, layout, w_ref, sem):
+    width = w_ref.shape[0]
+    b = width // NB
+    i = 0
+    for piece, first, count in layout:
+        for t in range(count):
+            slot = slots_ref[i]
+            row = pl.multiple_of(lax.rem(slot, NB) * b, b)
+            column = pl.multiple_of(slot // NB * width, width)
+            place = w_ref.at[pl.ds(row, b), pl.ds(column, width)]
+            pltpu.make_async_copy(pieces[piece].at[first + t], place, sem.at[slot]).start()
+            i += 1
+
+
+def wait_wide(w_ref, sem):
+    width = w_ref.shape[0]
+    b = width // NB
+    place = w_ref.at[pl.ds(0, b), pl.ds(0, width)]
+    for slot in range(32):
+        pltpu.make_async_copy(place, place, sem.at[slot]).wait()
 
 
 def wait_blocks(w_ref, sem, first, count):
@@ -300,18 +322,13 @@
 
     @pl.when(pl.program_id(0) == 0)
     def _():
-        start_blocks(slots_b, pieces_b, layout_b, wb_ref, sem_b)
+        start_wide(slots_b, pieces_b, layout_b, wb_ref, sem_b)
         start_blocks(slots_a, pieces_a, layout_a, wo_ref, sem_a, 3 * NB)
         sums_ref[...] = jnp.zeros_like(sums_ref)
-        wait_blocks(wb_ref, sem_b, 0, 32)
+        wait_wide(wb_ref, sem_b)
         wait_blocks(wo_ref, sem_a, 0, NB)
 
-    def slope(j):
-        return mm_nt(dh_ref[:, j * width : (j + 1) * width], square(wb_ref, j))
-
-    d_n2 = slope(0)
-    for j in range(1, 4):
-        d_n2 = d_n2 + slope(j)
+    d_n2 = mm_nt(dh_ref[...], wb_ref[...])
     xhat, inv = moments(middle_ref[...])
     sums_ref[0:1] += jnp.sum(d_n2 * xhat, axis=0, keepdims=True)
     sums_ref[1:2] += jnp.sum(d_n2, axis=0, keepdims=True)
@@ -325,9 +342,9 @@
     first = half_mask(length, 2 * HD)
     pairs = width // (2 * HD)
     every = [(r, hp) for r in range(rb) for hp in range(pairs)]
-    for start in range(0, len(every), 6):
+    for start in range(0, len(every), 12):
         some = []
-        for r, hp in every[start : start + 6]:
+        for r, hp in every[start : start + 12]:
             rows = slice(r * length, (r + 1) * length)
             lanes = slice(hp * 2 * HD, (hp + 1) * 2 * HD)
             dos = both(datt_ref[rows, lanes], first)
@@ -503,7 +520,7 @@
 def compute_b1(n2, cot, gp, group, gpos):
     n, width = n2.shape
     b = width // NB
-    chunk = 256 if n % 256 == 0 else n
+    chunk = n // 2 if n % 64 == 0 else n
     column = pl.BlockSpec((n, width), lambda i: (0, i))
     return call(
         functools.partial(b1_kernel, group.layout, chunk),
@@ -534,7 +551,7 @@
         + [hbm] * (len(ga.arrays) + len(gb.arrays)),
         [sds((n, width), f32), sds((n, width), bf16), sds((3, n, width), bf16), sds((8, width), f32)],
         [tile, tile, wide, full((8, width))],
-        [pltpu.VMEM((NB, b, width), bf16), pltpu.VMEM((32, b, width), bf16), pltpu.VMEM((block, width), bf16),
+        [pltpu.VMEM((NB, b, width), bf16), pltpu.VMEM((width, 4 * width), bf16), pltpu.VMEM((block, width), bf16),
          pltpu.SemaphoreType.DMA((NB,)), pltpu.SemaphoreType.DMA((32,))],
         2 * n * width * width * 10, 30 << 20,
         [ga.slots, gb.slots, dh, cot, middle, vecs, triple, att, *ga.arrays, *gb.arrays],
@@ -730,11 +747,12 @@
         self.add_two()
         self.send_two()
 
-    def three(self):
+    def three(self, after=()):
         at = [slice(4 * i, 4 * i + 2) for i in range(2)]
         halves = [plus(self.keep[1][at[i]], self.got[1][at[i]], self.r1[i][:2], self.r2[i]) for i in range(2)]
         self.h3 = [halves[k // 2][k % 2] for k in range(4)]
-        self.r3 = [self.h3[0]] + [z_shift(self.h3[k], k) for k in (1, 2, 3)]
+        last = tie(self.h3[1], after) if after else self.h3[1]
+        self.r3 = [self.h3[0], z_shift(last, 1), z_shift(self.h3[2], 2), z_shift(self.h3[3], 3)]
 
     def total(self):
         return sum(p.astype(f32) for p in self.r3).astype(bf16)
@@ -804,7 +822,8 @@
             (looked.reshape(rows, width), seg, pad, vecs, hb, gpos, slots, slots_c, marks)
         )
         sent = jnp.pad(looked, ((0, 16 - rows), (0, 0)))
-        got_e = jnp.stack(along_z(sent))
+        got_e = [sent, z_shift(sent, 1), z_shift(sent, 2), z_shift(tie(sent, got1[3]), 3)]
+        got_e = jnp.stack(got_e)
         mine_a, got1, got_e = lax.optimization_barrier((mine_a, got1, got_e))
         emb = shard_order(got_e, core_swap(got_e), z, c)[:, :rows].reshape(nf, nf, rows, width // nf)
         emb = pick(emb.transpose(1, 0, 2, 3), f)
@@ -818,20 +837,21 @@
         core_a = core_swap(mine_a)
         ga = Group([mine_a, core_a], quarter_major, slots)
         mine_b = columns(rows_of(got1, 0, b))
+        c0 = rows_of(got1, b, b)
         got2 = along_z(tie(down_weight[b : 3 * b], got1))
         tok_in = tie(tok, (core_a, emb))
     else:
         tok_in = tok
     normed, triple, att, attended, middle, n2 = compute_f1(tok_in, emb, seg, pad, vecs, ga, rows, length)
     if fast:
-        mine_b, n2, got2 = lax.optimization_barrier((mine_b.reshape(flat), n2, got2))
+        c0x = core_swap(c0)
+        mine_b, n2, got2, c0x = lax.optimization_barrier((mine_b.reshape(flat), n2, got2, c0x))
         core_b = core_swap(mine_b)
         gb = Group([mine_b, core_b], quarter_major, slots)
         got3 = along_z(tie(down_weight[3 * b :], got2))
-        c0 = rows_of(tie(got1, n2), b, b)
         c12 = jnp.stack(got2).reshape(8, b, width)
         n2, c12 = tie((n2, c12), core_b)
-        c0x, c12x = core_swap(c0), core_swap(c12)
+        c12x = core_swap(c12)
     active, gp, *grads_c = compute_f2(n2, cot, hb, gb, gpos)
     if fast:
         got3, c0x, c12x, gp, grads_c = lax.optimization_barrier((got3, c0x, c12x, gp, grads_c))
@@ -862,9 +882,9 @@
     grads_a = compute_ga(normed, attended, dt, dbr, gpos)
     if fast:
         grads_a, sc.r3, sb.r2, dt = lax.optimization_barrier((grads_a, sc.r3, sb.r2, dt))
-        sb.three()
         sa = Scatter(*grads_a)
         sa.split()
+        sb.three((sa.got[1],))
         dt, sa.out, active = lax.optimization_barrier((dt, sa.out, active))
         sa.one()
         mine_c = sc.total()

time: 277 us -> 270 us (0.975)
  local copies, waits for them, and re-layouts: 30.4 us -> 26.7 us
  waiting for transfers between devices: 57.3 us -> 54.3 us
    another operation x12 -> x8, local copies, waits for them, and re-layouts: 5.67 us -> 4.05 us  [rows_of(): return jnp.stack([g[first:first + count] for g in got])]
  transfers between devices with their start and end apart: 56 -> 56, of which waited for: 14 -> 15; matrix products, arithmetic and copies ran while one was open for 11% -> 10% of each run, Pallas kernels for 35% -> 36%
where the time goes in v6:
time: 270 us; the launch traced here: 269 us
  Pallas kernels  95.7 us (35%)
  starting transfers between devices  72.2 us (27%)
  waiting for transfers between devices  54.3 us (20%)
  local copies, waits for them, and re-layouts  26.7 us (10%)
  other arithmetic  15.9 us (6%)
    pallas_call x7, Pallas kernels, call(): pl.pallas_call(kernel, grid=grid, in_specs=in_specs, out_shape=out_shape,...  95.7 us
    ppermute x24, waiting for transfers between devices, z_shift(): return lax.ppermute(v, 'fsdp', [(i, (i + 2 * k) % 8) for i in range(8)])  45.6 us
    ppermute x24, starting transfers between devices, z_shift(): return lax.ppermute(v, 'fsdp', [(i, (i + 2 * k) % 8) for i in range(8)])  37.9 us
    all_to_all x3, starting transfers between devices, columns(): lax.all_to_all(jnp.broadcast_to(v[None], (4,) + v.shape), 'dp', 0, 0, til...  13 us
    ppermute x7, starting transfers between devices, x_swap(): return lax.ppermute(v, 'dp', xor_perm(4, 1))  7.19 us
    ppermute x7, starting transfers between devices, y_swap(): return lax.ppermute(v, 'dp', xor_perm(4, 2))  6.68 us
    convert_element_type x9, other arithmetic, plus(): return sum((v.astype(f32) for v in values)).astype(bf16)  6.34 us
  transfers between devices with their start and end apart: 56, of which 15 were waited for; matrix products, arithmetic and copies ran while one was open for 10% of the time, Pallas kernels for 36%

profile of v6, /device:TPU:0, one launch (start us, length us, event | category | flops | bytes accessed | tf_op | source)
XLA Modules:
  0.0 268.8 jit_solution(4969841591656112969)
XLA Ops:
  5.6 5.0 %collective-permute-start.2 = (bf16[112,768]{1,0:T(8,128)(2,1)}, bf16[112,768]{1,0:T(8,128)(2,1)S(1)}, u32[]{:S(2)}, u32[]{:S(2)}) collective-permute-start(bf16[112,768]{1,0:T(8,128)(2,1)} %pad_maximum_fusion.10), channel_id=1, source_target_pairs={{0,6},{1,7},{2,0},{3,1},{4,2},{5,3},{6,4},{7,5},{8,14},{9,15},{10,... | collective-permute-start | bytes 516104 | tf_op jit(solution)/shard_map/ppermute | solution.py:664
  15.8 9.6 %collective-permute-done.1 = bf16[112,768]{1,0:T(8,128)(2,1)S(1)} collective-permute-done((bf16[112,768]{1,0:T(8,128)(2,1)}, bf16[112,768]{1,0:T(8,128)(2,1)S(1)}, u32[]{:S(2)}, u32[]{:S(2)}) %collective-permute-start.1) | collective-permute-done | bytes 172064 | tf_op jit(solution)/shard_map/ppermute | solution.py:664
  25.6 1.6 broadcast_in_dim.11
  27.2 4.6 %all-to-all-start = ((bf16[4,4,96,768]{3,2,1,0:T(8,128)(2,1)}), bf16[4,4,96,768]{3,2,1,0:T(8,128)(2,1)S(1)}, u32[]{:S(2)}, u32[]{:S(2)}) async-start(bf16[4,4,96,768]{3,2,1,0:T(8,128)(2,1)} %broadcast_in_dim.11), calls=%async_computation | async-start | bytes 4718592 | tf_op jit(solution)/shard_map/all_to_all | solution.py:672
  34.4 1.9 collective-permute-start.5
  36.3 1.9 collective-permute-start.4
  40.5 2.3 collective-permute-start.7
  43.0 3.2 %collective-permute-start.9 = (bf16[16,768]{1,0:T(8,128)(2,1)S(1)}, bf16[16,768]{1,0:T(8,128)(2,1)S(1)}, u32[]{:S(2)}, u32[]{:S(2)}) collective-permute-start(bf16[16,768]{1,0:T(8,128)(2,1)S(1)} %get-tuple-element.187), channel_id=1, source_target_pairs={{0,6},{1,7},{2,0},{3,1},{4,2},{5,3},{6,4},{7,5},{8,14},{9,15},{10,... | collective-permute-start | bytes 73736 | tf_op jit(solution)/shard_map/ppermute | solution.py:664
  46.2 18.4 %collective-permute-done.8 = bf16[16,768]{1,0:T(8,128)(2,1)S(1)} collective-permute-done((bf16[16,768]{1,0:T(8,128)(2,1)S(1)}, bf16[16,768]{1,0:T(8,128)(2,1)S(1)}, u32[]{:S(2)}, u32[]{:S(2)}) %collective-permute-start.8) | collective-permute-done | bytes 24608 | tf_op jit(solution)/shard_map/ppermute | solution.py:664
  69.1 4.5 %all-to-all-start.1 = ((bf16[4,4,96,768]{3,2,1,0:T(8,128)(2,1)}), bf16[4,4,96,768]{3,2,1,0:T(8,128)(2,1)}, u32[]{:S(2)}, u32[]{:S(2)}) async-start(bf16[4,4,96,768]{3,2,1,0:T(8,128)(2,1)} %broadcast_in_dim.12), calls=%async_computation.1 | async-start | bytes 4718592 | tf_op jit(solution)/shard_map/all_to_all | solution.py:672
  74.5 1.7 collective-permute-start.14
  80.3 14.5 %shard_map.306 = (bf16[768,768]{1,0:T(8,128)(2,1)}, bf16[3,768,768]{2,1,0:T(8,128)(2,1)}, bf16[36,256,128]{2,1,0:T(8,128)(2,1)}, bf16[768,768]{1,0:T(8,128)(2,1)...) custom-call(s32[32]{0:T(128)} %stack.539.slots.slots_a.slots_b, bf16[768,768]{1,0:T(8,128)(2,1)} %bitcast.271, ...), custom_call_target="tpu_custom_call" | custom-call | flops 10871635968 | bytes 20971520 | tf_op jit(solution)/shard_map/pallas_call | solution.py:461
  94.8 8.3 %collective-permute-done.13 = bf16[192,768]{1,0:T(8,128)(2,1)} collective-permute-done((bf16[192,768]{1,0:T(8,128)(2,1)S(1)}, bf16[192,768]{1,0:T(8,128)(2,1)}, u32[]{:S(2)}, u32[]{:S(2)}) %collective-permute-start.13) | collective-permute-done | bytes 294944 | tf_op jit(solution)/shard_map/ppermute | solution.py:664
  105.6 1.9 collective-permute-start.17
  110.2 17.5 %shard_map.307 = (bf16[768,3072]{1,0:T(8,128)(2,1)}, bf16[768,3072]{1,0:T(8,128)(2,1)}, bf16[8,96,768]{2,1,0:T(8,128)(2,1)}, bf16[8,96,768]{2,1,0:T(8,128)(2,1)}...) custom-call(s32[32]{0:T(128)} %stack.539.slots.slots_a.slots_b, s32[17]{0:T(128)} %stack.506.gpos, ...), custom_call_target="tpu_custom_call" | custom-call | flops 14495514624 | bytes 20971520 | tf_op jit(solution)/shard_map/pallas_call | solution.py:461
  128.7 2.3 collective-permute-done.21
  131.3 2.1 collective-permute-start.23
  135.7 17.0 %shard_map.308 = (bf16[768,3072]{1,0:T(8,128)(2,1)}, f32[4,768]{1,0:T(4,128)}, f32[8,768]{1,0:T(8,128)}, bf16[8,96,768]{2,1,0:T(8,128)(2,1)}, bf16[8,96,768]{2,1...) custom-call(s32[32]{0:T(128)} %stack.572.slots, s32[17]{0:T(128)} %stack.506.gpos, ...), custom_call_target="tpu_custom_call" | custom-call | flops 14495514624 | bytes 20971520 | tf_op jit(solution)/shard_map/pallas_call | solution.py:461
  157.6 18.8 %shard_map.309 = (f32[768,768]{1,0:T(8,128)}, bf16[768,768]{1,0:T(8,128)(2,1)}, bf16[3,768,768]{2,1,0:T(8,128)(2,1)}, f32[8,768]{1,0:T(8,128)}) custom-call(s32[32]{0:T(128)} %stack.539.slots.slots_a.slots_b, s32[32]{0:T(128)} %stack.539.slots.slots_a.slots_b, bf16[768,3072]{1,0:T(8,128)(2,1)} %get-tuple-element.239.dh_ref, bf16[768,768]{1,0:T(8,128)(2,1)} %bitcast.270, ...), custom_call_target="tpu_custom_call" | custom-call | flops 9059696640 | bytes 31457280 | tf_op jit(solution)/shard_map/pallas_call | solution.py:461
  176.8 2.3 collective-permute-start.33
  183.6 8.2 %shard_map.310 = (bf16[8,96,768]{2,1,0:T(8,128)(2,1)}, bf16[8,96,768]{2,1,0:T(8,128)(2,1)}, bf16[8,96,768]{2,1,0:T(8,128)(2,1)}, bf16[8,96,768]{2,1,0:T(8,128)(2,1)}) custom-call(s32[17]{0:T(128)} %stack.506.gpos, bf16[768,768]{1,0:T(8,128)(2,1)} %get-tuple-element.194.normed_ref, bf16[3,768,768]{2,1,0:T(8,128)(2,1)} %get-tuple-element.273.dt_ref, ...), custom_call_target="tpu_custom_call" | custom-call | flops 7247757312 | bytes 12582912 | tf_op jit(solution)/shard_map/pallas_call | solution.py:461
  193.5 2.4 collective-permute-start.43
  201.6 2.0 collective-permute-start.41
  203.6 9.8 %shard_map.311 = (bf16[768,768]{1,0:T(8,128)(2,1)}, f32[16,768]{1,0:T(8,128)}) custom-call(s32[32]{0:T(128)} %stack.539.slots.slots_a.slots_b, bf16[768,768]{1,0:T(8,128)(2,1)} %bitcast.272, f32[6,768]{1,0:T(8,128)} %reshape.329.emb_ref, f32[768,768]{1,0:T(8,128)} %get-tuple-element.272.dmid_ref, bf16[3,768,768]{2,1,0:T(8,128)(2,1)} %get-tuple-element.273.dt_ref, ...), custom_call_target="tpu_custom_call" | custom-call | flops 5435817984 | bytes 12582912 | tf_op jit(solution)/shard_map/pallas_call | solution.py:461
  214.5 2.0 add_convert_fusion.8
  219.8 3.1 %all-to-all-start.2 = ((f32[32,1,1926]{2,1,0:T(1,128)}), f32[32,1,1926]{2,1,0:T(1,128)S(1)}, u32[]{:S(2)}, u32[]{:S(2)}) async-start(f32[32,1,1926]{2,1,0:T(1,128)} %all_to_all.19), calls=%async_computation.2 | async-start | bytes 524288 | tf_op jit(solution)/shard_map/all_to_all | solution.py:910
  222.9 9.8 %shard_map.312 = bf16[768,768]{1,0:T(8,128)(2,1)} custom-call(s32[32]{0:T(128)} %stack.572.slots, bf16[768,3072]{1,0:T(8,128)(2,1)} %get-tuple-element.299.act_ref, f32[768,768]{1,0:T(8,128)} %get-tuple-element.240.middle_ref, f32[8,768]{1,0:T(8,128)} %reshape.312.vec_ref, bf16[4,96,768]{2,1,0:T(8,128)(2,1)} %pad_maximum_fusion.4.rest_0_, ...), custom_call_target="tpu_custom_call" | custom-call | flops 7247757312 | bytes 12582912 | tf_op jit(solution)/shard_map/pallas_call | solution.py:461
  237.2 3.9 %all-to-all-start.3 = ((bf16[4,192,768]{2,1,0:T(8,128)(2,1)}), bf16[4,192,768]{2,1,0:T(8,128)(2,1)S(1)}, u32[]{:S(2)}, u32[]{:S(2)}) async-start(bf16[4,192,768]{2,1,0:T(8,128)(2,1)} %broadcast_in_dim.14), calls=%async_computation.3 | async-start | bytes 2359296 | tf_op jit(solution)/shard_map/all_to_all | solution.py:672
  241.1 3.4 %collective-permute-start.48 = (bf16[96,768]{1,0:T(8,128)(2,1)S(1)}, bf16[96,768]{1,0:T(8,128)(2,1)S(1)}, u32[]{:S(2)}, u32[]{:S(2)}) collective-permute-start(bf16[96,768]{1,0:T(8,128)(2,1)S(1)} %get-tuple-element.351), channel_id=1, source_target_pairs={{0,6},{1,7},{2,0},{3,1},{4,2},{5,3},{6,4},{7,5},{8,14},{9,15},{10,... | collective-permute-start | bytes 442376 | tf_op jit(solution)/shard_map/ppermute | solution.py:664
  248.8 8.5 %collective-permute-done.47 = bf16[96,768]{1,0:T(8,128)(2,1)S(1)} collective-permute-done((bf16[96,768]{1,0:T(8,128)(2,1)S(1)}, bf16[96,768]{1,0:T(8,128)(2,1)S(1)}, u32[]{:S(2)}, u32[]{:S(2)}) %collective-permute-start.47) | collective-permute-done | bytes 147488 | tf_op jit(solution)/shard_map/ppermute | solution.py:664
  257.5 2.6 collective-permute-start.51
  264.4 2.5 collective-permute-done.50
  (262 shorter events, 68.4 us)
Async XLA Ops:
  27.2 37.5 %all-to-all-start = ((bf16[4,4,96,768]{3,2,1,0:T(8,128)(2,1)}), bf16[4,4,96,768]{3,2,1,0:T(8,128)(2,1)S(1)}, u32[]{:S(2)}, u32[]{:S(2)}) async-start(bf16[4,4,96,768]{3,2,1,0:T(8,128)(2,1)} %broadcast_in_dim.11), calls=%async_computation | async-start | bytes 4718592 | tf_op jit(solution)/shard_map/all_to_all | solution.py:672
  34.4 30.3 %collective-permute-start.5 = (bf16[192,768]{1,0:T(8,128)(2,1)S(1)}, bf16[192,768]{1,0:T(8,128)(2,1)}, u32[]{:S(2)}, u32[]{:S(2)}) collective-permute-start(bf16[192,768]{1,0:T(8,128)(2,1)S(1)} %pad_maximum_fusion.7), channel_id=1, source_target_pairs={{0,4},{1,5},{2,6},{3,7},{4,0},{5,1},{6,2},{7,3},{8,12},{9,13},{10,... | collective-permute-start | bytes 884744 | tf_op jit(solution)/shard_map/ppermute | solution.py:664
  36.3 28.4 %collective-permute-start.4 = (bf16[192,768]{1,0:T(8,128)(2,1)S(1)}, bf16[192,768]{1,0:T(8,128)(2,1)}, u32[]{:S(2)}, u32[]{:S(2)}) collective-permute-start(bf16[192,768]{1,0:T(8,128)(2,1)S(1)} %pad_maximum_fusion.7), channel_id=1, source_target_pairs={{0,2},{1,3},{2,4},{3,5},{4,6},{5,7},{6,0},{7,1},{8,10},{9,11},{10,... | collective-permute-start | bytes 884744 | tf_op jit(solution)/shard_map/ppermute | solution.py:664
  40.2 24.4 %collective-permute-start.8 = (bf16[16,768]{1,0:T(8,128)(2,1)S(1)}, bf16[16,768]{1,0:T(8,128)(2,1)S(1)}, u32[]{:S(2)}, u32[]{:S(2)}) collective-permute-start(bf16[16,768]{1,0:T(8,128)(2,1)S(1)} %get-tuple-element.187), channel_id=1, source_target_pairs={{0,4},{1,5},{2,6},{3,7},{4,0},{5,1},{6,2},{7,3},{8,12},{9,13},{10,... | collective-permute-start | bytes 73736 | tf_op jit(solution)/shard_map/ppermute | solution.py:664
  40.5 24.2 %collective-permute-start.7 = (bf16[16,768]{1,0:T(8,128)(2,1)S(1)}, bf16[16,768]{1,0:T(8,128)(2,1)S(1)}, u32[]{:S(2)}, u32[]{:S(2)}) collective-permute-start(bf16[16,768]{1,0:T(8,128)(2,1)S(1)} %get-tuple-element.187), channel_id=1, source_target_pairs={{0,2},{1,3},{2,4},{3,5},{4,6},{5,7},{6,0},{7,1},{8,10},{9,11},{10,... | collective-permute-start | bytes 73736 | tf_op jit(solution)/shard_map/ppermute | solution.py:664
  43.0 21.7 %collective-permute-start.9 = (bf16[16,768]{1,0:T(8,128)(2,1)S(1)}, bf16[16,768]{1,0:T(8,128)(2,1)S(1)}, u32[]{:S(2)}, u32[]{:S(2)}) collective-permute-start(bf16[16,768]{1,0:T(8,128)(2,1)S(1)} %get-tuple-element.187), channel_id=1, source_target_pairs={{0,6},{1,7},{2,0},{3,1},{4,2},{5,3},{6,4},{7,5},{8,14},{9,15},{10,... | collective-permute-start | bytes 73736 | tf_op jit(solution)/shard_map/ppermute | solution.py:664
  64.7 15.6 %collective-permute-start.10 = (bf16[16,96,768]{2,1,0:T(8,128)(2,1)S(1)}, bf16[16,96,768]{2,1,0:T(8,128)(2,1)}, u32[]{:S(2)}, u32[]{:S(2)}) collective-permute-start(bf16[16,96,768]{2,1,0:T(8,128)(2,1)S(1)} %bitcast.229), channel_id=1, source_target_pairs={{0,1},{1,0},{2,3},{3,2},{4,5},{5,4},{6,7},{7,6},{8,9},{9,8},{10,11... | collective-permute-start | bytes 7077896 | tf_op jit(solution)/shard_map/ppermute | solution.py:648
  69.1 34.1 %all-to-all-start.1 = ((bf16[4,4,96,768]{3,2,1,0:T(8,128)(2,1)}), bf16[4,4,96,768]{3,2,1,0:T(8,128)(2,1)}, u32[]{:S(2)}, u32[]{:S(2)}) async-start(bf16[4,4,96,768]{3,2,1,0:T(8,128)(2,1)} %broadcast_in_dim.12), calls=%async_computation.1 | async-start | bytes 4718592 | tf_op jit(solution)/shard_map/all_to_all | solution.py:672
  74.5 20.3 %collective-permute-start.14 = (bf16[192,768]{1,0:T(8,128)(2,1)S(1)}, bf16[192,768]{1,0:T(8,128)(2,1)}, u32[]{:S(2)}, u32[]{:S(2)}) collective-permute-start(bf16[192,768]{1,0:T(8,128)(2,1)S(1)} %slice.406), channel_id=1, source_target_pairs={{0,6},{1,7},{2,0},{3,1},{4,2},{5,3},{6,4},{7,5},{8,14},{9,15},{10,... | collective-permute-start | bytes 884744 | tf_op jit(solution)/shard_map/ppermute | solution.py:664
  76.2 27.0 %collective-permute-start.13 = (bf16[192,768]{1,0:T(8,128)(2,1)S(1)}, bf16[192,768]{1,0:T(8,128)(2,1)}, u32[]{:S(2)}, u32[]{:S(2)}) collective-permute-start(bf16[192,768]{1,0:T(8,128)(2,1)S(1)} %slice.406), channel_id=1, source_target_pairs={{0,4},{1,5},{2,6},{3,7},{4,0},{5,1},{6,2},{7,3},{8,12},{9,13},{10,... | collective-permute-start | bytes 884744 | tf_op jit(solution)/shard_map/ppermute | solution.py:664
  76.9 26.2 %collective-permute-start.12 = (bf16[192,768]{1,0:T(8,128)(2,1)S(1)}, bf16[192,768]{1,0:T(8,128)(2,1)}, u32[]{:S(2)}, u32[]{:S(2)}) collective-permute-start(bf16[192,768]{1,0:T(8,128)(2,1)S(1)} %slice.406), channel_id=1, source_target_pairs={{0,2},{1,3},{2,4},{3,5},{4,6},{5,7},{6,0},{7,1},{8,10},{9,11},{10,... | collective-permute-start | bytes 884744 | tf_op jit(solution)/shard_map/ppermute | solution.py:664
  79.1 24.1 %collective-permute-start.15 = (bf16[4,96,768]{2,1,0:T(8,128)(2,1)}, bf16[4,96,768]{2,1,0:T(8,128)(2,1)}, u32[]{:S(2)}, u32[]{:S(2)}) collective-permute-start(bf16[4,96,768]{2,1,0:T(8,128)(2,1)} %pad_maximum_fusion.4.rest_0_), channel_id=1, source_target_pairs={{0,1},{1,0},{2,3},{3,2},{4,5},{5,4},{6,7},{7,6},{8,9},{9,8},{10,11... | collective-permute-start | bytes 1769480 | tf_op jit(solution)/shard_map/ppermute | solution.py:648
  103.3 24.5 %collective-permute-start.19 = (bf16[96,768]{1,0:T(8,128)(2,1)S(1)}, bf16[96,768]{1,0:T(8,128)(2,1)S(1)}, u32[]{:S(2)}, u32[]{:S(2)}) collective-permute-start(bf16[96,768]{1,0:T(8,128)(2,1)S(1)} %get-tuple-element.222), channel_id=1, source_target_pairs={{0,6},{1,7},{2,0},{3,1},{4,2},{5,3},{6,4},{7,5},{8,14},{9,15},{10,... | collective-permute-start | bytes 442376 | tf_op jit(solution)/shard_map/ppermute | solution.py:664
  104.0 23.8 %collective-permute-start.18 = (bf16[96,768]{1,0:T(8,128)(2,1)S(1)}, bf16[96,768]{1,0:T(8,128)(2,1)S(1)}, u32[]{:S(2)}, u32[]{:S(2)}) collective-permute-start(bf16[96,768]{1,0:T(8,128)(2,1)S(1)} %get-tuple-element.222), channel_id=1, source_target_pairs={{0,4},{1,5},{2,6},{3,7},{4,0},{5,1},{6,2},{7,3},{8,12},{9,13},{10,... | collective-permute-start | bytes 442376 | tf_op jit(solution)/shard_map/ppermute | solution.py:664
  105.6 22.2 %collective-permute-start.17 = (bf16[96,768]{1,0:T(8,128)(2,1)S(1)}, bf16[96,768]{1,0:T(8,128)(2,1)S(1)}, u32[]{:S(2)}, u32[]{:S(2)}) collective-permute-start(bf16[96,768]{1,0:T(8,128)(2,1)S(1)} %get-tuple-element.222), channel_id=1, source_target_pairs={{0,2},{1,3},{2,4},{3,5},{4,6},{5,7},{6,0},{7,1},{8,10},{9,11},{10,... | collective-permute-start | bytes 442376 | tf_op jit(solution)/shard_map/ppermute | solution.py:664
  108.8 19.0 %collective-permute-start.20 = (bf16[8,96,768]{2,1,0:T(8,128)(2,1)S(1)}, bf16[8,96,768]{2,1,0:T(8,128)(2,1)S(1)}, u32[]{:S(2)}, u32[]{:S(2)}) collective-permute-start(bf16[8,96,768]{2,1,0:T(8,128)(2,1)S(1)} %bitcast.235), channel_id=1, source_target_pairs={{0,1},{1,0},{2,3},{3,2},{4,5},{5,4},{6,7},{7,6},{8,9},{9,8},{10,11... | collective-permute-start | bytes 3538952 | tf_op jit(solution)/shard_map/ppermute | solution.py:648
  128.6 24.2 %collective-permute-start.25 = (bf16[8,96,768]{2,1,0:T(8,128)(2,1)}, bf16[8,96,768]{2,1,0:T(8,128)(2,1)S(1)}, u32[]{:S(2)}, u32[]{:S(2)}) collective-permute-start(bf16[8,96,768]{2,1,0:T(8,128)(2,1)} %get-tuple-element.235), channel_id=1, source_target_pairs={{0,1},{1,0},{2,3},{3,2},{4,5},{5,4},{6,7},{7,6},{8,9},{9,8},{10,11... | collective-permute-start | bytes 3538952 | tf_op jit(solution)/shard_map/ppermute | solution.py:648
  131.3 21.5 %collective-permute-start.23 = (bf16[4,96,768]{2,1,0:T(8,128)(2,1)S(1)}, bf16[4,96,768]{2,1,0:T(8,128)(2,1)S(1)}, u32[]{:S(2)}, u32[]{:S(2)}) collective-permute-start(bf16[4,96,768]{2,1,0:T(8,128)(2,1)S(1)} %get-tuple-element.233), channel_id=1, source_target_pairs={{0,8},{8,0},{16,24},{24,16},{1,9},{9,1},{17,25},{25,17},{2,10},{10... | collective-permute-start | bytes 1769480 | tf_op jit(solution)/shard_map/ppermute | solution.py:652
  133.4 19.3 %collective-permute-start.24 = (bf16[4,96,768]{2,1,0:T(8,128)(2,1)S(1)}, bf16[4,96,768]{2,1,0:T(8,128)(2,1)S(1)}, u32[]{:S(2)}, u32[]{:S(2)}) collective-permute-start(bf16[4,96,768]{2,1,0:T(8,128)(2,1)S(1)} %get-tuple-element.234), channel_id=1, source_target_pairs={{0,16},{8,24},{16,0},{24,8},{1,17},{9,25},{17,1},{25,9},{2,18},{10... | collective-permute-start | bytes 1769480 | tf_op jit(solution)/shard_map/ppermute | solution.py:656
  153.1 23.3 %collective-permute-start.30 = (bf16[2,96,768]{2,1,0:T(8,128)(2,1)S(1)}, bf16[2,96,768]{2,1,0:T(8,128)(2,1)S(1)}, u32[]{:S(2)}, u32[]{:S(2)}) collective-permute-start(bf16[2,96,768]{2,1,0:T(8,128)(2,1)S(1)} %get-tuple-element.326), channel_id=1, source_target_pairs={{0,8},{8,0},{16,24},{24,16},{1,9},{9,1},{17,25},{25,17},{2,10},{10... | collective-permute-start | bytes 884744 | tf_op jit(solution)/shard_map/ppermute | solution.py:652
  153.7 22.7 %collective-permute-start.29 = (bf16[2,96,768]{2,1,0:T(8,128)(2,1)S(1)}, bf16[2,96,768]{2,1,0:T(8,128)(2,1)S(1)}, u32[]{:S(2)}, u32[]{:S(2)}) collective-permute-start(bf16[2,96,768]{2,1,0:T(8,128)(2,1)S(1)} %get-tuple-element.327), channel_id=1, source_target_pairs={{0,16},{8,24},{16,0},{24,8},{1,17},{9,25},{17,1},{25,9},{2,18},{10... | collective-permute-start | bytes 884744 | tf_op jit(solution)/shard_map/ppermute | solution.py:656
  154.4 26.2 %collective-permute-start.34 = (bf16[8,96,768]{2,1,0:T(8,128)(2,1)}, bf16[8,96,768]{2,1,0:T(8,128)(2,1)S(1)}, u32[]{:S(2)}, u32[]{:S(2)}) collective-permute-start(bf16[8,96,768]{2,1,0:T(8,128)(2,1)} %get-tuple-element.261), channel_id=1, source_target_pairs={{0,1},{1,0},{2,3},{3,2},{4,5},{5,4},{6,7},{7,6},{8,9},{9,8},{10,11... | collective-permute-start | bytes 3538952 | tf_op jit(solution)/shard_map/ppermute | solution.py:648
  156.2 20.2 %collective-permute-start.27 = (bf16[4,96,768]{2,1,0:T(8,128)(2,1)S(1)}, bf16[4,96,768]{2,1,0:T(8,128)(2,1)S(1)}, u32[]{:S(2)}, u32[]{:S(2)}) collective-permute-start(bf16[4,96,768]{2,1,0:T(8,128)(2,1)S(1)} %get-tuple-element.244), channel_id=1, source_target_pairs={{0,8},{8,0},{16,24},{24,16},{1,9},{9,1},{17,25},{25,17},{2,10},{10... | collective-permute-start | bytes 1769480 | tf_op jit(solution)/shard_map/ppermute | solution.py:652
  156.8 19.6 %collective-permute-start.28 = (bf16[4,96,768]{2,1,0:T(8,128)(2,1)S(1)}, bf16[4,96,768]{2,1,0:T(8,128)(2,1)S(1)}, u32[]{:S(2)}, u32[]{:S(2)}) collective-permute-start(bf16[4,96,768]{2,1,0:T(8,128)(2,1)S(1)} %get-tuple-element.245), channel_id=1, source_target_pairs={{0,16},{8,24},{16,0},{24,8},{1,17},{9,25},{17,1},{25,9},{2,18},{10... | collective-permute-start | bytes 1769480 | tf_op jit(solution)/shard_map/ppermute | solution.py:656
  176.8 15.0 %collective-permute-start.33 = (bf16[96,768]{1,0:T(8,128)(2,1)S(1)}, bf16[96,768]{1,0:T(8,128)(2,1)S(1)}, u32[]{:S(2)}, u32[]{:S(2)}) collective-permute-start(bf16[96,768]{1,0:T(8,128)(2,1)S(1)} %get-tuple-element.359), channel_id=1, source_target_pairs={{0,6},{1,7},{2,0},{3,1},{4,2},{5,3},{6,4},{7,5},{8,14},{9,15},{10,... | collective-permute-start | bytes 442376 | tf_op jit(solution)/shard_map/ppermute | solution.py:664
  193.5 19.9 %collective-permute-start.43 = (bf16[96,768]{1,0:T(8,128)(2,1)}, bf16[96,768]{1,0:T(8,128)(2,1)S(1)}, u32[]{:S(2)}, u32[]{:S(2)}) collective-permute-start(bf16[96,768]{1,0:T(8,128)(2,1)} %get-tuple-element.355), channel_id=1, source_target_pairs={{0,6},{1,7},{2,0},{3,1},{4,2},{5,3},{6,4},{7,5},{8,14},{9,15},{10,... | collective-permute-start | bytes 442376 | tf_op jit(solution)/shard_map/ppermute | solution.py:664
  195.9 17.5 %collective-permute-start.42 = (bf16[96,768]{1,0:T(8,128)(2,1)}, bf16[96,768]{1,0:T(8,128)(2,1)S(1)}, u32[]{:S(2)}, u32[]{:S(2)}) collective-permute-start(bf16[96,768]{1,0:T(8,128)(2,1)} %get-tuple-element.356), channel_id=1, source_target_pairs={{0,4},{1,5},{2,6},{3,7},{4,0},{5,1},{6,2},{7,3},{8,12},{9,13},{10,... | collective-permute-start | bytes 442376 | tf_op jit(solution)/shard_map/ppermute | solution.py:664
  199.1 15.0 %collective-permute-start.39 = (bf16[4,96,768]{2,1,0:T(8,128)(2,1)}, bf16[4,96,768]{2,1,0:T(8,128)(2,1)S(1)}, u32[]{:S(2)}, u32[]{:S(2)}) collective-permute-start(bf16[4,96,768]{2,1,0:T(8,128)(2,1)} %get-tuple-element.270), channel_id=1, source_target_pairs={{0,8},{8,0},{16,24},{24,16},{1,9},{9,1},{17,25},{25,17},{2,10},{10... | collective-permute-start | bytes 1769480 | tf_op jit(solution)/shard_map/ppermute | solution.py:652
  199.7 14.8 %collective-permute-start.40 = (bf16[4,96,768]{2,1,0:T(8,128)(2,1)}, bf16[4,96,768]{2,1,0:T(8,128)(2,1)}, u32[]{:S(2)}, u32[]{:S(2)}) collective-permute-start(bf16[4,96,768]{2,1,0:T(8,128)(2,1)} %get-tuple-element.271), channel_id=1, source_target_pairs={{0,16},{8,24},{16,0},{24,8},{1,17},{9,25},{17,1},{25,9},{2,18},{10... | collective-permute-start | bytes 1769480 | tf_op jit(solution)/shard_map/ppermute | solution.py:656
  216.5 17.2 %collective-permute-start.45 = (bf16[2,96,768]{2,1,0:T(8,128)(2,1)}, bf16[2,96,768]{2,1,0:T(8,128)(2,1)}, u32[]{:S(2)}, u32[]{:S(2)}) collective-permute-start(bf16[2,96,768]{2,1,0:T(8,128)(2,1)} %get-tuple-element.316), channel_id=1, source_target_pairs={{0,8},{8,0},{16,24},{24,16},{1,9},{9,1},{17,25},{25,17},{2,10},{10... | collective-permute-start | bytes 884744 | tf_op jit(solution)/shard_map/ppermute | solution.py:652
  218.0 15.7 %collective-permute-start.44 = (bf16[2,96,768]{2,1,0:T(8,128)(2,1)}, bf16[2,96,768]{2,1,0:T(8,128)(2,1)}, u32[]{:S(2)}, u32[]{:S(2)}) collective-permute-start(bf16[2,96,768]{2,1,0:T(8,128)(2,1)} %get-tuple-element.317), channel_id=1, source_target_pairs={{0,16},{8,24},{16,0},{24,8},{1,17},{9,25},{17,1},{25,9},{2,18},{10... | collective-permute-start | bytes 884744 | tf_op jit(solution)/shard_map/ppermute | solution.py:656
  237.2 20.2 %all-to-all-start.3 = ((bf16[4,192,768]{2,1,0:T(8,128)(2,1)}), bf16[4,192,768]{2,1,0:T(8,128)(2,1)S(1)}, u32[]{:S(2)}, u32[]{:S(2)}) async-start(bf16[4,192,768]{2,1,0:T(8,128)(2,1)} %broadcast_in_dim.14), calls=%async_computation.3 | async-start | bytes 2359296 | tf_op jit(solution)/shard_map/all_to_all | solution.py:672
  (56 other events, 441.4 us)

commit v7 on v6

--- a/solution.py
+++ b/solution.py
@@ -895,8 +895,7 @@
             (sa.r1, sums, active, mine_c, hb_lanes, sb.r3)
         )
         sa.add_two()
-        sums, active = tie((sums, active), sa.on)
-        result = compute_f3(active, middle, vecs, gc)
+        sums = tie(sums, sa.on)
 
     lines = sums.shape[0]
     if not fast:
@@ -909,8 +908,9 @@
         everyone = jnp.broadcast_to(payload[None], (nd,) + payload.shape).reshape(nd * nf, payload.shape[1])
         moved = lax.all_to_all(everyone, ("dp", "fsdp"), 0, 0, tiled=True)
         mine_b = sb.total()
-        sa.r2, moved, mine_b, mine_c, result = lax.optimization_barrier((sa.r2, moved, mine_b, mine_c, result))
+        sa.r2, mine_b, mine_c, active = lax.optimization_barrier((sa.r2, mine_b, mine_c, active))
         sa.three()
+        result = compute_f3(tie(active, sa.h3), middle, vecs, gc)
         mine_b, mine_c = tie((mine_b, mine_c), sa.h3)
         out_bc = columns(jnp.concatenate([mine_b, mine_c], axis=0))
     else:
@@ -922,7 +922,7 @@
     if not fast:
         result = compute_f3(active, middle, vecs, gc)
     if fast:
-        sa.r3, out_bc, moved = lax.optimization_barrier((sa.r3, out_bc, moved))
+        sa.r3, out_bc, moved, result = lax.optimization_barrier((sa.r3, out_bc, moved, result))
         out_a = quarters(spread(sa.total()), d)
         out_b = out_bc[:, :b].astype(f32)
         down_grad = out_bc[:, b:].astype(f32).reshape(4 * b, width)

time: 270 us -> 269 us (level)
    ppermute x24, waiting for transfers between devices: 45.6 us -> 36.6 us  [z_shift(): return lax.ppermute(v, 'fsdp', [(i, (i + 2 * k) % 8) for i in range(8)])]
    all_to_all x3, waiting for transfers between devices: 0.01 us -> 3.24 us  [columns(): lax.all_to_all(jnp.broadcast_to(v[None], (4,) + v.shape), 'dp', 0, 0, til...]
  transfers between devices with their start and end apart: 56 -> 56, of which waited for: 15 -> 15; matrix products, arithmetic and copies ran while one was open for 10% -> 12% of each run, Pallas kernels for 36% -> 36%
where the time goes in v7:
time: 269 us; the launch traced here: 268 us
  Pallas kernels  95.9 us (36%)
  starting transfers between devices  70.6 us (26%)
  waiting for transfers between devices  53 us (20%)
  local copies, waits for them, and re-layouts  27.4 us (10%)
  other arithmetic  16.8 us (6%)
    pallas_call x7, Pallas kernels, call(): pl.pallas_call(kernel, grid=grid, in_specs=in_specs, out_shape=out_shape,...  95.9 us
    ppermute x24, starting transfers between devices, z_shift(): return lax.ppermute(v, 'fsdp', [(i, (i + 2 * k) % 8) for i in range(8)])  37.2 us
    ppermute x24, waiting for transfers between devices, z_shift(): return lax.ppermute(v, 'fsdp', [(i, (i + 2 * k) % 8) for i in range(8)])  36.6 us
    all_to_all x3, starting transfers between devices, columns(): lax.all_to_all(jnp.broadcast_to(v[None], (4,) + v.shape), 'dp', 0, 0, til...  12.6 us
    convert_element_type x9, other arithmetic, plus(): return sum((v.astype(f32) for v in values)).astype(bf16)  7.58 us
    ppermute x7, starting transfers between devices, x_swap(): return lax.ppermute(v, 'dp', xor_perm(4, 1))  7.31 us
    ppermute x7, starting transfers between devices, y_swap(): return lax.ppermute(v, 'dp', xor_perm(4, 2))  7.12 us
  transfers between devices with their start and end apart: 56, of which 15 were waited for; matrix products, arithmetic and copies ran while one was open for 12% of the time, Pallas kernels for 36%

profile of v7, /device:TPU:0, one launch (start us, length us, event | category | flops | bytes accessed | tf_op | source)
XLA Modules:
  0.0 267.9 jit_solution(5489572001138067922)
XLA Ops:
  5.6 5.0 %collective-permute-start.2 = (bf16[112,768]{1,0:T(8,128)(2,1)}, bf16[112,768]{1,0:T(8,128)(2,1)S(1)}, u32[]{:S(2)}, u32[]{:S(2)}) collective-permute-start(bf16[112,768]{1,0:T(8,128)(2,1)} %pad_maximum_fusion.10), channel_id=1, source_target_pairs={{0,6},{1,7},{2,0},{3,1},{4,2},{5,3},{6,4},{7,5},{8,14},{9,15},{10,... | collective-permute-start | bytes 516104 | tf_op jit(solution)/shard_map/ppermute | solution.py:664
  15.9 9.5 %collective-permute-done.1 = bf16[112,768]{1,0:T(8,128)(2,1)S(1)} collective-permute-done((bf16[112,768]{1,0:T(8,128)(2,1)}, bf16[112,768]{1,0:T(8,128)(2,1)S(1)}, u32[]{:S(2)}, u32[]{:S(2)}) %collective-permute-start.1) | collective-permute-done | bytes 172064 | tf_op jit(solution)/shard_map/ppermute | solution.py:664
  27.2 4.6 %all-to-all-start = ((bf16[4,4,96,768]{3,2,1,0:T(8,128)(2,1)}), bf16[4,4,96,768]{3,2,1,0:T(8,128)(2,1)S(1)}, u32[]{:S(2)}, u32[]{:S(2)}) async-start(bf16[4,4,96,768]{3,2,1,0:T(8,128)(2,1)} %broadcast_in_dim.11), calls=%async_computation | async-start | bytes 4718592 | tf_op jit(solution)/shard_map/all_to_all | solution.py:672
  34.4 1.9 collective-permute-start.5
  36.3 1.9 collective-permute-start.4
  40.5 2.3 collective-permute-start.7
  43.0 3.2 %collective-permute-start.9 = (bf16[16,768]{1,0:T(8,128)(2,1)S(1)}, bf16[16,768]{1,0:T(8,128)(2,1)S(1)}, u32[]{:S(2)}, u32[]{:S(2)}) collective-permute-start(bf16[16,768]{1,0:T(8,128)(2,1)S(1)} %get-tuple-element.187), channel_id=1, source_target_pairs={{0,6},{1,7},{2,0},{3,1},{4,2},{5,3},{6,4},{7,5},{8,14},{9,15},{10,... | collective-permute-start | bytes 73736 | tf_op jit(solution)/shard_map/ppermute | solution.py:664
  46.2 18.4 %collective-permute-done.8 = bf16[16,768]{1,0:T(8,128)(2,1)S(1)} collective-permute-done((bf16[16,768]{1,0:T(8,128)(2,1)S(1)}, bf16[16,768]{1,0:T(8,128)(2,1)S(1)}, u32[]{:S(2)}, u32[]{:S(2)}) %collective-permute-start.8) | collective-permute-done | bytes 24608 | tf_op jit(solution)/shard_map/ppermute | solution.py:664
  69.1 4.5 %all-to-all-start.1 = ((bf16[4,4,96,768]{3,2,1,0:T(8,128)(2,1)}), bf16[4,4,96,768]{3,2,1,0:T(8,128)(2,1)}, u32[]{:S(2)}, u32[]{:S(2)}) async-start(bf16[4,4,96,768]{3,2,1,0:T(8,128)(2,1)} %broadcast_in_dim.12), calls=%async_computation.1 | async-start | bytes 4718592 | tf_op jit(solution)/shard_map/all_to_all | solution.py:672
  74.6 1.7 collective-permute-start.14
  80.4 14.5 %shard_map.306 = (bf16[768,768]{1,0:T(8,128)(2,1)}, bf16[3,768,768]{2,1,0:T(8,128)(2,1)}, bf16[36,256,128]{2,1,0:T(8,128)(2,1)}, bf16[768,768]{1,0:T(8,128)(2,1)...) custom-call(s32[32]{0:T(128)} %stack.539.slots.slots_a.slots_b, bf16[768,768]{1,0:T(8,128)(2,1)} %bitcast.271, ...), custom_call_target="tpu_custom_call" | custom-call | flops 10871635968 | bytes 20971520 | tf_op jit(solution)/shard_map/pallas_call | solution.py:461
  94.9 8.3 %collective-permute-done.13 = bf16[192,768]{1,0:T(8,128)(2,1)} collective-permute-done((bf16[192,768]{1,0:T(8,128)(2,1)S(1)}, bf16[192,768]{1,0:T(8,128)(2,1)}, u32[]{:S(2)}, u32[]{:S(2)}) %collective-permute-start.13) | collective-permute-done | bytes 294944 | tf_op jit(solution)/shard_map/ppermute | solution.py:664
  105.6 1.9 collective-permute-start.17
  110.3 17.5 %shard_map.307 = (bf16[768,3072]{1,0:T(8,128)(2,1)}, bf16[768,3072]{1,0:T(8,128)(2,1)}, bf16[8,96,768]{2,1,0:T(8,128)(2,1)}, bf16[8,96,768]{2,1,0:T(8,128)(2,1)}...) custom-call(s32[32]{0:T(128)} %stack.539.slots.slots_a.slots_b, s32[17]{0:T(128)} %stack.506.gpos, ...), custom_call_target="tpu_custom_call" | custom-call | flops 14495514624 | bytes 20971520 | tf_op jit(solution)/shard_map/pallas_call | solution.py:461
  128.7 2.3 collective-permute-done.21
  131.4 2.1 collective-permute-start.23
  135.8 17.0 %shard_map.308 = (bf16[768,3072]{1,0:T(8,128)(2,1)}, f32[4,768]{1,0:T(4,128)}, f32[8,768]{1,0:T(8,128)}, bf16[8,96,768]{2,1,0:T(8,128)(2,1)}, bf16[8,96,768]{2,1...) custom-call(s32[32]{0:T(128)} %stack.572.slots, s32[17]{0:T(128)} %stack.506.gpos, ...), custom_call_target="tpu_custom_call" | custom-call | flops 14495514624 | bytes 20971520 | tf_op jit(solution)/shard_map/pallas_call | solution.py:461
  157.6 18.8 %shard_map.309 = (f32[768,768]{1,0:T(8,128)}, bf16[768,768]{1,0:T(8,128)(2,1)}, bf16[3,768,768]{2,1,0:T(8,128)(2,1)}, f32[8,768]{1,0:T(8,128)}) custom-call(s32[32]{0:T(128)} %stack.539.slots.slots_a.slots_b, s32[32]{0:T(128)} %stack.539.slots.slots_a.slots_b, bf16[768,3072]{1,0:T(8,128)(2,1)} %get-tuple-element.239.dh_ref, bf16[768,768]{1,0:T(8,128)(2,1)} %bitcast.270, ...), custom_call_target="tpu_custom_call" | custom-call | flops 9059696640 | bytes 31457280 | tf_op jit(solution)/shard_map/pallas_call | solution.py:461
  176.8 2.3 collective-permute-start.33
  184.3 8.2 %shard_map.310 = (bf16[8,96,768]{2,1,0:T(8,128)(2,1)}, bf16[8,96,768]{2,1,0:T(8,128)(2,1)}, bf16[8,96,768]{2,1,0:T(8,128)(2,1)}, bf16[8,96,768]{2,1,0:T(8,128)(2,1)}) custom-call(s32[17]{0:T(128)} %stack.506.gpos, bf16[768,768]{1,0:T(8,128)(2,1)} %get-tuple-element.194.normed_ref, bf16[3,768,768]{2,1,0:T(8,128)(2,1)} %get-tuple-element.273.dt_ref, ...), custom_call_target="tpu_custom_call" | custom-call | flops 7247757312 | bytes 12582912 | tf_op jit(solution)/shard_map/pallas_call | solution.py:461
  196.2 2.4 collective-permute-start.43
  203.3 1.8 collective-permute-start.41
  205.1 10.2 %shard_map.311 = (bf16[768,768]{1,0:T(8,128)(2,1)}, f32[16,768]{1,0:T(8,128)}) custom-call(s32[32]{0:T(128)} %stack.539.slots.slots_a.slots_b, bf16[768,768]{1,0:T(8,128)(2,1)} %bitcast.272, f32[6,768]{1,0:T(8,128)} %reshape.329.emb_ref, f32[768,768]{1,0:T(8,128)} %get-tuple-element.272.dmid_ref, bf16[3,768,768]{2,1,0:T(8,128)(2,1)} %get-tuple-element.273.dt_ref, ...), custom_call_target="tpu_custom_call" | custom-call | flops 5435817984 | bytes 12582912 | tf_op jit(solution)/shard_map/pallas_call | solution.py:461
  216.7 2.0 add_convert_fusion.8
  222.0 3.1 %all-to-all-start.3 = ((f32[32,1,1926]{2,1,0:T(1,128)}), f32[32,1,1926]{2,1,0:T(1,128)S(1)}, u32[]{:S(2)}, u32[]{:S(2)}) async-start(f32[32,1,1926]{2,1,0:T(1,128)} %all_to_all.20), calls=%async_computation.3 | async-start | bytes 524288 | tf_op jit(solution)/shard_map/all_to_all | solution.py:909
  229.0 2.3 collective-permute-start.48
  233.0 2.5 all-to-all-done.3
  236.6 3.5 %all-to-all-start.2 = ((bf16[4,192,768]{2,1,0:T(8,128)(2,1)}), bf16[4,192,768]{2,1,0:T(8,128)(2,1)S(1)}, u32[]{:S(2)}, u32[]{:S(2)}) async-start(bf16[4,192,768]{2,1,0:T(8,128)(2,1)} %broadcast_in_dim.13), calls=%async_computation.2 | async-start | bytes 2359296 | tf_op jit(solution)/shard_map/all_to_all | solution.py:672
  240.1 9.7 %shard_map.312 = bf16[768,768]{1,0:T(8,128)(2,1)} custom-call(s32[32]{0:T(128)} %stack.572.slots, bf16[768,3072]{1,0:T(8,128)(2,1)} %get-tuple-element.306.act_ref, f32[768,768]{1,0:T(8,128)} %get-tuple-element.240.middle_ref, f32[8,768]{1,0:T(8,128)} %reshape.312.vec_ref, bf16[4,96,768]{2,1,0:T(8,128)(2,1)} %pad_maximum_fusion.4.rest_0_, ...), custom_call_target="tpu_custom_call" | custom-call | flops 7247757312 | bytes 12582912 | tf_op jit(solution)/shard_map/pallas_call | solution.py:461
  253.0 3.2 %all-to-all-done.2 = bf16[4,192,768]{2,1,0:T(8,128)(2,1)S(1)} async-done(((bf16[4,192,768]{2,1,0:T(8,128)(2,1)}), bf16[4,192,768]{2,1,0:T(8,128)(2,1)S(1)}, u32[]{:S(2)}, u32[]{:S(2)}) %all-to-all-start.2) | async-done | bytes 1179680 | tf_op jit(solution)/shard_map/all_to_all | solution.py:672
  262.3 1.7 collective-permute-done.51
  264.0 2.0 collective-permute-done.50
  (270 shorter events, 74.7 us)
Async XLA Ops:
  27.2 37.5 %all-to-all-start = ((bf16[4,4,96,768]{3,2,1,0:T(8,128)(2,1)}), bf16[4,4,96,768]{3,2,1,0:T(8,128)(2,1)S(1)}, u32[]{:S(2)}, u32[]{:S(2)}) async-start(bf16[4,4,96,768]{3,2,1,0:T(8,128)(2,1)} %broadcast_in_dim.11), calls=%async_computation | async-start | bytes 4718592 | tf_op jit(solution)/shard_map/all_to_all | solution.py:672
  34.4 30.3 %collective-permute-start.5 = (bf16[192,768]{1,0:T(8,128)(2,1)S(1)}, bf16[192,768]{1,0:T(8,128)(2,1)}, u32[]{:S(2)}, u32[]{:S(2)}) collective-permute-start(bf16[192,768]{1,0:T(8,128)(2,1)S(1)} %pad_maximum_fusion.7), channel_id=1, source_target_pairs={{0,4},{1,5},{2,6},{3,7},{4,0},{5,1},{6,2},{7,3},{8,12},{9,13},{10,... | collective-permute-start | bytes 884744 | tf_op jit(solution)/shard_map/ppermute | solution.py:664
  36.3 28.4 %collective-permute-start.4 = (bf16[192,768]{1,0:T(8,128)(2,1)S(1)}, bf16[192,768]{1,0:T(8,128)(2,1)}, u32[]{:S(2)}, u32[]{:S(2)}) collective-permute-start(bf16[192,768]{1,0:T(8,128)(2,1)S(1)} %pad_maximum_fusion.7), channel_id=1, source_target_pairs={{0,2},{1,3},{2,4},{3,5},{4,6},{5,7},{6,0},{7,1},{8,10},{9,11},{10,... | collective-permute-start | bytes 884744 | tf_op jit(solution)/shard_map/ppermute | solution.py:664
  40.2 24.4 %collective-permute-start.8 = (bf16[16,768]{1,0:T(8,128)(2,1)S(1)}, bf16[16,768]{1,0:T(8,128)(2,1)S(1)}, u32[]{:S(2)}, u32[]{:S(2)}) collective-permute-start(bf16[16,768]{1,0:T(8,128)(2,1)S(1)} %get-tuple-element.187), channel_id=1, source_target_pairs={{0,4},{1,5},{2,6},{3,7},{4,0},{5,1},{6,2},{7,3},{8,12},{9,13},{10,... | collective-permute-start | bytes 73736 | tf_op jit(solution)/shard_map/ppermute | solution.py:664
  40.5 24.2 %collective-permute-start.7 = (bf16[16,768]{1,0:T(8,128)(2,1)S(1)}, bf16[16,768]{1,0:T(8,128)(2,1)S(1)}, u32[]{:S(2)}, u32[]{:S(2)}) collective-permute-start(bf16[16,768]{1,0:T(8,128)(2,1)S(1)} %get-tuple-element.187), channel_id=1, source_target_pairs={{0,2},{1,3},{2,4},{3,5},{4,6},{5,7},{6,0},{7,1},{8,10},{9,11},{10,... | collective-permute-start | bytes 73736 | tf_op jit(solution)/shard_map/ppermute | solution.py:664
  43.0 21.7 %collective-permute-start.9 = (bf16[16,768]{1,0:T(8,128)(2,1)S(1)}, bf16[16,768]{1,0:T(8,128)(2,1)S(1)}, u32[]{:S(2)}, u32[]{:S(2)}) collective-permute-start(bf16[16,768]{1,0:T(8,128)(2,1)S(1)} %get-tuple-element.187), channel_id=1, source_target_pairs={{0,6},{1,7},{2,0},{3,1},{4,2},{5,3},{6,4},{7,5},{8,14},{9,15},{10,... | collective-permute-start | bytes 73736 | tf_op jit(solution)/shard_map/ppermute | solution.py:664
  64.7 15.6 %collective-permute-start.10 = (bf16[16,96,768]{2,1,0:T(8,128)(2,1)S(1)}, bf16[16,96,768]{2,1,0:T(8,128)(2,1)}, u32[]{:S(2)}, u32[]{:S(2)}) collective-permute-start(bf16[16,96,768]{2,1,0:T(8,128)(2,1)S(1)} %bitcast.229), channel_id=1, source_target_pairs={{0,1},{1,0},{2,3},{3,2},{4,5},{5,4},{6,7},{7,6},{8,9},{9,8},{10,11... | collective-permute-start | bytes 7077896 | tf_op jit(solution)/shard_map/ppermute | solution.py:648
  69.1 34.1 %all-to-all-start.1 = ((bf16[4,4,96,768]{3,2,1,0:T(8,128)(2,1)}), bf16[4,4,96,768]{3,2,1,0:T(8,128)(2,1)}, u32[]{:S(2)}, u32[]{:S(2)}) async-start(bf16[4,4,96,768]{3,2,1,0:T(8,128)(2,1)} %broadcast_in_dim.12), calls=%async_computation.1 | async-start | bytes 4718592 | tf_op jit(solution)/shard_map/all_to_all | solution.py:672
  74.6 20.3 %collective-permute-start.14 = (bf16[192,768]{1,0:T(8,128)(2,1)S(1)}, bf16[192,768]{1,0:T(8,128)(2,1)}, u32[]{:S(2)}, u32[]{:S(2)}) collective-permute-start(bf16[192,768]{1,0:T(8,128)(2,1)S(1)} %slice.406), channel_id=1, source_target_pairs={{0,6},{1,7},{2,0},{3,1},{4,2},{5,3},{6,4},{7,5},{8,14},{9,15},{10,... | collective-permute-start | bytes 884744 | tf_op jit(solution)/shard_map/ppermute | solution.py:664
  76.3 27.0 %collective-permute-start.13 = (bf16[192,768]{1,0:T(8,128)(2,1)S(1)}, bf16[192,768]{1,0:T(8,128)(2,1)}, u32[]{:S(2)}, u32[]{:S(2)}) collective-permute-start(bf16[192,768]{1,0:T(8,128)(2,1)S(1)} %slice.406), channel_id=1, source_target_pairs={{0,4},{1,5},{2,6},{3,7},{4,0},{5,1},{6,2},{7,3},{8,12},{9,13},{10,... | collective-permute-start | bytes 884744 | tf_op jit(solution)/shard_map/ppermute | solution.py:664
  77.0 26.2 %collective-permute-start.12 = (bf16[192,768]{1,0:T(8,128)(2,1)S(1)}, bf16[192,768]{1,0:T(8,128)(2,1)}, u32[]{:S(2)}, u32[]{:S(2)}) collective-permute-start(bf16[192,768]{1,0:T(8,128)(2,1)S(1)} %slice.406), channel_id=1, source_target_pairs={{0,2},{1,3},{2,4},{3,5},{4,6},{5,7},{6,0},{7,1},{8,10},{9,11},{10,... | collective-permute-start | bytes 884744 | tf_op jit(solution)/shard_map/ppermute | solution.py:664
  79.2 24.1 %collective-permute-start.15 = (bf16[4,96,768]{2,1,0:T(8,128)(2,1)}, bf16[4,96,768]{2,1,0:T(8,128)(2,1)}, u32[]{:S(2)}, u32[]{:S(2)}) collective-permute-start(bf16[4,96,768]{2,1,0:T(8,128)(2,1)} %pad_maximum_fusion.4.rest_0_), channel_id=1, source_target_pairs={{0,1},{1,0},{2,3},{3,2},{4,5},{5,4},{6,7},{7,6},{8,9},{9,8},{10,11... | collective-permute-start | bytes 1769480 | tf_op jit(solution)/shard_map/ppermute | solution.py:648
  103.3 24.6 %collective-permute-start.19 = (bf16[96,768]{1,0:T(8,128)(2,1)S(1)}, bf16[96,768]{1,0:T(8,128)(2,1)S(1)}, u32[]{:S(2)}, u32[]{:S(2)}) collective-permute-start(bf16[96,768]{1,0:T(8,128)(2,1)S(1)} %get-tuple-element.222), channel_id=1, source_target_pairs={{0,6},{1,7},{2,0},{3,1},{4,2},{5,3},{6,4},{7,5},{8,14},{9,15},{10,... | collective-permute-start | bytes 442376 | tf_op jit(solution)/shard_map/ppermute | solution.py:664
  104.1 23.8 %collective-permute-start.18 = (bf16[96,768]{1,0:T(8,128)(2,1)S(1)}, bf16[96,768]{1,0:T(8,128)(2,1)S(1)}, u32[]{:S(2)}, u32[]{:S(2)}) collective-permute-start(bf16[96,768]{1,0:T(8,128)(2,1)S(1)} %get-tuple-element.222), channel_id=1, source_target_pairs={{0,4},{1,5},{2,6},{3,7},{4,0},{5,1},{6,2},{7,3},{8,12},{9,13},{10,... | collective-permute-start | bytes 442376 | tf_op jit(solution)/shard_map/ppermute | solution.py:664
  105.6 22.3 %collective-permute-start.17 = (bf16[96,768]{1,0:T(8,128)(2,1)S(1)}, bf16[96,768]{1,0:T(8,128)(2,1)S(1)}, u32[]{:S(2)}, u32[]{:S(2)}) collective-permute-start(bf16[96,768]{1,0:T(8,128)(2,1)S(1)} %get-tuple-element.222), channel_id=1, source_target_pairs={{0,2},{1,3},{2,4},{3,5},{4,6},{5,7},{6,0},{7,1},{8,10},{9,11},{10,... | collective-permute-start | bytes 442376 | tf_op jit(solution)/shard_map/ppermute | solution.py:664
  108.9 19.0 %collective-permute-start.20 = (bf16[8,96,768]{2,1,0:T(8,128)(2,1)S(1)}, bf16[8,96,768]{2,1,0:T(8,128)(2,1)S(1)}, u32[]{:S(2)}, u32[]{:S(2)}) collective-permute-start(bf16[8,96,768]{2,1,0:T(8,128)(2,1)S(1)} %bitcast.235), channel_id=1, source_target_pairs={{0,1},{1,0},{2,3},{3,2},{4,5},{5,4},{6,7},{7,6},{8,9},{9,8},{10,11... | collective-permute-start | bytes 3538952 | tf_op jit(solution)/shard_map/ppermute | solution.py:648
  128.7 24.1 %collective-permute-start.25 = (bf16[8,96,768]{2,1,0:T(8,128)(2,1)}, bf16[8,96,768]{2,1,0:T(8,128)(2,1)S(1)}, u32[]{:S(2)}, u32[]{:S(2)}) collective-permute-start(bf16[8,96,768]{2,1,0:T(8,128)(2,1)} %get-tuple-element.235), channel_id=1, source_target_pairs={{0,1},{1,0},{2,3},{3,2},{4,5},{5,4},{6,7},{7,6},{8,9},{9,8},{10,11... | collective-permute-start | bytes 3538952 | tf_op jit(solution)/shard_map/ppermute | solution.py:648
  131.4 21.4 %collective-permute-start.23 = (bf16[4,96,768]{2,1,0:T(8,128)(2,1)S(1)}, bf16[4,96,768]{2,1,0:T(8,128)(2,1)S(1)}, u32[]{:S(2)}, u32[]{:S(2)}) collective-permute-start(bf16[4,96,768]{2,1,0:T(8,128)(2,1)S(1)} %get-tuple-element.233), channel_id=1, source_target_pairs={{0,8},{8,0},{16,24},{24,16},{1,9},{9,1},{17,25},{25,17},{2,10},{10... | collective-permute-start | bytes 1769480 | tf_op jit(solution)/shard_map/ppermute | solution.py:652
  133.5 19.3 %collective-permute-start.24 = (bf16[4,96,768]{2,1,0:T(8,128)(2,1)S(1)}, bf16[4,96,768]{2,1,0:T(8,128)(2,1)S(1)}, u32[]{:S(2)}, u32[]{:S(2)}) collective-permute-start(bf16[4,96,768]{2,1,0:T(8,128)(2,1)S(1)} %get-tuple-element.234), channel_id=1, source_target_pairs={{0,16},{8,24},{16,0},{24,8},{1,17},{9,25},{17,1},{25,9},{2,18},{10... | collective-permute-start | bytes 1769480 | tf_op jit(solution)/shard_map/ppermute | solution.py:656
  153.1 23.3 %collective-permute-start.30 = (bf16[2,96,768]{2,1,0:T(8,128)(2,1)S(1)}, bf16[2,96,768]{2,1,0:T(8,128)(2,1)S(1)}, u32[]{:S(2)}, u32[]{:S(2)}) collective-permute-start(bf16[2,96,768]{2,1,0:T(8,128)(2,1)S(1)} %get-tuple-element.326), channel_id=1, source_target_pairs={{0,8},{8,0},{16,24},{24,16},{1,9},{9,1},{17,25},{25,17},{2,10},{10... | collective-permute-start | bytes 884744 | tf_op jit(solution)/shard_map/ppermute | solution.py:652
  153.8 22.7 %collective-permute-start.29 = (bf16[2,96,768]{2,1,0:T(8,128)(2,1)S(1)}, bf16[2,96,768]{2,1,0:T(8,128)(2,1)S(1)}, u32[]{:S(2)}, u32[]{:S(2)}) collective-permute-start(bf16[2,96,768]{2,1,0:T(8,128)(2,1)S(1)} %get-tuple-element.327), channel_id=1, source_target_pairs={{0,16},{8,24},{16,0},{24,8},{1,17},{9,25},{17,1},{25,9},{2,18},{10... | collective-permute-start | bytes 884744 | tf_op jit(solution)/shard_map/ppermute | solution.py:656
  154.4 26.8 %collective-permute-start.34 = (bf16[8,96,768]{2,1,0:T(8,128)(2,1)}, bf16[8,96,768]{2,1,0:T(8,128)(2,1)S(1)}, u32[]{:S(2)}, u32[]{:S(2)}) collective-permute-start(bf16[8,96,768]{2,1,0:T(8,128)(2,1)} %get-tuple-element.261), channel_id=1, source_target_pairs={{0,1},{1,0},{2,3},{3,2},{4,5},{5,4},{6,7},{7,6},{8,9},{9,8},{10,11... | collective-permute-start | bytes 3538952 | tf_op jit(solution)/shard_map/ppermute | solution.py:648
  156.3 20.2 %collective-permute-start.27 = (bf16[4,96,768]{2,1,0:T(8,128)(2,1)S(1)}, bf16[4,96,768]{2,1,0:T(8,128)(2,1)S(1)}, u32[]{:S(2)}, u32[]{:S(2)}) collective-permute-start(bf16[4,96,768]{2,1,0:T(8,128)(2,1)S(1)} %get-tuple-element.244), channel_id=1, source_target_pairs={{0,8},{8,0},{16,24},{24,16},{1,9},{9,1},{17,25},{25,17},{2,10},{10... | collective-permute-start | bytes 1769480 | tf_op jit(solution)/shard_map/ppermute | solution.py:652
  156.9 19.6 %collective-permute-start.28 = (bf16[4,96,768]{2,1,0:T(8,128)(2,1)S(1)}, bf16[4,96,768]{2,1,0:T(8,128)(2,1)S(1)}, u32[]{:S(2)}, u32[]{:S(2)}) collective-permute-start(bf16[4,96,768]{2,1,0:T(8,128)(2,1)S(1)} %get-tuple-element.245), channel_id=1, source_target_pairs={{0,16},{8,24},{16,0},{24,8},{1,17},{9,25},{17,1},{25,9},{2,18},{10... | collective-permute-start | bytes 1769480 | tf_op jit(solution)/shard_map/ppermute | solution.py:656
  176.8 15.6 %collective-permute-start.33 = (bf16[96,768]{1,0:T(8,128)(2,1)S(1)}, bf16[96,768]{1,0:T(8,128)(2,1)S(1)}, u32[]{:S(2)}, u32[]{:S(2)}) collective-permute-start(bf16[96,768]{1,0:T(8,128)(2,1)S(1)} %get-tuple-element.359), channel_id=1, source_target_pairs={{0,6},{1,7},{2,0},{3,1},{4,2},{5,3},{6,4},{7,5},{8,14},{9,15},{10,... | collective-permute-start | bytes 442376 | tf_op jit(solution)/shard_map/ppermute | solution.py:664
  196.2 19.1 %collective-permute-start.43 = (bf16[96,768]{1,0:T(8,128)(2,1)}, bf16[96,768]{1,0:T(8,128)(2,1)S(1)}, u32[]{:S(2)}, u32[]{:S(2)}) collective-permute-start(bf16[96,768]{1,0:T(8,128)(2,1)} %get-tuple-element.355), channel_id=1, source_target_pairs={{0,6},{1,7},{2,0},{3,1},{4,2},{5,3},{6,4},{7,5},{8,14},{9,15},{10,... | collective-permute-start | bytes 442376 | tf_op jit(solution)/shard_map/ppermute | solution.py:664
  198.7 16.7 %collective-permute-start.42 = (bf16[96,768]{1,0:T(8,128)(2,1)}, bf16[96,768]{1,0:T(8,128)(2,1)}, u32[]{:S(2)}, u32[]{:S(2)}) collective-permute-start(bf16[96,768]{1,0:T(8,128)(2,1)} %get-tuple-element.356), channel_id=1, source_target_pairs={{0,4},{1,5},{2,6},{3,7},{4,0},{5,1},{6,2},{7,3},{8,12},{9,13},{10,... | collective-permute-start | bytes 442376 | tf_op jit(solution)/shard_map/ppermute | solution.py:664
  201.2 15.1 %collective-permute-start.39 = (bf16[4,96,768]{2,1,0:T(8,128)(2,1)}, bf16[4,96,768]{2,1,0:T(8,128)(2,1)S(1)}, u32[]{:S(2)}, u32[]{:S(2)}) collective-permute-start(bf16[4,96,768]{2,1,0:T(8,128)(2,1)} %get-tuple-element.270), channel_id=1, source_target_pairs={{0,8},{8,0},{16,24},{24,16},{1,9},{9,1},{17,25},{25,17},{2,10},{10... | collective-permute-start | bytes 1769480 | tf_op jit(solution)/shard_map/ppermute | solution.py:652
  229.0 24.0 %collective-permute-start.48 = (bf16[96,768]{1,0:T(8,128)(2,1)S(1)}, bf16[96,768]{1,0:T(8,128)(2,1)S(1)}, u32[]{:S(2)}, u32[]{:S(2)}) collective-permute-start(bf16[96,768]{1,0:T(8,128)(2,1)S(1)} %get-tuple-element.351), channel_id=1, source_target_pairs={{0,6},{1,7},{2,0},{3,1},{4,2},{5,3},{6,4},{7,5},{8,14},{9,15},{10,... | collective-permute-start | bytes 442376 | tf_op jit(solution)/shard_map/ppermute | solution.py:664
  231.4 21.6 %collective-permute-start.47 = (bf16[96,768]{1,0:T(8,128)(2,1)S(1)}, bf16[96,768]{1,0:T(8,128)(2,1)S(1)}, u32[]{:S(2)}, u32[]{:S(2)}) collective-permute-start(bf16[96,768]{1,0:T(8,128)(2,1)S(1)} %get-tuple-element.352), channel_id=1, source_target_pairs={{0,4},{1,5},{2,6},{3,7},{4,0},{5,1},{6,2},{7,3},{8,12},{9,13},{10,... | collective-permute-start | bytes 442376 | tf_op jit(solution)/shard_map/ppermute | solution.py:664
  231.4 21.6 %collective-permute-start.46 = (bf16[96,768]{1,0:T(8,128)(2,1)S(1)}, bf16[96,768]{1,0:T(8,128)(2,1)S(1)}, u32[]{:S(2)}, u32[]{:S(2)}) collective-permute-start(bf16[96,768]{1,0:T(8,128)(2,1)S(1)} %get-tuple-element.353), channel_id=1, source_target_pairs={{0,2},{1,3},{2,4},{3,5},{4,6},{5,7},{6,0},{7,1},{8,10},{9,11},{10,... | collective-permute-start | bytes 442376 | tf_op jit(solution)/shard_map/ppermute | solution.py:664
  236.6 19.7 %all-to-all-start.2 = ((bf16[4,192,768]{2,1,0:T(8,128)(2,1)}), bf16[4,192,768]{2,1,0:T(8,128)(2,1)S(1)}, u32[]{:S(2)}, u32[]{:S(2)}) async-start(bf16[4,192,768]{2,1,0:T(8,128)(2,1)} %broadcast_in_dim.13), calls=%async_computation.2 | async-start | bytes 2359296 | tf_op jit(solution)/shard_map/all_to_all | solution.py:672
  (60 other events, 470.5 us)

commit v8 on v7

--- a/solution.py
+++ b/solution.py
@@ -818,8 +818,8 @@
     onehot = (here.reshape(nf * rows)[:, None] == steps[None, :]).astype(bf16)
     looked = jnp.dot(onehot, step_table, preferred_element_type=f32).astype(bf16)
     if fast:
-        looked, seg, pad, vecs, hb, gpos, slots, slots_c, marks = lax.optimization_barrier(
-            (looked.reshape(rows, width), seg, pad, vecs, hb, gpos, slots, slots_c, marks)
+        looked, seg, pad, vecs, hb, gpos, slots, slots_c, marks, own_c12 = lax.optimization_barrier(
+            (looked.reshape(rows, width), seg, pad, vecs, hb, gpos, slots, slots_c, marks, down_weight[b : 3 * b])
         )
         sent = jnp.pad(looked, ((0, 16 - rows), (0, 0)))
         got_e = [sent, z_shift(sent, 1), z_shift(sent, 2), z_shift(tie(sent, got1[3]), 3)]
@@ -838,7 +838,7 @@
         ga = Group([mine_a, core_a], quarter_major, slots)
         mine_b = columns(rows_of(got1, 0, b))
         c0 = rows_of(got1, b, b)
-        got2 = along_z(tie(down_weight[b : 3 * b], got1))
+        got2 = along_z(tie(own_c12, got1))
         tok_in = tie(tok, (core_a, emb))
     else:
         tok_in = tok
@@ -878,7 +878,7 @@
     if fast:
         dt, sb.r1, sc.r2, hb_sum = lax.optimization_barrier((dt, sb.r1, sc.r2, hb_sum))
         sb.two()
-        sc.three()
+        sc.three((sb.got[1],))
     grads_a = compute_ga(normed, attended, dt, dbr, gpos)
     if fast:
         grads_a, sc.r3, sb.r2, dt = lax.optimization_barrier((grads_a, sc.r3, sb.r2, dt))

time: 269 us -> 269 us (level)
  transfers between devices with their start and end apart: 56 -> 56, of which waited for: 15 -> 14; matrix products, arithmetic and copies ran while one was open for 12% -> 13% of each run, Pallas kernels for 36% -> 36%
where the time goes in v8:
time: 269 us; the launch traced here: 268 us
  Pallas kernels  96.1 us (36%)
  starting transfers between devices  68.8 us (26%)
  waiting for transfers between devices  51.3 us (19%)
  local copies, waits for them, and re-layouts  29.5 us (11%)
  other arithmetic  18.6 us (7%)
    pallas_call x7, Pallas kernels, call(): pl.pallas_call(kernel, grid=grid, in_specs=in_specs, out_shape=out_shape,...  96.1 us
    ppermute x24, starting transfers between devices, z_shift(): return lax.ppermute(v, 'fsdp', [(i, (i + 2 * k) % 8) for i in range(8)])  35.4 us
    ppermute x24, waiting for transfers between devices, z_shift(): return lax.ppermute(v, 'fsdp', [(i, (i + 2 * k) % 8) for i in range(8)])  34.8 us
    all_to_all x3, starting transfers between devices, columns(): lax.all_to_all(jnp.broadcast_to(v[None], (4,) + v.shape), 'dp', 0, 0, til...  12.6 us
    convert_element_type x9, other arithmetic, plus(): return sum((v.astype(f32) for v in values)).astype(bf16)  7.58 us
    ppermute x7, starting transfers between devices, x_swap(): return lax.ppermute(v, 'dp', xor_perm(4, 1))  7.36 us
    ppermute x7, starting transfers between devices, y_swap(): return lax.ppermute(v, 'dp', xor_perm(4, 2))  7.06 us
  transfers between devices with their start and end apart: 56, of which 14 were waited for; matrix products, arithmetic and copies ran while one was open for 13% of the time, Pallas kernels for 36%

profile of v8, /device:TPU:0, one launch (start us, length us, event | category | flops | bytes accessed | tf_op | source)
XLA Modules:
  0.0 268.0 jit_solution(4845555873040991511)
XLA Ops:
  5.6 5.0 %collective-permute-start.2 = (bf16[112,768]{1,0:T(8,128)(2,1)}, bf16[112,768]{1,0:T(8,128)(2,1)S(1)}, u32[]{:S(2)}, u32[]{:S(2)}) collective-permute-start(bf16[112,768]{1,0:T(8,128)(2,1)} %pad_maximum_fusion.10), channel_id=1, source_target_pairs={{0,6},{1,7},{2,0},{3,1},{4,2},{5,3},{6,4},{7,5},{8,14},{9,15},{10,... | collective-permute-start | bytes 516104 | tf_op jit(solution)/shard_map/ppermute | solution.py:664
  16.1 9.3 %collective-permute-done.1 = bf16[112,768]{1,0:T(8,128)(2,1)S(1)} collective-permute-done((bf16[112,768]{1,0:T(8,128)(2,1)}, bf16[112,768]{1,0:T(8,128)(2,1)S(1)}, u32[]{:S(2)}, u32[]{:S(2)}) %collective-permute-start.1) | collective-permute-done | bytes 172064 | tf_op jit(solution)/shard_map/ppermute | solution.py:664
  27.2 4.6 %all-to-all-start = ((bf16[4,4,96,768]{3,2,1,0:T(8,128)(2,1)}), bf16[4,4,96,768]{3,2,1,0:T(8,128)(2,1)S(1)}, u32[]{:S(2)}, u32[]{:S(2)}) async-start(bf16[4,4,96,768]{3,2,1,0:T(8,128)(2,1)} %broadcast_in_dim.11), calls=%async_computation | async-start | bytes 4718592 | tf_op jit(solution)/shard_map/all_to_all | solution.py:672
  35.3 1.9 collective-permute-start.5
  37.2 1.9 collective-permute-start.4
  44.6 2.3 collective-permute-start.7
  48.4 17.1 %collective-permute-done.8 = bf16[16,768]{1,0:T(8,128)(2,1)S(1)} collective-permute-done((bf16[16,768]{1,0:T(8,128)(2,1)S(1)}, bf16[16,768]{1,0:T(8,128)(2,1)S(1)}, u32[]{:S(2)}, u32[]{:S(2)}) %collective-permute-start.8) | collective-permute-done | bytes 24608 | tf_op jit(solution)/shard_map/ppermute | solution.py:664
  70.0 4.5 %all-to-all-start.1 = ((bf16[4,4,96,768]{3,2,1,0:T(8,128)(2,1)}), bf16[4,4,96,768]{3,2,1,0:T(8,128)(2,1)}, u32[]{:S(2)}, u32[]{:S(2)}) async-start(bf16[4,4,96,768]{3,2,1,0:T(8,128)(2,1)} %broadcast_in_dim.12), calls=%async_computation.1 | async-start | bytes 4718592 | tf_op jit(solution)/shard_map/all_to_all | solution.py:672
  74.5 1.7 collective-permute-start.14
  80.3 14.5 %shard_map.306 = (bf16[768,768]{1,0:T(8,128)(2,1)}, bf16[3,768,768]{2,1,0:T(8,128)(2,1)}, bf16[36,256,128]{2,1,0:T(8,128)(2,1)}, bf16[768,768]{1,0:T(8,128)(2,1)...) custom-call(s32[32]{0:T(128)} %stack.539.slots.slots_a.slots_b, bf16[768,768]{1,0:T(8,128)(2,1)} %bitcast.268, ...), custom_call_target="tpu_custom_call" | custom-call | flops 10871635968 | bytes 20971520 | tf_op jit(solution)/shard_map/pallas_call | solution.py:461
  94.8 8.3 %collective-permute-done.13 = bf16[192,768]{1,0:T(8,128)(2,1)} collective-permute-done((bf16[192,768]{1,0:T(8,128)(2,1)S(1)}, bf16[192,768]{1,0:T(8,128)(2,1)}, u32[]{:S(2)}, u32[]{:S(2)}) %collective-permute-start.13) | collective-permute-done | bytes 294944 | tf_op jit(solution)/shard_map/ppermute | solution.py:664
  103.2 1.8 collective-permute-start.19
  105.6 1.8 collective-permute-start.17
  110.2 17.6 %shard_map.307 = (bf16[768,3072]{1,0:T(8,128)(2,1)}, bf16[768,3072]{1,0:T(8,128)(2,1)}, bf16[8,96,768]{2,1,0:T(8,128)(2,1)}, bf16[8,96,768]{2,1,0:T(8,128)(2,1)}...) custom-call(s32[32]{0:T(128)} %stack.539.slots.slots_a.slots_b, s32[17]{0:T(128)} %stack.506.gpos, ...), custom_call_target="tpu_custom_call" | custom-call | flops 14495514624 | bytes 20971520 | tf_op jit(solution)/shard_map/pallas_call | solution.py:461
  128.7 2.3 collective-permute-done.21
  131.4 2.1 collective-permute-start.23
  135.8 17.0 %shard_map.308 = (bf16[768,3072]{1,0:T(8,128)(2,1)}, f32[4,768]{1,0:T(4,128)}, f32[8,768]{1,0:T(8,128)}, bf16[8,96,768]{2,1,0:T(8,128)(2,1)}, bf16[8,96,768]{2,1...) custom-call(s32[32]{0:T(128)} %stack.572.slots, s32[17]{0:T(128)} %stack.506.gpos, ...), custom_call_target="tpu_custom_call" | custom-call | flops 14495514624 | bytes 20971520 | tf_op jit(solution)/shard_map/pallas_call | solution.py:461
  157.7 18.8 %shard_map.309 = (f32[768,768]{1,0:T(8,128)}, bf16[768,768]{1,0:T(8,128)(2,1)}, bf16[3,768,768]{2,1,0:T(8,128)(2,1)}, f32[8,768]{1,0:T(8,128)}) custom-call(s32[32]{0:T(128)} %stack.539.slots.slots_a.slots_b, s32[32]{0:T(128)} %stack.539.slots.slots_a.slots_b, bf16[768,3072]{1,0:T(8,128)(2,1)} %get-tuple-element.242.dh_ref, bf16[768,768]{1,0:T(8,128)(2,1)} %bitcast.267, ...), custom_call_target="tpu_custom_call" | custom-call | flops 9059696640 | bytes 31457280 | tf_op jit(solution)/shard_map/pallas_call | solution.py:461
  176.9 2.3 collective-permute-start.34
  184.3 8.2 %shard_map.310 = (bf16[8,96,768]{2,1,0:T(8,128)(2,1)}, bf16[8,96,768]{2,1,0:T(8,128)(2,1)}, bf16[8,96,768]{2,1,0:T(8,128)(2,1)}, bf16[8,96,768]{2,1,0:T(8,128)(2,1)}) custom-call(s32[17]{0:T(128)} %stack.506.gpos, bf16[768,768]{1,0:T(8,128)(2,1)} %get-tuple-element.196.normed_ref, bf16[3,768,768]{2,1,0:T(8,128)(2,1)} %get-tuple-element.277.dt_ref, ...), custom_call_target="tpu_custom_call" | custom-call | flops 7247757312 | bytes 12582912 | tf_op jit(solution)/shard_map/pallas_call | solution.py:461
  196.4 2.4 collective-permute-start.43
  203.3 1.8 collective-permute-start.41
  205.1 10.2 %shard_map.311 = (bf16[768,768]{1,0:T(8,128)(2,1)}, f32[16,768]{1,0:T(8,128)}) custom-call(s32[32]{0:T(128)} %stack.539.slots.slots_a.slots_b, bf16[768,768]{1,0:T(8,128)(2,1)} %bitcast.269, f32[6,768]{1,0:T(8,128)} %reshape.329.emb_ref, f32[768,768]{1,0:T(8,128)} %get-tuple-element.276.dmid_ref, bf16[3,768,768]{2,1,0:T(8,128)(2,1)} %get-tuple-element.277.dt_ref, ...), custom_call_target="tpu_custom_call" | custom-call | flops 5435817984 | bytes 12582912 | tf_op jit(solution)/shard_map/pallas_call | solution.py:461
  216.9 2.0 add_convert_fusion.8
  222.1 3.1 %all-to-all-start.3 = ((f32[32,1,1926]{2,1,0:T(1,128)}), f32[32,1,1926]{2,1,0:T(1,128)S(1)}, u32[]{:S(2)}, u32[]{:S(2)}) async-start(f32[32,1,1926]{2,1,0:T(1,128)} %all_to_all.20), calls=%async_computation.3 | async-start | bytes 524288 | tf_op jit(solution)/shard_map/all_to_all | solution.py:909
  229.1 2.4 collective-permute-start.48
  233.1 2.5 all-to-all-done.3
  236.7 3.5 %all-to-all-start.2 = ((bf16[4,192,768]{2,1,0:T(8,128)(2,1)}), bf16[4,192,768]{2,1,0:T(8,128)(2,1)S(1)}, u32[]{:S(2)}, u32[]{:S(2)}) async-start(bf16[4,192,768]{2,1,0:T(8,128)(2,1)} %broadcast_in_dim.13), calls=%async_computation.2 | async-start | bytes 2359296 | tf_op jit(solution)/shard_map/all_to_all | solution.py:672
  240.2 9.7 %shard_map.312 = bf16[768,768]{1,0:T(8,128)(2,1)} custom-call(s32[32]{0:T(128)} %stack.572.slots, bf16[768,3072]{1,0:T(8,128)(2,1)} %get-tuple-element.310.act_ref, f32[768,768]{1,0:T(8,128)} %get-tuple-element.243.middle_ref, f32[8,768]{1,0:T(8,128)} %reshape.312.vec_ref, bf16[4,96,768]{2,1,0:T(8,128)(2,1)} %pad_maximum_fusion.4.rest_0_, ...), custom_call_target="tpu_custom_call" | custom-call | flops 7247757312 | bytes 12582912 | tf_op jit(solution)/shard_map/pallas_call | solution.py:461
  253.1 3.2 %all-to-all-done.2 = bf16[4,192,768]{2,1,0:T(8,128)(2,1)S(1)} async-done(((bf16[4,192,768]{2,1,0:T(8,128)(2,1)}), bf16[4,192,768]{2,1,0:T(8,128)(2,1)S(1)}, u32[]{:S(2)}, u32[]{:S(2)}) %all-to-all-start.2) | async-done | bytes 1179680 | tf_op jit(solution)/shard_map/all_to_all | solution.py:672
  262.5 1.7 collective-permute-done.51
  264.2 2.0 collective-permute-done.50
  (272 shorter events, 78.2 us)
Async XLA Ops:
  27.2 38.4 %all-to-all-start = ((bf16[4,4,96,768]{3,2,1,0:T(8,128)(2,1)}), bf16[4,4,96,768]{3,2,1,0:T(8,128)(2,1)S(1)}, u32[]{:S(2)}, u32[]{:S(2)}) async-start(bf16[4,4,96,768]{3,2,1,0:T(8,128)(2,1)} %broadcast_in_dim.11), calls=%async_computation | async-start | bytes 4718592 | tf_op jit(solution)/shard_map/all_to_all | solution.py:672
  35.3 30.3 %collective-permute-start.5 = (bf16[192,768]{1,0:T(8,128)(2,1)S(1)}, bf16[192,768]{1,0:T(8,128)(2,1)}, u32[]{:S(2)}, u32[]{:S(2)}) collective-permute-start(bf16[192,768]{1,0:T(8,128)(2,1)S(1)} %pad_maximum_fusion.7), channel_id=1, source_target_pairs={{0,4},{1,5},{2,6},{3,7},{4,0},{5,1},{6,2},{7,3},{8,12},{9,13},{10,... | collective-permute-start | bytes 884744 | tf_op jit(solution)/shard_map/ppermute | solution.py:664
  37.2 28.4 %collective-permute-start.4 = (bf16[192,768]{1,0:T(8,128)(2,1)S(1)}, bf16[192,768]{1,0:T(8,128)(2,1)}, u32[]{:S(2)}, u32[]{:S(2)}) collective-permute-start(bf16[192,768]{1,0:T(8,128)(2,1)S(1)} %pad_maximum_fusion.7), channel_id=1, source_target_pairs={{0,2},{1,3},{2,4},{3,5},{4,6},{5,7},{6,0},{7,1},{8,10},{9,11},{10,... | collective-permute-start | bytes 884744 | tf_op jit(solution)/shard_map/ppermute | solution.py:664
  44.4 21.2 %collective-permute-start.8 = (bf16[16,768]{1,0:T(8,128)(2,1)S(1)}, bf16[16,768]{1,0:T(8,128)(2,1)S(1)}, u32[]{:S(2)}, u32[]{:S(2)}) collective-permute-start(bf16[16,768]{1,0:T(8,128)(2,1)S(1)} %get-tuple-element.189), channel_id=1, source_target_pairs={{0,4},{1,5},{2,6},{3,7},{4,0},{5,1},{6,2},{7,3},{8,12},{9,13},{10,... | collective-permute-start | bytes 73736 | tf_op jit(solution)/shard_map/ppermute | solution.py:664
  44.6 21.0 %collective-permute-start.7 = (bf16[16,768]{1,0:T(8,128)(2,1)S(1)}, bf16[16,768]{1,0:T(8,128)(2,1)S(1)}, u32[]{:S(2)}, u32[]{:S(2)}) collective-permute-start(bf16[16,768]{1,0:T(8,128)(2,1)S(1)} %get-tuple-element.189), channel_id=1, source_target_pairs={{0,2},{1,3},{2,4},{3,5},{4,6},{5,7},{6,0},{7,1},{8,10},{9,11},{10,... | collective-permute-start | bytes 73736 | tf_op jit(solution)/shard_map/ppermute | solution.py:664
  46.9 18.7 %collective-permute-start.9 = (bf16[16,768]{1,0:T(8,128)(2,1)S(1)}, bf16[16,768]{1,0:T(8,128)(2,1)S(1)}, u32[]{:S(2)}, u32[]{:S(2)}) collective-permute-start(bf16[16,768]{1,0:T(8,128)(2,1)S(1)} %get-tuple-element.189), channel_id=1, source_target_pairs={{0,6},{1,7},{2,0},{3,1},{4,2},{5,3},{6,4},{7,5},{8,14},{9,15},{10,... | collective-permute-start | bytes 73736 | tf_op jit(solution)/shard_map/ppermute | solution.py:664
  70.0 33.1 %all-to-all-start.1 = ((bf16[4,4,96,768]{3,2,1,0:T(8,128)(2,1)}), bf16[4,4,96,768]{3,2,1,0:T(8,128)(2,1)}, u32[]{:S(2)}, u32[]{:S(2)}) async-start(bf16[4,4,96,768]{3,2,1,0:T(8,128)(2,1)} %broadcast_in_dim.12), calls=%async_computation.1 | async-start | bytes 4718592 | tf_op jit(solution)/shard_map/all_to_all | solution.py:672
  74.5 20.3 %collective-permute-start.14 = (bf16[192,768]{1,0:T(8,128)(2,1)S(1)}, bf16[192,768]{1,0:T(8,128)(2,1)}, u32[]{:S(2)}, u32[]{:S(2)}) collective-permute-start(bf16[192,768]{1,0:T(8,128)(2,1)S(1)} %slice.393), channel_id=1, source_target_pairs={{0,6},{1,7},{2,0},{3,1},{4,2},{5,3},{6,4},{7,5},{8,14},{9,15},{10,... | collective-permute-start | bytes 884744 | tf_op jit(solution)/shard_map/ppermute | solution.py:664
  76.2 27.0 %collective-permute-start.13 = (bf16[192,768]{1,0:T(8,128)(2,1)S(1)}, bf16[192,768]{1,0:T(8,128)(2,1)}, u32[]{:S(2)}, u32[]{:S(2)}) collective-permute-start(bf16[192,768]{1,0:T(8,128)(2,1)S(1)} %slice.393), channel_id=1, source_target_pairs={{0,4},{1,5},{2,6},{3,7},{4,0},{5,1},{6,2},{7,3},{8,12},{9,13},{10,... | collective-permute-start | bytes 884744 | tf_op jit(solution)/shard_map/ppermute | solution.py:664
  76.9 26.2 %collective-permute-start.12 = (bf16[192,768]{1,0:T(8,128)(2,1)S(1)}, bf16[192,768]{1,0:T(8,128)(2,1)}, u32[]{:S(2)}, u32[]{:S(2)}) collective-permute-start(bf16[192,768]{1,0:T(8,128)(2,1)S(1)} %slice.393), channel_id=1, source_target_pairs={{0,2},{1,3},{2,4},{3,5},{4,6},{5,7},{6,0},{7,1},{8,10},{9,11},{10,... | collective-permute-start | bytes 884744 | tf_op jit(solution)/shard_map/ppermute | solution.py:664
  79.1 24.1 %collective-permute-start.15 = (bf16[4,96,768]{2,1,0:T(8,128)(2,1)}, bf16[4,96,768]{2,1,0:T(8,128)(2,1)}, u32[]{:S(2)}, u32[]{:S(2)}) collective-permute-start(bf16[4,96,768]{2,1,0:T(8,128)(2,1)} %pad_maximum_fusion.4.rest_0_), channel_id=1, source_target_pairs={{0,1},{1,0},{2,3},{3,2},{4,5},{5,4},{6,7},{7,6},{8,9},{9,8},{10,11... | collective-permute-start | bytes 1769480 | tf_op jit(solution)/shard_map/ppermute | solution.py:648
  103.2 24.7 %collective-permute-start.19 = (bf16[96,768]{1,0:T(8,128)(2,1)S(1)}, bf16[96,768]{1,0:T(8,128)(2,1)S(1)}, u32[]{:S(2)}, u32[]{:S(2)}) collective-permute-start(bf16[96,768]{1,0:T(8,128)(2,1)S(1)} %get-tuple-element.225), channel_id=1, source_target_pairs={{0,6},{1,7},{2,0},{3,1},{4,2},{5,3},{6,4},{7,5},{8,14},{9,15},{10,... | collective-permute-start | bytes 442376 | tf_op jit(solution)/shard_map/ppermute | solution.py:664
  105.0 22.9 %collective-permute-start.18 = (bf16[96,768]{1,0:T(8,128)(2,1)S(1)}, bf16[96,768]{1,0:T(8,128)(2,1)S(1)}, u32[]{:S(2)}, u32[]{:S(2)}) collective-permute-start(bf16[96,768]{1,0:T(8,128)(2,1)S(1)} %get-tuple-element.225), channel_id=1, source_target_pairs={{0,4},{1,5},{2,6},{3,7},{4,0},{5,1},{6,2},{7,3},{8,12},{9,13},{10,... | collective-permute-start | bytes 442376 | tf_op jit(solution)/shard_map/ppermute | solution.py:664
  105.6 22.3 %collective-permute-start.17 = (bf16[96,768]{1,0:T(8,128)(2,1)S(1)}, bf16[96,768]{1,0:T(8,128)(2,1)S(1)}, u32[]{:S(2)}, u32[]{:S(2)}) collective-permute-start(bf16[96,768]{1,0:T(8,128)(2,1)S(1)} %get-tuple-element.225), channel_id=1, source_target_pairs={{0,2},{1,3},{2,4},{3,5},{4,6},{5,7},{6,0},{7,1},{8,10},{9,11},{10,... | collective-permute-start | bytes 442376 | tf_op jit(solution)/shard_map/ppermute | solution.py:664
  108.8 19.1 %collective-permute-start.20 = (bf16[8,96,768]{2,1,0:T(8,128)(2,1)S(1)}, bf16[8,96,768]{2,1,0:T(8,128)(2,1)S(1)}, u32[]{:S(2)}, u32[]{:S(2)}) collective-permute-start(bf16[8,96,768]{2,1,0:T(8,128)(2,1)S(1)} %bitcast.235), channel_id=1, source_target_pairs={{0,1},{1,0},{2,3},{3,2},{4,5},{5,4},{6,7},{7,6},{8,9},{9,8},{10,11... | collective-permute-start | bytes 3538952 | tf_op jit(solution)/shard_map/ppermute | solution.py:648
  128.7 24.2 %collective-permute-start.25 = (bf16[8,96,768]{2,1,0:T(8,128)(2,1)}, bf16[8,96,768]{2,1,0:T(8,128)(2,1)S(1)}, u32[]{:S(2)}, u32[]{:S(2)}) collective-permute-start(bf16[8,96,768]{2,1,0:T(8,128)(2,1)} %get-tuple-element.238), channel_id=1, source_target_pairs={{0,1},{1,0},{2,3},{3,2},{4,5},{5,4},{6,7},{7,6},{8,9},{9,8},{10,11... | collective-permute-start | bytes 3538952 | tf_op jit(solution)/shard_map/ppermute | solution.py:648
  131.4 21.4 %collective-permute-start.23 = (bf16[4,96,768]{2,1,0:T(8,128)(2,1)S(1)}, bf16[4,96,768]{2,1,0:T(8,128)(2,1)S(1)}, u32[]{:S(2)}, u32[]{:S(2)}) collective-permute-start(bf16[4,96,768]{2,1,0:T(8,128)(2,1)S(1)} %get-tuple-element.236), channel_id=1, source_target_pairs={{0,8},{8,0},{16,24},{24,16},{1,9},{9,1},{17,25},{25,17},{2,10},{10... | collective-permute-start | bytes 1769480 | tf_op jit(solution)/shard_map/ppermute | solution.py:652
  133.5 19.3 %collective-permute-start.24 = (bf16[4,96,768]{2,1,0:T(8,128)(2,1)S(1)}, bf16[4,96,768]{2,1,0:T(8,128)(2,1)S(1)}, u32[]{:S(2)}, u32[]{:S(2)}) collective-permute-start(bf16[4,96,768]{2,1,0:T(8,128)(2,1)S(1)} %get-tuple-element.237), channel_id=1, source_target_pairs={{0,16},{8,24},{16,0},{24,8},{1,17},{9,25},{17,1},{25,9},{2,18},{10... | collective-permute-start | bytes 1769480 | tf_op jit(solution)/shard_map/ppermute | solution.py:656
  153.2 23.3 %collective-permute-start.30 = (bf16[2,96,768]{2,1,0:T(8,128)(2,1)S(1)}, bf16[2,96,768]{2,1,0:T(8,128)(2,1)S(1)}, u32[]{:S(2)}, u32[]{:S(2)}) collective-permute-start(bf16[2,96,768]{2,1,0:T(8,128)(2,1)S(1)} %get-tuple-element.330), channel_id=1, source_target_pairs={{0,8},{8,0},{16,24},{24,16},{1,9},{9,1},{17,25},{25,17},{2,10},{10... | collective-permute-start | bytes 884744 | tf_op jit(solution)/shard_map/ppermute | solution.py:652
  153.8 22.7 %collective-permute-start.29 = (bf16[2,96,768]{2,1,0:T(8,128)(2,1)S(1)}, bf16[2,96,768]{2,1,0:T(8,128)(2,1)S(1)}, u32[]{:S(2)}, u32[]{:S(2)}) collective-permute-start(bf16[2,96,768]{2,1,0:T(8,128)(2,1)S(1)} %get-tuple-element.331), channel_id=1, source_target_pairs={{0,16},{8,24},{16,0},{24,8},{1,17},{9,25},{17,1},{25,9},{2,18},{10... | collective-permute-start | bytes 884744 | tf_op jit(solution)/shard_map/ppermute | solution.py:656
  154.5 25.4 %collective-permute-start.31 = (bf16[8,96,768]{2,1,0:T(8,128)(2,1)}, bf16[8,96,768]{2,1,0:T(8,128)(2,1)S(1)}, u32[]{:S(2)}, u32[]{:S(2)}) collective-permute-start(bf16[8,96,768]{2,1,0:T(8,128)(2,1)} %get-tuple-element.262), channel_id=1, source_target_pairs={{0,1},{1,0},{2,3},{3,2},{4,5},{5,4},{6,7},{7,6},{8,9},{9,8},{10,11... | collective-permute-start | bytes 3538952 | tf_op jit(solution)/shard_map/ppermute | solution.py:648
  156.3 20.2 %collective-permute-start.27 = (bf16[4,96,768]{2,1,0:T(8,128)(2,1)S(1)}, bf16[4,96,768]{2,1,0:T(8,128)(2,1)S(1)}, u32[]{:S(2)}, u32[]{:S(2)}) collective-permute-start(bf16[4,96,768]{2,1,0:T(8,128)(2,1)S(1)} %get-tuple-element.247), channel_id=1, source_target_pairs={{0,8},{8,0},{16,24},{24,16},{1,9},{9,1},{17,25},{25,17},{2,10},{10... | collective-permute-start | bytes 1769480 | tf_op jit(solution)/shard_map/ppermute | solution.py:652
  156.9 19.6 %collective-permute-start.28 = (bf16[4,96,768]{2,1,0:T(8,128)(2,1)S(1)}, bf16[4,96,768]{2,1,0:T(8,128)(2,1)S(1)}, u32[]{:S(2)}, u32[]{:S(2)}) collective-permute-start(bf16[4,96,768]{2,1,0:T(8,128)(2,1)S(1)} %get-tuple-element.248), channel_id=1, source_target_pairs={{0,16},{8,24},{16,0},{24,8},{1,17},{9,25},{17,1},{25,9},{2,18},{10... | collective-permute-start | bytes 1769480 | tf_op jit(solution)/shard_map/ppermute | solution.py:656
  176.9 15.6 %collective-permute-start.34 = (bf16[96,768]{1,0:T(8,128)(2,1)S(1)}, bf16[96,768]{1,0:T(8,128)(2,1)S(1)}, u32[]{:S(2)}, u32[]{:S(2)}) collective-permute-start(bf16[96,768]{1,0:T(8,128)(2,1)S(1)} %get-tuple-element.363), channel_id=1, source_target_pairs={{0,6},{1,7},{2,0},{3,1},{4,2},{5,3},{6,4},{7,5},{8,14},{9,15},{10,... | collective-permute-start | bytes 442376 | tf_op jit(solution)/shard_map/ppermute | solution.py:664
  196.4 19.1 %collective-permute-start.43 = (bf16[96,768]{1,0:T(8,128)(2,1)}, bf16[96,768]{1,0:T(8,128)(2,1)S(1)}, u32[]{:S(2)}, u32[]{:S(2)}) collective-permute-start(bf16[96,768]{1,0:T(8,128)(2,1)} %get-tuple-element.359), channel_id=1, source_target_pairs={{0,6},{1,7},{2,0},{3,1},{4,2},{5,3},{6,4},{7,5},{8,14},{9,15},{10,... | collective-permute-start | bytes 442376 | tf_op jit(solution)/shard_map/ppermute | solution.py:664
  198.8 16.7 %collective-permute-start.42 = (bf16[96,768]{1,0:T(8,128)(2,1)}, bf16[96,768]{1,0:T(8,128)(2,1)}, u32[]{:S(2)}, u32[]{:S(2)}) collective-permute-start(bf16[96,768]{1,0:T(8,128)(2,1)} %get-tuple-element.360), channel_id=1, source_target_pairs={{0,4},{1,5},{2,6},{3,7},{4,0},{5,1},{6,2},{7,3},{8,12},{9,13},{10,... | collective-permute-start | bytes 442376 | tf_op jit(solution)/shard_map/ppermute | solution.py:664
  201.3 15.1 %collective-permute-start.39 = (bf16[4,96,768]{2,1,0:T(8,128)(2,1)}, bf16[4,96,768]{2,1,0:T(8,128)(2,1)S(1)}, u32[]{:S(2)}, u32[]{:S(2)}) collective-permute-start(bf16[4,96,768]{2,1,0:T(8,128)(2,1)} %get-tuple-element.274), channel_id=1, source_target_pairs={{0,8},{8,0},{16,24},{24,16},{1,9},{9,1},{17,25},{25,17},{2,10},{10... | collective-permute-start | bytes 1769480 | tf_op jit(solution)/shard_map/ppermute | solution.py:652
  201.9 14.9 %collective-permute-start.40 = (bf16[4,96,768]{2,1,0:T(8,128)(2,1)}, bf16[4,96,768]{2,1,0:T(8,128)(2,1)}, u32[]{:S(2)}, u32[]{:S(2)}) collective-permute-start(bf16[4,96,768]{2,1,0:T(8,128)(2,1)} %get-tuple-element.275), channel_id=1, source_target_pairs={{0,16},{8,24},{16,0},{24,8},{1,17},{9,25},{17,1},{25,9},{2,18},{10... | collective-permute-start | bytes 1769480 | tf_op jit(solution)/shard_map/ppermute | solution.py:656
  229.1 24.0 %collective-permute-start.48 = (bf16[96,768]{1,0:T(8,128)(2,1)S(1)}, bf16[96,768]{1,0:T(8,128)(2,1)S(1)}, u32[]{:S(2)}, u32[]{:S(2)}) collective-permute-start(bf16[96,768]{1,0:T(8,128)(2,1)S(1)} %get-tuple-element.355), channel_id=1, source_target_pairs={{0,6},{1,7},{2,0},{3,1},{4,2},{5,3},{6,4},{7,5},{8,14},{9,15},{10,... | collective-permute-start | bytes 442376 | tf_op jit(solution)/shard_map/ppermute | solution.py:664
  231.5 21.6 %collective-permute-start.47 = (bf16[96,768]{1,0:T(8,128)(2,1)S(1)}, bf16[96,768]{1,0:T(8,128)(2,1)S(1)}, u32[]{:S(2)}, u32[]{:S(2)}) collective-permute-start(bf16[96,768]{1,0:T(8,128)(2,1)S(1)} %get-tuple-element.356), channel_id=1, source_target_pairs={{0,4},{1,5},{2,6},{3,7},{4,0},{5,1},{6,2},{7,3},{8,12},{9,13},{10,... | collective-permute-start | bytes 442376 | tf_op jit(solution)/shard_map/ppermute | solution.py:664
  231.5 21.6 %collective-permute-start.46 = (bf16[96,768]{1,0:T(8,128)(2,1)S(1)}, bf16[96,768]{1,0:T(8,128)(2,1)S(1)}, u32[]{:S(2)}, u32[]{:S(2)}) collective-permute-start(bf16[96,768]{1,0:T(8,128)(2,1)S(1)} %get-tuple-element.357), channel_id=1, source_target_pairs={{0,2},{1,3},{2,4},{3,5},{4,6},{5,7},{6,0},{7,1},{8,10},{9,11},{10,... | collective-permute-start | bytes 442376 | tf_op jit(solution)/shard_map/ppermute | solution.py:664
  236.7 19.7 %all-to-all-start.2 = ((bf16[4,192,768]{2,1,0:T(8,128)(2,1)}), bf16[4,192,768]{2,1,0:T(8,128)(2,1)S(1)}, u32[]{:S(2)}, u32[]{:S(2)}) async-start(bf16[4,192,768]{2,1,0:T(8,128)(2,1)} %broadcast_in_dim.13), calls=%async_computation.2 | async-start | bytes 2359296 | tf_op jit(solution)/shard_map/all_to_all | solution.py:672
  (61 other events, 466.4 us)
